TPU v7x, 256 devices: a whole 4x4x8 slice. The times are simulated.
256 devices in a mesh: space: 32 (over x, y, core), chan: 8 (over z).
Axes of the slice: x: 4, y: 4, z: 8, core: 2. Of those that a mesh axis runs over, the one named last changes fastest.
Arguments:
- features: bfloat16 [64, 16, 16, 1024], P('space', None, None, 'chan'), may hold values from -6 to 6
- filters: bfloat16 [1024, 27, 1024], P('space', None, 'chan'), may hold values from -0.0390625 to 0.0390625
- conv_bias: float32 [1024], P('chan'), may hold values from -3 to 3
- cotangent: bfloat16 [64, 16, 16, 1024], P('space', None, None, 'chan'), may hold values from -6 to 6
Outputs:
- activated: bfloat16 [64, 16, 16, 1024], P('space', None, None, 'chan')
- grad_input: bfloat16 [64, 16, 16, 1024], P('space', None, None, 'chan')
- grad_filters: float32 [1024, 27, 1024], P('space', None, 'chan')
- grad_bias: float32 [1024], P('chan')
All inputs are finite; a program needn't handle non-finite values.
Results may differ from a plain program's by a relative error of at most 0.007.
Values may be sent and summed in bfloat16 or wider, within the bound.
No kernel may reach another device: no remote copies, remote signals or barrier semaphores. Data moves between devices by JAX's collectives and lax.ppermute only.
A program may use at most 128 MiB of HBM per device.

v0:
```python
import math

import jax
import jax.numpy as jnp
from jax import lax
from jax.sharding import PartitionSpec as P

GRID = 16


KAPPA = 0.7978845608028654
CUBIC = 0.044715


def extended_2(cells, sides, width):
    for axis, dim in sides:
        count = lax.axis_size(axis)
        head = lax.slice_in_dim(cells, 0, width, axis=dim)
        tail = lax.slice_in_dim(cells, cells.shape[dim] - width, cells.shape[dim], axis=dim)
        cells = jnp.concatenate(
            [
                lax.ppermute(tail, axis, [(i, (i + 1) % count) for i in range(count)]),
                cells,
                lax.ppermute(head, axis, [((i + 1) % count, i) for i in range(count)]),
            ],
            axis=dim,
        )
    return cells


def gelu_pair(values):
    inner = KAPPA * (values + CUBIC * values * values * values)
    tangent = jnp.tanh(inner)
    output = 0.5 * values * (1.0 + tangent)
    slope = 0.5 * (1.0 + tangent) + 0.5 * values * (1.0 - tangent * tangent) * KAPPA * (
        1.0 + 3.0 * CUBIC * values * values
    )
    return (output, slope)


def plane_masks(first_plane, planes_count):
    depth_index = (first_plane + jnp.arange(planes_count, dtype=jnp.int32) - 1) % GRID
    low_mask = (depth_index != 0).astype(jnp.bfloat16)[:, None, None, None]
    high_mask = (depth_index != GRID - 1).astype(jnp.bfloat16)[:, None, None, None]
    return (low_mask, high_mask)


def depth_copies(padded, planes_count, masks):
    lower = padded[0:planes_count] * masks[0]
    middle = padded[1 : planes_count + 1]
    upper = padded[2 : planes_count + 2] * masks[1]
    return (lower, middle, upper)


def tap_slice(copies, tap_index):
    depth_off = tap_index // 9
    height_off = tap_index // 3 % 3
    width_off = tap_index % 3
    return copies[depth_off][:, height_off : height_off + GRID, width_off : width_off + GRID, :]


def side_pad(extended):
    return jnp.pad(extended, ((0, 0), (1, 1), (1, 1), (0, 0)))


def on_device(features, filters, conv_bias, cotangent):
    slab_planes = features.shape[0]
    space_count = lax.axis_size("space")
    first_plane = lax.axis_index("space") * slab_planes
    masks = plane_masks(first_plane, slab_planes)
    full_planes = lax.all_gather(features, "chan", axis=3, tiled=True)
    extended = extended_2(full_planes, (("space", 0),), 1)
    feature_copies = depth_copies(side_pad(extended), slab_planes, masks)
    cell_count = slab_planes * GRID * GRID
    out_local = filters.shape[2]
    summed_init = jnp.zeros((cell_count, out_local), jnp.float32)
    running = summed_init
    filter_piece = lax.all_gather(filters, "space", axis=0, tiled=True)
    row_count = filter_piece.shape[0]
    selected = tuple((copy_part for copy_part in feature_copies))
    for forward_tap_index in range(27):
        window_cells = tap_slice(selected, forward_tap_index).reshape(cell_count, row_count)
        running = running + jnp.dot(
            window_cells, filter_piece[:, forward_tap_index, :], preferred_element_type=jnp.float32
        )
    pre_act = running + conv_bias[None, :]
    output, slope = gelu_pair(pre_act)
    activated = output.astype(jnp.bfloat16).reshape(slab_planes, GRID, GRID, out_local)
    grad_pre = (cotangent.astype(jnp.float32).reshape(cell_count, out_local) * slope).astype(
        jnp.bfloat16
    )
    grad_planes = grad_pre.reshape(slab_planes, GRID, GRID, out_local)
    grad_ext = extended_2(grad_planes, (("space", 0),), 1)
    grad_copies = depth_copies(side_pad(grad_ext), slab_planes, masks)
    grad_columns = jnp.concatenate(
        [
            tap_slice(grad_copies, 26 - tap_index).reshape(cell_count, out_local)
            for tap_index in range(27)
        ],
        axis=1,
    )
    filter_piece = lax.all_gather(filters, "space", axis=0, tiled=True)
    row_count = filter_piece.shape[0]
    flat_filters = filter_piece.reshape(row_count, 27 * out_local)
    partial_input = lax.dot_general(
        grad_columns, flat_filters, (((1,), (1,)), ((), ())), preferred_element_type=jnp.float32
    )
    grad_input = (
        lax.psum_scatter(partial_input, "chan", scatter_dimension=1, tiled=True)
        .astype(jnp.bfloat16)
        .reshape(slab_planes, GRID, GRID, -1)
    )
    scale = 1.0 / math.sqrt(cell_count * space_count)
    row_count = filters.shape[0] * lax.axis_size("space")
    selected = tuple((copy_part for copy_part in feature_copies))
    terms = []
    for tap_index in range(27):
        window_cells = tap_slice(selected, tap_index).reshape(cell_count, row_count)
        terms.append(
            lax.dot_general(
                window_cells, grad_pre, (((0,), (0,)), ((), ())), preferred_element_type=jnp.float32
            )
            * scale
        )
    grad_filters = lax.psum_scatter(
        jnp.stack(terms, axis=1), "space", scatter_dimension=0, tiled=True
    )
    grad_bias = lax.psum(jnp.sum(grad_pre.astype(jnp.float32), axis=0) * scale, "space")
    return (activated, grad_input, grad_filters, grad_bias)


def solution(mesh):
    return jax.shard_map(
        on_device,
        mesh=mesh,
        in_specs=(
            P("space", None, None, "chan"),
            P("space", None, "chan"),
            P("chan"),
            P("space", None, None, "chan"),
        ),
        out_specs=(
            P("space", None, None, "chan"),
            P("space", None, None, "chan"),
            P("space", None, "chan"),
            P("chan"),
        ),
        check_vma=False,
    )
```

profile of v0, /device:TPU:16, one launch (start us, length us, event | category | flops | bytes accessed | tf_op | source)
XLA Modules:
  0.0 341.4 jit_solution(808731912955625859)
XLA Ops:
  8.7 43.5 %all-gather.3.cloned.1.call-done = bf16[2,16,16,1024]{3,2,1,0:T(8,128)(2,1)} async-done(((bf16[2,16,16,128]{3,2,1,0:T(8,128)(2,1)}), bf16[2,16,16,1024]{3,2,1,0:T(8,128)(2,1)}) %all-gather.3.cloned.1.call-update) | async-done | bytes 1048592 | tf_op jit(solution)/shard_map/all_gather | solution.py:71
  52.1 1.3 fusion.96
  53.5 1.7 collective-permute-start.1
  55.3 6.8 %collective-permute-done = bf16[1,16,16,1024]{3,2,1,0:T(8,128)(2,1)S(1)} collective-permute-done((bf16[1,16,16,1024]{3,2,1,0:T(8,128)(2,1)S(1)}, bf16[1,16,16,1024]{3,2,1,0:T(8,128)(2,1)S(1)}, u32[]{:S(2)}, u32[]{:S(2)}) %collective-permute-start) | collective-permute-done | bytes 524320 | tf_op jit(solution)/shard_map/ppermute | solution.py:22
  62.1 2.6 select_maximum_fusion
  65.0 4.1 %fusion.93 = (bf16[2,16,16,1024]{3,2,1,0:T(8,128)(2,1)}, bf16[2,16,16,1024]{3,2,1,0:T(8,128)(2,1)S(1)}, bf16[2,16,16,1024]{3,2,1,0:T(8,128)(2,1)}, bf16[2,16,16,...) fusion(bf16[4,18,18,1024]{3,2,1,0:T(8,128)(2,1)S(1)} %select_ma, ...), kind=kLoop, calls=%fused_computation.217 | loop fusion | bytes 16777216 | tf_op jit(solution)/shard_map/slice | solution.py:59
  69.1 4.7 %fusion.95 = (bf16[2,16,16,1024]{3,2,1,0:T(8,128)(2,1)}, bf16[2,16,16,1024]{3,2,1,0:T(8,128)(2,1)}, bf16[2,16,16,1024]{3,2,1,0:T(8,128)(2,1)}, bf16[2,16,16,1024...) fusion(bf16[2,18,18,1024]{3,2,1,0:T(8,128)(2,1)S(1)} %get-tuple, ...), kind=kLoop, calls=%fused_computation.219 | loop fusion | bytes 18874368 | tf_op jit(solution)/shard_map/slice | solution.py:59
  73.8 4.7 %fusion.94 = (bf16[2,16,16,1024]{3,2,1,0:T(8,128)(2,1)}, bf16[2,16,16,1024]{3,2,1,0:T(8,128)(2,1)S(1)}, bf16[2,16,16,1024]{3,2,1,0:T(8,128)(2,1)}, bf16[2,16,16,...) fusion(bf16[2,18,18,1024]{3,2,1,0:T(8,128)(2,1)S(1)} %get-tuple, ...), kind=kLoop, calls=%fused_computation.218 | loop fusion | bytes 18874368 | tf_op jit(solution)/shard_map/slice | solution.py:59
  78.5 35.1 %all-gather.5.cloned.1.call-done = bf16[1024,27,128]{2,0,1:T(8,128)(2,1)} async-done(((bf16[32,27,128]{2,0,1:T(8,128)(2,1)}), bf16[1024,27,128]{2,0,1:T(8,128)(2,1)}) %all-gather.5.cloned.1.call-update) | async-done | bytes 7077904 | tf_op jit(solution)/shard_map/all_gather | solution.py:78
  113.6 1.5 fusion.86
  115.2 2.0 fusion.83
  117.2 1.8 fusion.84
  119.0 1.7 fusion.85
  120.7 1.8 fusion.87
  122.5 1.7 fusion.88
  134.7 1.3 fusion.7
  136.0 1.6 collective-permute-start.3
  138.0 1.3 fusion.9
  139.3 1.3 fusion.11
  140.6 1.3 fusion.13
  141.8 1.3 fusion.15
  143.1 1.3 fusion.17
  144.4 1.3 fusion.19
  145.6 1.3 fusion.21
  146.9 1.3 fusion.23
  148.2 1.3 fusion.25
  149.5 1.3 fusion.27
  150.7 10.2 %copy.11 = bf16[1024,27,128]{0,2,1:T(8,128)(2,1)} copy(bf16[1024,27,128]{2,0,1:T(8,128)(2,1)} %all-gather.5.cloned.1.call-done) | data formatting | bytes 14155776 | tf_op jit(solution)/shard_map/all_gather | solution.py:78
  164.3 5.3 %fusion.101 = f32[512,1024]{1,0:T(8,128)} fusion(bf16[512,3456]{1,0:T(8,128)(2,1)S(1)} %constant_dynamic-update-slice_fusion, bf16[1024,3456]{0,1:T(8,128)(2,1)S(1)} %bitcast.394), kind=kOutput, calls=%fused_computation.225 | convolution fusion | flops 3623878656 | bytes 12713984 | tf_op jit(solution)/shard_map/dot_general | solution.py:105
  169.9 2.6 fusion.29
  172.5 2.6 fusion.31
  175.1 1.3 fusion.33
  176.5 2.6 fusion.35
  179.1 1.3 fusion.37
  180.4 1.3 fusion.39
  181.7 1.3 fusion.41
  183.0 1.3 fusion.43
  184.3 1.3 fusion.45
  185.6 1.3 fusion.47
  186.8 1.3 fusion.49
  188.1 1.3 fusion.51
  189.4 1.3 fusion.53
  190.7 1.3 fusion.55
  192.0 1.3 fusion.57
  193.3 1.3 fusion.59
  194.6 60.9 %psum.7 = f32[128]{0:T(128)} all-reduce(f32[128]{0:T(128)S(1)} %broadcast_multiply_fusion), channel_id=1, replica_groups=mesh['space'=32,'chan'=8] {'space'}, use_global_device_ids=true, to_apply=%region_3.4 | all-reduce | flops 128 | bytes 1024 | tf_op jit(solution)/shard_map/psum | solution.py:128
  255.5 1.6 convert_element_type.35
  257.1 77.6 %reduce-scatter.5.cloned.1.call-done = f32[32,27,128]{2,0,1:T(8,128)} async-done(((f32[1024,27,128]{2,0,1:T(8,128)}), f32[32,27,128]{2,0,1:T(8,128)}) %reduce-scatter.5.cloned.1.call-update) | async-done | bytes 442384 | tf_op jit(solution)/shard_map/reduce_scatter | solution.py:125
  (144 shorter events, 15.8 us)
Async XLA Ops:
  7.2 45.0 %all-gather.3.cloned.1.call-start = ((), (), s32[]{:S(2)}) async-start(), calls=%async_computation.2 | async-start | bytes 1179648 | tf_op jit(solution)/shard_map/all_gather | solution.py:71
  7.9 105.7 %all-gather.5.cloned.1.call-start = ((), (), s32[]{:S(2)}) async-start(), calls=%async_computation.3 | async-start | bytes 7299072 | tf_op jit(solution)/shard_map/all_gather | solution.py:78
  8.6 246.8 %reduce-scatter.3.cloned.1.call-start = ((), (), s32[]{:S(2)}) async-start(), calls=%async_computation.4 | async-start | bytes 2359296 | tf_op jit(solution)/shard_map/reduce_scatter | solution.py:109
  53.4 8.7 %collective-permute-start = (bf16[1,16,16,1024]{3,2,1,0:T(8,128)(2,1)S(1)}, bf16[1,16,16,1024]{3,2,1,0:T(8,128)(2,1)S(1)}, u32[]{:S(2)}, u32[]{:S(2)}) collective-permute-start(bf16[1,16,16,1024]{3,2,1,0:T(8,128)(2,1)S(1)} %get-tuple-element.34), channel_id=1, source_target_pairs={{0,8},{8,16},{16,24},{24,32},{32,40},{40,48},{48,56},{56,64},{64,7... | collective-permute-start | bytes 1572872 | tf_op jit(solution)/shard_map/ppermute | solution.py:22
  53.5 8.6 %collective-permute-start.1 = (bf16[1,16,16,1024]{3,2,1,0:T(8,128)(2,1)S(1)}, bf16[1,16,16,1024]{3,2,1,0:T(8,128)(2,1)S(1)}, u32[]{:S(2)}, u32[]{:S(2)}) collective-permute-start(bf16[1,16,16,1024]{3,2,1,0:T(8,128)(2,1)S(1)} %get-tuple-element.35), channel_id=1, source_target_pairs={{8,0},{16,8},{24,16},{32,24},{40,32},{48,40},{56,48},{64,56},{72,6... | collective-permute-start | bytes 1572872 | tf_op jit(solution)/shard_map/ppermute | solution.py:24
  73.8 39.8 %copy-start.1 = (bf16[2,16,16,1024]{3,2,1,0:T(8,128)(2,1)S(1)}, bf16[2,16,16,1024]{3,2,1,0:T(8,128)(2,1)}, u32[]{:S(2)}) copy-start(bf16[2,16,16,1024]{3,2,1,0:T(8,128)(2,1)} %all-gather.3.cloned.1.call-done) | copy-start | bytes 3145732
  113.6 8.9 %copy-start = (bf16[1024,27,128]{2,0,1:T(8,128)(2,1)S(1)}, bf16[1024,27,128]{2,0,1:T(8,128)(2,1)}, u32[]{:S(2)}) copy-start(bf16[1024,27,128]{2,0,1:T(8,128)(2,1)} %all-gather.5.cloned.1.call-done) | copy-start | bytes 21233668
  113.6 10.7 %copy-start.18 = (bf16[2,16,16,1024]{3,2,1,0:T(8,128)(2,1)S(1)}, bf16[2,16,16,1024]{3,2,1,0:T(8,128)(2,1)}, u32[]{:S(2)}) copy-start(bf16[2,16,16,1024]{3,2,1,0:T(8,128)(2,1)} %get-tuple-element.12) | copy-start | bytes 3145732
  113.6 11.1 %copy-start.26 = (bf16[2,16,16,1024]{3,2,1,0:T(8,128)(2,1)S(1)}, bf16[2,16,16,1024]{3,2,1,0:T(8,128)(2,1)}, u32[]{:S(2)}) copy-start(bf16[2,16,16,1024]{3,2,1,0:T(8,128)(2,1)} %get-tuple-element.32) | copy-start | bytes 3145732
  113.6 11.6 %copy-start.16 = (bf16[2,16,16,1024]{3,2,1,0:T(8,128)(2,1)S(1)}, bf16[2,16,16,1024]{3,2,1,0:T(8,128)(2,1)}, u32[]{:S(2)}) copy-start(bf16[2,16,16,1024]{3,2,1,0:T(8,128)(2,1)} %get-tuple-element.24) | copy-start | bytes 3145732
  113.6 12.1 %copy-start.27 = (bf16[2,16,16,1024]{3,2,1,0:T(8,128)(2,1)S(1)}, bf16[2,16,16,1024]{3,2,1,0:T(8,128)(2,1)}, u32[]{:S(2)}) copy-start(bf16[2,16,16,1024]{3,2,1,0:T(8,128)(2,1)} %get-tuple-element.33) | copy-start | bytes 3145732
  115.1 11.0 %copy-start.25 = (bf16[2,16,16,1024]{3,2,1,0:T(8,128)(2,1)S(1)}, bf16[2,16,16,1024]{3,2,1,0:T(8,128)(2,1)}, u32[]{:S(2)}) copy-start(bf16[2,16,16,1024]{3,2,1,0:T(8,128)(2,1)} %get-tuple-element.31) | copy-start | bytes 3145732
  117.2 9.4 %copy-start.24 = (bf16[2,16,16,1024]{3,2,1,0:T(8,128)(2,1)S(1)}, bf16[2,16,16,1024]{3,2,1,0:T(8,128)(2,1)}, u32[]{:S(2)}) copy-start(bf16[2,16,16,1024]{3,2,1,0:T(8,128)(2,1)} %get-tuple-element.30) | copy-start | bytes 3145732
  120.7 6.3 %copy-start.23 = (bf16[2,16,16,1024]{3,2,1,0:T(8,128)(2,1)S(1)}, bf16[2,16,16,1024]{3,2,1,0:T(8,128)(2,1)}, u32[]{:S(2)}) copy-start(bf16[2,16,16,1024]{3,2,1,0:T(8,128)(2,1)} %get-tuple-element.29) | copy-start | bytes 3145732
  122.5 5.0 %copy-start.22 = (bf16[2,16,16,1024]{3,2,1,0:T(8,128)(2,1)S(1)}, bf16[2,16,16,1024]{3,2,1,0:T(8,128)(2,1)}, u32[]{:S(2)}) copy-start(bf16[2,16,16,1024]{3,2,1,0:T(8,128)(2,1)} %get-tuple-element.28) | copy-start | bytes 3145732
  124.3 3.7 %copy-start.21 = (bf16[2,16,16,1024]{3,2,1,0:T(8,128)(2,1)S(1)}, bf16[2,16,16,1024]{3,2,1,0:T(8,128)(2,1)}, u32[]{:S(2)}) copy-start(bf16[2,16,16,1024]{3,2,1,0:T(8,128)(2,1)} %get-tuple-element.27) | copy-start | bytes 3145732
  124.7 3.7 %copy-start.20 = (bf16[2,16,16,1024]{3,2,1,0:T(8,128)(2,1)S(1)}, bf16[2,16,16,1024]{3,2,1,0:T(8,128)(2,1)}, u32[]{:S(2)}) copy-start(bf16[2,16,16,1024]{3,2,1,0:T(8,128)(2,1)} %get-tuple-element.26) | copy-start | bytes 3145732
  125.2 3.7 %copy-start.19 = (bf16[2,16,16,1024]{3,2,1,0:T(8,128)(2,1)S(1)}, bf16[2,16,16,1024]{3,2,1,0:T(8,128)(2,1)}, u32[]{:S(2)}) copy-start(bf16[2,16,16,1024]{3,2,1,0:T(8,128)(2,1)} %get-tuple-element.25) | copy-start | bytes 3145732
  125.7 3.7 %copy-start.29 = (bf16[2,16,16,1024]{3,2,1,0:T(8,128)(2,1)S(1)}, bf16[2,16,16,1024]{3,2,1,0:T(8,128)(2,1)}, u32[]{:S(2)}) copy-start(bf16[2,16,16,1024]{3,2,1,0:T(8,128)(2,1)} %get-tuple-element.13) | copy-start | bytes 3145732
  126.6 3.2 copy-start.28
  127.1 3.3 copy-start.14
  127.5 3.3 copy-start.12
  128.0 3.2 copy-start.10
  128.4 3.2 copy-start.8
  128.9 3.2 copy-start.5
  129.4 3.2 copy-start.2
  130.3 3.2 copy-start.30
  130.3 3.2 copy-start.32
  130.3 3.2 copy-start.33
  136.0 25.0 %collective-permute-start.3 = (bf16[1,16,16,128]{3,2,1,0:T(8,128)(2,1)S(1)}, bf16[1,16,16,128]{3,2,1,0:T(8,128)(2,1)S(1)}, u32[]{:S(2)}, u32[]{:S(2)}) collective-permute-start(bf16[1,16,16,128]{3,2,1,0:T(8,128)(2,1)S(1)} %bitcast.425), channel_id=1, source_target_pairs={{8,0},{16,8},{24,16},{32,24},{40,32},{48,40},{56,48},{64,56},{72,6... | collective-permute-start | bytes 196616 | tf_op jit(solution)/shard_map/ppermute | solution.py:24
  137.6 23.4 %collective-permute-start.2 = (bf16[1,16,16,128]{3,2,1,0:T(8,128)(2,1)S(1)}, bf16[1,16,16,128]{3,2,1,0:T(8,128)(2,1)S(1)}, u32[]{:S(2)}, u32[]{:S(2)}) collective-permute-start(bf16[1,16,16,128]{3,2,1,0:T(8,128)(2,1)S(1)} %bitcast.424), channel_id=1, source_target_pairs={{0,8},{8,16},{16,24},{24,32},{32,40},{40,48},{48,56},{56,64},{64,7... | collective-permute-start | bytes 196616 | tf_op jit(solution)/shard_map/ppermute | solution.py:22
  161.1 2.2 slice-start
  161.6 2.8 slice-start.1
  169.6 165.1 %reduce-scatter.5.cloned.1.call-start = ((), (), s32[]{:S(2)}) async-start(), calls=%async_computation.5 | async-start | bytes 14598144 | tf_op jit(solution)/shard_map/reduce_scatter | solution.py:125
  169.8 9.2 %copy-start.7 = (bf16[2,16,16,1024]{3,2,1,0:T(8,128)(2,1)S(1)}, bf16[2,16,16,1024]{3,2,1,0:T(8,128)(2,1)}, u32[]{:S(2)}) copy-start(bf16[2,16,16,1024]{3,2,1,0:T(8,128)(2,1)} %get-tuple-element.9) | copy-start | bytes 3145732
  169.9 10.6 %copy-start.4 = (bf16[2,16,16,1024]{3,2,1,0:T(8,128)(2,1)S(1)}, bf16[2,16,16,1024]{3,2,1,0:T(8,128)(2,1)}, u32[]{:S(2)}) copy-start(bf16[2,16,16,1024]{3,2,1,0:T(8,128)(2,1)} %get-tuple-element.8) | copy-start | bytes 3145732
  169.9 13.1 %copy-start.17 = (bf16[2,16,16,1024]{3,2,1,0:T(8,128)(2,1)S(1)}, bf16[2,16,16,1024]{3,2,1,0:T(8,128)(2,1)}, u32[]{:S(2)}) copy-start(bf16[2,16,16,1024]{3,2,1,0:T(8,128)(2,1)} %get-tuple-element.24) | copy-start | bytes 3145732
  169.9 14.4 %copy-start.15 = (bf16[2,16,16,1024]{3,2,1,0:T(8,128)(2,1)S(1)}, bf16[2,16,16,1024]{3,2,1,0:T(8,128)(2,1)}, u32[]{:S(2)}) copy-start(bf16[2,16,16,1024]{3,2,1,0:T(8,128)(2,1)} %get-tuple-element.23) | copy-start | bytes 3145732
  172.5 13.0 %copy-start.13 = (bf16[2,16,16,1024]{3,2,1,0:T(8,128)(2,1)S(1)}, bf16[2,16,16,1024]{3,2,1,0:T(8,128)(2,1)}, u32[]{:S(2)}) copy-start(bf16[2,16,16,1024]{3,2,1,0:T(8,128)(2,1)} %get-tuple-element.22) | copy-start | bytes 3145732
  175.1 11.7 %copy-start.11 = (bf16[2,16,16,1024]{3,2,1,0:T(8,128)(2,1)S(1)}, bf16[2,16,16,1024]{3,2,1,0:T(8,128)(2,1)}, u32[]{:S(2)}) copy-start(bf16[2,16,16,1024]{3,2,1,0:T(8,128)(2,1)} %get-tuple-element.21) | copy-start | bytes 3145732
  176.5 11.6 %copy-start.9 = (bf16[2,16,16,1024]{3,2,1,0:T(8,128)(2,1)S(1)}, bf16[2,16,16,1024]{3,2,1,0:T(8,128)(2,1)}, u32[]{:S(2)}) copy-start(bf16[2,16,16,1024]{3,2,1,0:T(8,128)(2,1)} %get-tuple-element.20) | copy-start | bytes 3145732
  179.1 10.3 %copy-start.6 = (bf16[2,16,16,1024]{3,2,1,0:T(8,128)(2,1)S(1)}, bf16[2,16,16,1024]{3,2,1,0:T(8,128)(2,1)}, u32[]{:S(2)}) copy-start(bf16[2,16,16,1024]{3,2,1,0:T(8,128)(2,1)} %get-tuple-element.19) | copy-start | bytes 3145732
  180.4 10.3 %copy-start.3 = (bf16[2,16,16,1024]{3,2,1,0:T(8,128)(2,1)S(1)}, bf16[2,16,16,1024]{3,2,1,0:T(8,128)(2,1)}, u32[]{:S(2)}) copy-start(bf16[2,16,16,1024]{3,2,1,0:T(8,128)(2,1)} %get-tuple-element.18) | copy-start | bytes 3145732
  183.0 10.3 %copy-start.31 = (bf16[2,16,16,1024]{3,2,1,0:T(8,128)(2,1)S(1)}, bf16[2,16,16,1024]{3,2,1,0:T(8,128)(2,1)}, u32[]{:S(2)}) copy-start(bf16[2,16,16,1024]{3,2,1,0:T(8,128)(2,1)} %get-tuple-element.16) | copy-start | bytes 3145732
Sparse Core Ops, SparseCore 0:
  9.7 42.3 all-gather.2
  54.6 58.9 all-gather.4
  169.7 45.6 reduce-scatter.2
  220.1 114.5 reduce-scatter.4
where the time goes:
time: 348 us; the launch traced here: 341 us
  waiting for transfers between devices  164 us (47%)
  matrix products  64.4 us (19%)
  blocking collectives  60.9 us (18%)
  local copies, waits for them, and re-layouts  28 us (8%)
  between operations  14.8 us (4%)
  other arithmetic  4.81 us (1%)
  starting transfers between devices  4.17 us (1%)
    reduce_scatter x1, waiting for transfers between devices, on_device(): lax.psum_scatter(jnp.stack(terms, axis=1), 'space', scatter_dimension=0,...  77.6 us
    psum x1, blocking collectives, on_device(): lax.psum(jnp.sum(grad_pre.astype(jnp.float32), axis=0) * scale, 'space')  60.9 us
    all_gather x1, waiting for transfers between devices, on_device(): full_planes = lax.all_gather(features, 'chan', axis=3, tiled=True)  43.5 us
    dot_general x27, matrix products, on_device(): lax.dot_general(window_cells, grad_pre, (((0,), (0,)), ((), ())), preferr...  38.6 us
    all_gather x1, waiting for transfers between devices, on_device(): filter_piece = lax.all_gather(filters, 'space', axis=0, tiled=True)  35.1 us
    dot_general x27, matrix products, on_device(): jnp.dot(window_cells, filter_piece[:, forward_tap_index, :], preferred_el...  20.6 us
    slice x6, local copies, waits for them, and re-layouts, tap_slice(): copies[depth_off]  13.9 us
    all_gather x1, local copies, waits for them, and re-layouts, on_device(): filter_piece = lax.all_gather(filters, 'space', axis=0, tiled=True)  10.2 us
  transfers between devices with their start and end apart: 8, of which 4 were waited for; matrix products, arithmetic and copies ran while one was open for 20% of the time, Pallas kernels for 0%

commit v1 on v0

v1 whole, which is shorter than its diff:
```python
import math

import jax
import jax.numpy as jnp
from jax import lax
from jax.experimental import pallas as pl
from jax.experimental.pallas import tpu as pltpu
from jax.sharding import PartitionSpec as P


GRID = 16
FACE = GRID * GRID
NX, NQ, NZ = 4, 8, 8
KAPPA = 0.7978845608028654
CUBIC = 0.044715
VMEM_LIMIT = 24 * 1024 * 1024
Z_STEPS = (0, 1, -1, 4, 2, -3, -2, 3)


def gelu_pair(values):
    inner = KAPPA * (values + CUBIC * values * values * values)
    tangent = jnp.tanh(inner)
    output = 0.5 * values * (1.0 + tangent)
    slope = 0.5 * (1.0 + tangent) + 0.5 * values * (1.0 - tangent * tangent) * KAPPA * (
        1.0 + 3.0 * CUBIC * values * values
    )
    return (output, slope)


def device(space, z):
    return space % (NX * NQ) * NZ + z % NZ


def at(x, q, z):
    return device(x % NX * NQ + q % NQ, z)


def permuted(array, target):
    pairs = [(at(x, q, z), target(x, q, z)) for x in range(NX) for q in range(NQ) for z in range(NZ)]
    return lax.ppermute(array, ("space", "chan"), pairs)


def group(q):
    return q // 2 + 4 * (q % 2)


def holder(group):
    return group % 4 * 2 + group // 4


def swapped(index):
    return index >> 1 | (index & 1) << 1


def position(where):
    space, z = where[0], where[1]
    q = space & (NQ - 1)
    return space >> 3, q, q >> 1, q & 1, z


def ring_pairs(where, steps):
    _, _, y, core, z = position(where)
    return [(z + r - y - 4 * core) & (NQ - 1) for r in steps]


def slope_pairs(where):
    _, _, y, core, _ = position(where)
    rows = [(y - r) & 3 for r in range(4)]
    return [2 * row + core for row in rows] + [2 * row + 1 - core for row in rows]


def store_columns(pairs, planes, columns):
    size = planes[0].shape[-1]
    width = lax.broadcasted_iota(jnp.int32, (FACE, size), 0) % GRID
    rows, whole = columns.shape[1:]
    columns[0] = jnp.zeros((rows, whole), jnp.bfloat16)
    columns[GRID + 1] = jnp.zeros((rows, whole), jnp.bfloat16)
    edge = jnp.zeros((GRID, whole), jnp.bfloat16)
    places = [(ref, 2 * index) for ref in planes for index in range(ref.shape[0] // 2)]
    for pair, (ref, start) in zip(pairs, places):
        for half in range(2):
            depth = 2 * pair + half + 1
            middle = ref[start + half]
            wide = middle.astype(jnp.float32)
            left = jnp.where(width == 0, 0.0, pltpu.roll(wide, 1, 0)).astype(jnp.bfloat16)
            right = jnp.where(width == GRID - 1, 0.0, pltpu.roll(wide, FACE - 1, 0)).astype(
                jnp.bfloat16
            )
            columns[depth, :GRID, :] = edge
            columns[depth, FACE + GRID :, :] = edge
            for c, value in enumerate((left, middle, right)):
                columns[depth, GRID : FACE + GRID, c * size : (c + 1) * size] = value


def window(columns, plane):
    return jnp.concatenate(
        [columns[plane, GRID * b : GRID * b + FACE, :] for b in range(3)], axis=1
    )


def convolved(columns, pairs, paired):
    product = None
    for j in range(2):
        left = jnp.concatenate(
            [
                jnp.concatenate([window(columns, 2 * pair + 2 * j + i) for i in range(2)], axis=1)
                for pair in pairs
            ],
            axis=0,
        )
        part = jnp.dot(left, paired[j], preferred_element_type=jnp.float32)
        product = part if product is None else product + part
    return product


def halves(product, index, size):
    rows = slice(index * FACE, (index + 1) * FACE)
    return [product[rows, o * size : (o + 1) * size] for o in range(2)]


def weights_kernel(where, *refs):
    blocks = refs[:NX]
    ahead, back, natural = refs[NX:]
    size, out_size, rows = natural.shape[1], natural.shape[2], blocks[0].shape[1]
    x = position(where)[0]
    for r in range(NX):
        offset = pl.multiple_of(swapped((x + r) & (NX - 1)) * rows, rows)
        for tap in range(27):
            natural[tap, pl.ds(offset, rows)] = blocks[r][tap]

    def store(ref, a, bc, block):
        height, width = block.shape
        for o in range(2):
            i = a + o
            first = ((i % 2) * 9 + bc) * height
            ref[i // 2, first : first + height, o * width : (o + 1) * width] = block

    for ref, height, width in ((ahead, size, out_size), (back, out_size, size)):
        none = jnp.zeros((9 * height, width), jnp.bfloat16)
        ref[0, : 9 * height, width:] = none
        ref[1, 9 * height :, :width] = none
    for tap in range(27):
        block = natural[tap]
        store(ahead, tap // 9, tap % 9, block)
        turned = block.astype(jnp.float32).T.astype(jnp.bfloat16)
        store(back, (26 - tap) // 9, (26 - tap) % 9, turned)


def forward_kernel(where, *refs):
    *planes, paired, keep, send, columns, total = refs
    size = total.shape[-1]
    _, _, y, core, _ = position(where)
    store_columns(ring_pairs(where, Z_STEPS), planes, columns)

    def step(index, carry):
        product = convolved(columns, [4 * index + p for p in range(4)], paired)
        for p in range(4):
            for o, value in enumerate(halves(product, p, size)):
                total[4 * index + p, o] = value
        return carry

    lax.fori_loop(0, NQ // 4, step, 0)
    for r in range(4):
        row = (y + r) & 3
        for half in range(2):
            keep[r, half] = total[2 * row + core, half]
            send[r, half] = total[2 * row + 1 - core, half].astype(jnp.bfloat16)


def slopes_kernel(where, *refs):
    store_columns(slope_pairs(where), refs[:NQ], refs[NQ])


def backward_kernel(steps, where, columns, paired, *outs):
    product = convolved(columns, ring_pairs(where, steps), paired)
    places = [(out, 2 * index) for out in outs for index in range(out.shape[0] // 2)]
    for index, (out, start) in enumerate(places):
        for half, value in enumerate(halves(product, index, out.shape[-1])):
            out[start + half] = value.astype(out.dtype)


def filters_kernel(scale, where, columns, *refs):
    planes, outs = refs[:NQ], refs[NQ : NQ + NX]
    turned, total, natural = refs[NQ + NX :]
    size, rows = natural.shape[-1], outs[0].shape[1]
    x = position(where)[0]
    turned[:, :FACE] = jnp.zeros((size, FACE), jnp.bfloat16)
    turned[:, (GRID + 1) * FACE :] = jnp.zeros((size, FACE), jnp.bfloat16)
    bias = jnp.zeros((8, size), jnp.float32)
    for pair, ref in zip(slope_pairs(where), planes):
        for half in range(2):
            value = ref[half].astype(jnp.float32)
            bias = bias + jnp.sum(value.reshape(FACE // 8, 8, size), axis=0)
            start = pl.multiple_of((2 * pair + half + 1) * FACE, FACE)
            turned[:, pl.ds(start, FACE)] = value.T.astype(jnp.bfloat16)
    total[...] = jnp.zeros_like(total)

    def step(index, carry):
        first = 8 * index
        left = jnp.concatenate(
            [
                turned[:, pl.ds(pl.multiple_of((first + 2 - a) * FACE, FACE), 8 * FACE)]
                for a in range(3)
            ],
            axis=0,
        )
        right = jnp.concatenate([window(columns, first + 1 + e) for e in range(8)], axis=0)
        total[...] += jnp.dot(left, right, preferred_element_type=jnp.float32)
        return carry

    lax.fori_loop(0, GRID // 8, step, 0)
    for tap in range(27):
        a, bc = tap // 9, tap % 9
        block = total[a * size : (a + 1) * size, bc * size : (bc + 1) * size]
        natural[tap] = block.T * scale
    whole = jnp.sum(bias, axis=0, keepdims=True) * scale
    upper = whole.astype(jnp.bfloat16)
    lower = (whole - upper.astype(jnp.float32)).astype(jnp.bfloat16)
    row = lax.broadcasted_iota(jnp.int32, (rows, size), 0)
    spread = jnp.where(
        row == 0, upper.astype(jnp.float32), jnp.where(row == 1, lower.astype(jnp.float32), 0.0)
    )
    for r in range(NX):
        offset = pl.multiple_of(swapped((x + r) & (NX - 1)) * rows, rows)
        for tap in range(27):
            outs[r][tap] = natural[tap, pl.ds(offset, rows)].astype(outs[r].dtype)
        outs[r][27] = spread.astype(outs[r].dtype)


def call(kernel, where, operands, outs, scratch, flops):
    moved = sum(o.size * o.dtype.itemsize for o in operands)
    moved += sum(math.prod(o.shape) * o.dtype.itemsize for o in outs)
    vmem = pl.BlockSpec(memory_space=pltpu.VMEM)
    return pl.pallas_call(
        kernel,
        out_shape=outs,
        in_specs=[pl.BlockSpec(memory_space=pltpu.SMEM)] + [vmem] * len(operands),
        out_specs=[vmem] * len(outs),
        scratch_shapes=scratch,
        compiler_params=pltpu.CompilerParams(vmem_limit_bytes=VMEM_LIMIT),
        cost_estimate=pl.CostEstimate(flops=flops, bytes_accessed=moved, transcendentals=0),
    )(where, *operands)


def on_device(features, filters, conv_bias, cotangent):
    where = jnp.stack([lax.axis_index("space"), lax.axis_index("chan")]).astype(jnp.int32)
    size, rows = features.shape[-1], filters.shape[0]
    out_size = filters.shape[-1]
    bf16, f32 = jnp.bfloat16, jnp.float32
    shaped = jax.ShapeDtypeStruct

    def along_z(piece, r):
        return permuted(piece, lambda x, q, z: at(x, q, z + r))

    block = permuted(
        filters.transpose(1, 0, 2),
        lambda x, q, z: at(swapped(q % NX), holder((NQ * x + q) // NX), z),
    )
    ahead = permuted(cotangent[0], lambda x, q, z: device(NQ * x + q - 1, z))
    first = permuted(features[1].reshape(FACE, size), lambda x, q, z: at(x, holder(z), z + q))
    second = permuted(
        features[0].reshape(FACE, size), lambda x, q, z: at(x - (q == 0), holder(z), z + q - 1)
    )
    own = jnp.stack([first, second])
    own, block, ahead = lax.optimization_barrier((own, block, ahead))
    blocks = [block] + [
        permuted(block, lambda x, q, z: at(x - shift, q, z)) for shift in range(1, NX)
    ]
    above, below, beyond = along_z(own, -1), along_z(own, 1), along_z(own, 4)
    above, below, beyond, blocks[1], blocks[2] = lax.optimization_barrier(
        (above, below, beyond, blocks[1], blocks[2])
    )
    planes = [
        own,
        above,
        below,
        beyond,
        along_z(jnp.concatenate([above, beyond]), -1),
        along_z(jnp.concatenate([below, beyond]), 1),
    ]

    flops = 2 * 27 * GRID * FACE * size * out_size
    paired_shape = lambda deep, wide: shaped((2, 18 * deep, 2 * wide), bf16)
    columns_shape = shaped((GRID + 2, FACE + 2 * GRID, 3 * size), bf16)
    ahead_weights, back_weights = call(
        weights_kernel,
        where,
        blocks,
        [paired_shape(size, out_size), paired_shape(out_size, size)],
        [pltpu.VMEM((27, size, out_size), bf16)],
        0,
    )
    keep, send, columns = call(
        forward_kernel,
        where,
        planes + [ahead_weights],
        [
            shaped((4, 2, FACE, out_size), f32),
            shaped((4, 2, FACE, out_size), bf16),
            columns_shape,
        ],
        [pltpu.VMEM((NQ, 2, FACE, out_size), f32)],
        flops,
    )
    keep = keep + permuted(send, lambda x, q, z: at(x, q ^ 1, z)).astype(f32)
    pre_act = keep[0]
    for r in range(1, 4):
        pre_act = pre_act + permuted(
            keep[r].astype(bf16), lambda x, q, z: at(x, q + 2 * r, z)
        ).astype(f32)
    pre_act = pre_act + conv_bias[None, None, :]

    target = jnp.stack([cotangent[1], ahead])
    output, slope = gelu_pair(pre_act)
    activated = output.astype(bf16)
    behind = permuted(activated[1], lambda x, q, z: device(NQ * x + q + 1, z))
    activated = jnp.stack([behind, activated[0]])
    grad_pre = (target.reshape(2, FACE, out_size).astype(f32) * slope).astype(bf16)

    slopes = [grad_pre]
    for r in range(1, 4):
        slopes.append(permuted(grad_pre, lambda x, q, z: at(x, q + 2 * r, z)))
    other = [permuted(piece, lambda x, q, z: at(x, q ^ 1, z)) for piece in slopes]
    slopes = slopes + other
    (slope_columns,) = call(slopes_kernel, where, slopes, [columns_shape], [], 0)

    scale = 1.0 / math.sqrt(NX * GRID * FACE)
    terms = call(
        lambda *refs: filters_kernel(scale, *refs),
        where,
        [columns] + slopes,
        [shaped((28, rows, out_size), f32 if r == 0 else bf16) for r in range(NX)],
        [
            pltpu.VMEM((out_size, (GRID + 2) * FACE), bf16),
            pltpu.VMEM((3 * out_size, 9 * size), f32),
            pltpu.VMEM((27, size, out_size), f32),
        ],
        flops,
    )
    where, terms = lax.optimization_barrier((where, terms))
    held = terms[0]
    for r in range(1, NX):
        held = held + permuted(terms[r], lambda x, q, z: at(x + r, q, z)).astype(f32)
    grad_bias = held[27, 0] + held[27, 1]
    held = held[:27].astype(bf16)

    def parts(steps, where, outs):
        return call(
            lambda *refs: backward_kernel(steps, *refs),
            where,
            [slope_columns, back_weights],
            outs,
            [],
            flops * len(steps) // NZ,
        )

    bundle = shaped((4, FACE, size), bf16)
    up, down = parts((2, -3, -2, 3), where, [bundle, bundle])
    up, down, where = lax.optimization_barrier((up, down, where))
    up, down = along_z(up, 1), along_z(down, -1)
    above, below, beyond, summed = parts((1, -1, 4, 0), where, [shaped((2, FACE, size), f32)] * 4)
    up, down, held = lax.optimization_barrier((up, down, held))
    above = (above + up[:2].astype(f32)).astype(bf16)
    below = (below + down[:2].astype(f32)).astype(bf16)
    beyond = (beyond + up[2:].astype(f32) + down[2:].astype(f32)).astype(bf16)
    for piece, r in ((beyond, 4), (above, 1), (below, -1)):
        summed = summed + along_z(piece, r).astype(f32)
    summed = summed.astype(bf16)

    grad_filters = permuted(
        held, lambda x, q, z: device(NX * group(q) + swapped(x), z)
    ).astype(f32)

    def home(half):
        return lambda x, q, z: device(NQ * x + (z - group(q)) % NZ + half, group(q))

    grad_input = jnp.stack([permuted(summed[1], home(1)), permuted(summed[0], home(0))])

    shape = (2, GRID, GRID)
    return (
        activated.reshape(*shape, out_size),
        grad_input.reshape(*shape, size),
        grad_filters.transpose(1, 0, 2),
        grad_bias,
    )


def solution(mesh):
    return jax.shard_map(
        on_device,
        mesh=mesh,
        in_specs=(
            P("space", None, None, "chan"),
            P("space", None, "chan"),
            P("chan"),
            P("space", None, None, "chan"),
        ),
        out_specs=(
            P("space", None, None, "chan"),
            P("space", None, None, "chan"),
            P("space", None, "chan"),
            P("chan"),
        ),
        check_vma=False,
    )
```

time: 348 us -> 145 us (0.42); the launches traced: 341 us -> 145 us
  waiting for transfers between devices: 164 us -> 56.6 us
  matrix products: 64.4 us -> 0 us
  blocking collectives: 60.9 us -> 0 us
  starting transfers between devices: 4.17 us -> 60.1 us
  local copies, waits for them, and re-layouts: 28 us -> 1.86 us
  Pallas kernels: 0 us -> 21.7 us
  between operations: 14.8 us -> 0.88 us
    all_gather x2 -> x0, waiting for transfers between devices: 78.5 us -> none  [the longest x1 43.5 us: on_device(): full_planes = lax.all_gather(features, 'chan', axis=3, tiled=True)]
    reduce_scatter x2 -> x0, waiting for transfers between devices: 77.6 us -> none  [the longest x1 77.6 us: on_device(): lax.psum_scatter(jnp.stack(terms, axis=1), 'space', scatter_dimension=0,...]
    dot_general x55 -> x0, matrix products: 64.4 us -> none  [the longest x27 38.6 us: on_device(): lax.dot_general(window_cells, grad_pre, (((0,), (0,)), ((), ())), preferr...]
    psum x1 -> x0, blocking collectives: 60.9 us -> none  [on_device(): lax.psum(jnp.sum(grad_pre.astype(jnp.float32), axis=0) * scale, 'space')]
    ppermute x4 -> x35, starting transfers between devices: 3.84 us -> 60.1 us  [permuted(): return lax.ppermute(array, ('space', 'chan'), pairs)]
    ppermute x4 -> x35, waiting for transfers between devices: 6.85 us -> 56.6 us  [permuted(): return lax.ppermute(array, ('space', 'chan'), pairs)]
    pallas_call x0 -> x6, Pallas kernels: none -> 21.7 us  [call(): pl.pallas_call(kernel, out_shape=outs, in_specs=[pl.BlockSpec(memory_spac...]
    slice x8 -> x3, local copies, waits for them, and re-layouts: 15.2 us -> 1.8 us  [the longest x1 0.89 us: on_device(): target = jnp.stack([cotangent[1], ahead])]
  transfers between devices with their start and end apart: 8 -> 35, of which waited for: 4 -> 21; matrix products, arithmetic and copies ran while one was open for 20% -> 2% of each run, Pallas kernels for 0% -> 10%
where the time goes in v1:
time: 145 us
  starting transfers between devices  60.1 us (41%)
  waiting for transfers between devices  56.6 us (39%)
  Pallas kernels  21.7 us (15%)
  other arithmetic  3.54 us (2%)
  local copies, waits for them, and re-layouts  1.86 us (1%)
    ppermute x35, starting transfers between devices, permuted(): return lax.ppermute(array, ('space', 'chan'), pairs)  60.1 us
    ppermute x35, waiting for transfers between devices, permuted(): return lax.ppermute(array, ('space', 'chan'), pairs)  56.6 us
    pallas_call x6, Pallas kernels, call(): pl.pallas_call(kernel, out_shape=outs, in_specs=[pl.BlockSpec(memory_spac...  21.7 us
  transfers between devices with their start and end apart: 35, of which 21 were waited for; matrix products, arithmetic and copies ran while one was open for 2% of the time, Pallas kernels for 10%

profile of v1, /device:TPU:16, one launch (start us, length us, event | category | flops | bytes accessed | tf_op | source)
XLA Modules:
  0.0 144.7 jit_solution(15084964798287508737)
XLA Ops:
  0.6 0.9 fusion.14
  1.5 6.3 %collective-permute-start.1 = (bf16[256,128]{1,0:T(8,128)(2,1)S(1)}, bf16[256,128]{1,0:T(8,128)(2,1)S(1)}, u32[]{:S(2)}, u32[]{:S(2)}) collective-permute-start(bf16[256,128]{1,0:T(8,128)(2,1)S(1)} %bitcast.50), channel_id=1, source_target_pairs={{0,199},{1,208},{2,225},{3,242},{4,203},{5,220},{6,237},{7,254},{8... | collective-permute-start | bytes 196616 | tf_op jit(solution)/shard_map/ppermute | solution.py:40
  7.8 6.2 %collective-permute-start = (bf16[256,128]{1,0:T(8,128)(2,1)S(1)}, bf16[256,128]{1,0:T(8,128)(2,1)S(1)}, u32[]{:S(2)}, u32[]{:S(2)}) collective-permute-start(bf16[256,128]{1,0:T(8,128)(2,1)S(1)} %bitcast.49), channel_id=1, source_target_pairs={{0,0},{1,17},{2,34},{3,51},{4,12},{5,29},{6,46},{7,63},{8,1},{9,18... | collective-permute-start | bytes 196616 | tf_op jit(solution)/shard_map/ppermute | solution.py:40
  14.1 1.9 %collective-permute-start.2 = (bf16[27,32,128]{2,1,0:T(8,128)(2,1)}, bf16[27,32,128]{2,1,0:T(8,128)(2,1)S(1)}, u32[]{:S(2)}, u32[]{:S(2)}) collective-permute-start(bf16[27,32,128]{2,1,0:T(8,128)(2,1)} %bitcast.55), channel_id=1, source_target_pairs={{0,0},{1,1},{2,2},{3,3},{4,4},{5,5},{6,6},{7,7},{8,128},{9,129},{1... | collective-permute-start | bytes 663560 | tf_op jit(solution)/shard_map/ppermute | solution.py:40
  16.0 0.9 fusion.13
  17.7 2.6 %collective-permute-done.3 = bf16[16,16,128]{2,1,0:T(8,128)(2,1)S(1)} collective-permute-done((bf16[16,16,128]{2,1,0:T(8,128)(2,1)S(1)}, bf16[16,16,128]{2,1,0:T(8,128)(2,1)S(1)}, u32[]{:S(2)}, u32[]{:S(2)}) %collective-permute-start.3) | collective-permute-done | bytes 65568 | tf_op jit(solution)/shard_map/ppermute | solution.py:40
  20.3 4.2 %collective-permute-done.2.refs_0_ = bf16[27,32,128]{2,1,0:T(8,128)(2,1)S(1)} collective-permute-done((bf16[27,32,128]{2,1,0:T(8,128)(2,1)}, bf16[27,32,128]{2,1,0:T(8,128)(2,1)S(1)}, u32[]{:S(2)}, u32[]{:S(2)}) %collective-permute-start.2) | collective-permute-done | bytes 221216 | tf_op jit(solution)/shard_map/ppermute | solution.py:40
  24.5 3.5 %collective-permute-start.8 = (bf16[27,32,128]{2,1,0:T(8,128)(2,1)S(1)}, bf16[27,32,128]{2,1,0:T(8,128)(2,1)S(1)}, u32[]{:S(2)}, u32[]{:S(2)}) collective-permute-start(bf16[27,32,128]{2,1,0:T(8,128)(2,1)S(1)} %collective-permute-done.2.refs_0_), channel_id=1, source_target_pairs={{0,128},{1,129},{2,130},{3,131},{4,132},{5,133},{6,134},{7,135},{8... | collective-permute-start | bytes 663560 | tf_op jit(solution)/shard_map/ppermute | solution.py:40
  28.0 0.9 collective-permute-start.7
  28.9 1.0 collective-permute-start.6
  29.9 2.2 %collective-permute-start.5 = (bf16[2,256,128]{2,1,0:T(8,128)(2,1)S(1)}, bf16[2,256,128]{2,1,0:T(8,128)(2,1)S(1)}, u32[]{:S(2)}, u32[]{:S(2)}) collective-permute-start(bf16[2,256,128]{2,1,0:T(8,128)(2,1)S(1)} %pad_maximum_fusion.2.refs_0_), channel_id=1, source_target_pairs={{0,1},{1,2},{2,3},{3,4},{4,5},{5,6},{6,7},{7,0},{8,9},{9,10},{10,1... | collective-permute-start | bytes 393224 | tf_op jit(solution)/shard_map/ppermute | solution.py:40
  32.1 2.9 %collective-permute-start.4 = (bf16[2,256,128]{2,1,0:T(8,128)(2,1)S(1)}, bf16[2,256,128]{2,1,0:T(8,128)(2,1)S(1)}, u32[]{:S(2)}, u32[]{:S(2)}) collective-permute-start(bf16[2,256,128]{2,1,0:T(8,128)(2,1)S(1)} %pad_maximum_fusion.2.refs_0_), channel_id=1, source_target_pairs={{0,7},{1,0},{2,1},{3,2},{4,3},{5,4},{6,5},{7,6},{8,15},{9,8},{10,9... | collective-permute-start | bytes 393224 | tf_op jit(solution)/shard_map/ppermute | solution.py:40
  35.0 4.2 %collective-permute-done.6.refs_3_ = bf16[2,256,128]{2,1,0:T(8,128)(2,1)S(1)} collective-permute-done((bf16[2,256,128]{2,1,0:T(8,128)(2,1)S(1)}, bf16[2,256,128]{2,1,0:T(8,128)(2,1)S(1)}, u32[]{:S(2)}, u32[]{:S(2)}) %collective-permute-start.6) | collective-permute-done | bytes 131104 | tf_op jit(solution)/shard_map/ppermute | solution.py:40
  39.2 3.6 %collective-permute-done.5.refs_2_ = bf16[2,256,128]{2,1,0:T(8,128)(2,1)S(1)} collective-permute-done((bf16[2,256,128]{2,1,0:T(8,128)(2,1)S(1)}, bf16[2,256,128]{2,1,0:T(8,128)(2,1)S(1)}, u32[]{:S(2)}, u32[]{:S(2)}) %collective-permute-start.5) | collective-permute-done | bytes 131104 | tf_op jit(solution)/shard_map/ppermute | solution.py:40
  42.9 1.0 collective-permute-start.10
  43.9 2.3 %collective-permute-start.9 = (bf16[4,256,128]{2,1,0:T(8,128)(2,1)S(1)}, bf16[4,256,128]{2,1,0:T(8,128)(2,1)S(1)}, u32[]{:S(2)}, u32[]{:S(2)}) collective-permute-start(bf16[4,256,128]{2,1,0:T(8,128)(2,1)S(1)} %get-tuple-element.89), channel_id=1, source_target_pairs={{0,7},{1,0},{2,1},{3,2},{4,3},{5,4},{6,5},{7,6},{8,15},{9,8},{10,9... | collective-permute-start | bytes 786440 | tf_op jit(solution)/shard_map/ppermute | solution.py:40
  46.2 0.9 collective-permute-start.11
  47.2 7.0 %collective-permute-done.11.refs_3_ = bf16[27,32,128]{2,1,0:T(8,128)(2,1)S(1)} collective-permute-done((bf16[27,32,128]{2,1,0:T(8,128)(2,1)S(1)}, bf16[27,32,128]{2,1,0:T(8,128)(2,1)S(1)}, u32[]{:S(2)}, u32[]{:S(2)}) %collective-permute-start.11) | collective-permute-done | bytes 221216 | tf_op jit(solution)/shard_map/ppermute | solution.py:40
  54.2 1.2 shard_map.75
  55.5 6.7 %shard_map.76 = (f32[4,2,256,128]{3,2,1,0:T(8,128)S(1)}, bf16[4,2,256,128]{3,2,1,0:T(8,128)(2,1)S(1)}, bf16[18,288,384]{2,1,0:T(8,128)(2,1)S(1)}) custom-call(s32[2]{0:T(128)S(1)} %pad_add_fusion.where.refs_0_, bf16[2,256,128]{2,1,0:T(8,128)(2,1)S(1)} %pad_maximum_fusion.2.refs_0_, bf16[2,256,128]{2,1,0:T(8,128)(2,1)S(1)} %collective-permute-done.4.refs_1_, ...), custom_call_target="tpu_custom_call" | custom-call | flops 3623878656 | bytes 8962048 | tf_op jit(solution)/shard_map/pallas_call | solution.py:234
  62.3 1.9 %collective-permute-done.12 = bf16[4,2,256,128]{3,2,1,0:T(8,128)(2,1)S(1)} collective-permute-done((bf16[4,2,256,128]{3,2,1,0:T(8,128)(2,1)S(1)}, bf16[4,2,256,128]{3,2,1,0:T(8,128)(2,1)S(1)}, u32[]{:S(2)}, u32[]{:S(2)}) %collective-permute-start.12) | collective-permute-done | bytes 524320 | tf_op jit(solution)/shard_map/ppermute | solution.py:40
  64.5 2.0 %collective-permute-start.15 = (bf16[2,256,128]{2,1,0:T(8,128)(2,1)S(1)}, bf16[2,256,128]{2,1,0:T(8,128)(2,1)S(1)}, u32[]{:S(2)}, u32[]{:S(2)}) collective-permute-start(bf16[2,256,128]{2,1,0:T(8,128)(2,1)S(1)} %get-tuple-element.77), channel_id=1, source_target_pairs={{0,48},{1,49},{2,50},{3,51},{4,52},{5,53},{6,54},{7,55},{8,56},{9,... | collective-permute-start | bytes 393224 | tf_op jit(solution)/shard_map/ppermute | solution.py:40
  66.5 1.8 %collective-permute-start.14 = (bf16[2,256,128]{2,1,0:T(8,128)(2,1)S(1)}, bf16[2,256,128]{2,1,0:T(8,128)(2,1)S(1)}, u32[]{:S(2)}, u32[]{:S(2)}) collective-permute-start(bf16[2,256,128]{2,1,0:T(8,128)(2,1)S(1)} %get-tuple-element.78), channel_id=1, source_target_pairs={{0,32},{1,33},{2,34},{3,35},{4,36},{5,37},{6,38},{7,39},{8,40},{9,... | collective-permute-start | bytes 393224 | tf_op jit(solution)/shard_map/ppermute | solution.py:40
  68.3 1.7 %collective-permute-done.13 = bf16[2,256,128]{2,1,0:T(8,128)(2,1)S(1)} collective-permute-done((bf16[2,256,128]{2,1,0:T(8,128)(2,1)S(1)}, bf16[2,256,128]{2,1,0:T(8,128)(2,1)S(1)}, u32[]{:S(2)}, u32[]{:S(2)}) %collective-permute-start.13) | collective-permute-done | bytes 131104 | tf_op jit(solution)/shard_map/ppermute | solution.py:40
  70.3 3.5 %collective-permute-done.14 = bf16[2,256,128]{2,1,0:T(8,128)(2,1)S(1)} collective-permute-done((bf16[2,256,128]{2,1,0:T(8,128)(2,1)S(1)}, bf16[2,256,128]{2,1,0:T(8,128)(2,1)S(1)}, u32[]{:S(2)}, u32[]{:S(2)}) %collective-permute-start.14) | collective-permute-done | bytes 131104 | tf_op jit(solution)/shard_map/ppermute | solution.py:40
  74.1 0.9 collective-permute-start.19
  75.0 3.6 %collective-permute-start.18 = (bf16[2,256,128]{2,1,0:T(8,128)(2,1)S(1)}, bf16[2,256,128]{2,1,0:T(8,128)(2,1)S(1)}, u32[]{:S(2)}, u32[]{:S(2)}) collective-permute-start(bf16[2,256,128]{2,1,0:T(8,128)(2,1)S(1)} %get-tuple-element.74.refs_2_.refs_0_), channel_id=1, source_target_pairs={{0,32},{1,33},{2,34},{3,35},{4,36},{5,37},{6,38},{7,39},{8,40},{9,... | collective-permute-start | bytes 393224 | tf_op jit(solution)/shard_map/ppermute | solution.py:40
  78.6 2.0 %collective-permute-done.19.refs_5_.refs_3_ = bf16[2,256,128]{2,1,0:T(8,128)(2,1)S(1)} collective-permute-done((bf16[2,256,128]{2,1,0:T(8,128)(2,1)S(1)}, bf16[2,256,128]{2,1,0:T(8,128)(2,1)S(1)}, u32[]{:S(2)}, u32[]{:S(2)}) %collective-permute-start.19) | collective-permute-done | bytes 131104 | tf_op jit(solution)/shard_map/ppermute | solution.py:40
  80.6 1.9 %collective-permute-done.18.refs_4_.refs_2_ = bf16[2,256,128]{2,1,0:T(8,128)(2,1)S(1)} collective-permute-done((bf16[2,256,128]{2,1,0:T(8,128)(2,1)S(1)}, bf16[2,256,128]{2,1,0:T(8,128)(2,1)S(1)}, u32[]{:S(2)}, u32[]{:S(2)}) %collective-permute-start.18) | collective-permute-done | bytes 131104 | tf_op jit(solution)/shard_map/ppermute | solution.py:40
  82.4 1.4 collective-permute-done.17.refs_3_.refs_1_
  85.2 6.1 %shard_map.77 = (f32[28,32,128]{2,1,0:T(8,128)S(1)}, bf16[28,32,128]{2,1,0:T(8,128)(2,1)S(1)}, bf16[28,32,128]{2,1,0:T(8,128)(2,1)S(1)}, bf16[28,32,128]{2,1,0:T(8,128)(2,1)S(1)}) custom-call(s32[2]{0:T(128)S(1)} %pad_add_fusion.where.refs_0_, bf16[18,288,384]{2,1,0:T(8,128)(2,1)S(1)} %get-tuple-element.48.refs_1_, ...), custom_call_target="tpu_custom_call" | custom-call | flops 3623878656 | bytes 6176768 | tf_op jit(solution)/shard_map/pallas_call | solution.py:234
  91.3 1.1 collective-permute-start.27
  92.4 2.1 %collective-permute-start.28 = (bf16[28,32,128]{2,1,0:T(8,128)(2,1)S(1)}, bf16[28,32,128]{2,1,0:T(8,128)(2,1)S(1)}, u32[]{:S(2)}, u32[]{:S(2)}) collective-permute-start(bf16[28,32,128]{2,1,0:T(8,128)(2,1)S(1)} %get-tuple-element.66), channel_id=1, source_target_pairs={{0,192},{1,193},{2,194},{3,195},{4,196},{5,197},{6,198},{7,199},{8... | collective-permute-start | bytes 688136 | tf_op jit(solution)/shard_map/ppermute | solution.py:40
  94.5 1.4 shard_map.78.refs_1_
  96.0 3.1 %shard_map.79 = (bf16[4,256,128]{2,1,0:T(8,128)(2,1)S(1)}, bf16[4,256,128]{2,1,0:T(8,128)(2,1)S(1)}) custom-call(s32[2]{0:T(128)S(1)} %pad_add_fusion.where.refs_0_, bf16[18,288,384]{2,1,0:T(8,128)(2,1)S(1)} %shard_map.78.refs_1_, bf16[2,2304,256]{2,1,0:T(8,128)(2,1)S(1)} %get-tuple-element.55.refs_2_), custom_call_target="tpu_custom_call" | custom-call | flops 1811939328 | bytes 6864896 | tf_op jit(solution)/shard_map/pallas_call | solution.py:234
  99.2 3.1 %shard_map.80 = (f32[2,256,128]{2,1,0:T(8,128)S(1)}, f32[2,256,128]{2,1,0:T(8,128)S(1)}, f32[2,256,128]{2,1,0:T(8,128)S(1)}, f32[2,256,128]{2,1,0:T(8,128)S(1)}) custom-call(s32[2]{0:T(128)S(1)} %pad_add_fusion.where.refs_0_, bf16[18,288,384]{2,1,0:T(8,128)(2,1)S(1)} %shard_map.78.refs_1_, bf16[2,2304,256]{2,1,0:T(8,128)(2,1)S(1)} %get-tuple-element.55.refs_2_), custom_call_target="tpu_custom_call" | custom-call | flops 1811939328 | bytes 7389184 | tf_op jit(solution)/shard_map/pallas_call | solution.py:234
  102.4 3.2 %collective-permute-done.26 = bf16[28,32,128]{2,1,0:T(8,128)(2,1)S(1)} collective-permute-done((bf16[28,32,128]{2,1,0:T(8,128)(2,1)S(1)}, bf16[28,32,128]{2,1,0:T(8,128)(2,1)S(1)}, u32[]{:S(2)}, u32[]{:S(2)}) %collective-permute-start.26) | collective-permute-done | bytes 229408 | tf_op jit(solution)/shard_map/ppermute | solution.py:40
  106.4 2.3 %collective-permute-done.24 = bf16[4,256,128]{2,1,0:T(8,128)(2,1)S(1)} collective-permute-done((bf16[4,256,128]{2,1,0:T(8,128)(2,1)S(1)}, bf16[4,256,128]{2,1,0:T(8,128)(2,1)S(1)}, u32[]{:S(2)}, u32[]{:S(2)}) %collective-permute-start.24) | collective-permute-done | bytes 262176 | tf_op jit(solution)/shard_map/ppermute | solution.py:40
  108.7 4.9 %collective-permute-done.25 = bf16[4,256,128]{2,1,0:T(8,128)(2,1)S(1)} collective-permute-done((bf16[4,256,128]{2,1,0:T(8,128)(2,1)S(1)}, bf16[4,256,128]{2,1,0:T(8,128)(2,1)S(1)}, u32[]{:S(2)}, u32[]{:S(2)}) %collective-permute-start.25) | collective-permute-done | bytes 262176 | tf_op jit(solution)/shard_map/ppermute | solution.py:40
  113.7 3.8 %collective-permute-start.29 = (bf16[2,256,128]{2,1,0:T(8,128)(2,1)S(1)}, bf16[2,256,128]{2,1,0:T(8,128)(2,1)S(1)}, u32[]{:S(2)}, u32[]{:S(2)}) collective-permute-start(bf16[2,256,128]{2,1,0:T(8,128)(2,1)S(1)} %get-tuple-element.79), channel_id=1, source_target_pairs={{0,4},{1,5},{2,6},{3,7},{4,0},{5,1},{6,2},{7,3},{8,12},{9,13},{10,... | collective-permute-start | bytes 393224 | tf_op jit(solution)/shard_map/ppermute | solution.py:40
  117.5 3.2 %collective-permute-start.31 = (bf16[2,256,128]{2,1,0:T(8,128)(2,1)S(1)}, bf16[2,256,128]{2,1,0:T(8,128)(2,1)S(1)}, u32[]{:S(2)}, u32[]{:S(2)}) collective-permute-start(bf16[2,256,128]{2,1,0:T(8,128)(2,1)S(1)} %get-tuple-element.81), channel_id=1, source_target_pairs={{0,7},{1,0},{2,1},{3,2},{4,3},{5,4},{6,5},{7,6},{8,15},{9,8},{10,9... | collective-permute-start | bytes 393224 | tf_op jit(solution)/shard_map/ppermute | solution.py:40
  121.4 2.6 %collective-permute-start.34 = (bf16[27,32,128]{2,1,0:T(8,128)(2,1)S(1)}, bf16[27,32,128]{2,1,0:T(8,128)(2,1)S(1)}, u32[]{:S(2)}, u32[]{:S(2)}) collective-permute-start(bf16[27,32,128]{2,1,0:T(8,128)(2,1)S(1)} %slice.120), channel_id=1, source_target_pairs={{0,0},{1,1},{2,2},{3,3},{4,4},{5,5},{6,6},{7,7},{8,128},{9,129},{1... | collective-permute-start | bytes 663560 | tf_op jit(solution)/shard_map/ppermute | solution.py:40
  124.1 1.5 %collective-permute-done.29 = bf16[2,256,128]{2,1,0:T(8,128)(2,1)S(1)} collective-permute-done((bf16[2,256,128]{2,1,0:T(8,128)(2,1)S(1)}, bf16[2,256,128]{2,1,0:T(8,128)(2,1)S(1)}, u32[]{:S(2)}, u32[]{:S(2)}) %collective-permute-start.29) | collective-permute-done | bytes 131104 | tf_op jit(solution)/shard_map/ppermute | solution.py:40
  126.3 4.4 %collective-permute-start.32 = (bf16[256,128]{1,0:T(8,128)(2,1)S(1)}, bf16[256,128]{1,0:T(8,128)(2,1)S(1)}, u32[]{:S(2)}, u32[]{:S(2)}) collective-permute-start(bf16[256,128]{1,0:T(8,128)(2,1)S(1)} %get-tuple-element.82), channel_id=1, source_target_pairs={{0,8},{1,16},{2,24},{3,32},{4,40},{5,48},{6,56},{7,64},{8,44},{9,5... | collective-permute-start | bytes 196616 | tf_op jit(solution)/shard_map/ppermute | solution.py:40
  130.8 3.2 %collective-permute-start.33 = (bf16[256,128]{1,0:T(8,128)(2,1)S(1)}, bf16[256,128]{1,0:T(8,128)(2,1)S(1)}, u32[]{:S(2)}, u32[]{:S(2)}) collective-permute-start(bf16[256,128]{1,0:T(8,128)(2,1)S(1)} %get-tuple-element.83), channel_id=1, source_target_pairs={{0,0},{1,8},{2,16},{3,24},{4,32},{5,40},{6,48},{7,56},{8,36},{9,44... | collective-permute-start | bytes 196616 | tf_op jit(solution)/shard_map/ppermute | solution.py:40
  134.5 2.3 %collective-permute-done.32 = bf16[256,128]{1,0:T(8,128)(2,1)S(1)} collective-permute-done((bf16[256,128]{1,0:T(8,128)(2,1)S(1)}, bf16[256,128]{1,0:T(8,128)(2,1)S(1)}, u32[]{:S(2)}, u32[]{:S(2)}) %collective-permute-start.32) | collective-permute-done | bytes 65568 | tf_op jit(solution)/shard_map/ppermute | solution.py:40
  136.7 6.5 %collective-permute-done.33 = bf16[256,128]{1,0:T(8,128)(2,1)S(1)} collective-permute-done((bf16[256,128]{1,0:T(8,128)(2,1)S(1)}, bf16[256,128]{1,0:T(8,128)(2,1)S(1)}, u32[]{:S(2)}, u32[]{:S(2)}) %collective-permute-start.33) | collective-permute-done | bytes 65568 | tf_op jit(solution)/shard_map/ppermute | solution.py:40
  143.9 0.8 convert_bitcast_fusion
  (48 shorter events, 6.9 us)
Async XLA Ops:
  1.5 16.2 %collective-permute-start.1 = (bf16[256,128]{1,0:T(8,128)(2,1)S(1)}, bf16[256,128]{1,0:T(8,128)(2,1)S(1)}, u32[]{:S(2)}, u32[]{:S(2)}) collective-permute-start(bf16[256,128]{1,0:T(8,128)(2,1)S(1)} %bitcast.50), channel_id=1, source_target_pairs={{0,199},{1,208},{2,225},{3,242},{4,203},{5,220},{6,237},{7,254},{8... | collective-permute-start | bytes 196616 | tf_op jit(solution)/shard_map/ppermute | solution.py:40
  7.8 9.9 %collective-permute-start = (bf16[256,128]{1,0:T(8,128)(2,1)S(1)}, bf16[256,128]{1,0:T(8,128)(2,1)S(1)}, u32[]{:S(2)}, u32[]{:S(2)}) collective-permute-start(bf16[256,128]{1,0:T(8,128)(2,1)S(1)} %bitcast.49), channel_id=1, source_target_pairs={{0,0},{1,17},{2,34},{3,51},{4,12},{5,29},{6,46},{7,63},{8,1},{9,18... | collective-permute-start | bytes 196616 | tf_op jit(solution)/shard_map/ppermute | solution.py:40
  14.1 10.4 %collective-permute-start.2 = (bf16[27,32,128]{2,1,0:T(8,128)(2,1)}, bf16[27,32,128]{2,1,0:T(8,128)(2,1)S(1)}, u32[]{:S(2)}, u32[]{:S(2)}) collective-permute-start(bf16[27,32,128]{2,1,0:T(8,128)(2,1)} %bitcast.55), channel_id=1, source_target_pairs={{0,0},{1,1},{2,2},{3,3},{4,4},{5,5},{6,6},{7,7},{8,128},{9,129},{1... | collective-permute-start | bytes 663560 | tf_op jit(solution)/shard_map/ppermute | solution.py:40
  16.9 3.5 %collective-permute-start.3 = (bf16[16,16,128]{2,1,0:T(8,128)(2,1)S(1)}, bf16[16,16,128]{2,1,0:T(8,128)(2,1)S(1)}, u32[]{:S(2)}, u32[]{:S(2)}) collective-permute-start(bf16[16,16,128]{2,1,0:T(8,128)(2,1)S(1)} %get-tuple-element.85), channel_id=1, source_target_pairs={{0,248},{1,249},{2,250},{3,251},{4,252},{5,253},{6,254},{7,255},{8... | collective-permute-start | bytes 196616 | tf_op jit(solution)/shard_map/ppermute | solution.py:40
  24.5 18.3 %collective-permute-start.8 = (bf16[27,32,128]{2,1,0:T(8,128)(2,1)S(1)}, bf16[27,32,128]{2,1,0:T(8,128)(2,1)S(1)}, u32[]{:S(2)}, u32[]{:S(2)}) collective-permute-start(bf16[27,32,128]{2,1,0:T(8,128)(2,1)S(1)} %collective-permute-done.2.refs_0_), channel_id=1, source_target_pairs={{0,128},{1,129},{2,130},{3,131},{4,132},{5,133},{6,134},{7,135},{8... | collective-permute-start | bytes 663560 | tf_op jit(solution)/shard_map/ppermute | solution.py:40
  28.0 14.8 %collective-permute-start.7 = (bf16[27,32,128]{2,1,0:T(8,128)(2,1)S(1)}, bf16[27,32,128]{2,1,0:T(8,128)(2,1)S(1)}, u32[]{:S(2)}, u32[]{:S(2)}) collective-permute-start(bf16[27,32,128]{2,1,0:T(8,128)(2,1)S(1)} %collective-permute-done.2.refs_0_), channel_id=1, source_target_pairs={{0,192},{1,193},{2,194},{3,195},{4,196},{5,197},{6,198},{7,199},{8... | collective-permute-start | bytes 663560 | tf_op jit(solution)/shard_map/ppermute | solution.py:40
  28.9 10.3 %collective-permute-start.6 = (bf16[2,256,128]{2,1,0:T(8,128)(2,1)S(1)}, bf16[2,256,128]{2,1,0:T(8,128)(2,1)S(1)}, u32[]{:S(2)}, u32[]{:S(2)}) collective-permute-start(bf16[2,256,128]{2,1,0:T(8,128)(2,1)S(1)} %pad_maximum_fusion.2.refs_0_), channel_id=1, source_target_pairs={{0,4},{1,5},{2,6},{3,7},{4,0},{5,1},{6,2},{7,3},{8,12},{9,13},{10,... | collective-permute-start | bytes 393224 | tf_op jit(solution)/shard_map/ppermute | solution.py:40
  29.9 12.9 %collective-permute-start.5 = (bf16[2,256,128]{2,1,0:T(8,128)(2,1)S(1)}, bf16[2,256,128]{2,1,0:T(8,128)(2,1)S(1)}, u32[]{:S(2)}, u32[]{:S(2)}) collective-permute-start(bf16[2,256,128]{2,1,0:T(8,128)(2,1)S(1)} %pad_maximum_fusion.2.refs_0_), channel_id=1, source_target_pairs={{0,1},{1,2},{2,3},{3,4},{4,5},{5,6},{6,7},{7,0},{8,9},{9,10},{10,1... | collective-permute-start | bytes 393224 | tf_op jit(solution)/shard_map/ppermute | solution.py:40
  32.1 10.7 %collective-permute-start.4 = (bf16[2,256,128]{2,1,0:T(8,128)(2,1)S(1)}, bf16[2,256,128]{2,1,0:T(8,128)(2,1)S(1)}, u32[]{:S(2)}, u32[]{:S(2)}) collective-permute-start(bf16[2,256,128]{2,1,0:T(8,128)(2,1)S(1)} %pad_maximum_fusion.2.refs_0_), channel_id=1, source_target_pairs={{0,7},{1,0},{2,1},{3,2},{4,3},{5,4},{6,5},{7,6},{8,15},{9,8},{10,9... | collective-permute-start | bytes 393224 | tf_op jit(solution)/shard_map/ppermute | solution.py:40
  42.9 12.6 %collective-permute-start.10 = (bf16[4,256,128]{2,1,0:T(8,128)(2,1)S(1)}, bf16[4,256,128]{2,1,0:T(8,128)(2,1)S(1)}, u32[]{:S(2)}, u32[]{:S(2)}) collective-permute-start(bf16[4,256,128]{2,1,0:T(8,128)(2,1)S(1)} %get-tuple-element.88), channel_id=1, source_target_pairs={{0,1},{1,2},{2,3},{3,4},{4,5},{5,6},{6,7},{7,0},{8,9},{9,10},{10,1... | collective-permute-start | bytes 786440 | tf_op jit(solution)/shard_map/ppermute | solution.py:40
  43.9 11.5 %collective-permute-start.9 = (bf16[4,256,128]{2,1,0:T(8,128)(2,1)S(1)}, bf16[4,256,128]{2,1,0:T(8,128)(2,1)S(1)}, u32[]{:S(2)}, u32[]{:S(2)}) collective-permute-start(bf16[4,256,128]{2,1,0:T(8,128)(2,1)S(1)} %get-tuple-element.89), channel_id=1, source_target_pairs={{0,7},{1,0},{2,1},{3,2},{4,3},{5,4},{6,5},{7,6},{8,15},{9,8},{10,9... | collective-permute-start | bytes 786440 | tf_op jit(solution)/shard_map/ppermute | solution.py:40
  46.2 8.0 %collective-permute-start.11 = (bf16[27,32,128]{2,1,0:T(8,128)(2,1)S(1)}, bf16[27,32,128]{2,1,0:T(8,128)(2,1)S(1)}, u32[]{:S(2)}, u32[]{:S(2)}) collective-permute-start(bf16[27,32,128]{2,1,0:T(8,128)(2,1)S(1)} %collective-permute-done.2.refs_0_), channel_id=1, source_target_pairs={{0,64},{1,65},{2,66},{3,67},{4,68},{5,69},{6,70},{7,71},{8,72},{9,... | collective-permute-start | bytes 663560 | tf_op jit(solution)/shard_map/ppermute | solution.py:40
  55.4 18.4 %copy-start = (f32[128]{0:T(128)S(1)}, f32[128]{0:T(128)}, u32[]{:S(2)}) copy-start(f32[128]{0:T(128)} %param.6) | copy-start | bytes 1540
  62.2 2.0 %collective-permute-start.12 = (bf16[4,2,256,128]{3,2,1,0:T(8,128)(2,1)S(1)}, bf16[4,2,256,128]{3,2,1,0:T(8,128)(2,1)S(1)}, u32[]{:S(2)}, u32[]{:S(2)}) collective-permute-start(bf16[4,2,256,128]{3,2,1,0:T(8,128)(2,1)S(1)} %get-tuple-element.47), channel_id=1, source_target_pairs={{0,8},{1,9},{2,10},{3,11},{4,12},{5,13},{6,14},{7,15},{8,0},{9,1},... | collective-permute-start | bytes 1572872 | tf_op jit(solution)/shard_map/ppermute | solution.py:40
  64.4 5.6 %collective-permute-start.13 = (bf16[2,256,128]{2,1,0:T(8,128)(2,1)S(1)}, bf16[2,256,128]{2,1,0:T(8,128)(2,1)S(1)}, u32[]{:S(2)}, u32[]{:S(2)}) collective-permute-start(bf16[2,256,128]{2,1,0:T(8,128)(2,1)S(1)} %get-tuple-element.76), channel_id=1, source_target_pairs={{0,16},{1,17},{2,18},{3,19},{4,20},{5,21},{6,22},{7,23},{8,24},{9,... | collective-permute-start | bytes 393224 | tf_op jit(solution)/shard_map/ppermute | solution.py:40
  64.5 5.8 %collective-permute-start.15 = (bf16[2,256,128]{2,1,0:T(8,128)(2,1)S(1)}, bf16[2,256,128]{2,1,0:T(8,128)(2,1)S(1)}, u32[]{:S(2)}, u32[]{:S(2)}) collective-permute-start(bf16[2,256,128]{2,1,0:T(8,128)(2,1)S(1)} %get-tuple-element.77), channel_id=1, source_target_pairs={{0,48},{1,49},{2,50},{3,51},{4,52},{5,53},{6,54},{7,55},{8,56},{9,... | collective-permute-start | bytes 393224 | tf_op jit(solution)/shard_map/ppermute | solution.py:40
  66.5 7.3 %collective-permute-start.14 = (bf16[2,256,128]{2,1,0:T(8,128)(2,1)S(1)}, bf16[2,256,128]{2,1,0:T(8,128)(2,1)S(1)}, u32[]{:S(2)}, u32[]{:S(2)}) collective-permute-start(bf16[2,256,128]{2,1,0:T(8,128)(2,1)S(1)} %get-tuple-element.78), channel_id=1, source_target_pairs={{0,32},{1,33},{2,34},{3,35},{4,36},{5,37},{6,38},{7,39},{8,40},{9,... | collective-permute-start | bytes 393224 | tf_op jit(solution)/shard_map/ppermute | solution.py:40
  74.1 6.5 %collective-permute-start.19 = (bf16[2,256,128]{2,1,0:T(8,128)(2,1)S(1)}, bf16[2,256,128]{2,1,0:T(8,128)(2,1)S(1)}, u32[]{:S(2)}, u32[]{:S(2)}) collective-permute-start(bf16[2,256,128]{2,1,0:T(8,128)(2,1)S(1)} %get-tuple-element.74.refs_2_.refs_0_), channel_id=1, source_target_pairs={{0,48},{1,49},{2,50},{3,51},{4,52},{5,53},{6,54},{7,55},{8,56},{9,... | collective-permute-start | bytes 393224 | tf_op jit(solution)/shard_map/ppermute | solution.py:40
  75.0 7.4 %collective-permute-start.18 = (bf16[2,256,128]{2,1,0:T(8,128)(2,1)S(1)}, bf16[2,256,128]{2,1,0:T(8,128)(2,1)S(1)}, u32[]{:S(2)}, u32[]{:S(2)}) collective-permute-start(bf16[2,256,128]{2,1,0:T(8,128)(2,1)S(1)} %get-tuple-element.74.refs_2_.refs_0_), channel_id=1, source_target_pairs={{0,32},{1,33},{2,34},{3,35},{4,36},{5,37},{6,38},{7,39},{8,40},{9,... | collective-permute-start | bytes 393224 | tf_op jit(solution)/shard_map/ppermute | solution.py:40
  78.6 5.2 %collective-permute-start.17 = (bf16[2,256,128]{2,1,0:T(8,128)(2,1)S(1)}, bf16[2,256,128]{2,1,0:T(8,128)(2,1)S(1)}, u32[]{:S(2)}, u32[]{:S(2)}) collective-permute-start(bf16[2,256,128]{2,1,0:T(8,128)(2,1)S(1)} %get-tuple-element.74.refs_2_.refs_0_), channel_id=1, source_target_pairs={{0,16},{1,17},{2,18},{3,19},{4,20},{5,21},{6,22},{7,23},{8,24},{9,... | collective-permute-start | bytes 393224 | tf_op jit(solution)/shard_map/ppermute | solution.py:40
  78.6 5.8 %collective-permute-start.20 = (bf16[2,256,128]{2,1,0:T(8,128)(2,1)S(1)}, bf16[2,256,128]{2,1,0:T(8,128)(2,1)S(1)}, u32[]{:S(2)}, u32[]{:S(2)}) collective-permute-start(bf16[2,256,128]{2,1,0:T(8,128)(2,1)S(1)} %get-tuple-element.74.refs_2_.refs_0_), channel_id=1, source_target_pairs={{0,8},{1,9},{2,10},{3,11},{4,12},{5,13},{6,14},{7,15},{8,0},{9,1},... | collective-permute-start | bytes 393224 | tf_op jit(solution)/shard_map/ppermute | solution.py:40
  80.6 3.9 %collective-permute-start.23 = (bf16[2,256,128]{2,1,0:T(8,128)(2,1)S(1)}, bf16[2,256,128]{2,1,0:T(8,128)(2,1)S(1)}, u32[]{:S(2)}, u32[]{:S(2)}) collective-permute-start(bf16[2,256,128]{2,1,0:T(8,128)(2,1)S(1)} %collective-permute-done.19.refs_5_.refs_3_), channel_id=1, source_target_pairs={{0,8},{1,9},{2,10},{3,11},{4,12},{5,13},{6,14},{7,15},{8,0},{9,1},... | collective-permute-start | bytes 393224 | tf_op jit(solution)/shard_map/ppermute | solution.py:40
  82.4 2.0 %collective-permute-start.22 = (bf16[2,256,128]{2,1,0:T(8,128)(2,1)S(1)}, bf16[2,256,128]{2,1,0:T(8,128)(2,1)S(1)}, u32[]{:S(2)}, u32[]{:S(2)}) collective-permute-start(bf16[2,256,128]{2,1,0:T(8,128)(2,1)S(1)} %collective-permute-done.18.refs_4_.refs_2_), channel_id=1, source_target_pairs={{0,8},{1,9},{2,10},{3,11},{4,12},{5,13},{6,14},{7,15},{8,0},{9,1},... | collective-permute-start | bytes 393224 | tf_op jit(solution)/shard_map/ppermute | solution.py:40
  83.8 1.3 collective-permute-start.21
  83.8 36.9 %collective-permute-start.16 = (bf16[256,128]{1,0:T(8,128)(2,1)S(1)}, bf16[256,128]{1,0:T(8,128)(2,1)S(1)}, u32[]{:S(2)}, u32[]{:S(2)}) collective-permute-start(bf16[256,128]{1,0:T(8,128)(2,1)S(1)} %get-tuple-element.86), channel_id=1, source_target_pairs={{0,8},{1,9},{2,10},{3,11},{4,12},{5,13},{6,14},{7,15},{8,16},{9,17... | collective-permute-start | bytes 196616 | tf_op jit(solution)/shard_map/ppermute | solution.py:40
  91.2 14.3 %collective-permute-start.26 = (bf16[28,32,128]{2,1,0:T(8,128)(2,1)S(1)}, bf16[28,32,128]{2,1,0:T(8,128)(2,1)S(1)}, u32[]{:S(2)}, u32[]{:S(2)}) collective-permute-start(bf16[28,32,128]{2,1,0:T(8,128)(2,1)S(1)} %get-tuple-element.64), channel_id=1, source_target_pairs={{0,64},{1,65},{2,66},{3,67},{4,68},{5,69},{6,70},{7,71},{8,72},{9,... | collective-permute-start | bytes 688136 | tf_op jit(solution)/shard_map/ppermute | solution.py:40
  91.3 14.5 %collective-permute-start.27 = (bf16[28,32,128]{2,1,0:T(8,128)(2,1)S(1)}, bf16[28,32,128]{2,1,0:T(8,128)(2,1)S(1)}, u32[]{:S(2)}, u32[]{:S(2)}) collective-permute-start(bf16[28,32,128]{2,1,0:T(8,128)(2,1)S(1)} %get-tuple-element.65), channel_id=1, source_target_pairs={{0,128},{1,129},{2,130},{3,131},{4,132},{5,133},{6,134},{7,135},{8... | collective-permute-start | bytes 688136 | tf_op jit(solution)/shard_map/ppermute | solution.py:40
  92.4 13.8 %collective-permute-start.28 = (bf16[28,32,128]{2,1,0:T(8,128)(2,1)S(1)}, bf16[28,32,128]{2,1,0:T(8,128)(2,1)S(1)}, u32[]{:S(2)}, u32[]{:S(2)}) collective-permute-start(bf16[28,32,128]{2,1,0:T(8,128)(2,1)S(1)} %get-tuple-element.66), channel_id=1, source_target_pairs={{0,192},{1,193},{2,194},{3,195},{4,196},{5,197},{6,198},{7,199},{8... | collective-permute-start | bytes 688136 | tf_op jit(solution)/shard_map/ppermute | solution.py:40
  99.1 9.6 %collective-permute-start.24 = (bf16[4,256,128]{2,1,0:T(8,128)(2,1)S(1)}, bf16[4,256,128]{2,1,0:T(8,128)(2,1)S(1)}, u32[]{:S(2)}, u32[]{:S(2)}) collective-permute-start(bf16[4,256,128]{2,1,0:T(8,128)(2,1)S(1)} %get-tuple-element.61), channel_id=1, source_target_pairs={{0,1},{1,2},{2,3},{3,4},{4,5},{5,6},{6,7},{7,0},{8,9},{9,10},{10,1... | collective-permute-start | bytes 786440 | tf_op jit(solution)/shard_map/ppermute | solution.py:40
  105.6 8.1 %collective-permute-start.25 = (bf16[4,256,128]{2,1,0:T(8,128)(2,1)S(1)}, bf16[4,256,128]{2,1,0:T(8,128)(2,1)S(1)}, u32[]{:S(2)}, u32[]{:S(2)}) collective-permute-start(bf16[4,256,128]{2,1,0:T(8,128)(2,1)S(1)} %get-tuple-element.62), channel_id=1, source_target_pairs={{0,7},{1,0},{2,1},{3,2},{4,3},{5,4},{6,5},{7,6},{8,15},{9,8},{10,9... | collective-permute-start | bytes 786440 | tf_op jit(solution)/shard_map/ppermute | solution.py:40
  113.7 11.8 %collective-permute-start.29 = (bf16[2,256,128]{2,1,0:T(8,128)(2,1)S(1)}, bf16[2,256,128]{2,1,0:T(8,128)(2,1)S(1)}, u32[]{:S(2)}, u32[]{:S(2)}) collective-permute-start(bf16[2,256,128]{2,1,0:T(8,128)(2,1)S(1)} %get-tuple-element.79), channel_id=1, source_target_pairs={{0,4},{1,5},{2,6},{3,7},{4,0},{5,1},{6,2},{7,3},{8,12},{9,13},{10,... | collective-permute-start | bytes 393224 | tf_op jit(solution)/shard_map/ppermute | solution.py:40
  117.5 8.7 %collective-permute-start.30 = (bf16[2,256,128]{2,1,0:T(8,128)(2,1)S(1)}, bf16[2,256,128]{2,1,0:T(8,128)(2,1)S(1)}, u32[]{:S(2)}, u32[]{:S(2)}) collective-permute-start(bf16[2,256,128]{2,1,0:T(8,128)(2,1)S(1)} %get-tuple-element.80), channel_id=1, source_target_pairs={{0,1},{1,2},{2,3},{3,4},{4,5},{5,6},{6,7},{7,0},{8,9},{9,10},{10,1... | collective-permute-start | bytes 393224 | tf_op jit(solution)/shard_map/ppermute | solution.py:40
  117.5 8.7 %collective-permute-start.31 = (bf16[2,256,128]{2,1,0:T(8,128)(2,1)S(1)}, bf16[2,256,128]{2,1,0:T(8,128)(2,1)S(1)}, u32[]{:S(2)}, u32[]{:S(2)}) collective-permute-start(bf16[2,256,128]{2,1,0:T(8,128)(2,1)S(1)} %get-tuple-element.81), channel_id=1, source_target_pairs={{0,7},{1,0},{2,1},{3,2},{4,3},{5,4},{6,5},{7,6},{8,15},{9,8},{10,9... | collective-permute-start | bytes 393224 | tf_op jit(solution)/shard_map/ppermute | solution.py:40
  121.4 22.5 %collective-permute-start.34 = (bf16[27,32,128]{2,1,0:T(8,128)(2,1)S(1)}, bf16[27,32,128]{2,1,0:T(8,128)(2,1)S(1)}, u32[]{:S(2)}, u32[]{:S(2)}) collective-permute-start(bf16[27,32,128]{2,1,0:T(8,128)(2,1)S(1)} %slice.120), channel_id=1, source_target_pairs={{0,0},{1,1},{2,2},{3,3},{4,4},{5,5},{6,6},{7,7},{8,128},{9,129},{1... | collective-permute-start | bytes 663560 | tf_op jit(solution)/shard_map/ppermute | solution.py:40
  126.3 10.4 %collective-permute-start.32 = (bf16[256,128]{1,0:T(8,128)(2,1)S(1)}, bf16[256,128]{1,0:T(8,128)(2,1)S(1)}, u32[]{:S(2)}, u32[]{:S(2)}) collective-permute-start(bf16[256,128]{1,0:T(8,128)(2,1)S(1)} %get-tuple-element.82), channel_id=1, source_target_pairs={{0,8},{1,16},{2,24},{3,32},{4,40},{5,48},{6,56},{7,64},{8,44},{9,5... | collective-permute-start | bytes 196616 | tf_op jit(solution)/shard_map/ppermute | solution.py:40
  130.8 12.5 %collective-permute-start.33 = (bf16[256,128]{1,0:T(8,128)(2,1)S(1)}, bf16[256,128]{1,0:T(8,128)(2,1)S(1)}, u32[]{:S(2)}, u32[]{:S(2)}) collective-permute-start(bf16[256,128]{1,0:T(8,128)(2,1)S(1)} %get-tuple-element.83), channel_id=1, source_target_pairs={{0,0},{1,8},{2,16},{3,24},{4,32},{5,40},{6,48},{7,56},{8,36},{9,44... | collective-permute-start | bytes 196616 | tf_op jit(solution)/shard_map/ppermute | solution.py:40

commit v2 on v1

--- a/solution.py
+++ b/solution.py
@@ -256,19 +256,19 @@
         filters.transpose(1, 0, 2),
         lambda x, q, z: at(swapped(q % NX), holder((NQ * x + q) // NX), z),
     )
-    ahead = permuted(cotangent[0], lambda x, q, z: device(NQ * x + q - 1, z))
-    first = permuted(features[1].reshape(FACE, size), lambda x, q, z: at(x, holder(z), z + q))
-    second = permuted(
-        features[0].reshape(FACE, size), lambda x, q, z: at(x - (q == 0), holder(z), z + q - 1)
-    )
-    own = jnp.stack([first, second])
-    own, block, ahead = lax.optimization_barrier((own, block, ahead))
+    seconds = permuted(
+        jnp.stack([features[0], cotangent[0]]), lambda x, q, z: device(NQ * x + q - 1, z)
+    )
+    ahead = seconds[1]
+    own = jnp.stack([features[1], seconds[0]]).reshape(2, FACE, size)
+    own = permuted(own, lambda x, q, z: at(x, holder(z), z + q))
+    own, block = lax.optimization_barrier((own, block))
     blocks = [block] + [
         permuted(block, lambda x, q, z: at(x - shift, q, z)) for shift in range(1, NX)
     ]
     above, below, beyond = along_z(own, -1), along_z(own, 1), along_z(own, 4)
-    above, below, beyond, blocks[1], blocks[2] = lax.optimization_barrier(
-        (above, below, beyond, blocks[1], blocks[2])
+    above, below, beyond, blocks[2] = lax.optimization_barrier(
+        (above, below, beyond, blocks[2])
     )
     planes = [
         own,
@@ -314,7 +314,6 @@
     output, slope = gelu_pair(pre_act)
     activated = output.astype(bf16)
     behind = permuted(activated[1], lambda x, q, z: device(NQ * x + q + 1, z))
-    activated = jnp.stack([behind, activated[0]])
     grad_pre = (target.reshape(2, FACE, out_size).astype(f32) * slope).astype(bf16)
 
     slopes = [grad_pre]
@@ -337,7 +336,7 @@
         ],
         flops,
     )
-    where, terms = lax.optimization_barrier((where, terms))
+    where, terms, behind = lax.optimization_barrier((where, terms, behind))
     held = terms[0]
     for r in range(1, NX):
         held = held + permuted(terms[r], lambda x, q, z: at(x + r, q, z)).astype(f32)
@@ -376,6 +375,7 @@
 
     grad_input = jnp.stack([permuted(summed[1], home(1)), permuted(summed[0], home(0))])
 
+    activated = jnp.stack([behind, activated[0]])
     shape = (2, GRID, GRID)
     return (
         activated.reshape(*shape, out_size),

time: 145 us -> 139 us (0.959)
  waiting for transfers between devices: 56.6 us -> 33 us
  starting transfers between devices: 60.1 us -> 77.3 us
    ppermute x35 -> x34, waiting for transfers between devices: 56.6 us -> 33 us  [permuted(): return lax.ppermute(array, ('space', 'chan'), pairs)]
    ppermute x35 -> x34, starting transfers between devices: 60.1 us -> 77.3 us  [permuted(): return lax.ppermute(array, ('space', 'chan'), pairs)]
  transfers between devices with their start and end apart: 35 -> 34, of which waited for: 21 -> 16; matrix products, arithmetic and copies ran while one was open for 2% -> 2% of each run, Pallas kernels for 10% -> 11%
where the time goes in v2:
time: 139 us; the launch traced here: 138 us
  starting transfers between devices  77.3 us (56%)
  waiting for transfers between devices  33 us (24%)
  Pallas kernels  21.8 us (16%)
  other arithmetic  3.58 us (3%)
    ppermute x34, starting transfers between devices, permuted(): return lax.ppermute(array, ('space', 'chan'), pairs)  77.3 us
    ppermute x34, waiting for transfers between devices, permuted(): return lax.ppermute(array, ('space', 'chan'), pairs)  33 us
    pallas_call x6, Pallas kernels, call(): pl.pallas_call(kernel, out_shape=outs, in_specs=[pl.BlockSpec(memory_spac...  21.8 us
  transfers between devices with their start and end apart: 34, of which 16 were waited for; matrix products, arithmetic and copies ran while one was open for 2% of the time, Pallas kernels for 11%

profile of v2, /device:TPU:16, one launch (start us, length us, event | category | flops | bytes accessed | tf_op | source)
XLA Modules:
  0.0 137.7 jit_solution(8490318680789088259)
XLA Ops:
  0.6 1.0 fusion.13
  1.7 2.4 %collective-permute-start.2 = (bf16[27,32,128]{2,1,0:T(8,128)(2,1)}, bf16[27,32,128]{2,1,0:T(8,128)(2,1)S(1)}, u32[]{:S(2)}, u32[]{:S(2)}) collective-permute-start(bf16[27,32,128]{2,1,0:T(8,128)(2,1)} %bitcast.46), channel_id=1, source_target_pairs={{0,0},{1,1},{2,2},{3,3},{4,4},{5,5},{6,6},{7,7},{8,128},{9,129},{1... | collective-permute-start | bytes 663560 | tf_op jit(solution)/shard_map/ppermute | solution.py:40
  4.3 13.5 %collective-permute-start.1 = (bf16[2,256,128]{2,1,0:T(8,128)(2,1)S(1)}, bf16[2,256,128]{2,1,0:T(8,128)(2,1)S(1)}, u32[]{:S(2)}, u32[]{:S(2)}) collective-permute-start(bf16[2,256,128]{2,1,0:T(8,128)(2,1)S(1)} %bitcast.42), channel_id=1, source_target_pairs={{0,0},{1,17},{2,34},{3,51},{4,12},{5,29},{6,46},{7,63},{8,1},{9,18... | collective-permute-start | bytes 393224 | tf_op jit(solution)/shard_map/ppermute | solution.py:40
  17.8 2.5 %collective-permute-done.1.refs_0_ = bf16[2,256,128]{2,1,0:T(8,128)(2,1)S(1)} collective-permute-done((bf16[2,256,128]{2,1,0:T(8,128)(2,1)S(1)}, bf16[2,256,128]{2,1,0:T(8,128)(2,1)S(1)}, u32[]{:S(2)}, u32[]{:S(2)}) %collective-permute-start.1) | collective-permute-done | bytes 131104 | tf_op jit(solution)/shard_map/ppermute | solution.py:40
  20.3 0.8 collective-permute-start.6
  21.1 7.3 %collective-permute-start.5 = (bf16[2,256,128]{2,1,0:T(8,128)(2,1)S(1)}, bf16[2,256,128]{2,1,0:T(8,128)(2,1)S(1)}, u32[]{:S(2)}, u32[]{:S(2)}) collective-permute-start(bf16[2,256,128]{2,1,0:T(8,128)(2,1)S(1)} %collective-permute-done.1.refs_0_), channel_id=1, source_target_pairs={{0,4},{1,5},{2,6},{3,7},{4,0},{5,1},{6,2},{7,3},{8,12},{9,13},{10,... | collective-permute-start | bytes 393224 | tf_op jit(solution)/shard_map/ppermute | solution.py:40
  28.4 1.4 collective-permute-start.4
  29.7 1.9 %collective-permute-start.3 = (bf16[2,256,128]{2,1,0:T(8,128)(2,1)S(1)}, bf16[2,256,128]{2,1,0:T(8,128)(2,1)S(1)}, u32[]{:S(2)}, u32[]{:S(2)}) collective-permute-start(bf16[2,256,128]{2,1,0:T(8,128)(2,1)S(1)} %collective-permute-done.1.refs_0_), channel_id=1, source_target_pairs={{0,7},{1,0},{2,1},{3,2},{4,3},{5,4},{6,5},{7,6},{8,15},{9,8},{10,9... | collective-permute-start | bytes 393224 | tf_op jit(solution)/shard_map/ppermute | solution.py:40
  31.6 3.8 %collective-permute-done.5.refs_3_ = bf16[2,256,128]{2,1,0:T(8,128)(2,1)S(1)} collective-permute-done((bf16[2,256,128]{2,1,0:T(8,128)(2,1)S(1)}, bf16[2,256,128]{2,1,0:T(8,128)(2,1)S(1)}, u32[]{:S(2)}, u32[]{:S(2)}) %collective-permute-start.5) | collective-permute-done | bytes 131104 | tf_op jit(solution)/shard_map/ppermute | solution.py:40
  35.8 4.1 %collective-permute-start.8 = (bf16[4,256,128]{2,1,0:T(8,128)(2,1)S(1)}, bf16[4,256,128]{2,1,0:T(8,128)(2,1)S(1)}, u32[]{:S(2)}, u32[]{:S(2)}) collective-permute-start(bf16[4,256,128]{2,1,0:T(8,128)(2,1)S(1)} %get-tuple-element.88), channel_id=1, source_target_pairs={{0,1},{1,2},{2,3},{3,4},{4,5},{5,6},{6,7},{7,0},{8,9},{9,10},{10,1... | collective-permute-start | bytes 786440 | tf_op jit(solution)/shard_map/ppermute | solution.py:40
  39.9 0.6 collective-permute-start.7
  40.5 2.1 %collective-permute-start.10 = (bf16[27,32,128]{2,1,0:T(8,128)(2,1)S(1)}, bf16[27,32,128]{2,1,0:T(8,128)(2,1)S(1)}, u32[]{:S(2)}, u32[]{:S(2)}) collective-permute-start(bf16[27,32,128]{2,1,0:T(8,128)(2,1)S(1)} %collective-permute-done.2.refs_0_), channel_id=1, source_target_pairs={{0,64},{1,65},{2,66},{3,67},{4,68},{5,69},{6,70},{7,71},{8,72},{9,... | collective-permute-start | bytes 663560 | tf_op jit(solution)/shard_map/ppermute | solution.py:40
  42.6 1.1 collective-permute-start.9
  43.8 4.4 %collective-permute-done.10.refs_3_ = bf16[27,32,128]{2,1,0:T(8,128)(2,1)S(1)} collective-permute-done((bf16[27,32,128]{2,1,0:T(8,128)(2,1)S(1)}, bf16[27,32,128]{2,1,0:T(8,128)(2,1)S(1)}, u32[]{:S(2)}, u32[]{:S(2)}) %collective-permute-start.10) | collective-permute-done | bytes 221216 | tf_op jit(solution)/shard_map/ppermute | solution.py:40
  48.5 1.2 shard_map.75
  49.8 6.7 %shard_map.76 = (f32[4,2,256,128]{3,2,1,0:T(8,128)S(1)}, bf16[4,2,256,128]{3,2,1,0:T(8,128)(2,1)S(1)}, bf16[18,288,384]{2,1,0:T(8,128)(2,1)S(1)}) custom-call(s32[2]{0:T(128)S(1)} %pad_add_fusion.where.refs_0_, bf16[2,256,128]{2,1,0:T(8,128)(2,1)S(1)} %collective-permute-done.1.refs_0_, bf16[2,256,128]{2,1,0:T(8,128)(2,1)S(1)} %collective-permute-done.3.refs_1_, ...), custom_call_target="tpu_custom_call" | custom-call | flops 3623878656 | bytes 8962048 | tf_op jit(solution)/shard_map/pallas_call | solution.py:234
  56.6 1.9 %collective-permute-done.11 = bf16[4,2,256,128]{3,2,1,0:T(8,128)(2,1)S(1)} collective-permute-done((bf16[4,2,256,128]{3,2,1,0:T(8,128)(2,1)S(1)}, bf16[4,2,256,128]{3,2,1,0:T(8,128)(2,1)S(1)}, u32[]{:S(2)}, u32[]{:S(2)}) %collective-permute-start.11) | collective-permute-done | bytes 524320 | tf_op jit(solution)/shard_map/ppermute | solution.py:40
  58.7 4.0 %collective-permute-start.12 = (bf16[2,256,128]{2,1,0:T(8,128)(2,1)S(1)}, bf16[2,256,128]{2,1,0:T(8,128)(2,1)S(1)}, u32[]{:S(2)}, u32[]{:S(2)}) collective-permute-start(bf16[2,256,128]{2,1,0:T(8,128)(2,1)S(1)} %get-tuple-element.74), channel_id=1, source_target_pairs={{0,16},{1,17},{2,18},{3,19},{4,20},{5,21},{6,22},{7,23},{8,24},{9,... | collective-permute-start | bytes 393224 | tf_op jit(solution)/shard_map/ppermute | solution.py:40
  62.7 2.3 %collective-permute-start.13 = (bf16[2,256,128]{2,1,0:T(8,128)(2,1)S(1)}, bf16[2,256,128]{2,1,0:T(8,128)(2,1)S(1)}, u32[]{:S(2)}, u32[]{:S(2)}) collective-permute-start(bf16[2,256,128]{2,1,0:T(8,128)(2,1)S(1)} %get-tuple-element.76), channel_id=1, source_target_pairs={{0,32},{1,33},{2,34},{3,35},{4,36},{5,37},{6,38},{7,39},{8,40},{9,... | collective-permute-start | bytes 393224 | tf_op jit(solution)/shard_map/ppermute | solution.py:40
  65.1 1.4 %collective-permute-done.12 = bf16[2,256,128]{2,1,0:T(8,128)(2,1)S(1)} collective-permute-done((bf16[2,256,128]{2,1,0:T(8,128)(2,1)S(1)}, bf16[2,256,128]{2,1,0:T(8,128)(2,1)S(1)}, u32[]{:S(2)}, u32[]{:S(2)}) %collective-permute-start.12) | collective-permute-done | bytes 131104 | tf_op jit(solution)/shard_map/ppermute | solution.py:40
  66.5 2.6 %collective-permute-done.14 = bf16[2,256,128]{2,1,0:T(8,128)(2,1)S(1)} collective-permute-done((bf16[2,256,128]{2,1,0:T(8,128)(2,1)S(1)}, bf16[2,256,128]{2,1,0:T(8,128)(2,1)S(1)}, u32[]{:S(2)}, u32[]{:S(2)}) %collective-permute-start.14) | collective-permute-done | bytes 131104 | tf_op jit(solution)/shard_map/ppermute | solution.py:40
  69.1 0.4 collective-permute-done.13
  69.8 2.8 %collective-permute-start.17 = (bf16[2,256,128]{2,1,0:T(8,128)(2,1)S(1)}, bf16[2,256,128]{2,1,0:T(8,128)(2,1)S(1)}, u32[]{:S(2)}, u32[]{:S(2)}) collective-permute-start(bf16[2,256,128]{2,1,0:T(8,128)(2,1)S(1)} %get-tuple-element.72.refs_2_.refs_0_), channel_id=1, source_target_pairs={{0,48},{1,49},{2,50},{3,51},{4,52},{5,53},{6,54},{7,55},{8,56},{9,... | collective-permute-start | bytes 393224 | tf_op jit(solution)/shard_map/ppermute | solution.py:40
  72.6 2.4 %collective-permute-start.16 = (bf16[2,256,128]{2,1,0:T(8,128)(2,1)S(1)}, bf16[2,256,128]{2,1,0:T(8,128)(2,1)S(1)}, u32[]{:S(2)}, u32[]{:S(2)}) collective-permute-start(bf16[2,256,128]{2,1,0:T(8,128)(2,1)S(1)} %get-tuple-element.72.refs_2_.refs_0_), channel_id=1, source_target_pairs={{0,32},{1,33},{2,34},{3,35},{4,36},{5,37},{6,38},{7,39},{8,40},{9,... | collective-permute-start | bytes 393224 | tf_op jit(solution)/shard_map/ppermute | solution.py:40
  75.0 0.6 collective-permute-start.15
  75.6 2.4 %collective-permute-done.17.refs_5_.refs_3_ = bf16[2,256,128]{2,1,0:T(8,128)(2,1)S(1)} collective-permute-done((bf16[2,256,128]{2,1,0:T(8,128)(2,1)S(1)}, bf16[2,256,128]{2,1,0:T(8,128)(2,1)S(1)}, u32[]{:S(2)}, u32[]{:S(2)}) %collective-permute-start.17) | collective-permute-done | bytes 131104 | tf_op jit(solution)/shard_map/ppermute | solution.py:40
  77.9 1.8 %collective-permute-done.16.refs_4_.refs_2_ = bf16[2,256,128]{2,1,0:T(8,128)(2,1)S(1)} collective-permute-done((bf16[2,256,128]{2,1,0:T(8,128)(2,1)S(1)}, bf16[2,256,128]{2,1,0:T(8,128)(2,1)S(1)}, u32[]{:S(2)}, u32[]{:S(2)}) %collective-permute-start.16) | collective-permute-done | bytes 131104 | tf_op jit(solution)/shard_map/ppermute | solution.py:40
  79.7 1.3 collective-permute-done.15.refs_3_.refs_1_
  81.1 0.6 collective-permute-start.22
  81.7 0.7 collective-permute-done.19.refs_7_.refs_5_
  82.4 6.1 %shard_map.77 = (f32[28,32,128]{2,1,0:T(8,128)S(1)}, bf16[28,32,128]{2,1,0:T(8,128)(2,1)S(1)}, bf16[28,32,128]{2,1,0:T(8,128)(2,1)S(1)}, bf16[28,32,128]{2,1,0:T(8,128)(2,1)S(1)}) custom-call(s32[2]{0:T(128)S(1)} %pad_add_fusion.where.refs_0_, bf16[18,288,384]{2,1,0:T(8,128)(2,1)S(1)} %get-tuple-element.44.refs_1_, ...), custom_call_target="tpu_custom_call" | custom-call | flops 3623878656 | bytes 6176768 | tf_op jit(solution)/shard_map/pallas_call | solution.py:234
  88.9 3.7 %collective-permute-start.26 = (bf16[28,32,128]{2,1,0:T(8,128)(2,1)S(1)}, bf16[28,32,128]{2,1,0:T(8,128)(2,1)S(1)}, u32[]{:S(2)}, u32[]{:S(2)}) collective-permute-start(bf16[28,32,128]{2,1,0:T(8,128)(2,1)S(1)} %get-tuple-element.63), channel_id=1, source_target_pairs={{0,128},{1,129},{2,130},{3,131},{4,132},{5,133},{6,134},{7,135},{8... | collective-permute-start | bytes 688136 | tf_op jit(solution)/shard_map/ppermute | solution.py:40
  92.6 1.4 %shard_map.78.refs_1_ = bf16[18,288,384]{2,1,0:T(8,128)(2,1)S(1)} custom-call(s32[2]{0:T(128)S(1)} %pad_add_fusion.where.refs_0_, bf16[2,256,128]{2,1,0:T(8,128)(2,1)S(1)} %get-tuple-element.72.refs_2_.refs_0_, bf16[2,256,128]{2,1,0:T(8,128)(2,1)S(1)} %collective-permute-done.15.refs_3_.refs_1_, ...), custom_call_target="tpu_custom_call" | custom-call | bytes 5029888 | tf_op jit(solution)/shard_map/pallas_call | solution.py:234
  94.0 3.1 %shard_map.79 = (bf16[4,256,128]{2,1,0:T(8,128)(2,1)S(1)}, bf16[4,256,128]{2,1,0:T(8,128)(2,1)S(1)}) custom-call(s32[2]{0:T(128)S(1)} %pad_add_fusion.where.refs_0_, bf16[18,288,384]{2,1,0:T(8,128)(2,1)S(1)} %shard_map.78.refs_1_, bf16[2,2304,256]{2,1,0:T(8,128)(2,1)S(1)} %get-tuple-element.53.refs_2_), custom_call_target="tpu_custom_call" | custom-call | flops 1811939328 | bytes 6864896 | tf_op jit(solution)/shard_map/pallas_call | solution.py:234
  97.3 3.2 %collective-permute-start.24 = (bf16[4,256,128]{2,1,0:T(8,128)(2,1)S(1)}, bf16[4,256,128]{2,1,0:T(8,128)(2,1)S(1)}, u32[]{:S(2)}, u32[]{:S(2)}) collective-permute-start(bf16[4,256,128]{2,1,0:T(8,128)(2,1)S(1)} %get-tuple-element.60), channel_id=1, source_target_pairs={{0,7},{1,0},{2,1},{3,2},{4,3},{5,4},{6,5},{7,6},{8,15},{9,8},{10,9... | collective-permute-start | bytes 786440 | tf_op jit(solution)/shard_map/ppermute | solution.py:40
  100.5 3.1 %shard_map.80 = (f32[2,256,128]{2,1,0:T(8,128)S(1)}, f32[2,256,128]{2,1,0:T(8,128)S(1)}, f32[2,256,128]{2,1,0:T(8,128)S(1)}, f32[2,256,128]{2,1,0:T(8,128)S(1)}) custom-call(s32[2]{0:T(128)S(1)} %pad_add_fusion.where.refs_0_, bf16[18,288,384]{2,1,0:T(8,128)(2,1)S(1)} %shard_map.78.refs_1_, bf16[2,2304,256]{2,1,0:T(8,128)(2,1)S(1)} %get-tuple-element.53.refs_2_), custom_call_target="tpu_custom_call" | custom-call | flops 1811939328 | bytes 7389184 | tf_op jit(solution)/shard_map/pallas_call | solution.py:234
  103.8 2.4 %collective-permute-done.23 = bf16[4,256,128]{2,1,0:T(8,128)(2,1)S(1)} collective-permute-done((bf16[4,256,128]{2,1,0:T(8,128)(2,1)S(1)}, bf16[4,256,128]{2,1,0:T(8,128)(2,1)S(1)}, u32[]{:S(2)}, u32[]{:S(2)}) %collective-permute-start.23) | collective-permute-done | bytes 262176 | tf_op jit(solution)/shard_map/ppermute | solution.py:40
  106.4 2.5 %collective-permute-start.28 = (bf16[2,256,128]{2,1,0:T(8,128)(2,1)S(1)}, bf16[2,256,128]{2,1,0:T(8,128)(2,1)S(1)}, u32[]{:S(2)}, u32[]{:S(2)}) collective-permute-start(bf16[2,256,128]{2,1,0:T(8,128)(2,1)S(1)} %get-tuple-element.77), channel_id=1, source_target_pairs={{0,4},{1,5},{2,6},{3,7},{4,0},{5,1},{6,2},{7,3},{8,12},{9,13},{10,... | collective-permute-start | bytes 393224 | tf_op jit(solution)/shard_map/ppermute | solution.py:40
  108.9 0.4 collective-permute-start.29
  109.3 2.8 %collective-permute-start.30 = (bf16[2,256,128]{2,1,0:T(8,128)(2,1)S(1)}, bf16[2,256,128]{2,1,0:T(8,128)(2,1)S(1)}, u32[]{:S(2)}, u32[]{:S(2)}) collective-permute-start(bf16[2,256,128]{2,1,0:T(8,128)(2,1)S(1)} %get-tuple-element.79), channel_id=1, source_target_pairs={{0,7},{1,0},{2,1},{3,2},{4,3},{5,4},{6,5},{7,6},{8,15},{9,8},{10,9... | collective-permute-start | bytes 393224 | tf_op jit(solution)/shard_map/ppermute | solution.py:40
  112.1 0.7 pad_maximum_fusion.5
  112.8 5.5 %collective-permute-start.33 = (bf16[27,32,128]{2,1,0:T(8,128)(2,1)S(1)}, bf16[27,32,128]{2,1,0:T(8,128)(2,1)S(1)}, u32[]{:S(2)}, u32[]{:S(2)}) collective-permute-start(bf16[27,32,128]{2,1,0:T(8,128)(2,1)S(1)} %slice.129), channel_id=1, source_target_pairs={{0,0},{1,1},{2,2},{3,3},{4,4},{5,5},{6,6},{7,7},{8,128},{9,129},{1... | collective-permute-start | bytes 663560 | tf_op jit(solution)/shard_map/ppermute | solution.py:40
  118.4 5.3 %collective-permute-start.31 = (bf16[256,128]{1,0:T(8,128)(2,1)S(1)}, bf16[256,128]{1,0:T(8,128)(2,1)S(1)}, u32[]{:S(2)}, u32[]{:S(2)}) collective-permute-start(bf16[256,128]{1,0:T(8,128)(2,1)S(1)} %get-tuple-element.80), channel_id=1, source_target_pairs={{0,8},{1,16},{2,24},{3,32},{4,40},{5,48},{6,56},{7,64},{8,44},{9,5... | collective-permute-start | bytes 196616 | tf_op jit(solution)/shard_map/ppermute | solution.py:40
  123.7 5.4 %collective-permute-start.32 = (bf16[256,128]{1,0:T(8,128)(2,1)S(1)}, bf16[256,128]{1,0:T(8,128)(2,1)S(1)}, u32[]{:S(2)}, u32[]{:S(2)}) collective-permute-start(bf16[256,128]{1,0:T(8,128)(2,1)S(1)} %get-tuple-element.81), channel_id=1, source_target_pairs={{0,0},{1,8},{2,16},{3,24},{4,32},{5,40},{6,48},{7,56},{8,36},{9,44... | collective-permute-start | bytes 196616 | tf_op jit(solution)/shard_map/ppermute | solution.py:40
  129.1 0.5 fusion.11
  129.6 6.6 %collective-permute-done.32 = bf16[256,128]{1,0:T(8,128)(2,1)S(1)} collective-permute-done((bf16[256,128]{1,0:T(8,128)(2,1)S(1)}, bf16[256,128]{1,0:T(8,128)(2,1)S(1)}, u32[]{:S(2)}, u32[]{:S(2)}) %collective-permute-start.32) | collective-permute-done | bytes 65568 | tf_op jit(solution)/shard_map/ppermute | solution.py:40
  136.2 0.7 pad_maximum_fusion.6
  136.9 0.8 convert_bitcast_fusion
  (48 shorter events, 2.5 us)
Async XLA Ops:
  1.6 2.6 %collective-permute-start = (bf16[2,16,16,128]{3,2,1,0:T(8,128)(2,1)S(1)}, bf16[2,16,16,128]{3,2,1,0:T(8,128)(2,1)S(1)}, u32[]{:S(2)}, u32[]{:S(2)}) collective-permute-start(bf16[2,16,16,128]{3,2,1,0:T(8,128)(2,1)S(1)} %pad_maximum_fusion.2), channel_id=1, source_target_pairs={{0,248},{1,249},{2,250},{3,251},{4,252},{5,253},{6,254},{7,255},{8... | collective-permute-start | bytes 393224 | tf_op jit(solution)/shard_map/ppermute | solution.py:40
  1.7 16.1 %collective-permute-start.2 = (bf16[27,32,128]{2,1,0:T(8,128)(2,1)}, bf16[27,32,128]{2,1,0:T(8,128)(2,1)S(1)}, u32[]{:S(2)}, u32[]{:S(2)}) collective-permute-start(bf16[27,32,128]{2,1,0:T(8,128)(2,1)} %bitcast.46), channel_id=1, source_target_pairs={{0,0},{1,1},{2,2},{3,3},{4,4},{5,5},{6,6},{7,7},{8,128},{9,129},{1... | collective-permute-start | bytes 663560 | tf_op jit(solution)/shard_map/ppermute | solution.py:40
  4.3 16.0 %collective-permute-start.1 = (bf16[2,256,128]{2,1,0:T(8,128)(2,1)S(1)}, bf16[2,256,128]{2,1,0:T(8,128)(2,1)S(1)}, u32[]{:S(2)}, u32[]{:S(2)}) collective-permute-start(bf16[2,256,128]{2,1,0:T(8,128)(2,1)S(1)} %bitcast.42), channel_id=1, source_target_pairs={{0,0},{1,17},{2,34},{3,51},{4,12},{5,29},{6,46},{7,63},{8,1},{9,18... | collective-permute-start | bytes 393224 | tf_op jit(solution)/shard_map/ppermute | solution.py:40
  20.3 15.5 %collective-permute-start.6 = (bf16[27,32,128]{2,1,0:T(8,128)(2,1)S(1)}, bf16[27,32,128]{2,1,0:T(8,128)(2,1)S(1)}, u32[]{:S(2)}, u32[]{:S(2)}) collective-permute-start(bf16[27,32,128]{2,1,0:T(8,128)(2,1)S(1)} %collective-permute-done.2.refs_0_), channel_id=1, source_target_pairs={{0,128},{1,129},{2,130},{3,131},{4,132},{5,133},{6,134},{7,135},{8... | collective-permute-start | bytes 663560 | tf_op jit(solution)/shard_map/ppermute | solution.py:40
  21.1 14.4 %collective-permute-start.5 = (bf16[2,256,128]{2,1,0:T(8,128)(2,1)S(1)}, bf16[2,256,128]{2,1,0:T(8,128)(2,1)S(1)}, u32[]{:S(2)}, u32[]{:S(2)}) collective-permute-start(bf16[2,256,128]{2,1,0:T(8,128)(2,1)S(1)} %collective-permute-done.1.refs_0_), channel_id=1, source_target_pairs={{0,4},{1,5},{2,6},{3,7},{4,0},{5,1},{6,2},{7,3},{8,12},{9,13},{10,... | collective-permute-start | bytes 393224 | tf_op jit(solution)/shard_map/ppermute | solution.py:40
  28.4 7.1 %collective-permute-start.4 = (bf16[2,256,128]{2,1,0:T(8,128)(2,1)S(1)}, bf16[2,256,128]{2,1,0:T(8,128)(2,1)S(1)}, u32[]{:S(2)}, u32[]{:S(2)}) collective-permute-start(bf16[2,256,128]{2,1,0:T(8,128)(2,1)S(1)} %collective-permute-done.1.refs_0_), channel_id=1, source_target_pairs={{0,1},{1,2},{2,3},{3,4},{4,5},{5,6},{6,7},{7,0},{8,9},{9,10},{10,1... | collective-permute-start | bytes 393224 | tf_op jit(solution)/shard_map/ppermute | solution.py:40
  29.7 6.0 %collective-permute-start.3 = (bf16[2,256,128]{2,1,0:T(8,128)(2,1)S(1)}, bf16[2,256,128]{2,1,0:T(8,128)(2,1)S(1)}, u32[]{:S(2)}, u32[]{:S(2)}) collective-permute-start(bf16[2,256,128]{2,1,0:T(8,128)(2,1)S(1)} %collective-permute-done.1.refs_0_), channel_id=1, source_target_pairs={{0,7},{1,0},{2,1},{3,2},{4,3},{5,4},{6,5},{7,6},{8,15},{9,8},{10,9... | collective-permute-start | bytes 393224 | tf_op jit(solution)/shard_map/ppermute | solution.py:40
  35.8 14.0 %collective-permute-start.8 = (bf16[4,256,128]{2,1,0:T(8,128)(2,1)S(1)}, bf16[4,256,128]{2,1,0:T(8,128)(2,1)S(1)}, u32[]{:S(2)}, u32[]{:S(2)}) collective-permute-start(bf16[4,256,128]{2,1,0:T(8,128)(2,1)S(1)} %get-tuple-element.88), channel_id=1, source_target_pairs={{0,1},{1,2},{2,3},{3,4},{4,5},{5,6},{6,7},{7,0},{8,9},{9,10},{10,1... | collective-permute-start | bytes 786440 | tf_op jit(solution)/shard_map/ppermute | solution.py:40
  39.9 9.9 %collective-permute-start.7 = (bf16[4,256,128]{2,1,0:T(8,128)(2,1)S(1)}, bf16[4,256,128]{2,1,0:T(8,128)(2,1)S(1)}, u32[]{:S(2)}, u32[]{:S(2)}) collective-permute-start(bf16[4,256,128]{2,1,0:T(8,128)(2,1)S(1)} %get-tuple-element.89), channel_id=1, source_target_pairs={{0,7},{1,0},{2,1},{3,2},{4,3},{5,4},{6,5},{7,6},{8,15},{9,8},{10,9... | collective-permute-start | bytes 786440 | tf_op jit(solution)/shard_map/ppermute | solution.py:40
  40.5 7.7 %collective-permute-start.10 = (bf16[27,32,128]{2,1,0:T(8,128)(2,1)S(1)}, bf16[27,32,128]{2,1,0:T(8,128)(2,1)S(1)}, u32[]{:S(2)}, u32[]{:S(2)}) collective-permute-start(bf16[27,32,128]{2,1,0:T(8,128)(2,1)S(1)} %collective-permute-done.2.refs_0_), channel_id=1, source_target_pairs={{0,64},{1,65},{2,66},{3,67},{4,68},{5,69},{6,70},{7,71},{8,72},{9,... | collective-permute-start | bytes 663560 | tf_op jit(solution)/shard_map/ppermute | solution.py:40
  42.6 5.9 %collective-permute-start.9 = (bf16[27,32,128]{2,1,0:T(8,128)(2,1)S(1)}, bf16[27,32,128]{2,1,0:T(8,128)(2,1)S(1)}, u32[]{:S(2)}, u32[]{:S(2)}) collective-permute-start(bf16[27,32,128]{2,1,0:T(8,128)(2,1)S(1)} %collective-permute-done.2.refs_0_), channel_id=1, source_target_pairs={{0,192},{1,193},{2,194},{3,195},{4,196},{5,197},{6,198},{7,199},{8... | collective-permute-start | bytes 663560 | tf_op jit(solution)/shard_map/ppermute | solution.py:40
  56.5 13.0 %copy-start = (f32[128]{0:T(128)S(1)}, f32[128]{0:T(128)}, u32[]{:S(2)}) copy-start(f32[128]{0:T(128)} %param.6) | copy-start | bytes 1540
  56.5 2.0 %collective-permute-start.11 = (bf16[4,2,256,128]{3,2,1,0:T(8,128)(2,1)S(1)}, bf16[4,2,256,128]{3,2,1,0:T(8,128)(2,1)S(1)}, u32[]{:S(2)}, u32[]{:S(2)}) collective-permute-start(bf16[4,2,256,128]{3,2,1,0:T(8,128)(2,1)S(1)} %get-tuple-element.46), channel_id=1, source_target_pairs={{0,8},{1,9},{2,10},{3,11},{4,12},{5,13},{6,14},{7,15},{8,0},{9,1},... | collective-permute-start | bytes 1572872 | tf_op jit(solution)/shard_map/ppermute | solution.py:40
  58.7 7.8 %collective-permute-start.12 = (bf16[2,256,128]{2,1,0:T(8,128)(2,1)S(1)}, bf16[2,256,128]{2,1,0:T(8,128)(2,1)S(1)}, u32[]{:S(2)}, u32[]{:S(2)}) collective-permute-start(bf16[2,256,128]{2,1,0:T(8,128)(2,1)S(1)} %get-tuple-element.74), channel_id=1, source_target_pairs={{0,16},{1,17},{2,18},{3,19},{4,20},{5,21},{6,22},{7,23},{8,24},{9,... | collective-permute-start | bytes 393224 | tf_op jit(solution)/shard_map/ppermute | solution.py:40
  62.7 6.4 %collective-permute-start.14 = (bf16[2,256,128]{2,1,0:T(8,128)(2,1)S(1)}, bf16[2,256,128]{2,1,0:T(8,128)(2,1)S(1)}, u32[]{:S(2)}, u32[]{:S(2)}) collective-permute-start(bf16[2,256,128]{2,1,0:T(8,128)(2,1)S(1)} %get-tuple-element.75), channel_id=1, source_target_pairs={{0,48},{1,49},{2,50},{3,51},{4,52},{5,53},{6,54},{7,55},{8,56},{9,... | collective-permute-start | bytes 393224 | tf_op jit(solution)/shard_map/ppermute | solution.py:40
  62.7 6.8 %collective-permute-start.13 = (bf16[2,256,128]{2,1,0:T(8,128)(2,1)S(1)}, bf16[2,256,128]{2,1,0:T(8,128)(2,1)S(1)}, u32[]{:S(2)}, u32[]{:S(2)}) collective-permute-start(bf16[2,256,128]{2,1,0:T(8,128)(2,1)S(1)} %get-tuple-element.76), channel_id=1, source_target_pairs={{0,32},{1,33},{2,34},{3,35},{4,36},{5,37},{6,38},{7,39},{8,40},{9,... | collective-permute-start | bytes 393224 | tf_op jit(solution)/shard_map/ppermute | solution.py:40
  69.8 8.2 %collective-permute-start.17 = (bf16[2,256,128]{2,1,0:T(8,128)(2,1)S(1)}, bf16[2,256,128]{2,1,0:T(8,128)(2,1)S(1)}, u32[]{:S(2)}, u32[]{:S(2)}) collective-permute-start(bf16[2,256,128]{2,1,0:T(8,128)(2,1)S(1)} %get-tuple-element.72.refs_2_.refs_0_), channel_id=1, source_target_pairs={{0,48},{1,49},{2,50},{3,51},{4,52},{5,53},{6,54},{7,55},{8,56},{9,... | collective-permute-start | bytes 393224 | tf_op jit(solution)/shard_map/ppermute | solution.py:40
  72.6 7.1 %collective-permute-start.16 = (bf16[2,256,128]{2,1,0:T(8,128)(2,1)S(1)}, bf16[2,256,128]{2,1,0:T(8,128)(2,1)S(1)}, u32[]{:S(2)}, u32[]{:S(2)}) collective-permute-start(bf16[2,256,128]{2,1,0:T(8,128)(2,1)S(1)} %get-tuple-element.72.refs_2_.refs_0_), channel_id=1, source_target_pairs={{0,32},{1,33},{2,34},{3,35},{4,36},{5,37},{6,38},{7,39},{8,40},{9,... | collective-permute-start | bytes 393224 | tf_op jit(solution)/shard_map/ppermute | solution.py:40
  75.0 6.0 %collective-permute-start.15 = (bf16[2,256,128]{2,1,0:T(8,128)(2,1)S(1)}, bf16[2,256,128]{2,1,0:T(8,128)(2,1)S(1)}, u32[]{:S(2)}, u32[]{:S(2)}) collective-permute-start(bf16[2,256,128]{2,1,0:T(8,128)(2,1)S(1)} %get-tuple-element.72.refs_2_.refs_0_), channel_id=1, source_target_pairs={{0,16},{1,17},{2,18},{3,19},{4,20},{5,21},{6,22},{7,23},{8,24},{9,... | collective-permute-start | bytes 393224 | tf_op jit(solution)/shard_map/ppermute | solution.py:40
  75.6 6.1 %collective-permute-start.18 = (bf16[2,256,128]{2,1,0:T(8,128)(2,1)S(1)}, bf16[2,256,128]{2,1,0:T(8,128)(2,1)S(1)}, u32[]{:S(2)}, u32[]{:S(2)}) collective-permute-start(bf16[2,256,128]{2,1,0:T(8,128)(2,1)S(1)} %get-tuple-element.72.refs_2_.refs_0_), channel_id=1, source_target_pairs={{0,8},{1,9},{2,10},{3,11},{4,12},{5,13},{6,14},{7,15},{8,0},{9,1},... | collective-permute-start | bytes 393224 | tf_op jit(solution)/shard_map/ppermute | solution.py:40
  77.9 3.7 %collective-permute-start.21 = (bf16[2,256,128]{2,1,0:T(8,128)(2,1)S(1)}, bf16[2,256,128]{2,1,0:T(8,128)(2,1)S(1)}, u32[]{:S(2)}, u32[]{:S(2)}) collective-permute-start(bf16[2,256,128]{2,1,0:T(8,128)(2,1)S(1)} %collective-permute-done.17.refs_5_.refs_3_), channel_id=1, source_target_pairs={{0,8},{1,9},{2,10},{3,11},{4,12},{5,13},{6,14},{7,15},{8,0},{9,1},... | collective-permute-start | bytes 393224 | tf_op jit(solution)/shard_map/ppermute | solution.py:40
  79.7 1.9 %collective-permute-start.20 = (bf16[2,256,128]{2,1,0:T(8,128)(2,1)S(1)}, bf16[2,256,128]{2,1,0:T(8,128)(2,1)S(1)}, u32[]{:S(2)}, u32[]{:S(2)}) collective-permute-start(bf16[2,256,128]{2,1,0:T(8,128)(2,1)S(1)} %collective-permute-done.16.refs_4_.refs_2_), channel_id=1, source_target_pairs={{0,8},{1,9},{2,10},{3,11},{4,12},{5,13},{6,14},{7,15},{8,0},{9,1},... | collective-permute-start | bytes 393224 | tf_op jit(solution)/shard_map/ppermute | solution.py:40
  81.0 1.3 collective-permute-start.19
  81.1 7.5 %collective-permute-start.22 = (bf16[256,128]{1,0:T(8,128)(2,1)S(1)}, bf16[256,128]{1,0:T(8,128)(2,1)S(1)}, u32[]{:S(2)}, u32[]{:S(2)}) collective-permute-start(bf16[256,128]{1,0:T(8,128)(2,1)S(1)} %get-tuple-element.82), channel_id=1, source_target_pairs={{0,8},{1,9},{2,10},{3,11},{4,12},{5,13},{6,14},{7,15},{8,16},{9,17... | collective-permute-start | bytes 196616 | tf_op jit(solution)/shard_map/ppermute | solution.py:40
  88.5 15.1 %collective-permute-start.25 = (bf16[28,32,128]{2,1,0:T(8,128)(2,1)S(1)}, bf16[28,32,128]{2,1,0:T(8,128)(2,1)S(1)}, u32[]{:S(2)}, u32[]{:S(2)}) collective-permute-start(bf16[28,32,128]{2,1,0:T(8,128)(2,1)S(1)} %get-tuple-element.62), channel_id=1, source_target_pairs={{0,64},{1,65},{2,66},{3,67},{4,68},{5,69},{6,70},{7,71},{8,72},{9,... | collective-permute-start | bytes 688136 | tf_op jit(solution)/shard_map/ppermute | solution.py:40
  88.9 14.8 %collective-permute-start.26 = (bf16[28,32,128]{2,1,0:T(8,128)(2,1)S(1)}, bf16[28,32,128]{2,1,0:T(8,128)(2,1)S(1)}, u32[]{:S(2)}, u32[]{:S(2)}) collective-permute-start(bf16[28,32,128]{2,1,0:T(8,128)(2,1)S(1)} %get-tuple-element.63), channel_id=1, source_target_pairs={{0,128},{1,129},{2,130},{3,131},{4,132},{5,133},{6,134},{7,135},{8... | collective-permute-start | bytes 688136 | tf_op jit(solution)/shard_map/ppermute | solution.py:40
  92.6 11.1 %collective-permute-start.27 = (bf16[28,32,128]{2,1,0:T(8,128)(2,1)S(1)}, bf16[28,32,128]{2,1,0:T(8,128)(2,1)S(1)}, u32[]{:S(2)}, u32[]{:S(2)}) collective-permute-start(bf16[28,32,128]{2,1,0:T(8,128)(2,1)S(1)} %get-tuple-element.64), channel_id=1, source_target_pairs={{0,192},{1,193},{2,194},{3,195},{4,196},{5,197},{6,198},{7,199},{8... | collective-permute-start | bytes 688136 | tf_op jit(solution)/shard_map/ppermute | solution.py:40
  97.2 9.1 %collective-permute-start.23 = (bf16[4,256,128]{2,1,0:T(8,128)(2,1)S(1)}, bf16[4,256,128]{2,1,0:T(8,128)(2,1)S(1)}, u32[]{:S(2)}, u32[]{:S(2)}) collective-permute-start(bf16[4,256,128]{2,1,0:T(8,128)(2,1)S(1)} %get-tuple-element.59), channel_id=1, source_target_pairs={{0,1},{1,2},{2,3},{3,4},{4,5},{5,6},{6,7},{7,0},{8,9},{9,10},{10,1... | collective-permute-start | bytes 786440 | tf_op jit(solution)/shard_map/ppermute | solution.py:40
  97.3 9.0 %collective-permute-start.24 = (bf16[4,256,128]{2,1,0:T(8,128)(2,1)S(1)}, bf16[4,256,128]{2,1,0:T(8,128)(2,1)S(1)}, u32[]{:S(2)}, u32[]{:S(2)}) collective-permute-start(bf16[4,256,128]{2,1,0:T(8,128)(2,1)S(1)} %get-tuple-element.60), channel_id=1, source_target_pairs={{0,7},{1,0},{2,1},{3,2},{4,3},{5,4},{6,5},{7,6},{8,15},{9,8},{10,9... | collective-permute-start | bytes 786440 | tf_op jit(solution)/shard_map/ppermute | solution.py:40
  106.4 11.9 %collective-permute-start.28 = (bf16[2,256,128]{2,1,0:T(8,128)(2,1)S(1)}, bf16[2,256,128]{2,1,0:T(8,128)(2,1)S(1)}, u32[]{:S(2)}, u32[]{:S(2)}) collective-permute-start(bf16[2,256,128]{2,1,0:T(8,128)(2,1)S(1)} %get-tuple-element.77), channel_id=1, source_target_pairs={{0,4},{1,5},{2,6},{3,7},{4,0},{5,1},{6,2},{7,3},{8,12},{9,13},{10,... | collective-permute-start | bytes 393224 | tf_op jit(solution)/shard_map/ppermute | solution.py:40
  108.9 9.4 %collective-permute-start.29 = (bf16[2,256,128]{2,1,0:T(8,128)(2,1)S(1)}, bf16[2,256,128]{2,1,0:T(8,128)(2,1)S(1)}, u32[]{:S(2)}, u32[]{:S(2)}) collective-permute-start(bf16[2,256,128]{2,1,0:T(8,128)(2,1)S(1)} %get-tuple-element.78), channel_id=1, source_target_pairs={{0,1},{1,2},{2,3},{3,4},{4,5},{5,6},{6,7},{7,0},{8,9},{9,10},{10,1... | collective-permute-start | bytes 393224 | tf_op jit(solution)/shard_map/ppermute | solution.py:40
  109.3 9.0 %collective-permute-start.30 = (bf16[2,256,128]{2,1,0:T(8,128)(2,1)S(1)}, bf16[2,256,128]{2,1,0:T(8,128)(2,1)S(1)}, u32[]{:S(2)}, u32[]{:S(2)}) collective-permute-start(bf16[2,256,128]{2,1,0:T(8,128)(2,1)S(1)} %get-tuple-element.79), channel_id=1, source_target_pairs={{0,7},{1,0},{2,1},{3,2},{4,3},{5,4},{6,5},{7,6},{8,15},{9,8},{10,9... | collective-permute-start | bytes 393224 | tf_op jit(solution)/shard_map/ppermute | solution.py:40
  112.8 24.1 %collective-permute-start.33 = (bf16[27,32,128]{2,1,0:T(8,128)(2,1)S(1)}, bf16[27,32,128]{2,1,0:T(8,128)(2,1)S(1)}, u32[]{:S(2)}, u32[]{:S(2)}) collective-permute-start(bf16[27,32,128]{2,1,0:T(8,128)(2,1)S(1)} %slice.129), channel_id=1, source_target_pairs={{0,0},{1,1},{2,2},{3,3},{4,4},{5,5},{6,6},{7,7},{8,128},{9,129},{1... | collective-permute-start | bytes 663560 | tf_op jit(solution)/shard_map/ppermute | solution.py:40
  118.4 11.3 %collective-permute-start.31 = (bf16[256,128]{1,0:T(8,128)(2,1)S(1)}, bf16[256,128]{1,0:T(8,128)(2,1)S(1)}, u32[]{:S(2)}, u32[]{:S(2)}) collective-permute-start(bf16[256,128]{1,0:T(8,128)(2,1)S(1)} %get-tuple-element.80), channel_id=1, source_target_pairs={{0,8},{1,16},{2,24},{3,32},{4,40},{5,48},{6,56},{7,64},{8,44},{9,5... | collective-permute-start | bytes 196616 | tf_op jit(solution)/shard_map/ppermute | solution.py:40
  123.7 12.5 %collective-permute-start.32 = (bf16[256,128]{1,0:T(8,128)(2,1)S(1)}, bf16[256,128]{1,0:T(8,128)(2,1)S(1)}, u32[]{:S(2)}, u32[]{:S(2)}) collective-permute-start(bf16[256,128]{1,0:T(8,128)(2,1)S(1)} %get-tuple-element.81), channel_id=1, source_target_pairs={{0,0},{1,8},{2,16},{3,24},{4,32},{5,40},{6,48},{7,56},{8,36},{9,44... | collective-permute-start | bytes 196616 | tf_op jit(solution)/shard_map/ppermute | solution.py:40

commit v3 on v2

--- a/solution.py
+++ b/solution.py
@@ -14,7 +14,7 @@
 KAPPA = 0.7978845608028654
 CUBIC = 0.044715
 VMEM_LIMIT = 24 * 1024 * 1024
-Z_STEPS = (0, 1, -1, 4, 2, -3, -2, 3)
+Z_STEPS = (0, 4, 1, -3, -1, 3, 2, -2)
 
 
 def gelu_pair(values):
@@ -146,33 +146,22 @@
         store(back, (26 - tap) // 9, (26 - tap) % 9, turned)
 
 
-def forward_kernel(where, *refs):
-    *planes, paired, keep, send, columns, total = refs
-    size = total.shape[-1]
+def own_pairs(where):
     _, _, y, core, _ = position(where)
-    store_columns(ring_pairs(where, Z_STEPS), planes, columns)
-
-    def step(index, carry):
-        product = convolved(columns, [4 * index + p for p in range(4)], paired)
-        for p in range(4):
-            for o, value in enumerate(halves(product, p, size)):
-                total[4 * index + p, o] = value
-        return carry
-
-    lax.fori_loop(0, NQ // 4, step, 0)
-    for r in range(4):
-        row = (y + r) & 3
-        for half in range(2):
-            keep[r, half] = total[2 * row + core, half]
-            send[r, half] = total[2 * row + 1 - core, half].astype(jnp.bfloat16)
+    return [2 * ((y + r) & 3) + core for r in range(4)]
+
+
+def other_pairs(where):
+    _, _, y, core, _ = position(where)
+    return [2 * ((y + r) & 3) + 1 - core for r in range(4)]
 
 
 def slopes_kernel(where, *refs):
     store_columns(slope_pairs(where), refs[:NQ], refs[NQ])
 
 
-def backward_kernel(steps, where, columns, paired, *outs):
-    product = convolved(columns, ring_pairs(where, steps), paired)
+def product_kernel(pairs, where, columns, paired, *outs):
+    product = convolved(columns, pairs(where), paired)
     places = [(out, 2 * index) for out in outs for index in range(out.shape[0] // 2)]
     for index, (out, start) in enumerate(places):
         for half, value in enumerate(halves(product, index, out.shape[-1])):
@@ -192,7 +181,7 @@
             value = ref[half].astype(jnp.float32)
             bias = bias + jnp.sum(value.reshape(FACE // 8, 8, size), axis=0)
             start = pl.multiple_of((2 * pair + half + 1) * FACE, FACE)
-            turned[:, pl.ds(start, FACE)] = value.T.astype(jnp.bfloat16)
+            turned[:, pl.ds(start, FACE)] = ref[half].T
     total[...] = jnp.zeros_like(total)
 
     def step(index, carry):
@@ -212,7 +201,7 @@
     for tap in range(27):
         a, bc = tap // 9, tap % 9
         block = total[a * size : (a + 1) * size, bc * size : (bc + 1) * size]
-        natural[tap] = block.T * scale
+        natural[tap] = (block * scale).astype(jnp.bfloat16).T
     whole = jnp.sum(bias, axis=0, keepdims=True) * scale
     upper = whole.astype(jnp.bfloat16)
     lower = (whole - upper.astype(jnp.float32)).astype(jnp.bfloat16)
@@ -223,7 +212,7 @@
     for r in range(NX):
         offset = pl.multiple_of(swapped((x + r) & (NX - 1)) * rows, rows)
         for tap in range(27):
-            outs[r][tap] = natural[tap, pl.ds(offset, rows)].astype(outs[r].dtype)
+            outs[r][tap] = natural[tap, pl.ds(offset, rows)]
         outs[r][27] = spread.astype(outs[r].dtype)
 
 
@@ -261,27 +250,28 @@
     )
     ahead = seconds[1]
     own = jnp.stack([features[1], seconds[0]]).reshape(2, FACE, size)
-    own = permuted(own, lambda x, q, z: at(x, holder(z), z + q))
-    own, block = lax.optimization_barrier((own, block))
+    own = jnp.concatenate(
+        [permuted(own, lambda x, q, z: at(x, holder(z), z + q + step)) for step in (0, 4)]
+    )
     blocks = [block] + [
         permuted(block, lambda x, q, z: at(x - shift, q, z)) for shift in range(1, NX)
     ]
-    above, below, beyond = along_z(own, -1), along_z(own, 1), along_z(own, 4)
-    above, below, beyond, blocks[2] = lax.optimization_barrier(
-        (above, below, beyond, blocks[2])
-    )
-    planes = [
-        own,
-        above,
-        below,
-        beyond,
-        along_z(jnp.concatenate([above, beyond]), -1),
-        along_z(jnp.concatenate([below, beyond]), 1),
-    ]
+    above, below = along_z(own, -1), along_z(own, 1)
+    above, below, block = lax.optimization_barrier((above, below, block))
+    planes = [own, above, below, along_z(above[:2], -1), along_z(below[:2], 1)]
 
     flops = 2 * 27 * GRID * FACE * size * out_size
     paired_shape = lambda deep, wide: shaped((2, 18 * deep, 2 * wide), bf16)
     columns_shape = shaped((GRID + 2, FACE + 2 * GRID, 3 * size), bf16)
+    (columns,) = call(
+        lambda where, *refs: store_columns(ring_pairs(where, Z_STEPS), refs[:-1], refs[-1]),
+        where,
+        planes,
+        [columns_shape],
+        [],
+        0,
+    )
+    columns, blocks[1], blocks[3] = lax.optimization_barrier((columns, blocks[1], blocks[3]))
     ahead_weights, back_weights = call(
         weights_kernel,
         where,
@@ -290,19 +280,21 @@
         [pltpu.VMEM((27, size, out_size), bf16)],
         0,
     )
-    keep, send, columns = call(
-        forward_kernel,
-        where,
-        planes + [ahead_weights],
-        [
-            shaped((4, 2, FACE, out_size), f32),
-            shaped((4, 2, FACE, out_size), bf16),
-            columns_shape,
-        ],
-        [pltpu.VMEM((NQ, 2, FACE, out_size), f32)],
-        flops,
-    )
-    keep = keep + permuted(send, lambda x, q, z: at(x, q ^ 1, z)).astype(f32)
+    def products(pairs, where, columns, weights, outs):
+        return call(
+            lambda *refs: product_kernel(pairs, *refs),
+            where,
+            [columns, weights],
+            outs,
+            [],
+            flops // 2,
+        )
+
+    (send,) = products(other_pairs, where, columns, ahead_weights, [shaped((8, FACE, out_size), bf16)])
+    where, send = lax.optimization_barrier((where, send))
+    send = permuted(send, lambda x, q, z: at(x, q ^ 1, z)).astype(f32)
+    keep = products(own_pairs, where, columns, ahead_weights, [shaped((2, FACE, out_size), f32)] * 4)
+    keep = [piece + send[2 * r : 2 * r + 2] for r, piece in enumerate(keep)]
     pre_act = keep[0]
     for r in range(1, 4):
         pre_act = pre_act + permuted(
@@ -313,7 +305,6 @@
     target = jnp.stack([cotangent[1], ahead])
     output, slope = gelu_pair(pre_act)
     activated = output.astype(bf16)
-    behind = permuted(activated[1], lambda x, q, z: device(NQ * x + q + 1, z))
     grad_pre = (target.reshape(2, FACE, out_size).astype(f32) * slope).astype(bf16)
 
     slopes = [grad_pre]
@@ -328,54 +319,59 @@
         lambda *refs: filters_kernel(scale, *refs),
         where,
         [columns] + slopes,
-        [shaped((28, rows, out_size), f32 if r == 0 else bf16) for r in range(NX)],
+        [shaped((28, rows, out_size), bf16)] * NX,
         [
             pltpu.VMEM((out_size, (GRID + 2) * FACE), bf16),
             pltpu.VMEM((3 * out_size, 9 * size), f32),
-            pltpu.VMEM((27, size, out_size), f32),
+            pltpu.VMEM((27, size, out_size), bf16),
         ],
         flops,
     )
-    where, terms, behind = lax.optimization_barrier((where, terms, behind))
-    held = terms[0]
+    where, terms = lax.optimization_barrier((where, terms))
+    held = terms[0].astype(f32)
     for r in range(1, NX):
         held = held + permuted(terms[r], lambda x, q, z: at(x + r, q, z)).astype(f32)
     grad_bias = held[27, 0] + held[27, 1]
     held = held[:27].astype(bf16)
 
-    def parts(steps, where, outs):
+    def parts(steps, where, kinds):
         return call(
-            lambda *refs: backward_kernel(steps, *refs),
+            lambda *refs: product_kernel(lambda where: ring_pairs(where, steps), *refs),
             where,
             [slope_columns, back_weights],
-            outs,
+            [shaped((2, FACE, size), kind) for kind in kinds],
             [],
             flops * len(steps) // NZ,
         )
 
-    bundle = shaped((4, FACE, size), bf16)
-    up, down = parts((2, -3, -2, 3), where, [bundle, bundle])
+    up, down = parts((2, -2), where, [bf16, bf16])
     up, down, where = lax.optimization_barrier((up, down, where))
-    up, down = along_z(up, 1), along_z(down, -1)
-    above, below, beyond, summed = parts((1, -1, 4, 0), where, [shaped((2, FACE, size), f32)] * 4)
-    up, down, held = lax.optimization_barrier((up, down, held))
-    above = (above + up[:2].astype(f32)).astype(bf16)
-    below = (below + down[:2].astype(f32)).astype(bf16)
-    beyond = (beyond + up[2:].astype(f32) + down[2:].astype(f32)).astype(bf16)
-    for piece, r in ((beyond, 4), (above, 1), (below, -1)):
-        summed = summed + along_z(piece, r).astype(f32)
-    summed = summed.astype(bf16)
+    up, down = along_z(up, 1).astype(f32), along_z(down, -1).astype(f32)
+    above, far_above, below, far_below = parts((1, -3, -1, 3), where, [f32, bf16, f32, bf16])
+    above, below, where = lax.optimization_barrier((above, below, where))
+    above = jnp.concatenate([(above + up).astype(bf16), far_above])
+    below = jnp.concatenate([(below + down).astype(bf16), far_below])
+    above, below, held = lax.optimization_barrier((above, below, held))
+    near, beyond = parts((0, 4), where, [f32, f32])
+    above, below = along_z(above, 1).astype(f32), along_z(below, -1).astype(f32)
+    near = (near + above[:2] + below[:2]).astype(bf16)
+    beyond = (beyond + above[2:] + below[2:]).astype(bf16)
 
     grad_filters = permuted(
         held, lambda x, q, z: device(NX * group(q) + swapped(x), z)
     ).astype(f32)
 
-    def home(half):
-        return lambda x, q, z: device(NQ * x + (z - group(q)) % NZ + half, group(q))
-
-    grad_input = jnp.stack([permuted(summed[1], home(1)), permuted(summed[0], home(0))])
-
-    activated = jnp.stack([behind, activated[0]])
+    def home(step):
+        return lambda x, q, z: device(NQ * x + (z - group(q) - step) % NZ, group(q))
+
+    near, beyond = permuted(near, home(0)).astype(f32), permuted(beyond, home(4)).astype(f32)
+    summed = (near + beyond).astype(bf16)
+    seconds = permuted(
+        jnp.stack([activated[1], summed[1]]), lambda x, q, z: device(NQ * x + q + 1, z)
+    )
+    activated = jnp.stack([seconds[0], activated[0]])
+    grad_input = jnp.stack([seconds[1], summed[0]])
+
     shape = (2, GRID, GRID)
     return (
         activated.reshape(*shape, out_size),

time: 139 us -> 134 us (0.964); the launches traced: 138 us -> 131 us
  starting transfers between devices: 77.3 us -> 62.3 us
  waiting for transfers between devices: 33 us -> 39.6 us
    ppermute x34 -> x33, starting transfers between devices: 77.3 us -> 62.3 us  [permuted(): return lax.ppermute(array, ('space', 'chan'), pairs)]
    ppermute x34 -> x33, waiting for transfers between devices: 33 us -> 39.6 us  [permuted(): return lax.ppermute(array, ('space', 'chan'), pairs)]
    pallas_call x6 -> x9, Pallas kernels: 21.8 us -> 23.1 us  [call(): pl.pallas_call(kernel, out_shape=outs, in_specs=[pl.BlockSpec(memory_spac...]
  transfers between devices with their start and end apart: 34 -> 33, of which waited for: 16 -> 13; matrix products, arithmetic and copies ran while one was open for 2% -> 1% of each run, Pallas kernels for 11% -> 10%
where the time goes in v3:
time: 134 us; the launch traced here: 131 us
  starting transfers between devices  62.3 us (46%)
  waiting for transfers between devices  39.6 us (30%)
  Pallas kernels  23.1 us (17%)
  other arithmetic  3.76 us (3%)
    ppermute x33, starting transfers between devices, permuted(): return lax.ppermute(array, ('space', 'chan'), pairs)  62.3 us
    ppermute x33, waiting for transfers between devices, permuted(): return lax.ppermute(array, ('space', 'chan'), pairs)  39.6 us
    pallas_call x9, Pallas kernels, call(): pl.pallas_call(kernel, out_shape=outs, in_specs=[pl.BlockSpec(memory_spac...  23.1 us
  transfers between devices with their start and end apart: 33, of which 13 were waited for; matrix products, arithmetic and copies ran while one was open for 1% of the time, Pallas kernels for 10%

profile of v3, /device:TPU:16, one launch (start us, length us, event | category | flops | bytes accessed | tf_op | source)
XLA Modules:
  0.0 130.9 jit_solution(10619746345419031109)
XLA Ops:
  0.6 1.0 fusion.21
  1.7 2.5 %collective-permute-done = bf16[2,16,16,128]{3,2,1,0:T(8,128)(2,1)S(1)} collective-permute-done((bf16[2,16,16,128]{3,2,1,0:T(8,128)(2,1)S(1)}, bf16[2,16,16,128]{3,2,1,0:T(8,128)(2,1)S(1)}, u32[]{:S(2)}, u32[]{:S(2)}) %collective-permute-start) | collective-permute-done | bytes 131104 | tf_op jit(solution)/shard_map/ppermute | solution.py:40
  4.3 13.5 %collective-permute-start.1 = (bf16[2,256,128]{2,1,0:T(8,128)(2,1)S(1)}, bf16[2,256,128]{2,1,0:T(8,128)(2,1)S(1)}, u32[]{:S(2)}, u32[]{:S(2)}) collective-permute-start(bf16[2,256,128]{2,1,0:T(8,128)(2,1)S(1)} %bitcast.13), channel_id=1, source_target_pairs={{0,0},{1,17},{2,34},{3,51},{4,12},{5,29},{6,46},{7,63},{8,1},{9,18... | collective-permute-start | bytes 393224 | tf_op jit(solution)/shard_map/ppermute | solution.py:40
  17.8 1.9 %collective-permute-start.2 = (bf16[2,256,128]{2,1,0:T(8,128)(2,1)S(1)}, bf16[2,256,128]{2,1,0:T(8,128)(2,1)S(1)}, u32[]{:S(2)}, u32[]{:S(2)}) collective-permute-start(bf16[2,256,128]{2,1,0:T(8,128)(2,1)S(1)} %bitcast.14), channel_id=1, source_target_pairs={{0,4},{1,21},{2,38},{3,55},{4,8},{5,25},{6,42},{7,59},{8,5},{9,22}... | collective-permute-start | bytes 393224 | tf_op jit(solution)/shard_map/ppermute | solution.py:40
  19.7 1.9 %collective-permute-start.5 = (bf16[27,32,128]{2,1,0:T(8,128)(2,1)}, bf16[27,32,128]{2,1,0:T(8,128)(2,1)S(1)}, u32[]{:S(2)}, u32[]{:S(2)}) collective-permute-start(bf16[27,32,128]{2,1,0:T(8,128)(2,1)} %bitcast.17), channel_id=1, source_target_pairs={{0,0},{1,1},{2,2},{3,3},{4,4},{5,5},{6,6},{7,7},{8,128},{9,129},{1... | collective-permute-start | bytes 663560 | tf_op jit(solution)/shard_map/ppermute | solution.py:40
  21.7 4.8 %collective-permute-done.2 = bf16[2,256,128]{2,1,0:T(8,128)(2,1)S(1)} collective-permute-done((bf16[2,256,128]{2,1,0:T(8,128)(2,1)S(1)}, bf16[2,256,128]{2,1,0:T(8,128)(2,1)S(1)}, u32[]{:S(2)}, u32[]{:S(2)}) %collective-permute-start.2) | collective-permute-done | bytes 131104 | tf_op jit(solution)/shard_map/ppermute | solution.py:40
  26.5 6.7 %collective-permute-start.3 = (bf16[4,256,128]{2,1,0:T(8,128)(2,1)S(1)}, bf16[4,256,128]{2,1,0:T(8,128)(2,1)S(1)}, u32[]{:S(2)}, u32[]{:S(2)}) collective-permute-start(bf16[4,256,128]{2,1,0:T(8,128)(2,1)S(1)} %constant_dynamic-update-slice_fusion.refs_0_), channel_id=1, source_target_pairs={{0,7},{1,0},{2,1},{3,2},{4,3},{5,4},{6,5},{7,6},{8,15},{9,8},{10,9... | collective-permute-start | bytes 786440 | tf_op jit(solution)/shard_map/ppermute | solution.py:40
  33.3 0.9 collective-permute-start.9
  34.2 2.3 %collective-permute-start.8 = (bf16[27,32,128]{2,1,0:T(8,128)(2,1)S(1)}, bf16[27,32,128]{2,1,0:T(8,128)(2,1)S(1)}, u32[]{:S(2)}, u32[]{:S(2)}) collective-permute-start(bf16[27,32,128]{2,1,0:T(8,128)(2,1)S(1)} %collective-permute-done.5.refs_0_), channel_id=1, source_target_pairs={{0,192},{1,193},{2,194},{3,195},{4,196},{5,197},{6,198},{7,199},{8... | collective-permute-start | bytes 663560 | tf_op jit(solution)/shard_map/ppermute | solution.py:40
  36.5 1.9 %collective-permute-start.10 = (bf16[27,32,128]{2,1,0:T(8,128)(2,1)S(1)}, bf16[27,32,128]{2,1,0:T(8,128)(2,1)S(1)}, u32[]{:S(2)}, u32[]{:S(2)}) collective-permute-start(bf16[27,32,128]{2,1,0:T(8,128)(2,1)S(1)} %collective-permute-done.5.refs_0_), channel_id=1, source_target_pairs={{0,128},{1,129},{2,130},{3,131},{4,132},{5,133},{6,134},{7,135},{8... | collective-permute-start | bytes 663560 | tf_op jit(solution)/shard_map/ppermute | solution.py:40
  38.5 3.2 %collective-permute-start.6 = (bf16[2,256,128]{2,1,0:T(8,128)(2,1)S(1)}, bf16[2,256,128]{2,1,0:T(8,128)(2,1)S(1)}, u32[]{:S(2)}, u32[]{:S(2)}) collective-permute-start(bf16[2,256,128]{2,1,0:T(8,128)(2,1)S(1)} %slice.80), channel_id=1, source_target_pairs={{0,7},{1,0},{2,1},{3,2},{4,3},{5,4},{6,5},{7,6},{8,15},{9,8},{10,9... | collective-permute-start | bytes 393224 | tf_op jit(solution)/shard_map/ppermute | solution.py:40
  41.8 2.9 %collective-permute-done.7.refs_4_ = bf16[2,256,128]{2,1,0:T(8,128)(2,1)S(1)} collective-permute-done((bf16[2,256,128]{2,1,0:T(8,128)(2,1)S(1)}, bf16[2,256,128]{2,1,0:T(8,128)(2,1)S(1)}, u32[]{:S(2)}, u32[]{:S(2)}) %collective-permute-start.7) | collective-permute-done | bytes 131104 | tf_op jit(solution)/shard_map/ppermute | solution.py:40
  44.7 1.4 %shard_map.75.refs_1_ = bf16[18,288,384]{2,1,0:T(8,128)(2,1)S(1)} custom-call(s32[2]{0:T(128)S(1)} %pad_add_fusion.where.refs_0_, bf16[4,256,128]{2,1,0:T(8,128)(2,1)S(1)} %constant_dynamic-update-slice_fusion.refs_0_, bf16[4,256,128]{2,1,0:T(8,128)(2,1)S(1)} %collective-permute-done.3.refs_1_, bf16[4,256,128]{2,1,0:T(8,128)(2,1)S(1)} %collective-permute-done.4.refs_2_, ...), custom_call_target="tpu_custom_call" | custom-call | bytes 5029888 | tf_op jit(solution)/shard_map/pallas_call | solution.py:223
  46.2 1.2 shard_map.76
  47.4 3.1 %shard_map.77 = bf16[8,256,128]{2,1,0:T(8,128)(2,1)S(1)} custom-call(s32[2]{0:T(128)S(1)} %pad_add_fusion.where.refs_0_, bf16[18,288,384]{2,1,0:T(8,128)(2,1)S(1)} %shard_map.75.refs_1_, bf16[2,2304,256]{2,1,0:T(8,128)(2,1)S(1)} %get-tuple-element.48.refs_2_), custom_call_target="tpu_custom_call" | custom-call | flops 1811939328 | bytes 6864896 | tf_op jit(solution)/shard_map/pallas_call | solution.py:223
  50.7 3.1 %shard_map.78 = (f32[2,256,128]{2,1,0:T(8,128)S(1)}, f32[2,256,128]{2,1,0:T(8,128)S(1)}, f32[2,256,128]{2,1,0:T(8,128)S(1)}, f32[2,256,128]{2,1,0:T(8,128)S(1)}) custom-call(s32[2]{0:T(128)S(1)} %pad_add_fusion.where.refs_0_, bf16[18,288,384]{2,1,0:T(8,128)(2,1)S(1)} %shard_map.75.refs_1_, bf16[2,2304,256]{2,1,0:T(8,128)(2,1)S(1)} %get-tuple-element.48.refs_2_), custom_call_target="tpu_custom_call" | custom-call | flops 1811939328 | bytes 7389184 | tf_op jit(solution)/shard_map/pallas_call | solution.py:223
  54.3 2.0 %collective-permute-start.14 = (bf16[2,256,128]{2,1,0:T(8,128)(2,1)S(1)}, bf16[2,256,128]{2,1,0:T(8,128)(2,1)S(1)}, u32[]{:S(2)}, u32[]{:S(2)}) collective-permute-start(bf16[2,256,128]{2,1,0:T(8,128)(2,1)S(1)} %get-tuple-element.87), channel_id=1, source_target_pairs={{0,48},{1,49},{2,50},{3,51},{4,52},{5,53},{6,54},{7,55},{8,56},{9,... | collective-permute-start | bytes 393224 | tf_op jit(solution)/shard_map/ppermute | solution.py:40
  56.3 0.5 collective-permute-start.13
  56.8 3.4 %collective-permute-done.12 = bf16[2,256,128]{2,1,0:T(8,128)(2,1)S(1)} collective-permute-done((bf16[2,256,128]{2,1,0:T(8,128)(2,1)S(1)}, bf16[2,256,128]{2,1,0:T(8,128)(2,1)S(1)}, u32[]{:S(2)}, u32[]{:S(2)}) %collective-permute-start.12) | collective-permute-done | bytes 131104 | tf_op jit(solution)/shard_map/ppermute | solution.py:40
  60.2 0.5 collective-permute-done.14
  60.6 2.5 %collective-permute-done.13 = bf16[2,256,128]{2,1,0:T(8,128)(2,1)S(1)} collective-permute-done((bf16[2,256,128]{2,1,0:T(8,128)(2,1)S(1)}, bf16[2,256,128]{2,1,0:T(8,128)(2,1)S(1)}, u32[]{:S(2)}, u32[]{:S(2)}) %collective-permute-start.13) | collective-permute-done | bytes 131104 | tf_op jit(solution)/shard_map/ppermute | solution.py:40
  63.4 1.7 %collective-permute-start.17 = (bf16[2,256,128]{2,1,0:T(8,128)(2,1)S(1)}, bf16[2,256,128]{2,1,0:T(8,128)(2,1)S(1)}, u32[]{:S(2)}, u32[]{:S(2)}) collective-permute-start(bf16[2,256,128]{2,1,0:T(8,128)(2,1)S(1)} %get-tuple-element.82.refs_2_.refs_0_), channel_id=1, source_target_pairs={{0,48},{1,49},{2,50},{3,51},{4,52},{5,53},{6,54},{7,55},{8,56},{9,... | collective-permute-start | bytes 393224 | tf_op jit(solution)/shard_map/ppermute | solution.py:40
  65.1 2.4 %collective-permute-start.16 = (bf16[2,256,128]{2,1,0:T(8,128)(2,1)S(1)}, bf16[2,256,128]{2,1,0:T(8,128)(2,1)S(1)}, u32[]{:S(2)}, u32[]{:S(2)}) collective-permute-start(bf16[2,256,128]{2,1,0:T(8,128)(2,1)S(1)} %get-tuple-element.82.refs_2_.refs_0_), channel_id=1, source_target_pairs={{0,32},{1,33},{2,34},{3,35},{4,36},{5,37},{6,38},{7,39},{8,40},{9,... | collective-permute-start | bytes 393224 | tf_op jit(solution)/shard_map/ppermute | solution.py:40
  67.7 1.2 collective-permute-done.17.refs_5_.refs_3_
  69.0 3.7 %collective-permute-done.16.refs_4_.refs_2_ = bf16[2,256,128]{2,1,0:T(8,128)(2,1)S(1)} collective-permute-done((bf16[2,256,128]{2,1,0:T(8,128)(2,1)S(1)}, bf16[2,256,128]{2,1,0:T(8,128)(2,1)S(1)}, u32[]{:S(2)}, u32[]{:S(2)}) %collective-permute-start.16) | collective-permute-done | bytes 131104 | tf_op jit(solution)/shard_map/ppermute | solution.py:40
  72.7 1.4 %collective-permute-done.15.refs_3_.refs_1_ = bf16[2,256,128]{2,1,0:T(8,128)(2,1)S(1)} collective-permute-done((bf16[2,256,128]{2,1,0:T(8,128)(2,1)S(1)}, bf16[2,256,128]{2,1,0:T(8,128)(2,1)S(1)}, u32[]{:S(2)}, u32[]{:S(2)}) %collective-permute-start.15) | collective-permute-done | bytes 131104 | tf_op jit(solution)/shard_map/ppermute | solution.py:40
  74.2 1.2 collective-permute-done.19.refs_7_.refs_5_
  75.4 5.8 %shard_map.79 = (bf16[28,32,128]{2,1,0:T(8,128)(2,1)S(1)}, bf16[28,32,128]{2,1,0:T(8,128)(2,1)S(1)}, bf16[28,32,128]{2,1,0:T(8,128)(2,1)S(1)}, bf16[28,32,128]{2,1,0:T(8,128)(2,1)S(1)}) custom-call(s32[2]{0:T(128)S(1)} %pad_add_fusion.where.refs_0_, bf16[18,288,384]{2,1,0:T(8,128)(2,1)S(1)} %shard_map.75.refs_1_, ...), custom_call_target="tpu_custom_call" | custom-call | flops 3623878656 | bytes 5947392 | tf_op jit(solution)/shard_map/pallas_call | solution.py:223
  81.2 2.7 %collective-permute-start.24 = (bf16[28,32,128]{2,1,0:T(8,128)(2,1)S(1)}, bf16[28,32,128]{2,1,0:T(8,128)(2,1)S(1)}, u32[]{:S(2)}, u32[]{:S(2)}) collective-permute-start(bf16[28,32,128]{2,1,0:T(8,128)(2,1)S(1)} %get-tuple-element.75), channel_id=1, source_target_pairs={{0,64},{1,65},{2,66},{3,67},{4,68},{5,69},{6,70},{7,71},{8,72},{9,... | collective-permute-start | bytes 688136 | tf_op jit(solution)/shard_map/ppermute | solution.py:40
  83.9 1.3 collective-permute-start.25
  85.2 1.5 %collective-permute-start.26 = (bf16[28,32,128]{2,1,0:T(8,128)(2,1)S(1)}, bf16[28,32,128]{2,1,0:T(8,128)(2,1)S(1)}, u32[]{:S(2)}, u32[]{:S(2)}) collective-permute-start(bf16[28,32,128]{2,1,0:T(8,128)(2,1)S(1)} %get-tuple-element.77), channel_id=1, source_target_pairs={{0,192},{1,193},{2,194},{3,195},{4,196},{5,197},{6,198},{7,199},{8... | collective-permute-start | bytes 688136 | tf_op jit(solution)/shard_map/ppermute | solution.py:40
  86.7 1.4 %shard_map.80.refs_1_ = bf16[18,288,384]{2,1,0:T(8,128)(2,1)S(1)} custom-call(s32[2]{0:T(128)S(1)} %pad_add_fusion.where.refs_0_, bf16[2,256,128]{2,1,0:T(8,128)(2,1)S(1)} %get-tuple-element.82.refs_2_.refs_0_, bf16[2,256,128]{2,1,0:T(8,128)(2,1)S(1)} %collective-permute-done.15.refs_3_.refs_1_, ...), custom_call_target="tpu_custom_call" | custom-call | bytes 5029888 | tf_op jit(solution)/shard_map/pallas_call | solution.py:223
  88.1 1.9 %shard_map.81 = (bf16[2,256,128]{2,1,0:T(8,128)(2,1)S(1)}, bf16[2,256,128]{2,1,0:T(8,128)(2,1)S(1)}) custom-call(s32[2]{0:T(128)S(1)} %pad_add_fusion.where.refs_0_, bf16[18,288,384]{2,1,0:T(8,128)(2,1)S(1)} %shard_map.80.refs_1_, bf16[2,2304,256]{2,1,0:T(8,128)(2,1)S(1)} %get-tuple-element.60.refs_2_), custom_call_target="tpu_custom_call" | custom-call | flops 905969664 | bytes 6602752 | tf_op jit(solution)/shard_map/pallas_call | solution.py:223
  90.3 3.2 %collective-permute-start.23 = (bf16[2,256,128]{2,1,0:T(8,128)(2,1)S(1)}, bf16[2,256,128]{2,1,0:T(8,128)(2,1)S(1)}, u32[]{:S(2)}, u32[]{:S(2)}) collective-permute-start(bf16[2,256,128]{2,1,0:T(8,128)(2,1)S(1)} %get-tuple-element.72), channel_id=1, source_target_pairs={{0,7},{1,0},{2,1},{3,2},{4,3},{5,4},{6,5},{7,6},{8,15},{9,8},{10,9... | collective-permute-start | bytes 393224 | tf_op jit(solution)/shard_map/ppermute | solution.py:40
  93.6 3.1 %shard_map.82 = (f32[2,256,128]{2,1,0:T(8,128)S(1)}, bf16[2,256,128]{2,1,0:T(8,128)(2,1)S(1)}, f32[2,256,128]{2,1,0:T(8,128)S(1)}, bf16[2,256,128]{2,1,0:T(8,128)(2,1)S(1)}) custom-call(s32[2]{0:T(128)S(1)} %pad_add_fusion.where.refs_0_, bf16[18,288,384]{2,1,0:T(8,128)(2,1)S(1)} %shard_map.80.refs_1_, bf16[2,2304,256]{2,1,0:T(8,128)(2,1)S(1)} %get-tuple-element.60.refs_2_), custom_call_target="tpu_custom_call" | custom-call | flops 1811939328 | bytes 7127040 | tf_op jit(solution)/shard_map/pallas_call | solution.py:223
  97.2 3.2 %collective-permute-start.28 = (bf16[4,256,128]{2,1,0:T(8,128)(2,1)S(1)}, bf16[4,256,128]{2,1,0:T(8,128)(2,1)S(1)}, u32[]{:S(2)}, u32[]{:S(2)}) collective-permute-start(bf16[4,256,128]{2,1,0:T(8,128)(2,1)S(1)} %pad_maximum_fusion.1), channel_id=1, source_target_pairs={{0,7},{1,0},{2,1},{3,2},{4,3},{5,4},{6,5},{7,6},{8,15},{9,8},{10,9... | collective-permute-start | bytes 786440 | tf_op jit(solution)/shard_map/ppermute | solution.py:40
  100.4 1.9 %shard_map.83 = (f32[2,256,128]{2,1,0:T(8,128)S(1)}, f32[2,256,128]{2,1,0:T(8,128)S(1)}) custom-call(s32[2]{0:T(128)S(1)} %pad_add_fusion.where.refs_0_, bf16[18,288,384]{2,1,0:T(8,128)(2,1)S(1)} %shard_map.80.refs_1_, bf16[2,2304,256]{2,1,0:T(8,128)(2,1)S(1)} %get-tuple-element.60.refs_2_), custom_call_target="tpu_custom_call" | custom-call | flops 905969664 | bytes 6864896 | tf_op jit(solution)/shard_map/pallas_call | solution.py:223
  102.3 4.6 %collective-permute-start.32 = (bf16[27,32,128]{2,1,0:T(8,128)(2,1)S(1)}, bf16[27,32,128]{2,1,0:T(8,128)(2,1)S(1)}, u32[]{:S(2)}, u32[]{:S(2)}) collective-permute-start(bf16[27,32,128]{2,1,0:T(8,128)(2,1)S(1)} %slice.155), channel_id=1, source_target_pairs={{0,0},{1,1},{2,2},{3,3},{4,4},{5,5},{6,6},{7,7},{8,128},{9,129},{1... | collective-permute-start | bytes 663560 | tf_op jit(solution)/shard_map/ppermute | solution.py:40
  107.2 2.6 %collective-permute-start.29 = (bf16[2,256,128]{2,1,0:T(8,128)(2,1)S(1)}, bf16[2,256,128]{2,1,0:T(8,128)(2,1)S(1)}, u32[]{:S(2)}, u32[]{:S(2)}) collective-permute-start(bf16[2,256,128]{2,1,0:T(8,128)(2,1)S(1)} %get-tuple-element.84), channel_id=1, source_target_pairs={{0,0},{1,8},{2,16},{3,24},{4,32},{5,40},{6,48},{7,56},{8,36},{9,44... | collective-permute-start | bytes 393224 | tf_op jit(solution)/shard_map/ppermute | solution.py:40
  109.8 2.4 %collective-permute-start.30 = (bf16[2,256,128]{2,1,0:T(8,128)(2,1)S(1)}, bf16[2,256,128]{2,1,0:T(8,128)(2,1)S(1)}, u32[]{:S(2)}, u32[]{:S(2)}) collective-permute-start(bf16[2,256,128]{2,1,0:T(8,128)(2,1)S(1)} %get-tuple-element.85), channel_id=1, source_target_pairs={{0,32},{1,40},{2,48},{3,56},{4,0},{5,8},{6,16},{7,24},{8,4},{9,12}... | collective-permute-start | bytes 393224 | tf_op jit(solution)/shard_map/ppermute | solution.py:40
  112.1 0.5 fusion.16
  112.6 9.3 %collective-permute-done.29 = bf16[2,256,128]{2,1,0:T(8,128)(2,1)S(1)} collective-permute-done((bf16[2,256,128]{2,1,0:T(8,128)(2,1)S(1)}, bf16[2,256,128]{2,1,0:T(8,128)(2,1)S(1)}, u32[]{:S(2)}, u32[]{:S(2)}) %collective-permute-start.29) | collective-permute-done | bytes 131104 | tf_op jit(solution)/shard_map/ppermute | solution.py:40
  122.0 1.1 collective-permute-done.30
  123.2 0.6 collective-permute-start.31
  123.7 0.8 convert_bitcast_fusion
  124.6 5.0 %collective-permute-done.31 = bf16[2,256,128]{2,1,0:T(8,128)(2,1)S(1)} collective-permute-done((bf16[2,256,128]{2,1,0:T(8,128)(2,1)S(1)}, bf16[2,256,128]{2,1,0:T(8,128)(2,1)S(1)}, u32[]{:S(2)}, u32[]{:S(2)}) %collective-permute-start.31) | collective-permute-done | bytes 131104 | tf_op jit(solution)/shard_map/ppermute | solution.py:40
  129.6 0.7 pad_maximum_fusion.7
  130.3 0.7 pad_maximum_fusion.6
  (61 shorter events, 2.6 us)
Async XLA Ops:
  1.6 2.6 %collective-permute-start = (bf16[2,16,16,128]{3,2,1,0:T(8,128)(2,1)S(1)}, bf16[2,16,16,128]{3,2,1,0:T(8,128)(2,1)S(1)}, u32[]{:S(2)}, u32[]{:S(2)}) collective-permute-start(bf16[2,16,16,128]{3,2,1,0:T(8,128)(2,1)S(1)} %pad_maximum_fusion.2), channel_id=1, source_target_pairs={{0,248},{1,249},{2,250},{3,251},{4,252},{5,253},{6,254},{7,255},{8... | collective-permute-start | bytes 393224 | tf_op jit(solution)/shard_map/ppermute | solution.py:40
  4.3 17.4 %collective-permute-start.1 = (bf16[2,256,128]{2,1,0:T(8,128)(2,1)S(1)}, bf16[2,256,128]{2,1,0:T(8,128)(2,1)S(1)}, u32[]{:S(2)}, u32[]{:S(2)}) collective-permute-start(bf16[2,256,128]{2,1,0:T(8,128)(2,1)S(1)} %bitcast.13), channel_id=1, source_target_pairs={{0,0},{1,17},{2,34},{3,51},{4,12},{5,29},{6,46},{7,63},{8,1},{9,18... | collective-permute-start | bytes 393224 | tf_op jit(solution)/shard_map/ppermute | solution.py:40
  17.8 8.7 %collective-permute-start.2 = (bf16[2,256,128]{2,1,0:T(8,128)(2,1)S(1)}, bf16[2,256,128]{2,1,0:T(8,128)(2,1)S(1)}, u32[]{:S(2)}, u32[]{:S(2)}) collective-permute-start(bf16[2,256,128]{2,1,0:T(8,128)(2,1)S(1)} %bitcast.14), channel_id=1, source_target_pairs={{0,4},{1,21},{2,38},{3,55},{4,8},{5,25},{6,42},{7,59},{8,5},{9,22}... | collective-permute-start | bytes 393224 | tf_op jit(solution)/shard_map/ppermute | solution.py:40
  19.7 13.6 %collective-permute-start.5 = (bf16[27,32,128]{2,1,0:T(8,128)(2,1)}, bf16[27,32,128]{2,1,0:T(8,128)(2,1)S(1)}, u32[]{:S(2)}, u32[]{:S(2)}) collective-permute-start(bf16[27,32,128]{2,1,0:T(8,128)(2,1)} %bitcast.17), channel_id=1, source_target_pairs={{0,0},{1,1},{2,2},{3,3},{4,4},{5,5},{6,6},{7,7},{8,128},{9,129},{1... | collective-permute-start | bytes 663560 | tf_op jit(solution)/shard_map/ppermute | solution.py:40
  26.5 12.0 %collective-permute-start.4 = (bf16[4,256,128]{2,1,0:T(8,128)(2,1)S(1)}, bf16[4,256,128]{2,1,0:T(8,128)(2,1)S(1)}, u32[]{:S(2)}, u32[]{:S(2)}) collective-permute-start(bf16[4,256,128]{2,1,0:T(8,128)(2,1)S(1)} %constant_dynamic-update-slice_fusion.refs_0_), channel_id=1, source_target_pairs={{0,1},{1,2},{2,3},{3,4},{4,5},{5,6},{6,7},{7,0},{8,9},{9,10},{10,1... | collective-permute-start | bytes 786440 | tf_op jit(solution)/shard_map/ppermute | solution.py:40
  26.5 11.9 %collective-permute-start.3 = (bf16[4,256,128]{2,1,0:T(8,128)(2,1)S(1)}, bf16[4,256,128]{2,1,0:T(8,128)(2,1)S(1)}, u32[]{:S(2)}, u32[]{:S(2)}) collective-permute-start(bf16[4,256,128]{2,1,0:T(8,128)(2,1)S(1)} %constant_dynamic-update-slice_fusion.refs_0_), channel_id=1, source_target_pairs={{0,7},{1,0},{2,1},{3,2},{4,3},{5,4},{6,5},{7,6},{8,15},{9,8},{10,9... | collective-permute-start | bytes 786440 | tf_op jit(solution)/shard_map/ppermute | solution.py:40
  33.3 12.9 %collective-permute-start.9 = (bf16[27,32,128]{2,1,0:T(8,128)(2,1)S(1)}, bf16[27,32,128]{2,1,0:T(8,128)(2,1)S(1)}, u32[]{:S(2)}, u32[]{:S(2)}) collective-permute-start(bf16[27,32,128]{2,1,0:T(8,128)(2,1)S(1)} %collective-permute-done.5.refs_0_), channel_id=1, source_target_pairs={{0,64},{1,65},{2,66},{3,67},{4,68},{5,69},{6,70},{7,71},{8,72},{9,... | collective-permute-start | bytes 663560 | tf_op jit(solution)/shard_map/ppermute | solution.py:40
  34.2 11.9 %collective-permute-start.8 = (bf16[27,32,128]{2,1,0:T(8,128)(2,1)S(1)}, bf16[27,32,128]{2,1,0:T(8,128)(2,1)S(1)}, u32[]{:S(2)}, u32[]{:S(2)}) collective-permute-start(bf16[27,32,128]{2,1,0:T(8,128)(2,1)S(1)} %collective-permute-done.5.refs_0_), channel_id=1, source_target_pairs={{0,192},{1,193},{2,194},{3,195},{4,196},{5,197},{6,198},{7,199},{8... | collective-permute-start | bytes 663560 | tf_op jit(solution)/shard_map/ppermute | solution.py:40
  36.5 9.6 %collective-permute-start.10 = (bf16[27,32,128]{2,1,0:T(8,128)(2,1)S(1)}, bf16[27,32,128]{2,1,0:T(8,128)(2,1)S(1)}, u32[]{:S(2)}, u32[]{:S(2)}) collective-permute-start(bf16[27,32,128]{2,1,0:T(8,128)(2,1)S(1)} %collective-permute-done.5.refs_0_), channel_id=1, source_target_pairs={{0,128},{1,129},{2,130},{3,131},{4,132},{5,133},{6,134},{7,135},{8... | collective-permute-start | bytes 663560 | tf_op jit(solution)/shard_map/ppermute | solution.py:40
  38.5 6.3 %collective-permute-start.7 = (bf16[2,256,128]{2,1,0:T(8,128)(2,1)S(1)}, bf16[2,256,128]{2,1,0:T(8,128)(2,1)S(1)}, u32[]{:S(2)}, u32[]{:S(2)}) collective-permute-start(bf16[2,256,128]{2,1,0:T(8,128)(2,1)S(1)} %slice.81), channel_id=1, source_target_pairs={{0,1},{1,2},{2,3},{3,4},{4,5},{5,6},{6,7},{7,0},{8,9},{9,10},{10,1... | collective-permute-start | bytes 393224 | tf_op jit(solution)/shard_map/ppermute | solution.py:40
  38.5 6.2 %collective-permute-start.6 = (bf16[2,256,128]{2,1,0:T(8,128)(2,1)S(1)}, bf16[2,256,128]{2,1,0:T(8,128)(2,1)S(1)}, u32[]{:S(2)}, u32[]{:S(2)}) collective-permute-start(bf16[2,256,128]{2,1,0:T(8,128)(2,1)S(1)} %slice.80), channel_id=1, source_target_pairs={{0,7},{1,0},{2,1},{3,2},{4,3},{5,4},{6,5},{7,6},{8,15},{9,8},{10,9... | collective-permute-start | bytes 393224 | tf_op jit(solution)/shard_map/ppermute | solution.py:40
  50.6 12.6 %copy-start = (f32[128]{0:T(128)S(1)}, f32[128]{0:T(128)}, u32[]{:S(2)}) copy-start(f32[128]{0:T(128)} %param.6) | copy-start | bytes 1540
  50.6 3.2 %collective-permute-start.11 = (bf16[8,256,128]{2,1,0:T(8,128)(2,1)S(1)}, bf16[8,256,128]{2,1,0:T(8,128)(2,1)S(1)}, u32[]{:S(2)}, u32[]{:S(2)}) collective-permute-start(bf16[8,256,128]{2,1,0:T(8,128)(2,1)S(1)} %shard_map.77), channel_id=1, source_target_pairs={{0,8},{1,9},{2,10},{3,11},{4,12},{5,13},{6,14},{7,15},{8,0},{9,1},... | collective-permute-start | bytes 1572872 | tf_op jit(solution)/shard_map/ppermute | solution.py:40
  54.0 6.2 %collective-permute-start.12 = (bf16[2,256,128]{2,1,0:T(8,128)(2,1)S(1)}, bf16[2,256,128]{2,1,0:T(8,128)(2,1)S(1)}, u32[]{:S(2)}, u32[]{:S(2)}) collective-permute-start(bf16[2,256,128]{2,1,0:T(8,128)(2,1)S(1)} %get-tuple-element.86), channel_id=1, source_target_pairs={{0,16},{1,17},{2,18},{3,19},{4,20},{5,21},{6,22},{7,23},{8,24},{9,... | collective-permute-start | bytes 393224 | tf_op jit(solution)/shard_map/ppermute | solution.py:40
  54.3 6.4 %collective-permute-start.14 = (bf16[2,256,128]{2,1,0:T(8,128)(2,1)S(1)}, bf16[2,256,128]{2,1,0:T(8,128)(2,1)S(1)}, u32[]{:S(2)}, u32[]{:S(2)}) collective-permute-start(bf16[2,256,128]{2,1,0:T(8,128)(2,1)S(1)} %get-tuple-element.87), channel_id=1, source_target_pairs={{0,48},{1,49},{2,50},{3,51},{4,52},{5,53},{6,54},{7,55},{8,56},{9,... | collective-permute-start | bytes 393224 | tf_op jit(solution)/shard_map/ppermute | solution.py:40
  56.3 6.8 %collective-permute-start.13 = (bf16[2,256,128]{2,1,0:T(8,128)(2,1)S(1)}, bf16[2,256,128]{2,1,0:T(8,128)(2,1)S(1)}, u32[]{:S(2)}, u32[]{:S(2)}) collective-permute-start(bf16[2,256,128]{2,1,0:T(8,128)(2,1)S(1)} %get-tuple-element.88), channel_id=1, source_target_pairs={{0,32},{1,33},{2,34},{3,35},{4,36},{5,37},{6,38},{7,39},{8,40},{9,... | collective-permute-start | bytes 393224 | tf_op jit(solution)/shard_map/ppermute | solution.py:40
  63.4 5.6 %collective-permute-start.17 = (bf16[2,256,128]{2,1,0:T(8,128)(2,1)S(1)}, bf16[2,256,128]{2,1,0:T(8,128)(2,1)S(1)}, u32[]{:S(2)}, u32[]{:S(2)}) collective-permute-start(bf16[2,256,128]{2,1,0:T(8,128)(2,1)S(1)} %get-tuple-element.82.refs_2_.refs_0_), channel_id=1, source_target_pairs={{0,48},{1,49},{2,50},{3,51},{4,52},{5,53},{6,54},{7,55},{8,56},{9,... | collective-permute-start | bytes 393224 | tf_op jit(solution)/shard_map/ppermute | solution.py:40
  65.1 7.6 %collective-permute-start.16 = (bf16[2,256,128]{2,1,0:T(8,128)(2,1)S(1)}, bf16[2,256,128]{2,1,0:T(8,128)(2,1)S(1)}, u32[]{:S(2)}, u32[]{:S(2)}) collective-permute-start(bf16[2,256,128]{2,1,0:T(8,128)(2,1)S(1)} %get-tuple-element.82.refs_2_.refs_0_), channel_id=1, source_target_pairs={{0,32},{1,33},{2,34},{3,35},{4,36},{5,37},{6,38},{7,39},{8,40},{9,... | collective-permute-start | bytes 393224 | tf_op jit(solution)/shard_map/ppermute | solution.py:40
  67.5 6.6 %collective-permute-start.15 = (bf16[2,256,128]{2,1,0:T(8,128)(2,1)S(1)}, bf16[2,256,128]{2,1,0:T(8,128)(2,1)S(1)}, u32[]{:S(2)}, u32[]{:S(2)}) collective-permute-start(bf16[2,256,128]{2,1,0:T(8,128)(2,1)S(1)} %get-tuple-element.82.refs_2_.refs_0_), channel_id=1, source_target_pairs={{0,16},{1,17},{2,18},{3,19},{4,20},{5,21},{6,22},{7,23},{8,24},{9,... | collective-permute-start | bytes 393224 | tf_op jit(solution)/shard_map/ppermute | solution.py:40
  67.7 6.4 %collective-permute-start.18 = (bf16[2,256,128]{2,1,0:T(8,128)(2,1)S(1)}, bf16[2,256,128]{2,1,0:T(8,128)(2,1)S(1)}, u32[]{:S(2)}, u32[]{:S(2)}) collective-permute-start(bf16[2,256,128]{2,1,0:T(8,128)(2,1)S(1)} %get-tuple-element.82.refs_2_.refs_0_), channel_id=1, source_target_pairs={{0,8},{1,9},{2,10},{3,11},{4,12},{5,13},{6,14},{7,15},{8,0},{9,1},... | collective-permute-start | bytes 393224 | tf_op jit(solution)/shard_map/ppermute | solution.py:40
  69.0 5.2 %collective-permute-start.21 = (bf16[2,256,128]{2,1,0:T(8,128)(2,1)S(1)}, bf16[2,256,128]{2,1,0:T(8,128)(2,1)S(1)}, u32[]{:S(2)}, u32[]{:S(2)}) collective-permute-start(bf16[2,256,128]{2,1,0:T(8,128)(2,1)S(1)} %collective-permute-done.17.refs_5_.refs_3_), channel_id=1, source_target_pairs={{0,8},{1,9},{2,10},{3,11},{4,12},{5,13},{6,14},{7,15},{8,0},{9,1},... | collective-permute-start | bytes 393224 | tf_op jit(solution)/shard_map/ppermute | solution.py:40
  72.7 1.5 %collective-permute-start.20 = (bf16[2,256,128]{2,1,0:T(8,128)(2,1)S(1)}, bf16[2,256,128]{2,1,0:T(8,128)(2,1)S(1)}, u32[]{:S(2)}, u32[]{:S(2)}) collective-permute-start(bf16[2,256,128]{2,1,0:T(8,128)(2,1)S(1)} %collective-permute-done.16.refs_4_.refs_2_), channel_id=1, source_target_pairs={{0,8},{1,9},{2,10},{3,11},{4,12},{5,13},{6,14},{7,15},{8,0},{9,1},... | collective-permute-start | bytes 393224 | tf_op jit(solution)/shard_map/ppermute | solution.py:40
  74.1 1.3 %collective-permute-start.19 = (bf16[2,256,128]{2,1,0:T(8,128)(2,1)S(1)}, bf16[2,256,128]{2,1,0:T(8,128)(2,1)S(1)}, u32[]{:S(2)}, u32[]{:S(2)}) collective-permute-start(bf16[2,256,128]{2,1,0:T(8,128)(2,1)S(1)} %collective-permute-done.15.refs_3_.refs_1_), channel_id=1, source_target_pairs={{0,8},{1,9},{2,10},{3,11},{4,12},{5,13},{6,14},{7,15},{8,0},{9,1},... | collective-permute-start | bytes 393224 | tf_op jit(solution)/shard_map/ppermute | solution.py:40
  81.2 15.7 %collective-permute-start.24 = (bf16[28,32,128]{2,1,0:T(8,128)(2,1)S(1)}, bf16[28,32,128]{2,1,0:T(8,128)(2,1)S(1)}, u32[]{:S(2)}, u32[]{:S(2)}) collective-permute-start(bf16[28,32,128]{2,1,0:T(8,128)(2,1)S(1)} %get-tuple-element.75), channel_id=1, source_target_pairs={{0,64},{1,65},{2,66},{3,67},{4,68},{5,69},{6,70},{7,71},{8,72},{9,... | collective-permute-start | bytes 688136 | tf_op jit(solution)/shard_map/ppermute | solution.py:40
  83.9 13.0 %collective-permute-start.25 = (bf16[28,32,128]{2,1,0:T(8,128)(2,1)S(1)}, bf16[28,32,128]{2,1,0:T(8,128)(2,1)S(1)}, u32[]{:S(2)}, u32[]{:S(2)}) collective-permute-start(bf16[28,32,128]{2,1,0:T(8,128)(2,1)S(1)} %get-tuple-element.76), channel_id=1, source_target_pairs={{0,128},{1,129},{2,130},{3,131},{4,132},{5,133},{6,134},{7,135},{8... | collective-permute-start | bytes 688136 | tf_op jit(solution)/shard_map/ppermute | solution.py:40
  85.2 11.7 %collective-permute-start.26 = (bf16[28,32,128]{2,1,0:T(8,128)(2,1)S(1)}, bf16[28,32,128]{2,1,0:T(8,128)(2,1)S(1)}, u32[]{:S(2)}, u32[]{:S(2)}) collective-permute-start(bf16[28,32,128]{2,1,0:T(8,128)(2,1)S(1)} %get-tuple-element.77), channel_id=1, source_target_pairs={{0,192},{1,193},{2,194},{3,195},{4,196},{5,197},{6,198},{7,199},{8... | collective-permute-start | bytes 688136 | tf_op jit(solution)/shard_map/ppermute | solution.py:40
  90.0 6.7 %collective-permute-start.22 = (bf16[2,256,128]{2,1,0:T(8,128)(2,1)S(1)}, bf16[2,256,128]{2,1,0:T(8,128)(2,1)S(1)}, u32[]{:S(2)}, u32[]{:S(2)}) collective-permute-start(bf16[2,256,128]{2,1,0:T(8,128)(2,1)S(1)} %get-tuple-element.69), channel_id=1, source_target_pairs={{0,1},{1,2},{2,3},{3,4},{4,5},{5,6},{6,7},{7,0},{8,9},{9,10},{10,1... | collective-permute-start | bytes 393224 | tf_op jit(solution)/shard_map/ppermute | solution.py:40
  90.3 6.4 %collective-permute-start.23 = (bf16[2,256,128]{2,1,0:T(8,128)(2,1)S(1)}, bf16[2,256,128]{2,1,0:T(8,128)(2,1)S(1)}, u32[]{:S(2)}, u32[]{:S(2)}) collective-permute-start(bf16[2,256,128]{2,1,0:T(8,128)(2,1)S(1)} %get-tuple-element.72), channel_id=1, source_target_pairs={{0,7},{1,0},{2,1},{3,2},{4,3},{5,4},{6,5},{7,6},{8,15},{9,8},{10,9... | collective-permute-start | bytes 393224 | tf_op jit(solution)/shard_map/ppermute | solution.py:40
  97.1 9.9 %collective-permute-start.27 = (bf16[4,256,128]{2,1,0:T(8,128)(2,1)S(1)}, bf16[4,256,128]{2,1,0:T(8,128)(2,1)S(1)}, u32[]{:S(2)}, u32[]{:S(2)}) collective-permute-start(bf16[4,256,128]{2,1,0:T(8,128)(2,1)S(1)} %pad_maximum_fusion), channel_id=1, source_target_pairs={{0,1},{1,2},{2,3},{3,4},{4,5},{5,6},{6,7},{7,0},{8,9},{9,10},{10,1... | collective-permute-start | bytes 786440 | tf_op jit(solution)/shard_map/ppermute | solution.py:40
  97.2 9.9 %collective-permute-start.28 = (bf16[4,256,128]{2,1,0:T(8,128)(2,1)S(1)}, bf16[4,256,128]{2,1,0:T(8,128)(2,1)S(1)}, u32[]{:S(2)}, u32[]{:S(2)}) collective-permute-start(bf16[4,256,128]{2,1,0:T(8,128)(2,1)S(1)} %pad_maximum_fusion.1), channel_id=1, source_target_pairs={{0,7},{1,0},{2,1},{3,2},{4,3},{5,4},{6,5},{7,6},{8,15},{9,8},{10,9... | collective-permute-start | bytes 786440 | tf_op jit(solution)/shard_map/ppermute | solution.py:40
  102.3 21.4 %collective-permute-start.32 = (bf16[27,32,128]{2,1,0:T(8,128)(2,1)S(1)}, bf16[27,32,128]{2,1,0:T(8,128)(2,1)S(1)}, u32[]{:S(2)}, u32[]{:S(2)}) collective-permute-start(bf16[27,32,128]{2,1,0:T(8,128)(2,1)S(1)} %slice.155), channel_id=1, source_target_pairs={{0,0},{1,1},{2,2},{3,3},{4,4},{5,5},{6,6},{7,7},{8,128},{9,129},{1... | collective-permute-start | bytes 663560 | tf_op jit(solution)/shard_map/ppermute | solution.py:40
  107.2 14.8 %collective-permute-start.29 = (bf16[2,256,128]{2,1,0:T(8,128)(2,1)S(1)}, bf16[2,256,128]{2,1,0:T(8,128)(2,1)S(1)}, u32[]{:S(2)}, u32[]{:S(2)}) collective-permute-start(bf16[2,256,128]{2,1,0:T(8,128)(2,1)S(1)} %get-tuple-element.84), channel_id=1, source_target_pairs={{0,0},{1,8},{2,16},{3,24},{4,32},{5,40},{6,48},{7,56},{8,36},{9,44... | collective-permute-start | bytes 393224 | tf_op jit(solution)/shard_map/ppermute | solution.py:40
  109.8 13.3 %collective-permute-start.30 = (bf16[2,256,128]{2,1,0:T(8,128)(2,1)S(1)}, bf16[2,256,128]{2,1,0:T(8,128)(2,1)S(1)}, u32[]{:S(2)}, u32[]{:S(2)}) collective-permute-start(bf16[2,256,128]{2,1,0:T(8,128)(2,1)S(1)} %get-tuple-element.85), channel_id=1, source_target_pairs={{0,32},{1,40},{2,48},{3,56},{4,0},{5,8},{6,16},{7,24},{8,4},{9,12}... | collective-permute-start | bytes 393224 | tf_op jit(solution)/shard_map/ppermute | solution.py:40
  123.2 6.4 %collective-permute-start.31 = (bf16[2,256,128]{2,1,0:T(8,128)(2,1)S(1)}, bf16[2,256,128]{2,1,0:T(8,128)(2,1)S(1)}, u32[]{:S(2)}, u32[]{:S(2)}) collective-permute-start(bf16[2,256,128]{2,1,0:T(8,128)(2,1)S(1)} %pad_maximum_fusion.5), channel_id=1, source_target_pairs={{0,8},{1,9},{2,10},{3,11},{4,12},{5,13},{6,14},{7,15},{8,16},{9,17... | collective-permute-start | bytes 393224 | tf_op jit(solution)/shard_map/ppermute | solution.py:40

commit v4 on v3

--- a/solution.py
+++ b/solution.py
@@ -296,7 +296,7 @@
     keep = products(own_pairs, where, columns, ahead_weights, [shaped((2, FACE, out_size), f32)] * 4)
     keep = [piece + send[2 * r : 2 * r + 2] for r, piece in enumerate(keep)]
     pre_act = keep[0]
-    for r in range(1, 4):
+    for r in (2, 1, 3):
         pre_act = pre_act + permuted(
             keep[r].astype(bf16), lambda x, q, z: at(x, q + 2 * r, z)
         ).astype(f32)
@@ -351,27 +351,28 @@
     above, below, where = lax.optimization_barrier((above, below, where))
     above = jnp.concatenate([(above + up).astype(bf16), far_above])
     below = jnp.concatenate([(below + down).astype(bf16), far_below])
-    above, below, held = lax.optimization_barrier((above, below, held))
+    above, below, where = lax.optimization_barrier((above, below, where))
     near, beyond = parts((0, 4), where, [f32, f32])
     above, below = along_z(above, 1).astype(f32), along_z(below, -1).astype(f32)
     near = (near + above[:2] + below[:2]).astype(bf16)
     beyond = (beyond + above[2:] + below[2:]).astype(bf16)
 
+    near, beyond, held, activated = lax.optimization_barrier((near, beyond, held, activated))
+
+    def next_slab(plane):
+        return permuted(plane, lambda x, q, z: device(NQ * x + q + 1, z))
+
+    def home(step):
+        return lambda x, q, z: device(NQ * x + (z - group(q) - step) % NZ, group(q))
+
+    near, beyond = permuted(near, home(0)).astype(f32), permuted(beyond, home(4)).astype(f32)
+    summed = (near + beyond).astype(bf16)
     grad_filters = permuted(
         held, lambda x, q, z: device(NX * group(q) + swapped(x), z)
     ).astype(f32)
 
-    def home(step):
-        return lambda x, q, z: device(NQ * x + (z - group(q) - step) % NZ, group(q))
-
-    near, beyond = permuted(near, home(0)).astype(f32), permuted(beyond, home(4)).astype(f32)
-    summed = (near + beyond).astype(bf16)
-    seconds = permuted(
-        jnp.stack([activated[1], summed[1]]), lambda x, q, z: device(NQ * x + q + 1, z)
-    )
-    activated = jnp.stack([seconds[0], activated[0]])
-    grad_input = jnp.stack([seconds[1], summed[0]])
-
+    activated = jnp.stack([next_slab(activated[1]), activated[0]])
+    grad_input = jnp.stack([next_slab(summed[1]), summed[0]])
     shape = (2, GRID, GRID)
     return (
         activated.reshape(*shape, out_size),

time: 134 us -> 137 us (1.022); the launches traced: 131 us -> 136 us
  starting transfers between devices: 62.3 us -> 65.9 us
  waiting for transfers between devices: 39.6 us -> 41.3 us
    ppermute x33 -> x34, starting transfers between devices: 62.3 us -> 65.9 us  [permuted(): return lax.ppermute(array, ('space', 'chan'), pairs)]
    ppermute x33 -> x34, waiting for transfers between devices: 39.6 us -> 41.3 us  [permuted(): return lax.ppermute(array, ('space', 'chan'), pairs)]
  transfers between devices with their start and end apart: 33 -> 34, of which waited for: 13 -> 14; matrix products, arithmetic and copies ran while one was open for 1% -> 2% of each run, Pallas kernels for 10% -> 10%
where the time goes in v4:
time: 137 us; the launch traced here: 136 us
  starting transfers between devices  65.9 us (48%)
  waiting for transfers between devices  41.3 us (30%)
  Pallas kernels  23.1 us (17%)
  other arithmetic  3.76 us (3%)
    ppermute x34, starting transfers between devices, permuted(): return lax.ppermute(array, ('space', 'chan'), pairs)  65.9 us
    ppermute x34, waiting for transfers between devices, permuted(): return lax.ppermute(array, ('space', 'chan'), pairs)  41.3 us
    pallas_call x9, Pallas kernels, call(): pl.pallas_call(kernel, out_shape=outs, in_specs=[pl.BlockSpec(memory_spac...  23.1 us
  transfers between devices with their start and end apart: 34, of which 14 were waited for; matrix products, arithmetic and copies ran while one was open for 2% of the time, Pallas kernels for 10%

profile of v4, /device:TPU:16, one launch (start us, length us, event | category | flops | bytes accessed | tf_op | source)
XLA Modules:
  0.0 136.2 jit_solution(1605313832091134034)
XLA Ops:
  0.6 1.0 fusion.18
  1.7 2.5 %collective-permute-done = bf16[2,16,16,128]{3,2,1,0:T(8,128)(2,1)S(1)} collective-permute-done((bf16[2,16,16,128]{3,2,1,0:T(8,128)(2,1)S(1)}, bf16[2,16,16,128]{3,2,1,0:T(8,128)(2,1)S(1)}, u32[]{:S(2)}, u32[]{:S(2)}) %collective-permute-start) | collective-permute-done | bytes 131104 | tf_op jit(solution)/shard_map/ppermute | solution.py:40
  4.3 13.5 %collective-permute-start.1 = (bf16[2,256,128]{2,1,0:T(8,128)(2,1)S(1)}, bf16[2,256,128]{2,1,0:T(8,128)(2,1)S(1)}, u32[]{:S(2)}, u32[]{:S(2)}) collective-permute-start(bf16[2,256,128]{2,1,0:T(8,128)(2,1)S(1)} %bitcast.21), channel_id=1, source_target_pairs={{0,0},{1,17},{2,34},{3,51},{4,12},{5,29},{6,46},{7,63},{8,1},{9,18... | collective-permute-start | bytes 393224 | tf_op jit(solution)/shard_map/ppermute | solution.py:40
  17.8 1.9 %collective-permute-start.2 = (bf16[2,256,128]{2,1,0:T(8,128)(2,1)S(1)}, bf16[2,256,128]{2,1,0:T(8,128)(2,1)S(1)}, u32[]{:S(2)}, u32[]{:S(2)}) collective-permute-start(bf16[2,256,128]{2,1,0:T(8,128)(2,1)S(1)} %bitcast.22), channel_id=1, source_target_pairs={{0,4},{1,21},{2,38},{3,55},{4,8},{5,25},{6,42},{7,59},{8,5},{9,22}... | collective-permute-start | bytes 393224 | tf_op jit(solution)/shard_map/ppermute | solution.py:40
  19.7 1.9 %collective-permute-start.5 = (bf16[27,32,128]{2,1,0:T(8,128)(2,1)}, bf16[27,32,128]{2,1,0:T(8,128)(2,1)S(1)}, u32[]{:S(2)}, u32[]{:S(2)}) collective-permute-start(bf16[27,32,128]{2,1,0:T(8,128)(2,1)} %bitcast.25), channel_id=1, source_target_pairs={{0,0},{1,1},{2,2},{3,3},{4,4},{5,5},{6,6},{7,7},{8,128},{9,129},{1... | collective-permute-start | bytes 663560 | tf_op jit(solution)/shard_map/ppermute | solution.py:40
  21.7 4.8 %collective-permute-done.2 = bf16[2,256,128]{2,1,0:T(8,128)(2,1)S(1)} collective-permute-done((bf16[2,256,128]{2,1,0:T(8,128)(2,1)S(1)}, bf16[2,256,128]{2,1,0:T(8,128)(2,1)S(1)}, u32[]{:S(2)}, u32[]{:S(2)}) %collective-permute-start.2) | collective-permute-done | bytes 131104 | tf_op jit(solution)/shard_map/ppermute | solution.py:40
  26.5 6.7 %collective-permute-start.3 = (bf16[4,256,128]{2,1,0:T(8,128)(2,1)S(1)}, bf16[4,256,128]{2,1,0:T(8,128)(2,1)S(1)}, u32[]{:S(2)}, u32[]{:S(2)}) collective-permute-start(bf16[4,256,128]{2,1,0:T(8,128)(2,1)S(1)} %constant_dynamic-update-slice_fusion.refs_0_), channel_id=1, source_target_pairs={{0,7},{1,0},{2,1},{3,2},{4,3},{5,4},{6,5},{7,6},{8,15},{9,8},{10,9... | collective-permute-start | bytes 786440 | tf_op jit(solution)/shard_map/ppermute | solution.py:40
  33.3 0.9 collective-permute-start.9
  34.2 2.3 %collective-permute-start.8 = (bf16[27,32,128]{2,1,0:T(8,128)(2,1)S(1)}, bf16[27,32,128]{2,1,0:T(8,128)(2,1)S(1)}, u32[]{:S(2)}, u32[]{:S(2)}) collective-permute-start(bf16[27,32,128]{2,1,0:T(8,128)(2,1)S(1)} %collective-permute-done.5.refs_0_), channel_id=1, source_target_pairs={{0,192},{1,193},{2,194},{3,195},{4,196},{5,197},{6,198},{7,199},{8... | collective-permute-start | bytes 663560 | tf_op jit(solution)/shard_map/ppermute | solution.py:40
  36.5 1.9 %collective-permute-start.10 = (bf16[27,32,128]{2,1,0:T(8,128)(2,1)S(1)}, bf16[27,32,128]{2,1,0:T(8,128)(2,1)S(1)}, u32[]{:S(2)}, u32[]{:S(2)}) collective-permute-start(bf16[27,32,128]{2,1,0:T(8,128)(2,1)S(1)} %collective-permute-done.5.refs_0_), channel_id=1, source_target_pairs={{0,128},{1,129},{2,130},{3,131},{4,132},{5,133},{6,134},{7,135},{8... | collective-permute-start | bytes 663560 | tf_op jit(solution)/shard_map/ppermute | solution.py:40
  38.5 3.2 %collective-permute-start.6 = (bf16[2,256,128]{2,1,0:T(8,128)(2,1)S(1)}, bf16[2,256,128]{2,1,0:T(8,128)(2,1)S(1)}, u32[]{:S(2)}, u32[]{:S(2)}) collective-permute-start(bf16[2,256,128]{2,1,0:T(8,128)(2,1)S(1)} %slice.74), channel_id=1, source_target_pairs={{0,7},{1,0},{2,1},{3,2},{4,3},{5,4},{6,5},{7,6},{8,15},{9,8},{10,9... | collective-permute-start | bytes 393224 | tf_op jit(solution)/shard_map/ppermute | solution.py:40
  41.8 2.9 %collective-permute-done.7.refs_4_ = bf16[2,256,128]{2,1,0:T(8,128)(2,1)S(1)} collective-permute-done((bf16[2,256,128]{2,1,0:T(8,128)(2,1)S(1)}, bf16[2,256,128]{2,1,0:T(8,128)(2,1)S(1)}, u32[]{:S(2)}, u32[]{:S(2)}) %collective-permute-start.7) | collective-permute-done | bytes 131104 | tf_op jit(solution)/shard_map/ppermute | solution.py:40
  44.7 1.4 %shard_map.75.refs_1_ = bf16[18,288,384]{2,1,0:T(8,128)(2,1)S(1)} custom-call(s32[2]{0:T(128)S(1)} %pad_add_fusion.where.refs_0_, bf16[4,256,128]{2,1,0:T(8,128)(2,1)S(1)} %constant_dynamic-update-slice_fusion.refs_0_, bf16[4,256,128]{2,1,0:T(8,128)(2,1)S(1)} %collective-permute-done.3.refs_1_, bf16[4,256,128]{2,1,0:T(8,128)(2,1)S(1)} %collective-permute-done.4.refs_2_, ...), custom_call_target="tpu_custom_call" | custom-call | bytes 5029888 | tf_op jit(solution)/shard_map/pallas_call | solution.py:223
  46.2 1.2 shard_map.76
  47.4 3.1 %shard_map.77 = bf16[8,256,128]{2,1,0:T(8,128)(2,1)S(1)} custom-call(s32[2]{0:T(128)S(1)} %pad_add_fusion.where.refs_0_, bf16[18,288,384]{2,1,0:T(8,128)(2,1)S(1)} %shard_map.75.refs_1_, bf16[2,2304,256]{2,1,0:T(8,128)(2,1)S(1)} %get-tuple-element.52.refs_2_), custom_call_target="tpu_custom_call" | custom-call | flops 1811939328 | bytes 6864896 | tf_op jit(solution)/shard_map/pallas_call | solution.py:223
  50.7 3.1 %shard_map.78 = (f32[2,256,128]{2,1,0:T(8,128)S(1)}, f32[2,256,128]{2,1,0:T(8,128)S(1)}, f32[2,256,128]{2,1,0:T(8,128)S(1)}, f32[2,256,128]{2,1,0:T(8,128)S(1)}) custom-call(s32[2]{0:T(128)S(1)} %pad_add_fusion.where.refs_0_, bf16[18,288,384]{2,1,0:T(8,128)(2,1)S(1)} %shard_map.75.refs_1_, bf16[2,2304,256]{2,1,0:T(8,128)(2,1)S(1)} %get-tuple-element.52.refs_2_), custom_call_target="tpu_custom_call" | custom-call | flops 1811939328 | bytes 7389184 | tf_op jit(solution)/shard_map/pallas_call | solution.py:223
  54.3 1.1 collective-permute-start.14
  55.4 1.4 %collective-permute-start.13 = (bf16[2,256,128]{2,1,0:T(8,128)(2,1)S(1)}, bf16[2,256,128]{2,1,0:T(8,128)(2,1)S(1)}, u32[]{:S(2)}, u32[]{:S(2)}) collective-permute-start(bf16[2,256,128]{2,1,0:T(8,128)(2,1)S(1)} %get-tuple-element.96), channel_id=1, source_target_pairs={{0,16},{1,17},{2,18},{3,19},{4,20},{5,21},{6,22},{7,23},{8,24},{9,... | collective-permute-start | bytes 393224 | tf_op jit(solution)/shard_map/ppermute | solution.py:40
  56.8 5.3 %collective-permute-done.12 = bf16[2,256,128]{2,1,0:T(8,128)(2,1)S(1)} collective-permute-done((bf16[2,256,128]{2,1,0:T(8,128)(2,1)S(1)}, bf16[2,256,128]{2,1,0:T(8,128)(2,1)S(1)}, u32[]{:S(2)}, u32[]{:S(2)}) %collective-permute-start.12) | collective-permute-done | bytes 131104 | tf_op jit(solution)/shard_map/ppermute | solution.py:40
  62.1 1.2 collective-permute-done.14
  63.4 1.1 collective-permute-done.13
  64.9 0.7 collective-permute-start.17
  65.5 1.1 collective-permute-start.16
  66.6 1.7 %collective-permute-start.15 = (bf16[2,256,128]{2,1,0:T(8,128)(2,1)S(1)}, bf16[2,256,128]{2,1,0:T(8,128)(2,1)S(1)}, u32[]{:S(2)}, u32[]{:S(2)}) collective-permute-start(bf16[2,256,128]{2,1,0:T(8,128)(2,1)S(1)} %fusion.6.refs_2_.refs_0_), channel_id=1, source_target_pairs={{0,16},{1,17},{2,18},{3,19},{4,20},{5,21},{6,22},{7,23},{8,24},{9,... | collective-permute-start | bytes 393224 | tf_op jit(solution)/shard_map/ppermute | solution.py:40
  68.3 3.0 %collective-permute-done.17.refs_5_.refs_3_ = bf16[2,256,128]{2,1,0:T(8,128)(2,1)S(1)} collective-permute-done((bf16[2,256,128]{2,1,0:T(8,128)(2,1)S(1)}, bf16[2,256,128]{2,1,0:T(8,128)(2,1)S(1)}, u32[]{:S(2)}, u32[]{:S(2)}) %collective-permute-start.17) | collective-permute-done | bytes 131104 | tf_op jit(solution)/shard_map/ppermute | solution.py:40
  71.3 2.1 %collective-permute-done.16.refs_4_.refs_2_ = bf16[2,256,128]{2,1,0:T(8,128)(2,1)S(1)} collective-permute-done((bf16[2,256,128]{2,1,0:T(8,128)(2,1)S(1)}, bf16[2,256,128]{2,1,0:T(8,128)(2,1)S(1)}, u32[]{:S(2)}, u32[]{:S(2)}) %collective-permute-start.16) | collective-permute-done | bytes 131104 | tf_op jit(solution)/shard_map/ppermute | solution.py:40
  73.4 0.9 collective-permute-done.15.refs_3_.refs_1_
  74.8 0.9 collective-permute-done.19.refs_7_.refs_5_
  75.7 5.8 %shard_map.79 = (bf16[28,32,128]{2,1,0:T(8,128)(2,1)S(1)}, bf16[28,32,128]{2,1,0:T(8,128)(2,1)S(1)}, bf16[28,32,128]{2,1,0:T(8,128)(2,1)S(1)}, bf16[28,32,128]{2,1,0:T(8,128)(2,1)S(1)}) custom-call(s32[2]{0:T(128)S(1)} %pad_add_fusion.where.refs_0_, bf16[18,288,384]{2,1,0:T(8,128)(2,1)S(1)} %shard_map.75.refs_1_, ...), custom_call_target="tpu_custom_call" | custom-call | flops 3623878656 | bytes 5947392 | tf_op jit(solution)/shard_map/pallas_call | solution.py:223
  81.5 2.7 %collective-permute-start.26 = (bf16[28,32,128]{2,1,0:T(8,128)(2,1)S(1)}, bf16[28,32,128]{2,1,0:T(8,128)(2,1)S(1)}, u32[]{:S(2)}, u32[]{:S(2)}) collective-permute-start(bf16[28,32,128]{2,1,0:T(8,128)(2,1)S(1)} %get-tuple-element.83), channel_id=1, source_target_pairs={{0,64},{1,65},{2,66},{3,67},{4,68},{5,69},{6,70},{7,71},{8,72},{9,... | collective-permute-start | bytes 688136 | tf_op jit(solution)/shard_map/ppermute | solution.py:40
  84.2 1.3 collective-permute-start.27
  85.5 1.5 %collective-permute-start.28 = (bf16[28,32,128]{2,1,0:T(8,128)(2,1)S(1)}, bf16[28,32,128]{2,1,0:T(8,128)(2,1)S(1)}, u32[]{:S(2)}, u32[]{:S(2)}) collective-permute-start(bf16[28,32,128]{2,1,0:T(8,128)(2,1)S(1)} %get-tuple-element.85), channel_id=1, source_target_pairs={{0,192},{1,193},{2,194},{3,195},{4,196},{5,197},{6,198},{7,199},{8... | collective-permute-start | bytes 688136 | tf_op jit(solution)/shard_map/ppermute | solution.py:40
  87.0 1.4 %shard_map.80.refs_1_ = bf16[18,288,384]{2,1,0:T(8,128)(2,1)S(1)} custom-call(s32[2]{0:T(128)S(1)} %pad_add_fusion.where.refs_0_, bf16[2,256,128]{2,1,0:T(8,128)(2,1)S(1)} %fusion.6.refs_2_.refs_0_, bf16[2,256,128]{2,1,0:T(8,128)(2,1)S(1)} %collective-permute-done.15.refs_3_.refs_1_, bf16[2,256,128]{2,1,0:T(8,128)(2,1)S(1)} %collective-permute-done.16.refs_4_.refs_2_, ...), custom_call_target="tpu_custom_call" | custom-call | bytes 5029888 | tf_op jit(solution)/shard_map/pallas_call | solution.py:223
  88.4 1.9 %shard_map.81 = (bf16[2,256,128]{2,1,0:T(8,128)(2,1)S(1)}, bf16[2,256,128]{2,1,0:T(8,128)(2,1)S(1)}) custom-call(s32[2]{0:T(128)S(1)} %pad_add_fusion.where.refs_0_, bf16[18,288,384]{2,1,0:T(8,128)(2,1)S(1)} %shard_map.80.refs_1_, bf16[2,2304,256]{2,1,0:T(8,128)(2,1)S(1)} %get-tuple-element.64.refs_2_), custom_call_target="tpu_custom_call" | custom-call | flops 905969664 | bytes 6602752 | tf_op jit(solution)/shard_map/pallas_call | solution.py:223
  90.4 3.2 %collective-permute-start.23 = (bf16[2,256,128]{2,1,0:T(8,128)(2,1)S(1)}, bf16[2,256,128]{2,1,0:T(8,128)(2,1)S(1)}, u32[]{:S(2)}, u32[]{:S(2)}) collective-permute-start(bf16[2,256,128]{2,1,0:T(8,128)(2,1)S(1)} %get-tuple-element.74), channel_id=1, source_target_pairs={{0,7},{1,0},{2,1},{3,2},{4,3},{5,4},{6,5},{7,6},{8,15},{9,8},{10,9... | collective-permute-start | bytes 393224 | tf_op jit(solution)/shard_map/ppermute | solution.py:40
  93.7 3.1 %shard_map.82 = (f32[2,256,128]{2,1,0:T(8,128)S(1)}, bf16[2,256,128]{2,1,0:T(8,128)(2,1)S(1)}, f32[2,256,128]{2,1,0:T(8,128)S(1)}, bf16[2,256,128]{2,1,0:T(8,128)(2,1)S(1)}) custom-call(s32[2]{0:T(128)S(1)} %pad_add_fusion.where.refs_0_, bf16[18,288,384]{2,1,0:T(8,128)(2,1)S(1)} %shard_map.80.refs_1_, bf16[2,2304,256]{2,1,0:T(8,128)(2,1)S(1)} %get-tuple-element.64.refs_2_), custom_call_target="tpu_custom_call" | custom-call | flops 1811939328 | bytes 7127040 | tf_op jit(solution)/shard_map/pallas_call | solution.py:223
  97.1 3.2 %collective-permute-start.25 = (bf16[4,256,128]{2,1,0:T(8,128)(2,1)S(1)}, bf16[4,256,128]{2,1,0:T(8,128)(2,1)S(1)}, u32[]{:S(2)}, u32[]{:S(2)}) collective-permute-start(bf16[4,256,128]{2,1,0:T(8,128)(2,1)S(1)} %pad_maximum_fusion.1), channel_id=1, source_target_pairs={{0,7},{1,0},{2,1},{3,2},{4,3},{5,4},{6,5},{7,6},{8,15},{9,8},{10,9... | collective-permute-start | bytes 786440 | tf_op jit(solution)/shard_map/ppermute | solution.py:40
  100.3 1.9 %shard_map.83 = (f32[2,256,128]{2,1,0:T(8,128)S(1)}, f32[2,256,128]{2,1,0:T(8,128)S(1)}) custom-call(s32[2]{0:T(128)S(1)} %pad_add_fusion.where.refs_0_, bf16[18,288,384]{2,1,0:T(8,128)(2,1)S(1)} %shard_map.80.refs_1_, bf16[2,2304,256]{2,1,0:T(8,128)(2,1)S(1)} %get-tuple-element.64.refs_2_), custom_call_target="tpu_custom_call" | custom-call | flops 905969664 | bytes 6864896 | tf_op jit(solution)/shard_map/pallas_call | solution.py:223
  102.9 2.7 %collective-permute-done.24 = bf16[4,256,128]{2,1,0:T(8,128)(2,1)S(1)} collective-permute-done((bf16[4,256,128]{2,1,0:T(8,128)(2,1)S(1)}, bf16[4,256,128]{2,1,0:T(8,128)(2,1)S(1)}, u32[]{:S(2)}, u32[]{:S(2)}) %collective-permute-start.24) | collective-permute-done | bytes 262176 | tf_op jit(solution)/shard_map/ppermute | solution.py:40
  105.8 3.7 %collective-permute-start.30 = (bf16[2,256,128]{2,1,0:T(8,128)(2,1)S(1)}, bf16[2,256,128]{2,1,0:T(8,128)(2,1)S(1)}, u32[]{:S(2)}, u32[]{:S(2)}) collective-permute-start(bf16[2,256,128]{2,1,0:T(8,128)(2,1)S(1)} %get-tuple-element.87), channel_id=1, source_target_pairs={{0,0},{1,8},{2,16},{3,24},{4,32},{5,40},{6,48},{7,56},{8,36},{9,44... | collective-permute-start | bytes 393224 | tf_op jit(solution)/shard_map/ppermute | solution.py:40
  109.6 1.9 %collective-permute-start.31 = (bf16[2,256,128]{2,1,0:T(8,128)(2,1)S(1)}, bf16[2,256,128]{2,1,0:T(8,128)(2,1)S(1)}, u32[]{:S(2)}, u32[]{:S(2)}) collective-permute-start(bf16[2,256,128]{2,1,0:T(8,128)(2,1)S(1)} %get-tuple-element.88), channel_id=1, source_target_pairs={{0,32},{1,40},{2,48},{3,56},{4,0},{5,8},{6,16},{7,24},{8,4},{9,12}... | collective-permute-start | bytes 393224 | tf_op jit(solution)/shard_map/ppermute | solution.py:40
  111.5 2.0 %collective-permute-start.29 = (bf16[256,128]{1,0:T(8,128)(2,1)S(1)}, bf16[256,128]{1,0:T(8,128)(2,1)S(1)}, u32[]{:S(2)}, u32[]{:S(2)}) collective-permute-start(bf16[256,128]{1,0:T(8,128)(2,1)S(1)} %get-tuple-element.99), channel_id=1, source_target_pairs={{0,8},{1,9},{2,10},{3,11},{4,12},{5,13},{6,14},{7,15},{8,16},{9,17... | collective-permute-start | bytes 196616 | tf_op jit(solution)/shard_map/ppermute | solution.py:40
  113.6 7.0 %collective-permute-start.33 = (bf16[27,32,128]{2,1,0:T(8,128)(2,1)S(1)}, bf16[27,32,128]{2,1,0:T(8,128)(2,1)S(1)}, u32[]{:S(2)}, u32[]{:S(2)}) collective-permute-start(bf16[27,32,128]{2,1,0:T(8,128)(2,1)S(1)} %slice.145), channel_id=1, source_target_pairs={{0,0},{1,1},{2,2},{3,3},{4,4},{5,5},{6,6},{7,7},{8,128},{9,129},{1... | collective-permute-start | bytes 663560 | tf_op jit(solution)/shard_map/ppermute | solution.py:40
  120.6 10.2 %collective-permute-done.31 = bf16[2,256,128]{2,1,0:T(8,128)(2,1)S(1)} collective-permute-done((bf16[2,256,128]{2,1,0:T(8,128)(2,1)S(1)}, bf16[2,256,128]{2,1,0:T(8,128)(2,1)S(1)}, u32[]{:S(2)}, u32[]{:S(2)}) %collective-permute-start.31) | collective-permute-done | bytes 131104 | tf_op jit(solution)/shard_map/ppermute | solution.py:40
  131.0 0.7 pad_maximum_fusion.5
  131.7 3.0 %collective-permute-done.32 = bf16[256,128]{1,0:T(8,128)(2,1)S(1)} collective-permute-done((bf16[256,128]{1,0:T(8,128)(2,1)S(1)}, bf16[256,128]{1,0:T(8,128)(2,1)S(1)}, u32[]{:S(2)}, u32[]{:S(2)}) %collective-permute-start.32) | collective-permute-done | bytes 65568 | tf_op jit(solution)/shard_map/ppermute | solution.py:40
  134.7 0.7 pad_maximum_fusion.6
  135.3 0.8 convert_bitcast_fusion
  (61 shorter events, 3.1 us)
Async XLA Ops:
  1.6 2.6 %collective-permute-start = (bf16[2,16,16,128]{3,2,1,0:T(8,128)(2,1)S(1)}, bf16[2,16,16,128]{3,2,1,0:T(8,128)(2,1)S(1)}, u32[]{:S(2)}, u32[]{:S(2)}) collective-permute-start(bf16[2,16,16,128]{3,2,1,0:T(8,128)(2,1)S(1)} %pad_maximum_fusion.2), channel_id=1, source_target_pairs={{0,248},{1,249},{2,250},{3,251},{4,252},{5,253},{6,254},{7,255},{8... | collective-permute-start | bytes 393224 | tf_op jit(solution)/shard_map/ppermute | solution.py:40
  4.3 17.4 %collective-permute-start.1 = (bf16[2,256,128]{2,1,0:T(8,128)(2,1)S(1)}, bf16[2,256,128]{2,1,0:T(8,128)(2,1)S(1)}, u32[]{:S(2)}, u32[]{:S(2)}) collective-permute-start(bf16[2,256,128]{2,1,0:T(8,128)(2,1)S(1)} %bitcast.21), channel_id=1, source_target_pairs={{0,0},{1,17},{2,34},{3,51},{4,12},{5,29},{6,46},{7,63},{8,1},{9,18... | collective-permute-start | bytes 393224 | tf_op jit(solution)/shard_map/ppermute | solution.py:40
  17.8 8.7 %collective-permute-start.2 = (bf16[2,256,128]{2,1,0:T(8,128)(2,1)S(1)}, bf16[2,256,128]{2,1,0:T(8,128)(2,1)S(1)}, u32[]{:S(2)}, u32[]{:S(2)}) collective-permute-start(bf16[2,256,128]{2,1,0:T(8,128)(2,1)S(1)} %bitcast.22), channel_id=1, source_target_pairs={{0,4},{1,21},{2,38},{3,55},{4,8},{5,25},{6,42},{7,59},{8,5},{9,22}... | collective-permute-start | bytes 393224 | tf_op jit(solution)/shard_map/ppermute | solution.py:40
  19.7 13.6 %collective-permute-start.5 = (bf16[27,32,128]{2,1,0:T(8,128)(2,1)}, bf16[27,32,128]{2,1,0:T(8,128)(2,1)S(1)}, u32[]{:S(2)}, u32[]{:S(2)}) collective-permute-start(bf16[27,32,128]{2,1,0:T(8,128)(2,1)} %bitcast.25), channel_id=1, source_target_pairs={{0,0},{1,1},{2,2},{3,3},{4,4},{5,5},{6,6},{7,7},{8,128},{9,129},{1... | collective-permute-start | bytes 663560 | tf_op jit(solution)/shard_map/ppermute | solution.py:40
  26.5 12.0 %collective-permute-start.4 = (bf16[4,256,128]{2,1,0:T(8,128)(2,1)S(1)}, bf16[4,256,128]{2,1,0:T(8,128)(2,1)S(1)}, u32[]{:S(2)}, u32[]{:S(2)}) collective-permute-start(bf16[4,256,128]{2,1,0:T(8,128)(2,1)S(1)} %constant_dynamic-update-slice_fusion.refs_0_), channel_id=1, source_target_pairs={{0,1},{1,2},{2,3},{3,4},{4,5},{5,6},{6,7},{7,0},{8,9},{9,10},{10,1... | collective-permute-start | bytes 786440 | tf_op jit(solution)/shard_map/ppermute | solution.py:40
  26.5 11.9 %collective-permute-start.3 = (bf16[4,256,128]{2,1,0:T(8,128)(2,1)S(1)}, bf16[4,256,128]{2,1,0:T(8,128)(2,1)S(1)}, u32[]{:S(2)}, u32[]{:S(2)}) collective-permute-start(bf16[4,256,128]{2,1,0:T(8,128)(2,1)S(1)} %constant_dynamic-update-slice_fusion.refs_0_), channel_id=1, source_target_pairs={{0,7},{1,0},{2,1},{3,2},{4,3},{5,4},{6,5},{7,6},{8,15},{9,8},{10,9... | collective-permute-start | bytes 786440 | tf_op jit(solution)/shard_map/ppermute | solution.py:40
  33.3 12.9 %collective-permute-start.9 = (bf16[27,32,128]{2,1,0:T(8,128)(2,1)S(1)}, bf16[27,32,128]{2,1,0:T(8,128)(2,1)S(1)}, u32[]{:S(2)}, u32[]{:S(2)}) collective-permute-start(bf16[27,32,128]{2,1,0:T(8,128)(2,1)S(1)} %collective-permute-done.5.refs_0_), channel_id=1, source_target_pairs={{0,64},{1,65},{2,66},{3,67},{4,68},{5,69},{6,70},{7,71},{8,72},{9,... | collective-permute-start | bytes 663560 | tf_op jit(solution)/shard_map/ppermute | solution.py:40
  34.2 11.9 %collective-permute-start.8 = (bf16[27,32,128]{2,1,0:T(8,128)(2,1)S(1)}, bf16[27,32,128]{2,1,0:T(8,128)(2,1)S(1)}, u32[]{:S(2)}, u32[]{:S(2)}) collective-permute-start(bf16[27,32,128]{2,1,0:T(8,128)(2,1)S(1)} %collective-permute-done.5.refs_0_), channel_id=1, source_target_pairs={{0,192},{1,193},{2,194},{3,195},{4,196},{5,197},{6,198},{7,199},{8... | collective-permute-start | bytes 663560 | tf_op jit(solution)/shard_map/ppermute | solution.py:40
  36.5 9.6 %collective-permute-start.10 = (bf16[27,32,128]{2,1,0:T(8,128)(2,1)S(1)}, bf16[27,32,128]{2,1,0:T(8,128)(2,1)S(1)}, u32[]{:S(2)}, u32[]{:S(2)}) collective-permute-start(bf16[27,32,128]{2,1,0:T(8,128)(2,1)S(1)} %collective-permute-done.5.refs_0_), channel_id=1, source_target_pairs={{0,128},{1,129},{2,130},{3,131},{4,132},{5,133},{6,134},{7,135},{8... | collective-permute-start | bytes 663560 | tf_op jit(solution)/shard_map/ppermute | solution.py:40
  38.5 6.3 %collective-permute-start.7 = (bf16[2,256,128]{2,1,0:T(8,128)(2,1)S(1)}, bf16[2,256,128]{2,1,0:T(8,128)(2,1)S(1)}, u32[]{:S(2)}, u32[]{:S(2)}) collective-permute-start(bf16[2,256,128]{2,1,0:T(8,128)(2,1)S(1)} %slice.75), channel_id=1, source_target_pairs={{0,1},{1,2},{2,3},{3,4},{4,5},{5,6},{6,7},{7,0},{8,9},{9,10},{10,1... | collective-permute-start | bytes 393224 | tf_op jit(solution)/shard_map/ppermute | solution.py:40
  38.5 6.2 %collective-permute-start.6 = (bf16[2,256,128]{2,1,0:T(8,128)(2,1)S(1)}, bf16[2,256,128]{2,1,0:T(8,128)(2,1)S(1)}, u32[]{:S(2)}, u32[]{:S(2)}) collective-permute-start(bf16[2,256,128]{2,1,0:T(8,128)(2,1)S(1)} %slice.74), channel_id=1, source_target_pairs={{0,7},{1,0},{2,1},{3,2},{4,3},{5,4},{6,5},{7,6},{8,15},{9,8},{10,9... | collective-permute-start | bytes 393224 | tf_op jit(solution)/shard_map/ppermute | solution.py:40
  50.6 13.9 %copy-start = (f32[128]{0:T(128)S(1)}, f32[128]{0:T(128)}, u32[]{:S(2)}) copy-start(f32[128]{0:T(128)} %param.6) | copy-start | bytes 1540
  50.6 3.2 %collective-permute-start.11 = (bf16[8,256,128]{2,1,0:T(8,128)(2,1)S(1)}, bf16[8,256,128]{2,1,0:T(8,128)(2,1)S(1)}, u32[]{:S(2)}, u32[]{:S(2)}) collective-permute-start(bf16[8,256,128]{2,1,0:T(8,128)(2,1)S(1)} %shard_map.77), channel_id=1, source_target_pairs={{0,8},{1,9},{2,10},{3,11},{4,12},{5,13},{6,14},{7,15},{8,0},{9,1},... | collective-permute-start | bytes 1572872 | tf_op jit(solution)/shard_map/ppermute | solution.py:40
  54.0 8.1 %collective-permute-start.12 = (bf16[2,256,128]{2,1,0:T(8,128)(2,1)S(1)}, bf16[2,256,128]{2,1,0:T(8,128)(2,1)S(1)}, u32[]{:S(2)}, u32[]{:S(2)}) collective-permute-start(bf16[2,256,128]{2,1,0:T(8,128)(2,1)S(1)} %get-tuple-element.94), channel_id=1, source_target_pairs={{0,32},{1,33},{2,34},{3,35},{4,36},{5,37},{6,38},{7,39},{8,40},{9,... | collective-permute-start | bytes 393224 | tf_op jit(solution)/shard_map/ppermute | solution.py:40
  54.3 9.1 %collective-permute-start.14 = (bf16[2,256,128]{2,1,0:T(8,128)(2,1)S(1)}, bf16[2,256,128]{2,1,0:T(8,128)(2,1)S(1)}, u32[]{:S(2)}, u32[]{:S(2)}) collective-permute-start(bf16[2,256,128]{2,1,0:T(8,128)(2,1)S(1)} %get-tuple-element.95), channel_id=1, source_target_pairs={{0,48},{1,49},{2,50},{3,51},{4,52},{5,53},{6,54},{7,55},{8,56},{9,... | collective-permute-start | bytes 393224 | tf_op jit(solution)/shard_map/ppermute | solution.py:40
  55.4 9.1 %collective-permute-start.13 = (bf16[2,256,128]{2,1,0:T(8,128)(2,1)S(1)}, bf16[2,256,128]{2,1,0:T(8,128)(2,1)S(1)}, u32[]{:S(2)}, u32[]{:S(2)}) collective-permute-start(bf16[2,256,128]{2,1,0:T(8,128)(2,1)S(1)} %get-tuple-element.96), channel_id=1, source_target_pairs={{0,16},{1,17},{2,18},{3,19},{4,20},{5,21},{6,22},{7,23},{8,24},{9,... | collective-permute-start | bytes 393224 | tf_op jit(solution)/shard_map/ppermute | solution.py:40
  64.9 6.4 %collective-permute-start.17 = (bf16[2,256,128]{2,1,0:T(8,128)(2,1)S(1)}, bf16[2,256,128]{2,1,0:T(8,128)(2,1)S(1)}, u32[]{:S(2)}, u32[]{:S(2)}) collective-permute-start(bf16[2,256,128]{2,1,0:T(8,128)(2,1)S(1)} %fusion.6.refs_2_.refs_0_), channel_id=1, source_target_pairs={{0,48},{1,49},{2,50},{3,51},{4,52},{5,53},{6,54},{7,55},{8,56},{9,... | collective-permute-start | bytes 393224 | tf_op jit(solution)/shard_map/ppermute | solution.py:40
  65.5 7.9 %collective-permute-start.16 = (bf16[2,256,128]{2,1,0:T(8,128)(2,1)S(1)}, bf16[2,256,128]{2,1,0:T(8,128)(2,1)S(1)}, u32[]{:S(2)}, u32[]{:S(2)}) collective-permute-start(bf16[2,256,128]{2,1,0:T(8,128)(2,1)S(1)} %fusion.6.refs_2_.refs_0_), channel_id=1, source_target_pairs={{0,32},{1,33},{2,34},{3,35},{4,36},{5,37},{6,38},{7,39},{8,40},{9,... | collective-permute-start | bytes 393224 | tf_op jit(solution)/shard_map/ppermute | solution.py:40
  66.6 7.7 %collective-permute-start.15 = (bf16[2,256,128]{2,1,0:T(8,128)(2,1)S(1)}, bf16[2,256,128]{2,1,0:T(8,128)(2,1)S(1)}, u32[]{:S(2)}, u32[]{:S(2)}) collective-permute-start(bf16[2,256,128]{2,1,0:T(8,128)(2,1)S(1)} %fusion.6.refs_2_.refs_0_), channel_id=1, source_target_pairs={{0,16},{1,17},{2,18},{3,19},{4,20},{5,21},{6,22},{7,23},{8,24},{9,... | collective-permute-start | bytes 393224 | tf_op jit(solution)/shard_map/ppermute | solution.py:40
  68.3 6.1 %collective-permute-start.18 = (bf16[2,256,128]{2,1,0:T(8,128)(2,1)S(1)}, bf16[2,256,128]{2,1,0:T(8,128)(2,1)S(1)}, u32[]{:S(2)}, u32[]{:S(2)}) collective-permute-start(bf16[2,256,128]{2,1,0:T(8,128)(2,1)S(1)} %fusion.6.refs_2_.refs_0_), channel_id=1, source_target_pairs={{0,8},{1,9},{2,10},{3,11},{4,12},{5,13},{6,14},{7,15},{8,0},{9,1},... | collective-permute-start | bytes 393224 | tf_op jit(solution)/shard_map/ppermute | solution.py:40
  71.3 3.1 %collective-permute-start.21 = (bf16[2,256,128]{2,1,0:T(8,128)(2,1)S(1)}, bf16[2,256,128]{2,1,0:T(8,128)(2,1)S(1)}, u32[]{:S(2)}, u32[]{:S(2)}) collective-permute-start(bf16[2,256,128]{2,1,0:T(8,128)(2,1)S(1)} %collective-permute-done.17.refs_5_.refs_3_), channel_id=1, source_target_pairs={{0,8},{1,9},{2,10},{3,11},{4,12},{5,13},{6,14},{7,15},{8,0},{9,1},... | collective-permute-start | bytes 393224 | tf_op jit(solution)/shard_map/ppermute | solution.py:40
  73.4 1.3 collective-permute-start.20
  74.4 1.3 collective-permute-start.19
  81.5 20.7 %collective-permute-start.26 = (bf16[28,32,128]{2,1,0:T(8,128)(2,1)S(1)}, bf16[28,32,128]{2,1,0:T(8,128)(2,1)S(1)}, u32[]{:S(2)}, u32[]{:S(2)}) collective-permute-start(bf16[28,32,128]{2,1,0:T(8,128)(2,1)S(1)} %get-tuple-element.83), channel_id=1, source_target_pairs={{0,64},{1,65},{2,66},{3,67},{4,68},{5,69},{6,70},{7,71},{8,72},{9,... | collective-permute-start | bytes 688136 | tf_op jit(solution)/shard_map/ppermute | solution.py:40
  84.2 18.0 %collective-permute-start.27 = (bf16[28,32,128]{2,1,0:T(8,128)(2,1)S(1)}, bf16[28,32,128]{2,1,0:T(8,128)(2,1)S(1)}, u32[]{:S(2)}, u32[]{:S(2)}) collective-permute-start(bf16[28,32,128]{2,1,0:T(8,128)(2,1)S(1)} %get-tuple-element.84), channel_id=1, source_target_pairs={{0,128},{1,129},{2,130},{3,131},{4,132},{5,133},{6,134},{7,135},{8... | collective-permute-start | bytes 688136 | tf_op jit(solution)/shard_map/ppermute | solution.py:40
  85.5 16.8 %collective-permute-start.28 = (bf16[28,32,128]{2,1,0:T(8,128)(2,1)S(1)}, bf16[28,32,128]{2,1,0:T(8,128)(2,1)S(1)}, u32[]{:S(2)}, u32[]{:S(2)}) collective-permute-start(bf16[28,32,128]{2,1,0:T(8,128)(2,1)S(1)} %get-tuple-element.85), channel_id=1, source_target_pairs={{0,192},{1,193},{2,194},{3,195},{4,196},{5,197},{6,198},{7,199},{8... | collective-permute-start | bytes 688136 | tf_op jit(solution)/shard_map/ppermute | solution.py:40
  90.3 6.5 %collective-permute-start.22 = (bf16[2,256,128]{2,1,0:T(8,128)(2,1)S(1)}, bf16[2,256,128]{2,1,0:T(8,128)(2,1)S(1)}, u32[]{:S(2)}, u32[]{:S(2)}) collective-permute-start(bf16[2,256,128]{2,1,0:T(8,128)(2,1)S(1)} %get-tuple-element.71), channel_id=1, source_target_pairs={{0,1},{1,2},{2,3},{3,4},{4,5},{5,6},{6,7},{7,0},{8,9},{9,10},{10,1... | collective-permute-start | bytes 393224 | tf_op jit(solution)/shard_map/ppermute | solution.py:40
  90.4 6.4 %collective-permute-start.23 = (bf16[2,256,128]{2,1,0:T(8,128)(2,1)S(1)}, bf16[2,256,128]{2,1,0:T(8,128)(2,1)S(1)}, u32[]{:S(2)}, u32[]{:S(2)}) collective-permute-start(bf16[2,256,128]{2,1,0:T(8,128)(2,1)S(1)} %get-tuple-element.74), channel_id=1, source_target_pairs={{0,7},{1,0},{2,1},{3,2},{4,3},{5,4},{6,5},{7,6},{8,15},{9,8},{10,9... | collective-permute-start | bytes 393224 | tf_op jit(solution)/shard_map/ppermute | solution.py:40
  97.0 8.7 %collective-permute-start.24 = (bf16[4,256,128]{2,1,0:T(8,128)(2,1)S(1)}, bf16[4,256,128]{2,1,0:T(8,128)(2,1)S(1)}, u32[]{:S(2)}, u32[]{:S(2)}) collective-permute-start(bf16[4,256,128]{2,1,0:T(8,128)(2,1)S(1)} %pad_maximum_fusion), channel_id=1, source_target_pairs={{0,1},{1,2},{2,3},{3,4},{4,5},{5,6},{6,7},{7,0},{8,9},{9,10},{10,1... | collective-permute-start | bytes 786440 | tf_op jit(solution)/shard_map/ppermute | solution.py:40
  97.1 8.6 %collective-permute-start.25 = (bf16[4,256,128]{2,1,0:T(8,128)(2,1)S(1)}, bf16[4,256,128]{2,1,0:T(8,128)(2,1)S(1)}, u32[]{:S(2)}, u32[]{:S(2)}) collective-permute-start(bf16[4,256,128]{2,1,0:T(8,128)(2,1)S(1)} %pad_maximum_fusion.1), channel_id=1, source_target_pairs={{0,7},{1,0},{2,1},{3,2},{4,3},{5,4},{6,5},{7,6},{8,15},{9,8},{10,9... | collective-permute-start | bytes 786440 | tf_op jit(solution)/shard_map/ppermute | solution.py:40
  105.8 14.7 %collective-permute-start.30 = (bf16[2,256,128]{2,1,0:T(8,128)(2,1)S(1)}, bf16[2,256,128]{2,1,0:T(8,128)(2,1)S(1)}, u32[]{:S(2)}, u32[]{:S(2)}) collective-permute-start(bf16[2,256,128]{2,1,0:T(8,128)(2,1)S(1)} %get-tuple-element.87), channel_id=1, source_target_pairs={{0,0},{1,8},{2,16},{3,24},{4,32},{5,40},{6,48},{7,56},{8,36},{9,44... | collective-permute-start | bytes 393224 | tf_op jit(solution)/shard_map/ppermute | solution.py:40
  109.6 21.3 %collective-permute-start.31 = (bf16[2,256,128]{2,1,0:T(8,128)(2,1)S(1)}, bf16[2,256,128]{2,1,0:T(8,128)(2,1)S(1)}, u32[]{:S(2)}, u32[]{:S(2)}) collective-permute-start(bf16[2,256,128]{2,1,0:T(8,128)(2,1)S(1)} %get-tuple-element.88), channel_id=1, source_target_pairs={{0,32},{1,40},{2,48},{3,56},{4,0},{5,8},{6,16},{7,24},{8,4},{9,12}... | collective-permute-start | bytes 393224 | tf_op jit(solution)/shard_map/ppermute | solution.py:40
  111.5 19.5 %collective-permute-start.29 = (bf16[256,128]{1,0:T(8,128)(2,1)S(1)}, bf16[256,128]{1,0:T(8,128)(2,1)S(1)}, u32[]{:S(2)}, u32[]{:S(2)}) collective-permute-start(bf16[256,128]{1,0:T(8,128)(2,1)S(1)} %get-tuple-element.99), channel_id=1, source_target_pairs={{0,8},{1,9},{2,10},{3,11},{4,12},{5,13},{6,14},{7,15},{8,16},{9,17... | collective-permute-start | bytes 196616 | tf_op jit(solution)/shard_map/ppermute | solution.py:40
  113.6 21.8 %collective-permute-start.33 = (bf16[27,32,128]{2,1,0:T(8,128)(2,1)S(1)}, bf16[27,32,128]{2,1,0:T(8,128)(2,1)S(1)}, u32[]{:S(2)}, u32[]{:S(2)}) collective-permute-start(bf16[27,32,128]{2,1,0:T(8,128)(2,1)S(1)} %slice.145), channel_id=1, source_target_pairs={{0,0},{1,1},{2,2},{3,3},{4,4},{5,5},{6,6},{7,7},{8,128},{9,129},{1... | collective-permute-start | bytes 663560 | tf_op jit(solution)/shard_map/ppermute | solution.py:40
  130.9 3.8 %collective-permute-start.32 = (bf16[256,128]{1,0:T(8,128)(2,1)S(1)}, bf16[256,128]{1,0:T(8,128)(2,1)S(1)}, u32[]{:S(2)}, u32[]{:S(2)}) collective-permute-start(bf16[256,128]{1,0:T(8,128)(2,1)S(1)} %get-tuple-element.97), channel_id=1, source_target_pairs={{0,8},{1,9},{2,10},{3,11},{4,12},{5,13},{6,14},{7,15},{8,16},{9,17... | collective-permute-start | bytes 196616 | tf_op jit(solution)/shard_map/ppermute | solution.py:40

commit v5 on v4

--- a/solution.py
+++ b/solution.py
@@ -328,12 +328,6 @@
         flops,
     )
     where, terms = lax.optimization_barrier((where, terms))
-    held = terms[0].astype(f32)
-    for r in range(1, NX):
-        held = held + permuted(terms[r], lambda x, q, z: at(x + r, q, z)).astype(f32)
-    grad_bias = held[27, 0] + held[27, 1]
-    held = held[:27].astype(bf16)
-
     def parts(steps, where, kinds):
         return call(
             lambda *refs: product_kernel(lambda where: ring_pairs(where, steps), *refs),
@@ -353,11 +347,15 @@
     below = jnp.concatenate([(below + down).astype(bf16), far_below])
     above, below, where = lax.optimization_barrier((above, below, where))
     near, beyond = parts((0, 4), where, [f32, f32])
+    near, beyond, terms = lax.optimization_barrier((near, beyond, terms))
+    received = [
+        permuted(terms[r], lambda x, q, z: at(x + r, q, z)) for r in range(1, NX)
+    ]
     above, below = along_z(above, 1).astype(f32), along_z(below, -1).astype(f32)
     near = (near + above[:2] + below[:2]).astype(bf16)
     beyond = (beyond + above[2:] + below[2:]).astype(bf16)
 
-    near, beyond, held, activated = lax.optimization_barrier((near, beyond, held, activated))
+    near, beyond, activated = lax.optimization_barrier((near, beyond, activated))
 
     def next_slab(plane):
         return permuted(plane, lambda x, q, z: device(NQ * x + q + 1, z))
@@ -367,12 +365,16 @@
 
     near, beyond = permuted(near, home(0)).astype(f32), permuted(beyond, home(4)).astype(f32)
     summed = (near + beyond).astype(bf16)
+    shifted, received = lax.optimization_barrier((next_slab(activated[1]), received))
+    held = sum((piece.astype(f32) for piece in received), terms[0].astype(f32))
+    grad_bias = held[27, 0] + held[27, 1]
     grad_filters = permuted(
-        held, lambda x, q, z: device(NX * group(q) + swapped(x), z)
+        held[:27].astype(bf16), lambda x, q, z: device(NX * group(q) + swapped(x), z)
     ).astype(f32)
 
-    activated = jnp.stack([next_slab(activated[1]), activated[0]])
-    grad_input = jnp.stack([next_slab(summed[1]), summed[0]])
+    activated = jnp.stack([shifted, activated[0]])
+    second, grad_filters = lax.optimization_barrier((next_slab(summed[1]), grad_filters))
+    grad_input = jnp.stack([second, summed[0]])
     shape = (2, GRID, GRID)
     return (
         activated.reshape(*shape, out_size),

time: 137 us -> 133 us (0.971)
  starting transfers between devices: 65.9 us -> 60.8 us
    ppermute x34, starting transfers between devices: 65.9 us -> 60.8 us  [permuted(): return lax.ppermute(array, ('space', 'chan'), pairs)]
  transfers between devices with their start and end apart: 34 -> 34, of which waited for: 14 -> 17; matrix products, arithmetic and copies ran while one was open for 2% -> 2% of each run, Pallas kernels for 10% -> 7%
where the time goes in v5:
time: 133 us; the launch traced here: 132 us
  starting transfers between devices  60.8 us (46%)
  waiting for transfers between devices  42 us (32%)
  Pallas kernels  23.1 us (17%)
  other arithmetic  3.75 us (3%)
    ppermute x34, starting transfers between devices, permuted(): return lax.ppermute(array, ('space', 'chan'), pairs)  60.8 us
    ppermute x34, waiting for transfers between devices, permuted(): return lax.ppermute(array, ('space', 'chan'), pairs)  42 us
    pallas_call x9, Pallas kernels, call(): pl.pallas_call(kernel, out_shape=outs, in_specs=[pl.BlockSpec(memory_spac...  23.1 us
  transfers between devices with their start and end apart: 34, of which 17 were waited for; matrix products, arithmetic and copies ran while one was open for 2% of the time, Pallas kernels for 7%

profile of v5, /device:TPU:16, one launch (start us, length us, event | category | flops | bytes accessed | tf_op | source)
XLA Modules:
  0.0 131.8 jit_solution(12239662229167643827)
XLA Ops:
  0.6 1.0 fusion.18
  1.7 2.5 %collective-permute-done = bf16[2,16,16,128]{3,2,1,0:T(8,128)(2,1)S(1)} collective-permute-done((bf16[2,16,16,128]{3,2,1,0:T(8,128)(2,1)S(1)}, bf16[2,16,16,128]{3,2,1,0:T(8,128)(2,1)S(1)}, u32[]{:S(2)}, u32[]{:S(2)}) %collective-permute-start) | collective-permute-done | bytes 131104 | tf_op jit(solution)/shard_map/ppermute | solution.py:40
  4.3 13.5 %collective-permute-start.1 = (bf16[2,256,128]{2,1,0:T(8,128)(2,1)S(1)}, bf16[2,256,128]{2,1,0:T(8,128)(2,1)S(1)}, u32[]{:S(2)}, u32[]{:S(2)}) collective-permute-start(bf16[2,256,128]{2,1,0:T(8,128)(2,1)S(1)} %bitcast.21), channel_id=1, source_target_pairs={{0,0},{1,17},{2,34},{3,51},{4,12},{5,29},{6,46},{7,63},{8,1},{9,18... | collective-permute-start | bytes 393224 | tf_op jit(solution)/shard_map/ppermute | solution.py:40
  17.8 1.9 %collective-permute-start.2 = (bf16[2,256,128]{2,1,0:T(8,128)(2,1)S(1)}, bf16[2,256,128]{2,1,0:T(8,128)(2,1)S(1)}, u32[]{:S(2)}, u32[]{:S(2)}) collective-permute-start(bf16[2,256,128]{2,1,0:T(8,128)(2,1)S(1)} %bitcast.22), channel_id=1, source_target_pairs={{0,4},{1,21},{2,38},{3,55},{4,8},{5,25},{6,42},{7,59},{8,5},{9,22}... | collective-permute-start | bytes 393224 | tf_op jit(solution)/shard_map/ppermute | solution.py:40
  19.7 1.9 %collective-permute-start.5 = (bf16[27,32,128]{2,1,0:T(8,128)(2,1)}, bf16[27,32,128]{2,1,0:T(8,128)(2,1)S(1)}, u32[]{:S(2)}, u32[]{:S(2)}) collective-permute-start(bf16[27,32,128]{2,1,0:T(8,128)(2,1)} %bitcast.25), channel_id=1, source_target_pairs={{0,0},{1,1},{2,2},{3,3},{4,4},{5,5},{6,6},{7,7},{8,128},{9,129},{1... | collective-permute-start | bytes 663560 | tf_op jit(solution)/shard_map/ppermute | solution.py:40
  21.7 4.8 %collective-permute-done.2 = bf16[2,256,128]{2,1,0:T(8,128)(2,1)S(1)} collective-permute-done((bf16[2,256,128]{2,1,0:T(8,128)(2,1)S(1)}, bf16[2,256,128]{2,1,0:T(8,128)(2,1)S(1)}, u32[]{:S(2)}, u32[]{:S(2)}) %collective-permute-start.2) | collective-permute-done | bytes 131104 | tf_op jit(solution)/shard_map/ppermute | solution.py:40
  26.5 6.7 %collective-permute-start.3 = (bf16[4,256,128]{2,1,0:T(8,128)(2,1)S(1)}, bf16[4,256,128]{2,1,0:T(8,128)(2,1)S(1)}, u32[]{:S(2)}, u32[]{:S(2)}) collective-permute-start(bf16[4,256,128]{2,1,0:T(8,128)(2,1)S(1)} %constant_dynamic-update-slice_fusion.refs_0_), channel_id=1, source_target_pairs={{0,7},{1,0},{2,1},{3,2},{4,3},{5,4},{6,5},{7,6},{8,15},{9,8},{10,9... | collective-permute-start | bytes 786440 | tf_op jit(solution)/shard_map/ppermute | solution.py:40
  33.3 0.9 collective-permute-start.9
  34.2 2.3 %collective-permute-start.8 = (bf16[27,32,128]{2,1,0:T(8,128)(2,1)S(1)}, bf16[27,32,128]{2,1,0:T(8,128)(2,1)S(1)}, u32[]{:S(2)}, u32[]{:S(2)}) collective-permute-start(bf16[27,32,128]{2,1,0:T(8,128)(2,1)S(1)} %collective-permute-done.5.refs_0_), channel_id=1, source_target_pairs={{0,192},{1,193},{2,194},{3,195},{4,196},{5,197},{6,198},{7,199},{8... | collective-permute-start | bytes 663560 | tf_op jit(solution)/shard_map/ppermute | solution.py:40
  36.5 1.9 %collective-permute-start.10 = (bf16[27,32,128]{2,1,0:T(8,128)(2,1)S(1)}, bf16[27,32,128]{2,1,0:T(8,128)(2,1)S(1)}, u32[]{:S(2)}, u32[]{:S(2)}) collective-permute-start(bf16[27,32,128]{2,1,0:T(8,128)(2,1)S(1)} %collective-permute-done.5.refs_0_), channel_id=1, source_target_pairs={{0,128},{1,129},{2,130},{3,131},{4,132},{5,133},{6,134},{7,135},{8... | collective-permute-start | bytes 663560 | tf_op jit(solution)/shard_map/ppermute | solution.py:40
  38.5 3.2 %collective-permute-start.6 = (bf16[2,256,128]{2,1,0:T(8,128)(2,1)S(1)}, bf16[2,256,128]{2,1,0:T(8,128)(2,1)S(1)}, u32[]{:S(2)}, u32[]{:S(2)}) collective-permute-start(bf16[2,256,128]{2,1,0:T(8,128)(2,1)S(1)} %slice.74), channel_id=1, source_target_pairs={{0,7},{1,0},{2,1},{3,2},{4,3},{5,4},{6,5},{7,6},{8,15},{9,8},{10,9... | collective-permute-start | bytes 393224 | tf_op jit(solution)/shard_map/ppermute | solution.py:40
  41.8 2.9 %collective-permute-done.7.refs_4_ = bf16[2,256,128]{2,1,0:T(8,128)(2,1)S(1)} collective-permute-done((bf16[2,256,128]{2,1,0:T(8,128)(2,1)S(1)}, bf16[2,256,128]{2,1,0:T(8,128)(2,1)S(1)}, u32[]{:S(2)}, u32[]{:S(2)}) %collective-permute-start.7) | collective-permute-done | bytes 131104 | tf_op jit(solution)/shard_map/ppermute | solution.py:40
  44.7 1.4 %shard_map.75.refs_1_ = bf16[18,288,384]{2,1,0:T(8,128)(2,1)S(1)} custom-call(s32[2]{0:T(128)S(1)} %pad_add_fusion.where.refs_0_, bf16[4,256,128]{2,1,0:T(8,128)(2,1)S(1)} %constant_dynamic-update-slice_fusion.refs_0_, bf16[4,256,128]{2,1,0:T(8,128)(2,1)S(1)} %collective-permute-done.3.refs_1_, bf16[4,256,128]{2,1,0:T(8,128)(2,1)S(1)} %collective-permute-done.4.refs_2_, ...), custom_call_target="tpu_custom_call" | custom-call | bytes 5029888 | tf_op jit(solution)/shard_map/pallas_call | solution.py:223
  46.2 1.2 shard_map.76
  47.4 3.1 %shard_map.77 = bf16[8,256,128]{2,1,0:T(8,128)(2,1)S(1)} custom-call(s32[2]{0:T(128)S(1)} %pad_add_fusion.where.refs_0_, bf16[18,288,384]{2,1,0:T(8,128)(2,1)S(1)} %shard_map.75.refs_1_, bf16[2,2304,256]{2,1,0:T(8,128)(2,1)S(1)} %get-tuple-element.63.refs_2_), custom_call_target="tpu_custom_call" | custom-call | flops 1811939328 | bytes 6864896 | tf_op jit(solution)/shard_map/pallas_call | solution.py:223
  50.7 3.1 %shard_map.78 = (f32[2,256,128]{2,1,0:T(8,128)S(1)}, f32[2,256,128]{2,1,0:T(8,128)S(1)}, f32[2,256,128]{2,1,0:T(8,128)S(1)}, f32[2,256,128]{2,1,0:T(8,128)S(1)}) custom-call(s32[2]{0:T(128)S(1)} %pad_add_fusion.where.refs_0_, bf16[18,288,384]{2,1,0:T(8,128)(2,1)S(1)} %shard_map.75.refs_1_, bf16[2,2304,256]{2,1,0:T(8,128)(2,1)S(1)} %get-tuple-element.63.refs_2_), custom_call_target="tpu_custom_call" | custom-call | flops 1811939328 | bytes 7389184 | tf_op jit(solution)/shard_map/pallas_call | solution.py:223
  54.3 1.1 collective-permute-start.14
  55.4 1.4 %collective-permute-start.13 = (bf16[2,256,128]{2,1,0:T(8,128)(2,1)S(1)}, bf16[2,256,128]{2,1,0:T(8,128)(2,1)S(1)}, u32[]{:S(2)}, u32[]{:S(2)}) collective-permute-start(bf16[2,256,128]{2,1,0:T(8,128)(2,1)S(1)} %get-tuple-element.118), channel_id=1, source_target_pairs={{0,16},{1,17},{2,18},{3,19},{4,20},{5,21},{6,22},{7,23},{8,24},{9,... | collective-permute-start | bytes 393224 | tf_op jit(solution)/shard_map/ppermute | solution.py:40
  56.8 5.3 %collective-permute-done.12 = bf16[2,256,128]{2,1,0:T(8,128)(2,1)S(1)} collective-permute-done((bf16[2,256,128]{2,1,0:T(8,128)(2,1)S(1)}, bf16[2,256,128]{2,1,0:T(8,128)(2,1)S(1)}, u32[]{:S(2)}, u32[]{:S(2)}) %collective-permute-start.12) | collective-permute-done | bytes 131104 | tf_op jit(solution)/shard_map/ppermute | solution.py:40
  62.1 1.2 collective-permute-done.14
  63.4 1.1 collective-permute-done.13
  64.9 0.7 collective-permute-start.17
  65.5 1.1 collective-permute-start.16
  66.6 1.7 %collective-permute-start.15 = (bf16[2,256,128]{2,1,0:T(8,128)(2,1)S(1)}, bf16[2,256,128]{2,1,0:T(8,128)(2,1)S(1)}, u32[]{:S(2)}, u32[]{:S(2)}) collective-permute-start(bf16[2,256,128]{2,1,0:T(8,128)(2,1)S(1)} %fusion.6.refs_2_.refs_0_), channel_id=1, source_target_pairs={{0,16},{1,17},{2,18},{3,19},{4,20},{5,21},{6,22},{7,23},{8,24},{9,... | collective-permute-start | bytes 393224 | tf_op jit(solution)/shard_map/ppermute | solution.py:40
  68.3 3.0 %collective-permute-done.17.refs_5_.refs_3_ = bf16[2,256,128]{2,1,0:T(8,128)(2,1)S(1)} collective-permute-done((bf16[2,256,128]{2,1,0:T(8,128)(2,1)S(1)}, bf16[2,256,128]{2,1,0:T(8,128)(2,1)S(1)}, u32[]{:S(2)}, u32[]{:S(2)}) %collective-permute-start.17) | collective-permute-done | bytes 131104 | tf_op jit(solution)/shard_map/ppermute | solution.py:40
  71.3 2.1 %collective-permute-done.16.refs_4_.refs_2_ = bf16[2,256,128]{2,1,0:T(8,128)(2,1)S(1)} collective-permute-done((bf16[2,256,128]{2,1,0:T(8,128)(2,1)S(1)}, bf16[2,256,128]{2,1,0:T(8,128)(2,1)S(1)}, u32[]{:S(2)}, u32[]{:S(2)}) %collective-permute-start.16) | collective-permute-done | bytes 131104 | tf_op jit(solution)/shard_map/ppermute | solution.py:40
  73.4 0.9 collective-permute-done.15.refs_3_.refs_1_
  74.8 0.9 collective-permute-done.19.refs_7_.refs_5_
  75.7 5.8 %shard_map.79 = (bf16[28,32,128]{2,1,0:T(8,128)(2,1)S(1)}, bf16[28,32,128]{2,1,0:T(8,128)(2,1)S(1)}, bf16[28,32,128]{2,1,0:T(8,128)(2,1)S(1)}, bf16[28,32,128]{2,1,0:T(8,128)(2,1)S(1)}) custom-call(s32[2]{0:T(128)S(1)} %pad_add_fusion.where.refs_0_, bf16[18,288,384]{2,1,0:T(8,128)(2,1)S(1)} %shard_map.75.refs_1_, ...), custom_call_target="tpu_custom_call" | custom-call | flops 3623878656 | bytes 5947392 | tf_op jit(solution)/shard_map/pallas_call | solution.py:223
  81.5 1.4 %shard_map.80.refs_1_ = bf16[18,288,384]{2,1,0:T(8,128)(2,1)S(1)} custom-call(s32[2]{0:T(128)S(1)} %pad_add_fusion.where.refs_0_, bf16[2,256,128]{2,1,0:T(8,128)(2,1)S(1)} %fusion.6.refs_2_.refs_0_, bf16[2,256,128]{2,1,0:T(8,128)(2,1)S(1)} %collective-permute-done.15.refs_3_.refs_1_, bf16[2,256,128]{2,1,0:T(8,128)(2,1)S(1)} %collective-permute-done.16.refs_4_.refs_2_, ...), custom_call_target="tpu_custom_call" | custom-call | bytes 5029888 | tf_op jit(solution)/shard_map/pallas_call | solution.py:223
  82.9 1.9 %shard_map.81 = (bf16[2,256,128]{2,1,0:T(8,128)(2,1)S(1)}, bf16[2,256,128]{2,1,0:T(8,128)(2,1)S(1)}) custom-call(s32[2]{0:T(128)S(1)} %pad_add_fusion.where.refs_0_, bf16[18,288,384]{2,1,0:T(8,128)(2,1)S(1)} %shard_map.80.refs_1_, bf16[2,2304,256]{2,1,0:T(8,128)(2,1)S(1)} %get-tuple-element.75.refs_2_), custom_call_target="tpu_custom_call" | custom-call | flops 905969664 | bytes 6602752 | tf_op jit(solution)/shard_map/pallas_call | solution.py:223
  85.4 3.2 %collective-permute-start.23 = (bf16[2,256,128]{2,1,0:T(8,128)(2,1)S(1)}, bf16[2,256,128]{2,1,0:T(8,128)(2,1)S(1)}, u32[]{:S(2)}, u32[]{:S(2)}) collective-permute-start(bf16[2,256,128]{2,1,0:T(8,128)(2,1)S(1)} %get-tuple-element.85), channel_id=1, source_target_pairs={{0,7},{1,0},{2,1},{3,2},{4,3},{5,4},{6,5},{7,6},{8,15},{9,8},{10,9... | collective-permute-start | bytes 393224 | tf_op jit(solution)/shard_map/ppermute | solution.py:40
  88.6 3.1 %shard_map.82 = (f32[2,256,128]{2,1,0:T(8,128)S(1)}, bf16[2,256,128]{2,1,0:T(8,128)(2,1)S(1)}, f32[2,256,128]{2,1,0:T(8,128)S(1)}, bf16[2,256,128]{2,1,0:T(8,128)(2,1)S(1)}) custom-call(s32[2]{0:T(128)S(1)} %pad_add_fusion.where.refs_0_, bf16[18,288,384]{2,1,0:T(8,128)(2,1)S(1)} %shard_map.80.refs_1_, bf16[2,2304,256]{2,1,0:T(8,128)(2,1)S(1)} %get-tuple-element.75.refs_2_), custom_call_target="tpu_custom_call" | custom-call | flops 1811939328 | bytes 7127040 | tf_op jit(solution)/shard_map/pallas_call | solution.py:223
  92.4 3.2 %collective-permute-start.25 = (bf16[4,256,128]{2,1,0:T(8,128)(2,1)S(1)}, bf16[4,256,128]{2,1,0:T(8,128)(2,1)S(1)}, u32[]{:S(2)}, u32[]{:S(2)}) collective-permute-start(bf16[4,256,128]{2,1,0:T(8,128)(2,1)S(1)} %pad_maximum_fusion.1), channel_id=1, source_target_pairs={{0,7},{1,0},{2,1},{3,2},{4,3},{5,4},{6,5},{7,6},{8,15},{9,8},{10,9... | collective-permute-start | bytes 786440 | tf_op jit(solution)/shard_map/ppermute | solution.py:40
  95.6 1.9 %shard_map.83 = (f32[2,256,128]{2,1,0:T(8,128)S(1)}, f32[2,256,128]{2,1,0:T(8,128)S(1)}) custom-call(s32[2]{0:T(128)S(1)} %pad_add_fusion.where.refs_0_, bf16[18,288,384]{2,1,0:T(8,128)(2,1)S(1)} %shard_map.80.refs_1_, bf16[2,2304,256]{2,1,0:T(8,128)(2,1)S(1)} %get-tuple-element.75.refs_2_), custom_call_target="tpu_custom_call" | custom-call | flops 905969664 | bytes 6864896 | tf_op jit(solution)/shard_map/pallas_call | solution.py:223
  97.5 2.4 %collective-permute-start.27 = (bf16[28,32,128]{2,1,0:T(8,128)(2,1)S(1)}, bf16[28,32,128]{2,1,0:T(8,128)(2,1)S(1)}, u32[]{:S(2)}, u32[]{:S(2)}) collective-permute-start(bf16[28,32,128]{2,1,0:T(8,128)(2,1)S(1)} %get-tuple-element.100), channel_id=1, source_target_pairs={{0,64},{1,65},{2,66},{3,67},{4,68},{5,69},{6,70},{7,71},{8,72},{9,... | collective-permute-start | bytes 688136 | tf_op jit(solution)/shard_map/ppermute | solution.py:40
  99.9 1.5 %collective-permute-start.28 = (bf16[28,32,128]{2,1,0:T(8,128)(2,1)S(1)}, bf16[28,32,128]{2,1,0:T(8,128)(2,1)S(1)}, u32[]{:S(2)}, u32[]{:S(2)}) collective-permute-start(bf16[28,32,128]{2,1,0:T(8,128)(2,1)S(1)} %get-tuple-element.101), channel_id=1, source_target_pairs={{0,128},{1,129},{2,130},{3,131},{4,132},{5,133},{6,134},{7,135},{8... | collective-permute-start | bytes 688136 | tf_op jit(solution)/shard_map/ppermute | solution.py:40
  101.4 1.3 collective-permute-start.29
  103.0 2.6 %collective-permute-start.30 = (bf16[2,256,128]{2,1,0:T(8,128)(2,1)S(1)}, bf16[2,256,128]{2,1,0:T(8,128)(2,1)S(1)}, u32[]{:S(2)}, u32[]{:S(2)}) collective-permute-start(bf16[2,256,128]{2,1,0:T(8,128)(2,1)S(1)} %get-tuple-element.104), channel_id=1, source_target_pairs={{0,0},{1,8},{2,16},{3,24},{4,32},{5,40},{6,48},{7,56},{8,36},{9,44... | collective-permute-start | bytes 393224 | tf_op jit(solution)/shard_map/ppermute | solution.py:40
  105.6 1.2 collective-permute-done.27
  106.7 2.0 %collective-permute-start.31 = (bf16[2,256,128]{2,1,0:T(8,128)(2,1)S(1)}, bf16[2,256,128]{2,1,0:T(8,128)(2,1)S(1)}, u32[]{:S(2)}, u32[]{:S(2)}) collective-permute-start(bf16[2,256,128]{2,1,0:T(8,128)(2,1)S(1)} %get-tuple-element.105), channel_id=1, source_target_pairs={{0,32},{1,40},{2,48},{3,56},{4,0},{5,8},{6,16},{7,24},{8,4},{9,12}... | collective-permute-start | bytes 393224 | tf_op jit(solution)/shard_map/ppermute | solution.py:40
  108.8 2.1 %collective-permute-done.28 = bf16[28,32,128]{2,1,0:T(8,128)(2,1)S(1)} collective-permute-done((bf16[28,32,128]{2,1,0:T(8,128)(2,1)S(1)}, bf16[28,32,128]{2,1,0:T(8,128)(2,1)S(1)}, u32[]{:S(2)}, u32[]{:S(2)}) %collective-permute-start.28) | collective-permute-done | bytes 229408 | tf_op jit(solution)/shard_map/ppermute | solution.py:40
  111.0 4.9 %collective-permute-start.33 = (bf16[27,32,128]{2,1,0:T(8,128)(2,1)S(1)}, bf16[27,32,128]{2,1,0:T(8,128)(2,1)S(1)}, u32[]{:S(2)}, u32[]{:S(2)}) collective-permute-start(bf16[27,32,128]{2,1,0:T(8,128)(2,1)S(1)} %slice.145), channel_id=1, source_target_pairs={{0,0},{1,1},{2,2},{3,3},{4,4},{5,5},{6,6},{7,7},{8,128},{9,129},{1... | collective-permute-start | bytes 663560 | tf_op jit(solution)/shard_map/ppermute | solution.py:40
  116.4 1.4 %collective-permute-done.30 = bf16[2,256,128]{2,1,0:T(8,128)(2,1)S(1)} collective-permute-done((bf16[2,256,128]{2,1,0:T(8,128)(2,1)S(1)}, bf16[2,256,128]{2,1,0:T(8,128)(2,1)S(1)}, u32[]{:S(2)}, u32[]{:S(2)}) %collective-permute-start.30) | collective-permute-done | bytes 131104 | tf_op jit(solution)/shard_map/ppermute | solution.py:40
  117.8 9.5 %collective-permute-done.31 = bf16[2,256,128]{2,1,0:T(8,128)(2,1)S(1)} collective-permute-done((bf16[2,256,128]{2,1,0:T(8,128)(2,1)S(1)}, bf16[2,256,128]{2,1,0:T(8,128)(2,1)S(1)}, u32[]{:S(2)}, u32[]{:S(2)}) %collective-permute-start.31) | collective-permute-done | bytes 131104 | tf_op jit(solution)/shard_map/ppermute | solution.py:40
  127.4 0.7 pad_maximum_fusion.5
  128.1 0.8 convert_element_type.108
  128.9 2.2 %collective-permute-done.32 = bf16[256,128]{1,0:T(8,128)(2,1)S(1)} collective-permute-done((bf16[256,128]{1,0:T(8,128)(2,1)S(1)}, bf16[256,128]{1,0:T(8,128)(2,1)S(1)}, u32[]{:S(2)}, u32[]{:S(2)}) %collective-permute-start.32) | collective-permute-done | bytes 65568 | tf_op jit(solution)/shard_map/ppermute | solution.py:40
  (61 shorter events, 4.6 us)
Async XLA Ops:
  1.6 2.6 %collective-permute-start = (bf16[2,16,16,128]{3,2,1,0:T(8,128)(2,1)S(1)}, bf16[2,16,16,128]{3,2,1,0:T(8,128)(2,1)S(1)}, u32[]{:S(2)}, u32[]{:S(2)}) collective-permute-start(bf16[2,16,16,128]{3,2,1,0:T(8,128)(2,1)S(1)} %pad_maximum_fusion.2), channel_id=1, source_target_pairs={{0,248},{1,249},{2,250},{3,251},{4,252},{5,253},{6,254},{7,255},{8... | collective-permute-start | bytes 393224 | tf_op jit(solution)/shard_map/ppermute | solution.py:40
  4.3 17.4 %collective-permute-start.1 = (bf16[2,256,128]{2,1,0:T(8,128)(2,1)S(1)}, bf16[2,256,128]{2,1,0:T(8,128)(2,1)S(1)}, u32[]{:S(2)}, u32[]{:S(2)}) collective-permute-start(bf16[2,256,128]{2,1,0:T(8,128)(2,1)S(1)} %bitcast.21), channel_id=1, source_target_pairs={{0,0},{1,17},{2,34},{3,51},{4,12},{5,29},{6,46},{7,63},{8,1},{9,18... | collective-permute-start | bytes 393224 | tf_op jit(solution)/shard_map/ppermute | solution.py:40
  17.8 8.7 %collective-permute-start.2 = (bf16[2,256,128]{2,1,0:T(8,128)(2,1)S(1)}, bf16[2,256,128]{2,1,0:T(8,128)(2,1)S(1)}, u32[]{:S(2)}, u32[]{:S(2)}) collective-permute-start(bf16[2,256,128]{2,1,0:T(8,128)(2,1)S(1)} %bitcast.22), channel_id=1, source_target_pairs={{0,4},{1,21},{2,38},{3,55},{4,8},{5,25},{6,42},{7,59},{8,5},{9,22}... | collective-permute-start | bytes 393224 | tf_op jit(solution)/shard_map/ppermute | solution.py:40
  19.7 13.6 %collective-permute-start.5 = (bf16[27,32,128]{2,1,0:T(8,128)(2,1)}, bf16[27,32,128]{2,1,0:T(8,128)(2,1)S(1)}, u32[]{:S(2)}, u32[]{:S(2)}) collective-permute-start(bf16[27,32,128]{2,1,0:T(8,128)(2,1)} %bitcast.25), channel_id=1, source_target_pairs={{0,0},{1,1},{2,2},{3,3},{4,4},{5,5},{6,6},{7,7},{8,128},{9,129},{1... | collective-permute-start | bytes 663560 | tf_op jit(solution)/shard_map/ppermute | solution.py:40
  26.5 12.0 %collective-permute-start.4 = (bf16[4,256,128]{2,1,0:T(8,128)(2,1)S(1)}, bf16[4,256,128]{2,1,0:T(8,128)(2,1)S(1)}, u32[]{:S(2)}, u32[]{:S(2)}) collective-permute-start(bf16[4,256,128]{2,1,0:T(8,128)(2,1)S(1)} %constant_dynamic-update-slice_fusion.refs_0_), channel_id=1, source_target_pairs={{0,1},{1,2},{2,3},{3,4},{4,5},{5,6},{6,7},{7,0},{8,9},{9,10},{10,1... | collective-permute-start | bytes 786440 | tf_op jit(solution)/shard_map/ppermute | solution.py:40
  26.5 11.9 %collective-permute-start.3 = (bf16[4,256,128]{2,1,0:T(8,128)(2,1)S(1)}, bf16[4,256,128]{2,1,0:T(8,128)(2,1)S(1)}, u32[]{:S(2)}, u32[]{:S(2)}) collective-permute-start(bf16[4,256,128]{2,1,0:T(8,128)(2,1)S(1)} %constant_dynamic-update-slice_fusion.refs_0_), channel_id=1, source_target_pairs={{0,7},{1,0},{2,1},{3,2},{4,3},{5,4},{6,5},{7,6},{8,15},{9,8},{10,9... | collective-permute-start | bytes 786440 | tf_op jit(solution)/shard_map/ppermute | solution.py:40
  33.3 12.9 %collective-permute-start.9 = (bf16[27,32,128]{2,1,0:T(8,128)(2,1)S(1)}, bf16[27,32,128]{2,1,0:T(8,128)(2,1)S(1)}, u32[]{:S(2)}, u32[]{:S(2)}) collective-permute-start(bf16[27,32,128]{2,1,0:T(8,128)(2,1)S(1)} %collective-permute-done.5.refs_0_), channel_id=1, source_target_pairs={{0,64},{1,65},{2,66},{3,67},{4,68},{5,69},{6,70},{7,71},{8,72},{9,... | collective-permute-start | bytes 663560 | tf_op jit(solution)/shard_map/ppermute | solution.py:40
  34.2 11.9 %collective-permute-start.8 = (bf16[27,32,128]{2,1,0:T(8,128)(2,1)S(1)}, bf16[27,32,128]{2,1,0:T(8,128)(2,1)S(1)}, u32[]{:S(2)}, u32[]{:S(2)}) collective-permute-start(bf16[27,32,128]{2,1,0:T(8,128)(2,1)S(1)} %collective-permute-done.5.refs_0_), channel_id=1, source_target_pairs={{0,192},{1,193},{2,194},{3,195},{4,196},{5,197},{6,198},{7,199},{8... | collective-permute-start | bytes 663560 | tf_op jit(solution)/shard_map/ppermute | solution.py:40
  36.5 9.6 %collective-permute-start.10 = (bf16[27,32,128]{2,1,0:T(8,128)(2,1)S(1)}, bf16[27,32,128]{2,1,0:T(8,128)(2,1)S(1)}, u32[]{:S(2)}, u32[]{:S(2)}) collective-permute-start(bf16[27,32,128]{2,1,0:T(8,128)(2,1)S(1)} %collective-permute-done.5.refs_0_), channel_id=1, source_target_pairs={{0,128},{1,129},{2,130},{3,131},{4,132},{5,133},{6,134},{7,135},{8... | collective-permute-start | bytes 663560 | tf_op jit(solution)/shard_map/ppermute | solution.py:40
  38.5 6.3 %collective-permute-start.7 = (bf16[2,256,128]{2,1,0:T(8,128)(2,1)S(1)}, bf16[2,256,128]{2,1,0:T(8,128)(2,1)S(1)}, u32[]{:S(2)}, u32[]{:S(2)}) collective-permute-start(bf16[2,256,128]{2,1,0:T(8,128)(2,1)S(1)} %slice.75), channel_id=1, source_target_pairs={{0,1},{1,2},{2,3},{3,4},{4,5},{5,6},{6,7},{7,0},{8,9},{9,10},{10,1... | collective-permute-start | bytes 393224 | tf_op jit(solution)/shard_map/ppermute | solution.py:40
  38.5 6.2 %collective-permute-start.6 = (bf16[2,256,128]{2,1,0:T(8,128)(2,1)S(1)}, bf16[2,256,128]{2,1,0:T(8,128)(2,1)S(1)}, u32[]{:S(2)}, u32[]{:S(2)}) collective-permute-start(bf16[2,256,128]{2,1,0:T(8,128)(2,1)S(1)} %slice.74), channel_id=1, source_target_pairs={{0,7},{1,0},{2,1},{3,2},{4,3},{5,4},{6,5},{7,6},{8,15},{9,8},{10,9... | collective-permute-start | bytes 393224 | tf_op jit(solution)/shard_map/ppermute | solution.py:40
  50.6 13.9 %copy-start = (f32[128]{0:T(128)S(1)}, f32[128]{0:T(128)}, u32[]{:S(2)}) copy-start(f32[128]{0:T(128)} %param.6) | copy-start | bytes 1540
  50.6 3.2 %collective-permute-start.11 = (bf16[8,256,128]{2,1,0:T(8,128)(2,1)S(1)}, bf16[8,256,128]{2,1,0:T(8,128)(2,1)S(1)}, u32[]{:S(2)}, u32[]{:S(2)}) collective-permute-start(bf16[8,256,128]{2,1,0:T(8,128)(2,1)S(1)} %shard_map.77), channel_id=1, source_target_pairs={{0,8},{1,9},{2,10},{3,11},{4,12},{5,13},{6,14},{7,15},{8,0},{9,1},... | collective-permute-start | bytes 1572872 | tf_op jit(solution)/shard_map/ppermute | solution.py:40
  54.0 8.1 %collective-permute-start.12 = (bf16[2,256,128]{2,1,0:T(8,128)(2,1)S(1)}, bf16[2,256,128]{2,1,0:T(8,128)(2,1)S(1)}, u32[]{:S(2)}, u32[]{:S(2)}) collective-permute-start(bf16[2,256,128]{2,1,0:T(8,128)(2,1)S(1)} %get-tuple-element.116), channel_id=1, source_target_pairs={{0,32},{1,33},{2,34},{3,35},{4,36},{5,37},{6,38},{7,39},{8,40},{9,... | collective-permute-start | bytes 393224 | tf_op jit(solution)/shard_map/ppermute | solution.py:40
  54.3 9.1 %collective-permute-start.14 = (bf16[2,256,128]{2,1,0:T(8,128)(2,1)S(1)}, bf16[2,256,128]{2,1,0:T(8,128)(2,1)S(1)}, u32[]{:S(2)}, u32[]{:S(2)}) collective-permute-start(bf16[2,256,128]{2,1,0:T(8,128)(2,1)S(1)} %get-tuple-element.117), channel_id=1, source_target_pairs={{0,48},{1,49},{2,50},{3,51},{4,52},{5,53},{6,54},{7,55},{8,56},{9,... | collective-permute-start | bytes 393224 | tf_op jit(solution)/shard_map/ppermute | solution.py:40
  55.4 9.1 %collective-permute-start.13 = (bf16[2,256,128]{2,1,0:T(8,128)(2,1)S(1)}, bf16[2,256,128]{2,1,0:T(8,128)(2,1)S(1)}, u32[]{:S(2)}, u32[]{:S(2)}) collective-permute-start(bf16[2,256,128]{2,1,0:T(8,128)(2,1)S(1)} %get-tuple-element.118), channel_id=1, source_target_pairs={{0,16},{1,17},{2,18},{3,19},{4,20},{5,21},{6,22},{7,23},{8,24},{9,... | collective-permute-start | bytes 393224 | tf_op jit(solution)/shard_map/ppermute | solution.py:40
  64.9 6.4 %collective-permute-start.17 = (bf16[2,256,128]{2,1,0:T(8,128)(2,1)S(1)}, bf16[2,256,128]{2,1,0:T(8,128)(2,1)S(1)}, u32[]{:S(2)}, u32[]{:S(2)}) collective-permute-start(bf16[2,256,128]{2,1,0:T(8,128)(2,1)S(1)} %fusion.6.refs_2_.refs_0_), channel_id=1, source_target_pairs={{0,48},{1,49},{2,50},{3,51},{4,52},{5,53},{6,54},{7,55},{8,56},{9,... | collective-permute-start | bytes 393224 | tf_op jit(solution)/shard_map/ppermute | solution.py:40
  65.5 7.9 %collective-permute-start.16 = (bf16[2,256,128]{2,1,0:T(8,128)(2,1)S(1)}, bf16[2,256,128]{2,1,0:T(8,128)(2,1)S(1)}, u32[]{:S(2)}, u32[]{:S(2)}) collective-permute-start(bf16[2,256,128]{2,1,0:T(8,128)(2,1)S(1)} %fusion.6.refs_2_.refs_0_), channel_id=1, source_target_pairs={{0,32},{1,33},{2,34},{3,35},{4,36},{5,37},{6,38},{7,39},{8,40},{9,... | collective-permute-start | bytes 393224 | tf_op jit(solution)/shard_map/ppermute | solution.py:40
  66.6 7.7 %collective-permute-start.15 = (bf16[2,256,128]{2,1,0:T(8,128)(2,1)S(1)}, bf16[2,256,128]{2,1,0:T(8,128)(2,1)S(1)}, u32[]{:S(2)}, u32[]{:S(2)}) collective-permute-start(bf16[2,256,128]{2,1,0:T(8,128)(2,1)S(1)} %fusion.6.refs_2_.refs_0_), channel_id=1, source_target_pairs={{0,16},{1,17},{2,18},{3,19},{4,20},{5,21},{6,22},{7,23},{8,24},{9,... | collective-permute-start | bytes 393224 | tf_op jit(solution)/shard_map/ppermute | solution.py:40
  68.3 6.1 %collective-permute-start.18 = (bf16[2,256,128]{2,1,0:T(8,128)(2,1)S(1)}, bf16[2,256,128]{2,1,0:T(8,128)(2,1)S(1)}, u32[]{:S(2)}, u32[]{:S(2)}) collective-permute-start(bf16[2,256,128]{2,1,0:T(8,128)(2,1)S(1)} %fusion.6.refs_2_.refs_0_), channel_id=1, source_target_pairs={{0,8},{1,9},{2,10},{3,11},{4,12},{5,13},{6,14},{7,15},{8,0},{9,1},... | collective-permute-start | bytes 393224 | tf_op jit(solution)/shard_map/ppermute | solution.py:40
  71.3 3.1 %collective-permute-start.21 = (bf16[2,256,128]{2,1,0:T(8,128)(2,1)S(1)}, bf16[2,256,128]{2,1,0:T(8,128)(2,1)S(1)}, u32[]{:S(2)}, u32[]{:S(2)}) collective-permute-start(bf16[2,256,128]{2,1,0:T(8,128)(2,1)S(1)} %collective-permute-done.17.refs_5_.refs_3_), channel_id=1, source_target_pairs={{0,8},{1,9},{2,10},{3,11},{4,12},{5,13},{6,14},{7,15},{8,0},{9,1},... | collective-permute-start | bytes 393224 | tf_op jit(solution)/shard_map/ppermute | solution.py:40
  73.4 1.3 %collective-permute-start.20 = (bf16[2,256,128]{2,1,0:T(8,128)(2,1)S(1)}, bf16[2,256,128]{2,1,0:T(8,128)(2,1)S(1)}, u32[]{:S(2)}, u32[]{:S(2)}) collective-permute-start(bf16[2,256,128]{2,1,0:T(8,128)(2,1)S(1)} %collective-permute-done.16.refs_4_.refs_2_), channel_id=1, source_target_pairs={{0,8},{1,9},{2,10},{3,11},{4,12},{5,13},{6,14},{7,15},{8,0},{9,1},... | collective-permute-start | bytes 393224 | tf_op jit(solution)/shard_map/ppermute | solution.py:40
  74.4 1.3 %collective-permute-start.19 = (bf16[2,256,128]{2,1,0:T(8,128)(2,1)S(1)}, bf16[2,256,128]{2,1,0:T(8,128)(2,1)S(1)}, u32[]{:S(2)}, u32[]{:S(2)}) collective-permute-start(bf16[2,256,128]{2,1,0:T(8,128)(2,1)S(1)} %collective-permute-done.15.refs_3_.refs_1_), channel_id=1, source_target_pairs={{0,8},{1,9},{2,10},{3,11},{4,12},{5,13},{6,14},{7,15},{8,0},{9,1},... | collective-permute-start | bytes 393224 | tf_op jit(solution)/shard_map/ppermute | solution.py:40
  84.9 7.2 %collective-permute-start.22 = (bf16[2,256,128]{2,1,0:T(8,128)(2,1)S(1)}, bf16[2,256,128]{2,1,0:T(8,128)(2,1)S(1)}, u32[]{:S(2)}, u32[]{:S(2)}) collective-permute-start(bf16[2,256,128]{2,1,0:T(8,128)(2,1)S(1)} %get-tuple-element.82), channel_id=1, source_target_pairs={{0,1},{1,2},{2,3},{3,4},{4,5},{5,6},{6,7},{7,0},{8,9},{9,10},{10,1... | collective-permute-start | bytes 393224 | tf_op jit(solution)/shard_map/ppermute | solution.py:40
  85.4 6.8 %collective-permute-start.23 = (bf16[2,256,128]{2,1,0:T(8,128)(2,1)S(1)}, bf16[2,256,128]{2,1,0:T(8,128)(2,1)S(1)}, u32[]{:S(2)}, u32[]{:S(2)}) collective-permute-start(bf16[2,256,128]{2,1,0:T(8,128)(2,1)S(1)} %get-tuple-element.85), channel_id=1, source_target_pairs={{0,7},{1,0},{2,1},{3,2},{4,3},{5,4},{6,5},{7,6},{8,15},{9,8},{10,9... | collective-permute-start | bytes 393224 | tf_op jit(solution)/shard_map/ppermute | solution.py:40
  92.2 10.5 %collective-permute-start.24 = (bf16[4,256,128]{2,1,0:T(8,128)(2,1)S(1)}, bf16[4,256,128]{2,1,0:T(8,128)(2,1)S(1)}, u32[]{:S(2)}, u32[]{:S(2)}) collective-permute-start(bf16[4,256,128]{2,1,0:T(8,128)(2,1)S(1)} %pad_maximum_fusion), channel_id=1, source_target_pairs={{0,1},{1,2},{2,3},{3,4},{4,5},{5,6},{6,7},{7,0},{8,9},{9,10},{10,1... | collective-permute-start | bytes 786440 | tf_op jit(solution)/shard_map/ppermute | solution.py:40
  92.4 10.3 %collective-permute-start.25 = (bf16[4,256,128]{2,1,0:T(8,128)(2,1)S(1)}, bf16[4,256,128]{2,1,0:T(8,128)(2,1)S(1)}, u32[]{:S(2)}, u32[]{:S(2)}) collective-permute-start(bf16[4,256,128]{2,1,0:T(8,128)(2,1)S(1)} %pad_maximum_fusion.1), channel_id=1, source_target_pairs={{0,7},{1,0},{2,1},{3,2},{4,3},{5,4},{6,5},{7,6},{8,15},{9,8},{10,9... | collective-permute-start | bytes 786440 | tf_op jit(solution)/shard_map/ppermute | solution.py:40
  97.5 9.2 %collective-permute-start.27 = (bf16[28,32,128]{2,1,0:T(8,128)(2,1)S(1)}, bf16[28,32,128]{2,1,0:T(8,128)(2,1)S(1)}, u32[]{:S(2)}, u32[]{:S(2)}) collective-permute-start(bf16[28,32,128]{2,1,0:T(8,128)(2,1)S(1)} %get-tuple-element.100), channel_id=1, source_target_pairs={{0,64},{1,65},{2,66},{3,67},{4,68},{5,69},{6,70},{7,71},{8,72},{9,... | collective-permute-start | bytes 688136 | tf_op jit(solution)/shard_map/ppermute | solution.py:40
  99.9 10.9 %collective-permute-start.28 = (bf16[28,32,128]{2,1,0:T(8,128)(2,1)S(1)}, bf16[28,32,128]{2,1,0:T(8,128)(2,1)S(1)}, u32[]{:S(2)}, u32[]{:S(2)}) collective-permute-start(bf16[28,32,128]{2,1,0:T(8,128)(2,1)S(1)} %get-tuple-element.101), channel_id=1, source_target_pairs={{0,128},{1,129},{2,130},{3,131},{4,132},{5,133},{6,134},{7,135},{8... | collective-permute-start | bytes 688136 | tf_op jit(solution)/shard_map/ppermute | solution.py:40
  101.4 9.4 %collective-permute-start.29 = (bf16[28,32,128]{2,1,0:T(8,128)(2,1)S(1)}, bf16[28,32,128]{2,1,0:T(8,128)(2,1)S(1)}, u32[]{:S(2)}, u32[]{:S(2)}) collective-permute-start(bf16[28,32,128]{2,1,0:T(8,128)(2,1)S(1)} %get-tuple-element.102), channel_id=1, source_target_pairs={{0,192},{1,193},{2,194},{3,195},{4,196},{5,197},{6,198},{7,199},{8... | collective-permute-start | bytes 688136 | tf_op jit(solution)/shard_map/ppermute | solution.py:40
  102.9 8.0 %collective-permute-start.26 = (bf16[256,128]{1,0:T(8,128)(2,1)S(1)}, bf16[256,128]{1,0:T(8,128)(2,1)S(1)}, u32[]{:S(2)}, u32[]{:S(2)}) collective-permute-start(bf16[256,128]{1,0:T(8,128)(2,1)S(1)} %get-tuple-element.121), channel_id=1, source_target_pairs={{0,8},{1,9},{2,10},{3,11},{4,12},{5,13},{6,14},{7,15},{8,16},{9,17... | collective-permute-start | bytes 196616 | tf_op jit(solution)/shard_map/ppermute | solution.py:40
  103.0 14.8 %collective-permute-start.30 = (bf16[2,256,128]{2,1,0:T(8,128)(2,1)S(1)}, bf16[2,256,128]{2,1,0:T(8,128)(2,1)S(1)}, u32[]{:S(2)}, u32[]{:S(2)}) collective-permute-start(bf16[2,256,128]{2,1,0:T(8,128)(2,1)S(1)} %get-tuple-element.104), channel_id=1, source_target_pairs={{0,0},{1,8},{2,16},{3,24},{4,32},{5,40},{6,48},{7,56},{8,36},{9,44... | collective-permute-start | bytes 393224 | tf_op jit(solution)/shard_map/ppermute | solution.py:40
  106.7 20.5 %collective-permute-start.31 = (bf16[2,256,128]{2,1,0:T(8,128)(2,1)S(1)}, bf16[2,256,128]{2,1,0:T(8,128)(2,1)S(1)}, u32[]{:S(2)}, u32[]{:S(2)}) collective-permute-start(bf16[2,256,128]{2,1,0:T(8,128)(2,1)S(1)} %get-tuple-element.105), channel_id=1, source_target_pairs={{0,32},{1,40},{2,48},{3,56},{4,0},{5,8},{6,16},{7,24},{8,4},{9,12}... | collective-permute-start | bytes 393224 | tf_op jit(solution)/shard_map/ppermute | solution.py:40
  111.0 17.1 %collective-permute-start.33 = (bf16[27,32,128]{2,1,0:T(8,128)(2,1)S(1)}, bf16[27,32,128]{2,1,0:T(8,128)(2,1)S(1)}, u32[]{:S(2)}, u32[]{:S(2)}) collective-permute-start(bf16[27,32,128]{2,1,0:T(8,128)(2,1)S(1)} %slice.145), channel_id=1, source_target_pairs={{0,0},{1,1},{2,2},{3,3},{4,4},{5,5},{6,6},{7,7},{8,128},{9,129},{1... | collective-permute-start | bytes 663560 | tf_op jit(solution)/shard_map/ppermute | solution.py:40
  127.3 3.8 %collective-permute-start.32 = (bf16[256,128]{1,0:T(8,128)(2,1)S(1)}, bf16[256,128]{1,0:T(8,128)(2,1)S(1)}, u32[]{:S(2)}, u32[]{:S(2)}) collective-permute-start(bf16[256,128]{1,0:T(8,128)(2,1)S(1)} %get-tuple-element.119), channel_id=1, source_target_pairs={{0,8},{1,9},{2,10},{3,11},{4,12},{5,13},{6,14},{7,15},{8,16},{9,17... | collective-permute-start | bytes 196616 | tf_op jit(solution)/shard_map/ppermute | solution.py:40

commit v6 on v5

--- a/solution.py
+++ b/solution.py
@@ -99,18 +99,14 @@
 
 
 def convolved(columns, pairs, paired):
-    product = None
-    for j in range(2):
-        left = jnp.concatenate(
-            [
-                jnp.concatenate([window(columns, 2 * pair + 2 * j + i) for i in range(2)], axis=1)
-                for pair in pairs
-            ],
-            axis=0,
-        )
-        part = jnp.dot(left, paired[j], preferred_element_type=jnp.float32)
-        product = part if product is None else product + part
-    return product
+    left = jnp.concatenate(
+        [
+            jnp.concatenate([window(columns, 2 * pair + i) for i in range(4)], axis=1)
+            for pair in pairs
+        ],
+        axis=0,
+    )
+    return jnp.dot(left, paired[...], preferred_element_type=jnp.float32)
 
 
 def halves(product, index, size):
@@ -118,32 +114,26 @@
     return [product[rows, o * size : (o + 1) * size] for o in range(2)]
 
 
-def weights_kernel(where, *refs):
-    blocks = refs[:NX]
-    ahead, back, natural = refs[NX:]
-    size, out_size, rows = natural.shape[1], natural.shape[2], blocks[0].shape[1]
+def weights_kernel(turned, where, *refs):
+    *blocks, paired, natural = refs
+    rows = blocks[0].shape[1]
     x = position(where)[0]
     for r in range(NX):
         offset = pl.multiple_of(swapped((x + r) & (NX - 1)) * rows, rows)
         for tap in range(27):
             natural[tap, pl.ds(offset, rows)] = blocks[r][tap]
-
-    def store(ref, a, bc, block):
-        height, width = block.shape
-        for o in range(2):
-            i = a + o
-            first = ((i % 2) * 9 + bc) * height
-            ref[i // 2, first : first + height, o * width : (o + 1) * width] = block
-
-    for ref, height, width in ((ahead, size, out_size), (back, out_size, size)):
-        none = jnp.zeros((9 * height, width), jnp.bfloat16)
-        ref[0, : 9 * height, width:] = none
-        ref[1, 9 * height :, :width] = none
+    deep, wide = natural.shape[1:][::-1] if turned else natural.shape[1:]
+    none = jnp.zeros((9 * deep, wide), jnp.bfloat16)
+    paired[: 9 * deep, wide:] = none
+    paired[27 * deep :, :wide] = none
     for tap in range(27):
         block = natural[tap]
-        store(ahead, tap // 9, tap % 9, block)
-        turned = block.astype(jnp.float32).T.astype(jnp.bfloat16)
-        store(back, (26 - tap) // 9, (26 - tap) % 9, turned)
+        if turned:
+            block = block.T
+        a, bc = (26 - tap) // 9 if turned else tap // 9, (26 - tap) % 9 if turned else tap % 9
+        for o in range(2):
+            first = ((a + o) * 9 + bc) * deep
+            paired[first : first + deep, o * wide : (o + 1) * wide] = block
 
 
 def own_pairs(where):
@@ -182,22 +172,18 @@
             bias = bias + jnp.sum(value.reshape(FACE // 8, 8, size), axis=0)
             start = pl.multiple_of((2 * pair + half + 1) * FACE, FACE)
             turned[:, pl.ds(start, FACE)] = ref[half].T
-    total[...] = jnp.zeros_like(total)
-
-    def step(index, carry):
-        first = 8 * index
+    product = None
+    for first in range(0, GRID, GRID // 2):
         left = jnp.concatenate(
-            [
-                turned[:, pl.ds(pl.multiple_of((first + 2 - a) * FACE, FACE), 8 * FACE)]
-                for a in range(3)
-            ],
+            [turned[:, (first + 2 - a) * FACE : (first + 2 - a + GRID // 2) * FACE] for a in range(3)],
             axis=0,
         )
-        right = jnp.concatenate([window(columns, first + 1 + e) for e in range(8)], axis=0)
-        total[...] += jnp.dot(left, right, preferred_element_type=jnp.float32)
-        return carry
-
-    lax.fori_loop(0, GRID // 8, step, 0)
+        right = jnp.concatenate(
+            [window(columns, first + 1 + e) for e in range(GRID // 2)], axis=0
+        )
+        part = jnp.dot(left, right, preferred_element_type=jnp.float32)
+        product = part if product is None else product + part
+    total[...] = product
     for tap in range(27):
         a, bc = tap // 9, tap % 9
         block = total[a * size : (a + 1) * size, bc * size : (bc + 1) * size]
@@ -261,7 +247,7 @@
     planes = [own, above, below, along_z(above[:2], -1), along_z(below[:2], 1)]
 
     flops = 2 * 27 * GRID * FACE * size * out_size
-    paired_shape = lambda deep, wide: shaped((2, 18 * deep, 2 * wide), bf16)
+    paired_shape = lambda deep, wide: shaped((36 * deep, 2 * wide), bf16)
     columns_shape = shaped((GRID + 2, FACE + 2 * GRID, 3 * size), bf16)
     (columns,) = call(
         lambda where, *refs: store_columns(ring_pairs(where, Z_STEPS), refs[:-1], refs[-1]),
@@ -272,14 +258,19 @@
         0,
     )
     columns, blocks[1], blocks[3] = lax.optimization_barrier((columns, blocks[1], blocks[3]))
-    ahead_weights, back_weights = call(
-        weights_kernel,
-        where,
-        blocks,
-        [paired_shape(size, out_size), paired_shape(out_size, size)],
-        [pltpu.VMEM((27, size, out_size), bf16)],
-        0,
-    )
+
+    def weights(turned, where):
+        (paired,) = call(
+            lambda *refs: weights_kernel(turned, *refs),
+            where,
+            blocks,
+            [paired_shape(out_size, size) if turned else paired_shape(size, out_size)],
+            [pltpu.VMEM((27, size, out_size), bf16)],
+            0,
+        )
+        return paired
+
+    ahead_weights = weights(False, where)
     def products(pairs, where, columns, weights, outs):
         return call(
             lambda *refs: product_kernel(pairs, *refs),
@@ -300,6 +291,8 @@
         pre_act = pre_act + permuted(
             keep[r].astype(bf16), lambda x, q, z: at(x, q + 2 * r, z)
         ).astype(f32)
+    back_weights = weights(True, where)
+    pre_act, back_weights = lax.optimization_barrier((pre_act, back_weights))
     pre_act = pre_act + conv_bias[None, None, :]
 
     target = jnp.stack([cotangent[1], ahead])

time: 133 us -> 132 us (level)
    pallas_call x9 -> x10, Pallas kernels: 23.1 us -> 23.2 us  [call(): pl.pallas_call(kernel, out_shape=outs, in_specs=[pl.BlockSpec(memory_spac...]
  transfers between devices with their start and end apart: 34 -> 34, of which waited for: 17 -> 17; matrix products, arithmetic and copies ran while one was open for 2% -> 2% of each run, Pallas kernels for 7% -> 8%
where the time goes in v6:
time: 132 us; the launch traced here: 131 us
  starting transfers between devices  61 us (46%)
  waiting for transfers between devices  40.8 us (31%)
  Pallas kernels  23.2 us (18%)
  other arithmetic  3.69 us (3%)
    ppermute x34, starting transfers between devices, permuted(): return lax.ppermute(array, ('space', 'chan'), pairs)  61 us
    ppermute x34, waiting for transfers between devices, permuted(): return lax.ppermute(array, ('space', 'chan'), pairs)  40.8 us
    pallas_call x10, Pallas kernels, call(): pl.pallas_call(kernel, out_shape=outs, in_specs=[pl.BlockSpec(memory_spac...  23.2 us
  transfers between devices with their start and end apart: 34, of which 17 were waited for; matrix products, arithmetic and copies ran while one was open for 2% of the time, Pallas kernels for 8%

profile of v6, /device:TPU:16, one launch (start us, length us, event | category | flops | bytes accessed | tf_op | source)
XLA Modules:
  0.0 130.8 jit_solution(13655899903011775912)
XLA Ops:
  0.6 1.0 fusion.16
  1.7 2.5 %collective-permute-done = bf16[2,16,16,128]{3,2,1,0:T(8,128)(2,1)S(1)} collective-permute-done((bf16[2,16,16,128]{3,2,1,0:T(8,128)(2,1)S(1)}, bf16[2,16,16,128]{3,2,1,0:T(8,128)(2,1)S(1)}, u32[]{:S(2)}, u32[]{:S(2)}) %collective-permute-start) | collective-permute-done | bytes 131104 | tf_op jit(solution)/shard_map/ppermute | solution.py:40
  4.3 13.5 %collective-permute-start.1 = (bf16[2,256,128]{2,1,0:T(8,128)(2,1)S(1)}, bf16[2,256,128]{2,1,0:T(8,128)(2,1)S(1)}, u32[]{:S(2)}, u32[]{:S(2)}) collective-permute-start(bf16[2,256,128]{2,1,0:T(8,128)(2,1)S(1)} %bitcast.21), channel_id=1, source_target_pairs={{0,0},{1,17},{2,34},{3,51},{4,12},{5,29},{6,46},{7,63},{8,1},{9,18... | collective-permute-start | bytes 393224 | tf_op jit(solution)/shard_map/ppermute | solution.py:40
  17.8 1.9 %collective-permute-start.2 = (bf16[2,256,128]{2,1,0:T(8,128)(2,1)S(1)}, bf16[2,256,128]{2,1,0:T(8,128)(2,1)S(1)}, u32[]{:S(2)}, u32[]{:S(2)}) collective-permute-start(bf16[2,256,128]{2,1,0:T(8,128)(2,1)S(1)} %bitcast.22), channel_id=1, source_target_pairs={{0,4},{1,21},{2,38},{3,55},{4,8},{5,25},{6,42},{7,59},{8,5},{9,22}... | collective-permute-start | bytes 393224 | tf_op jit(solution)/shard_map/ppermute | solution.py:40
  19.7 1.9 %collective-permute-start.5 = (bf16[27,32,128]{2,1,0:T(8,128)(2,1)}, bf16[27,32,128]{2,1,0:T(8,128)(2,1)S(1)}, u32[]{:S(2)}, u32[]{:S(2)}) collective-permute-start(bf16[27,32,128]{2,1,0:T(8,128)(2,1)} %bitcast.25), channel_id=1, source_target_pairs={{0,0},{1,1},{2,2},{3,3},{4,4},{5,5},{6,6},{7,7},{8,128},{9,129},{1... | collective-permute-start | bytes 663560 | tf_op jit(solution)/shard_map/ppermute | solution.py:40
  21.7 4.8 %collective-permute-done.2 = bf16[2,256,128]{2,1,0:T(8,128)(2,1)S(1)} collective-permute-done((bf16[2,256,128]{2,1,0:T(8,128)(2,1)S(1)}, bf16[2,256,128]{2,1,0:T(8,128)(2,1)S(1)}, u32[]{:S(2)}, u32[]{:S(2)}) %collective-permute-start.2) | collective-permute-done | bytes 131104 | tf_op jit(solution)/shard_map/ppermute | solution.py:40
  26.5 6.7 %collective-permute-start.3 = (bf16[4,256,128]{2,1,0:T(8,128)(2,1)S(1)}, bf16[4,256,128]{2,1,0:T(8,128)(2,1)S(1)}, u32[]{:S(2)}, u32[]{:S(2)}) collective-permute-start(bf16[4,256,128]{2,1,0:T(8,128)(2,1)S(1)} %constant_dynamic-update-slice_fusion.refs_0_), channel_id=1, source_target_pairs={{0,7},{1,0},{2,1},{3,2},{4,3},{5,4},{6,5},{7,6},{8,15},{9,8},{10,9... | collective-permute-start | bytes 786440 | tf_op jit(solution)/shard_map/ppermute | solution.py:40
  33.3 0.9 collective-permute-start.9
  34.2 2.3 %collective-permute-start.8 = (bf16[27,32,128]{2,1,0:T(8,128)(2,1)S(1)}, bf16[27,32,128]{2,1,0:T(8,128)(2,1)S(1)}, u32[]{:S(2)}, u32[]{:S(2)}) collective-permute-start(bf16[27,32,128]{2,1,0:T(8,128)(2,1)S(1)} %collective-permute-done.5.refs_1_), channel_id=1, source_target_pairs={{0,192},{1,193},{2,194},{3,195},{4,196},{5,197},{6,198},{7,199},{8... | collective-permute-start | bytes 663560 | tf_op jit(solution)/shard_map/ppermute | solution.py:40
  36.5 1.9 %collective-permute-start.10 = (bf16[27,32,128]{2,1,0:T(8,128)(2,1)S(1)}, bf16[27,32,128]{2,1,0:T(8,128)(2,1)S(1)}, u32[]{:S(2)}, u32[]{:S(2)}) collective-permute-start(bf16[27,32,128]{2,1,0:T(8,128)(2,1)S(1)} %collective-permute-done.5.refs_1_), channel_id=1, source_target_pairs={{0,128},{1,129},{2,130},{3,131},{4,132},{5,133},{6,134},{7,135},{8... | collective-permute-start | bytes 663560 | tf_op jit(solution)/shard_map/ppermute | solution.py:40
  38.5 3.2 %collective-permute-start.6 = (bf16[2,256,128]{2,1,0:T(8,128)(2,1)S(1)}, bf16[2,256,128]{2,1,0:T(8,128)(2,1)S(1)}, u32[]{:S(2)}, u32[]{:S(2)}) collective-permute-start(bf16[2,256,128]{2,1,0:T(8,128)(2,1)S(1)} %slice.74), channel_id=1, source_target_pairs={{0,7},{1,0},{2,1},{3,2},{4,3},{5,4},{6,5},{7,6},{8,15},{9,8},{10,9... | collective-permute-start | bytes 393224 | tf_op jit(solution)/shard_map/ppermute | solution.py:40
  41.8 2.9 %collective-permute-done.7.refs_4_ = bf16[2,256,128]{2,1,0:T(8,128)(2,1)S(1)} collective-permute-done((bf16[2,256,128]{2,1,0:T(8,128)(2,1)S(1)}, bf16[2,256,128]{2,1,0:T(8,128)(2,1)S(1)}, u32[]{:S(2)}, u32[]{:S(2)}) %collective-permute-start.7) | collective-permute-done | bytes 131104 | tf_op jit(solution)/shard_map/ppermute | solution.py:40
  44.7 1.4 %shard_map.75.refs_1_ = bf16[18,288,384]{2,1,0:T(8,128)(2,1)S(1)} custom-call(s32[2]{0:T(128)S(1)} %pad_add_fusion.where.refs_0_, bf16[4,256,128]{2,1,0:T(8,128)(2,1)S(1)} %constant_dynamic-update-slice_fusion.refs_0_, bf16[4,256,128]{2,1,0:T(8,128)(2,1)S(1)} %collective-permute-done.3.refs_1_, bf16[4,256,128]{2,1,0:T(8,128)(2,1)S(1)} %collective-permute-done.4.refs_2_, ...), custom_call_target="tpu_custom_call" | custom-call | bytes 5029888 | tf_op jit(solution)/shard_map/pallas_call | solution.py:209
  46.2 0.9 shard_map.76.refs_2_
  47.1 3.1 %shard_map.77 = bf16[8,256,128]{2,1,0:T(8,128)(2,1)S(1)} custom-call(s32[2]{0:T(128)S(1)} %pad_add_fusion.where.refs_0_, bf16[18,288,384]{2,1,0:T(8,128)(2,1)S(1)} %shard_map.75.refs_1_, bf16[4608,256]{1,0:T(8,128)(2,1)S(1)} %shard_map.76.refs_2_), custom_call_target="tpu_custom_call" | custom-call | flops 1811939328 | bytes 6864896 | tf_op jit(solution)/shard_map/pallas_call | solution.py:209
  50.3 3.1 %shard_map.78 = (f32[2,256,128]{2,1,0:T(8,128)S(1)}, f32[2,256,128]{2,1,0:T(8,128)S(1)}, f32[2,256,128]{2,1,0:T(8,128)S(1)}, f32[2,256,128]{2,1,0:T(8,128)S(1)}) custom-call(s32[2]{0:T(128)S(1)} %pad_add_fusion.where.refs_0_, bf16[18,288,384]{2,1,0:T(8,128)(2,1)S(1)} %shard_map.75.refs_1_, bf16[4608,256]{1,0:T(8,128)(2,1)S(1)} %shard_map.76.refs_2_), custom_call_target="tpu_custom_call" | custom-call | flops 1811939328 | bytes 7389184 | tf_op jit(solution)/shard_map/pallas_call | solution.py:209
  53.8 1.1 collective-permute-start.14
  54.9 1.3 %collective-permute-start.13 = (bf16[2,256,128]{2,1,0:T(8,128)(2,1)S(1)}, bf16[2,256,128]{2,1,0:T(8,128)(2,1)S(1)}, u32[]{:S(2)}, u32[]{:S(2)}) collective-permute-start(bf16[2,256,128]{2,1,0:T(8,128)(2,1)S(1)} %get-tuple-element.116), channel_id=1, source_target_pairs={{0,16},{1,17},{2,18},{3,19},{4,20},{5,21},{6,22},{7,23},{8,24},{9,... | collective-permute-start | bytes 393224 | tf_op jit(solution)/shard_map/ppermute | solution.py:40
  56.2 1.0 shard_map.79.refs_2_
  57.2 4.4 %collective-permute-done.12 = bf16[2,256,128]{2,1,0:T(8,128)(2,1)S(1)} collective-permute-done((bf16[2,256,128]{2,1,0:T(8,128)(2,1)S(1)}, bf16[2,256,128]{2,1,0:T(8,128)(2,1)S(1)}, u32[]{:S(2)}, u32[]{:S(2)}) %collective-permute-start.12) | collective-permute-done | bytes 131104 | tf_op jit(solution)/shard_map/ppermute | solution.py:40
  61.6 1.3 collective-permute-done.14
  62.9 1.1 collective-permute-done.13
  64.3 0.7 collective-permute-start.17
  65.0 1.1 collective-permute-start.16
  66.1 1.7 %collective-permute-start.15 = (bf16[2,256,128]{2,1,0:T(8,128)(2,1)S(1)}, bf16[2,256,128]{2,1,0:T(8,128)(2,1)S(1)}, u32[]{:S(2)}, u32[]{:S(2)}) collective-permute-start(bf16[2,256,128]{2,1,0:T(8,128)(2,1)S(1)} %get-tuple-element.118.refs_2_.refs_0_), channel_id=1, source_target_pairs={{0,16},{1,17},{2,18},{3,19},{4,20},{5,21},{6,22},{7,23},{8,24},{9,... | collective-permute-start | bytes 393224 | tf_op jit(solution)/shard_map/ppermute | solution.py:40
  67.8 2.9 %collective-permute-done.17.refs_5_.refs_3_ = bf16[2,256,128]{2,1,0:T(8,128)(2,1)S(1)} collective-permute-done((bf16[2,256,128]{2,1,0:T(8,128)(2,1)S(1)}, bf16[2,256,128]{2,1,0:T(8,128)(2,1)S(1)}, u32[]{:S(2)}, u32[]{:S(2)}) %collective-permute-start.17) | collective-permute-done | bytes 131104 | tf_op jit(solution)/shard_map/ppermute | solution.py:40
  70.7 2.1 %collective-permute-done.16.refs_4_.refs_2_ = bf16[2,256,128]{2,1,0:T(8,128)(2,1)S(1)} collective-permute-done((bf16[2,256,128]{2,1,0:T(8,128)(2,1)S(1)}, bf16[2,256,128]{2,1,0:T(8,128)(2,1)S(1)}, u32[]{:S(2)}, u32[]{:S(2)}) %collective-permute-start.16) | collective-permute-done | bytes 131104 | tf_op jit(solution)/shard_map/ppermute | solution.py:40
  72.9 0.9 collective-permute-done.15.refs_3_.refs_1_
  74.2 0.9 collective-permute-done.19.refs_7_.refs_5_
  75.2 5.2 %shard_map.80 = (bf16[28,32,128]{2,1,0:T(8,128)(2,1)S(1)}, bf16[28,32,128]{2,1,0:T(8,128)(2,1)S(1)}, bf16[28,32,128]{2,1,0:T(8,128)(2,1)S(1)}, bf16[28,32,128]{2,1,0:T(8,128)(2,1)S(1)}) custom-call(s32[2]{0:T(128)S(1)} %pad_add_fusion.where.refs_0_, bf16[18,288,384]{2,1,0:T(8,128)(2,1)S(1)} %shard_map.75.refs_1_, ...), custom_call_target="tpu_custom_call" | custom-call | flops 3623878656 | bytes 5947392 | tf_op jit(solution)/shard_map/pallas_call | solution.py:209
  80.4 1.4 %shard_map.81.refs_1_ = bf16[18,288,384]{2,1,0:T(8,128)(2,1)S(1)} custom-call(s32[2]{0:T(128)S(1)} %pad_add_fusion.where.refs_0_, bf16[2,256,128]{2,1,0:T(8,128)(2,1)S(1)} %get-tuple-element.118.refs_2_.refs_0_, bf16[2,256,128]{2,1,0:T(8,128)(2,1)S(1)} %collective-permute-done.15.refs_3_.refs_1_, ...), custom_call_target="tpu_custom_call" | custom-call | bytes 5029888 | tf_op jit(solution)/shard_map/pallas_call | solution.py:209
  81.8 1.9 %shard_map.82 = (bf16[2,256,128]{2,1,0:T(8,128)(2,1)S(1)}, bf16[2,256,128]{2,1,0:T(8,128)(2,1)S(1)}) custom-call(s32[2]{0:T(128)S(1)} %pad_add_fusion.where.refs_0_, bf16[18,288,384]{2,1,0:T(8,128)(2,1)S(1)} %shard_map.81.refs_1_, bf16[4608,256]{1,0:T(8,128)(2,1)S(1)} %shard_map.79.refs_2_), custom_call_target="tpu_custom_call" | custom-call | flops 905969664 | bytes 6602752 | tf_op jit(solution)/shard_map/pallas_call | solution.py:209
  84.2 3.2 %collective-permute-start.23 = (bf16[2,256,128]{2,1,0:T(8,128)(2,1)S(1)}, bf16[2,256,128]{2,1,0:T(8,128)(2,1)S(1)}, u32[]{:S(2)}, u32[]{:S(2)}) collective-permute-start(bf16[2,256,128]{2,1,0:T(8,128)(2,1)S(1)} %get-tuple-element.85), channel_id=1, source_target_pairs={{0,7},{1,0},{2,1},{3,2},{4,3},{5,4},{6,5},{7,6},{8,15},{9,8},{10,9... | collective-permute-start | bytes 393224 | tf_op jit(solution)/shard_map/ppermute | solution.py:40
  87.4 3.1 %shard_map.83 = (f32[2,256,128]{2,1,0:T(8,128)S(1)}, bf16[2,256,128]{2,1,0:T(8,128)(2,1)S(1)}, f32[2,256,128]{2,1,0:T(8,128)S(1)}, bf16[2,256,128]{2,1,0:T(8,128)(2,1)S(1)}) custom-call(s32[2]{0:T(128)S(1)} %pad_add_fusion.where.refs_0_, bf16[18,288,384]{2,1,0:T(8,128)(2,1)S(1)} %shard_map.81.refs_1_, bf16[4608,256]{1,0:T(8,128)(2,1)S(1)} %shard_map.79.refs_2_), custom_call_target="tpu_custom_call" | custom-call | flops 1811939328 | bytes 7127040 | tf_op jit(solution)/shard_map/pallas_call | solution.py:209
  91.3 3.2 %collective-permute-start.25 = (bf16[4,256,128]{2,1,0:T(8,128)(2,1)S(1)}, bf16[4,256,128]{2,1,0:T(8,128)(2,1)S(1)}, u32[]{:S(2)}, u32[]{:S(2)}) collective-permute-start(bf16[4,256,128]{2,1,0:T(8,128)(2,1)S(1)} %pad_maximum_fusion.1), channel_id=1, source_target_pairs={{0,7},{1,0},{2,1},{3,2},{4,3},{5,4},{6,5},{7,6},{8,15},{9,8},{10,9... | collective-permute-start | bytes 786440 | tf_op jit(solution)/shard_map/ppermute | solution.py:40
  94.4 1.9 %shard_map.84 = (f32[2,256,128]{2,1,0:T(8,128)S(1)}, f32[2,256,128]{2,1,0:T(8,128)S(1)}) custom-call(s32[2]{0:T(128)S(1)} %pad_add_fusion.where.refs_0_, bf16[18,288,384]{2,1,0:T(8,128)(2,1)S(1)} %shard_map.81.refs_1_, bf16[4608,256]{1,0:T(8,128)(2,1)S(1)} %shard_map.79.refs_2_), custom_call_target="tpu_custom_call" | custom-call | flops 905969664 | bytes 6864896 | tf_op jit(solution)/shard_map/pallas_call | solution.py:209
  96.4 2.4 %collective-permute-start.27 = (bf16[28,32,128]{2,1,0:T(8,128)(2,1)S(1)}, bf16[28,32,128]{2,1,0:T(8,128)(2,1)S(1)}, u32[]{:S(2)}, u32[]{:S(2)}) collective-permute-start(bf16[28,32,128]{2,1,0:T(8,128)(2,1)S(1)} %get-tuple-element.100), channel_id=1, source_target_pairs={{0,64},{1,65},{2,66},{3,67},{4,68},{5,69},{6,70},{7,71},{8,72},{9,... | collective-permute-start | bytes 688136 | tf_op jit(solution)/shard_map/ppermute | solution.py:40
  98.8 1.5 %collective-permute-start.28 = (bf16[28,32,128]{2,1,0:T(8,128)(2,1)S(1)}, bf16[28,32,128]{2,1,0:T(8,128)(2,1)S(1)}, u32[]{:S(2)}, u32[]{:S(2)}) collective-permute-start(bf16[28,32,128]{2,1,0:T(8,128)(2,1)S(1)} %get-tuple-element.101), channel_id=1, source_target_pairs={{0,128},{1,129},{2,130},{3,131},{4,132},{5,133},{6,134},{7,135},{8... | collective-permute-start | bytes 688136 | tf_op jit(solution)/shard_map/ppermute | solution.py:40
  100.3 1.3 collective-permute-start.29
  101.9 2.9 %collective-permute-start.30 = (bf16[2,256,128]{2,1,0:T(8,128)(2,1)S(1)}, bf16[2,256,128]{2,1,0:T(8,128)(2,1)S(1)}, u32[]{:S(2)}, u32[]{:S(2)}) collective-permute-start(bf16[2,256,128]{2,1,0:T(8,128)(2,1)S(1)} %get-tuple-element.104), channel_id=1, source_target_pairs={{0,0},{1,8},{2,16},{3,24},{4,32},{5,40},{6,48},{7,56},{8,36},{9,44... | collective-permute-start | bytes 393224 | tf_op jit(solution)/shard_map/ppermute | solution.py:40
  104.7 0.9 collective-permute-done.27
  105.6 2.0 %collective-permute-start.31 = (bf16[2,256,128]{2,1,0:T(8,128)(2,1)S(1)}, bf16[2,256,128]{2,1,0:T(8,128)(2,1)S(1)}, u32[]{:S(2)}, u32[]{:S(2)}) collective-permute-start(bf16[2,256,128]{2,1,0:T(8,128)(2,1)S(1)} %get-tuple-element.105), channel_id=1, source_target_pairs={{0,32},{1,40},{2,48},{3,56},{4,0},{5,8},{6,16},{7,24},{8,4},{9,12}... | collective-permute-start | bytes 393224 | tf_op jit(solution)/shard_map/ppermute | solution.py:40
  107.6 2.1 %collective-permute-done.28 = bf16[28,32,128]{2,1,0:T(8,128)(2,1)S(1)} collective-permute-done((bf16[28,32,128]{2,1,0:T(8,128)(2,1)S(1)}, bf16[28,32,128]{2,1,0:T(8,128)(2,1)S(1)}, u32[]{:S(2)}, u32[]{:S(2)}) %collective-permute-start.28) | collective-permute-done | bytes 229408 | tf_op jit(solution)/shard_map/ppermute | solution.py:40
  109.9 4.9 %collective-permute-start.33 = (bf16[27,32,128]{2,1,0:T(8,128)(2,1)S(1)}, bf16[27,32,128]{2,1,0:T(8,128)(2,1)S(1)}, u32[]{:S(2)}, u32[]{:S(2)}) collective-permute-start(bf16[27,32,128]{2,1,0:T(8,128)(2,1)S(1)} %slice.143), channel_id=1, source_target_pairs={{0,0},{1,1},{2,2},{3,3},{4,4},{5,5},{6,6},{7,7},{8,128},{9,129},{1... | collective-permute-start | bytes 663560 | tf_op jit(solution)/shard_map/ppermute | solution.py:40
  115.3 1.4 %collective-permute-done.30 = bf16[2,256,128]{2,1,0:T(8,128)(2,1)S(1)} collective-permute-done((bf16[2,256,128]{2,1,0:T(8,128)(2,1)S(1)}, bf16[2,256,128]{2,1,0:T(8,128)(2,1)S(1)}, u32[]{:S(2)}, u32[]{:S(2)}) %collective-permute-start.30) | collective-permute-done | bytes 131104 | tf_op jit(solution)/shard_map/ppermute | solution.py:40
  116.7 9.6 %collective-permute-done.31 = bf16[2,256,128]{2,1,0:T(8,128)(2,1)S(1)} collective-permute-done((bf16[2,256,128]{2,1,0:T(8,128)(2,1)S(1)}, bf16[2,256,128]{2,1,0:T(8,128)(2,1)S(1)}, u32[]{:S(2)}, u32[]{:S(2)}) %collective-permute-start.31) | collective-permute-done | bytes 131104 | tf_op jit(solution)/shard_map/ppermute | solution.py:40
  127.1 0.8 convert_element_type.108
  127.9 2.2 %collective-permute-done.32 = bf16[256,128]{1,0:T(8,128)(2,1)S(1)} collective-permute-done((bf16[256,128]{1,0:T(8,128)(2,1)S(1)}, bf16[256,128]{1,0:T(8,128)(2,1)S(1)}, u32[]{:S(2)}, u32[]{:S(2)}) %collective-permute-start.32) | collective-permute-done | bytes 65568 | tf_op jit(solution)/shard_map/ppermute | solution.py:40
  (62 shorter events, 5.1 us)
Async XLA Ops:
  1.6 2.6 %collective-permute-start = (bf16[2,16,16,128]{3,2,1,0:T(8,128)(2,1)S(1)}, bf16[2,16,16,128]{3,2,1,0:T(8,128)(2,1)S(1)}, u32[]{:S(2)}, u32[]{:S(2)}) collective-permute-start(bf16[2,16,16,128]{3,2,1,0:T(8,128)(2,1)S(1)} %pad_maximum_fusion.2), channel_id=1, source_target_pairs={{0,248},{1,249},{2,250},{3,251},{4,252},{5,253},{6,254},{7,255},{8... | collective-permute-start | bytes 393224 | tf_op jit(solution)/shard_map/ppermute | solution.py:40
  4.3 17.4 %collective-permute-start.1 = (bf16[2,256,128]{2,1,0:T(8,128)(2,1)S(1)}, bf16[2,256,128]{2,1,0:T(8,128)(2,1)S(1)}, u32[]{:S(2)}, u32[]{:S(2)}) collective-permute-start(bf16[2,256,128]{2,1,0:T(8,128)(2,1)S(1)} %bitcast.21), channel_id=1, source_target_pairs={{0,0},{1,17},{2,34},{3,51},{4,12},{5,29},{6,46},{7,63},{8,1},{9,18... | collective-permute-start | bytes 393224 | tf_op jit(solution)/shard_map/ppermute | solution.py:40
  17.8 8.7 %collective-permute-start.2 = (bf16[2,256,128]{2,1,0:T(8,128)(2,1)S(1)}, bf16[2,256,128]{2,1,0:T(8,128)(2,1)S(1)}, u32[]{:S(2)}, u32[]{:S(2)}) collective-permute-start(bf16[2,256,128]{2,1,0:T(8,128)(2,1)S(1)} %bitcast.22), channel_id=1, source_target_pairs={{0,4},{1,21},{2,38},{3,55},{4,8},{5,25},{6,42},{7,59},{8,5},{9,22}... | collective-permute-start | bytes 393224 | tf_op jit(solution)/shard_map/ppermute | solution.py:40
  19.7 13.6 %collective-permute-start.5 = (bf16[27,32,128]{2,1,0:T(8,128)(2,1)}, bf16[27,32,128]{2,1,0:T(8,128)(2,1)S(1)}, u32[]{:S(2)}, u32[]{:S(2)}) collective-permute-start(bf16[27,32,128]{2,1,0:T(8,128)(2,1)} %bitcast.25), channel_id=1, source_target_pairs={{0,0},{1,1},{2,2},{3,3},{4,4},{5,5},{6,6},{7,7},{8,128},{9,129},{1... | collective-permute-start | bytes 663560 | tf_op jit(solution)/shard_map/ppermute | solution.py:40
  26.5 12.0 %collective-permute-start.4 = (bf16[4,256,128]{2,1,0:T(8,128)(2,1)S(1)}, bf16[4,256,128]{2,1,0:T(8,128)(2,1)S(1)}, u32[]{:S(2)}, u32[]{:S(2)}) collective-permute-start(bf16[4,256,128]{2,1,0:T(8,128)(2,1)S(1)} %constant_dynamic-update-slice_fusion.refs_0_), channel_id=1, source_target_pairs={{0,1},{1,2},{2,3},{3,4},{4,5},{5,6},{6,7},{7,0},{8,9},{9,10},{10,1... | collective-permute-start | bytes 786440 | tf_op jit(solution)/shard_map/ppermute | solution.py:40
  26.5 11.9 %collective-permute-start.3 = (bf16[4,256,128]{2,1,0:T(8,128)(2,1)S(1)}, bf16[4,256,128]{2,1,0:T(8,128)(2,1)S(1)}, u32[]{:S(2)}, u32[]{:S(2)}) collective-permute-start(bf16[4,256,128]{2,1,0:T(8,128)(2,1)S(1)} %constant_dynamic-update-slice_fusion.refs_0_), channel_id=1, source_target_pairs={{0,7},{1,0},{2,1},{3,2},{4,3},{5,4},{6,5},{7,6},{8,15},{9,8},{10,9... | collective-permute-start | bytes 786440 | tf_op jit(solution)/shard_map/ppermute | solution.py:40
  33.3 12.9 %collective-permute-start.9 = (bf16[27,32,128]{2,1,0:T(8,128)(2,1)S(1)}, bf16[27,32,128]{2,1,0:T(8,128)(2,1)S(1)}, u32[]{:S(2)}, u32[]{:S(2)}) collective-permute-start(bf16[27,32,128]{2,1,0:T(8,128)(2,1)S(1)} %collective-permute-done.5.refs_1_), channel_id=1, source_target_pairs={{0,64},{1,65},{2,66},{3,67},{4,68},{5,69},{6,70},{7,71},{8,72},{9,... | collective-permute-start | bytes 663560 | tf_op jit(solution)/shard_map/ppermute | solution.py:40
  34.2 11.9 %collective-permute-start.8 = (bf16[27,32,128]{2,1,0:T(8,128)(2,1)S(1)}, bf16[27,32,128]{2,1,0:T(8,128)(2,1)S(1)}, u32[]{:S(2)}, u32[]{:S(2)}) collective-permute-start(bf16[27,32,128]{2,1,0:T(8,128)(2,1)S(1)} %collective-permute-done.5.refs_1_), channel_id=1, source_target_pairs={{0,192},{1,193},{2,194},{3,195},{4,196},{5,197},{6,198},{7,199},{8... | collective-permute-start | bytes 663560 | tf_op jit(solution)/shard_map/ppermute | solution.py:40
  36.5 9.6 %collective-permute-start.10 = (bf16[27,32,128]{2,1,0:T(8,128)(2,1)S(1)}, bf16[27,32,128]{2,1,0:T(8,128)(2,1)S(1)}, u32[]{:S(2)}, u32[]{:S(2)}) collective-permute-start(bf16[27,32,128]{2,1,0:T(8,128)(2,1)S(1)} %collective-permute-done.5.refs_1_), channel_id=1, source_target_pairs={{0,128},{1,129},{2,130},{3,131},{4,132},{5,133},{6,134},{7,135},{8... | collective-permute-start | bytes 663560 | tf_op jit(solution)/shard_map/ppermute | solution.py:40
  38.5 6.3 %collective-permute-start.7 = (bf16[2,256,128]{2,1,0:T(8,128)(2,1)S(1)}, bf16[2,256,128]{2,1,0:T(8,128)(2,1)S(1)}, u32[]{:S(2)}, u32[]{:S(2)}) collective-permute-start(bf16[2,256,128]{2,1,0:T(8,128)(2,1)S(1)} %slice.75), channel_id=1, source_target_pairs={{0,1},{1,2},{2,3},{3,4},{4,5},{5,6},{6,7},{7,0},{8,9},{9,10},{10,1... | collective-permute-start | bytes 393224 | tf_op jit(solution)/shard_map/ppermute | solution.py:40
  38.5 6.2 %collective-permute-start.6 = (bf16[2,256,128]{2,1,0:T(8,128)(2,1)S(1)}, bf16[2,256,128]{2,1,0:T(8,128)(2,1)S(1)}, u32[]{:S(2)}, u32[]{:S(2)}) collective-permute-start(bf16[2,256,128]{2,1,0:T(8,128)(2,1)S(1)} %slice.74), channel_id=1, source_target_pairs={{0,7},{1,0},{2,1},{3,2},{4,3},{5,4},{6,5},{7,6},{8,15},{9,8},{10,9... | collective-permute-start | bytes 393224 | tf_op jit(solution)/shard_map/ppermute | solution.py:40
  50.2 3.3 %collective-permute-start.11 = (bf16[8,256,128]{2,1,0:T(8,128)(2,1)S(1)}, bf16[8,256,128]{2,1,0:T(8,128)(2,1)S(1)}, u32[]{:S(2)}, u32[]{:S(2)}) collective-permute-start(bf16[8,256,128]{2,1,0:T(8,128)(2,1)S(1)} %shard_map.77), channel_id=1, source_target_pairs={{0,8},{1,9},{2,10},{3,11},{4,12},{5,13},{6,14},{7,15},{8,0},{9,1},... | collective-permute-start | bytes 1572872 | tf_op jit(solution)/shard_map/ppermute | solution.py:40
  53.5 10.6 %copy-start = (f32[128]{0:T(128)S(1)}, f32[128]{0:T(128)}, u32[]{:S(2)}) copy-start(f32[128]{0:T(128)} %param.6) | copy-start | bytes 1540
  53.7 7.9 %collective-permute-start.12 = (bf16[2,256,128]{2,1,0:T(8,128)(2,1)S(1)}, bf16[2,256,128]{2,1,0:T(8,128)(2,1)S(1)}, u32[]{:S(2)}, u32[]{:S(2)}) collective-permute-start(bf16[2,256,128]{2,1,0:T(8,128)(2,1)S(1)} %get-tuple-element.114), channel_id=1, source_target_pairs={{0,32},{1,33},{2,34},{3,35},{4,36},{5,37},{6,38},{7,39},{8,40},{9,... | collective-permute-start | bytes 393224 | tf_op jit(solution)/shard_map/ppermute | solution.py:40
  53.8 9.1 %collective-permute-start.14 = (bf16[2,256,128]{2,1,0:T(8,128)(2,1)S(1)}, bf16[2,256,128]{2,1,0:T(8,128)(2,1)S(1)}, u32[]{:S(2)}, u32[]{:S(2)}) collective-permute-start(bf16[2,256,128]{2,1,0:T(8,128)(2,1)S(1)} %get-tuple-element.115), channel_id=1, source_target_pairs={{0,48},{1,49},{2,50},{3,51},{4,52},{5,53},{6,54},{7,55},{8,56},{9,... | collective-permute-start | bytes 393224 | tf_op jit(solution)/shard_map/ppermute | solution.py:40
  54.9 9.1 %collective-permute-start.13 = (bf16[2,256,128]{2,1,0:T(8,128)(2,1)S(1)}, bf16[2,256,128]{2,1,0:T(8,128)(2,1)S(1)}, u32[]{:S(2)}, u32[]{:S(2)}) collective-permute-start(bf16[2,256,128]{2,1,0:T(8,128)(2,1)S(1)} %get-tuple-element.116), channel_id=1, source_target_pairs={{0,16},{1,17},{2,18},{3,19},{4,20},{5,21},{6,22},{7,23},{8,24},{9,... | collective-permute-start | bytes 393224 | tf_op jit(solution)/shard_map/ppermute | solution.py:40
  64.3 6.4 %collective-permute-start.17 = (bf16[2,256,128]{2,1,0:T(8,128)(2,1)S(1)}, bf16[2,256,128]{2,1,0:T(8,128)(2,1)S(1)}, u32[]{:S(2)}, u32[]{:S(2)}) collective-permute-start(bf16[2,256,128]{2,1,0:T(8,128)(2,1)S(1)} %get-tuple-element.118.refs_2_.refs_0_), channel_id=1, source_target_pairs={{0,48},{1,49},{2,50},{3,51},{4,52},{5,53},{6,54},{7,55},{8,56},{9,... | collective-permute-start | bytes 393224 | tf_op jit(solution)/shard_map/ppermute | solution.py:40
  65.0 7.9 %collective-permute-start.16 = (bf16[2,256,128]{2,1,0:T(8,128)(2,1)S(1)}, bf16[2,256,128]{2,1,0:T(8,128)(2,1)S(1)}, u32[]{:S(2)}, u32[]{:S(2)}) collective-permute-start(bf16[2,256,128]{2,1,0:T(8,128)(2,1)S(1)} %get-tuple-element.118.refs_2_.refs_0_), channel_id=1, source_target_pairs={{0,32},{1,33},{2,34},{3,35},{4,36},{5,37},{6,38},{7,39},{8,40},{9,... | collective-permute-start | bytes 393224 | tf_op jit(solution)/shard_map/ppermute | solution.py:40
  66.1 7.7 %collective-permute-start.15 = (bf16[2,256,128]{2,1,0:T(8,128)(2,1)S(1)}, bf16[2,256,128]{2,1,0:T(8,128)(2,1)S(1)}, u32[]{:S(2)}, u32[]{:S(2)}) collective-permute-start(bf16[2,256,128]{2,1,0:T(8,128)(2,1)S(1)} %get-tuple-element.118.refs_2_.refs_0_), channel_id=1, source_target_pairs={{0,16},{1,17},{2,18},{3,19},{4,20},{5,21},{6,22},{7,23},{8,24},{9,... | collective-permute-start | bytes 393224 | tf_op jit(solution)/shard_map/ppermute | solution.py:40
  67.8 6.0 %collective-permute-start.18 = (bf16[2,256,128]{2,1,0:T(8,128)(2,1)S(1)}, bf16[2,256,128]{2,1,0:T(8,128)(2,1)S(1)}, u32[]{:S(2)}, u32[]{:S(2)}) collective-permute-start(bf16[2,256,128]{2,1,0:T(8,128)(2,1)S(1)} %get-tuple-element.118.refs_2_.refs_0_), channel_id=1, source_target_pairs={{0,8},{1,9},{2,10},{3,11},{4,12},{5,13},{6,14},{7,15},{8,0},{9,1},... | collective-permute-start | bytes 393224 | tf_op jit(solution)/shard_map/ppermute | solution.py:40
  70.7 3.1 %collective-permute-start.21 = (bf16[2,256,128]{2,1,0:T(8,128)(2,1)S(1)}, bf16[2,256,128]{2,1,0:T(8,128)(2,1)S(1)}, u32[]{:S(2)}, u32[]{:S(2)}) collective-permute-start(bf16[2,256,128]{2,1,0:T(8,128)(2,1)S(1)} %collective-permute-done.17.refs_5_.refs_3_), channel_id=1, source_target_pairs={{0,8},{1,9},{2,10},{3,11},{4,12},{5,13},{6,14},{7,15},{8,0},{9,1},... | collective-permute-start | bytes 393224 | tf_op jit(solution)/shard_map/ppermute | solution.py:40
  72.9 1.3 %collective-permute-start.20 = (bf16[2,256,128]{2,1,0:T(8,128)(2,1)S(1)}, bf16[2,256,128]{2,1,0:T(8,128)(2,1)S(1)}, u32[]{:S(2)}, u32[]{:S(2)}) collective-permute-start(bf16[2,256,128]{2,1,0:T(8,128)(2,1)S(1)} %collective-permute-done.16.refs_4_.refs_2_), channel_id=1, source_target_pairs={{0,8},{1,9},{2,10},{3,11},{4,12},{5,13},{6,14},{7,15},{8,0},{9,1},... | collective-permute-start | bytes 393224 | tf_op jit(solution)/shard_map/ppermute | solution.py:40
  73.8 1.3 %collective-permute-start.19 = (bf16[2,256,128]{2,1,0:T(8,128)(2,1)S(1)}, bf16[2,256,128]{2,1,0:T(8,128)(2,1)S(1)}, u32[]{:S(2)}, u32[]{:S(2)}) collective-permute-start(bf16[2,256,128]{2,1,0:T(8,128)(2,1)S(1)} %collective-permute-done.15.refs_3_.refs_1_), channel_id=1, source_target_pairs={{0,8},{1,9},{2,10},{3,11},{4,12},{5,13},{6,14},{7,15},{8,0},{9,1},... | collective-permute-start | bytes 393224 | tf_op jit(solution)/shard_map/ppermute | solution.py:40
  83.8 7.2 %collective-permute-start.22 = (bf16[2,256,128]{2,1,0:T(8,128)(2,1)S(1)}, bf16[2,256,128]{2,1,0:T(8,128)(2,1)S(1)}, u32[]{:S(2)}, u32[]{:S(2)}) collective-permute-start(bf16[2,256,128]{2,1,0:T(8,128)(2,1)S(1)} %get-tuple-element.82), channel_id=1, source_target_pairs={{0,1},{1,2},{2,3},{3,4},{4,5},{5,6},{6,7},{7,0},{8,9},{9,10},{10,1... | collective-permute-start | bytes 393224 | tf_op jit(solution)/shard_map/ppermute | solution.py:40
  84.2 6.8 %collective-permute-start.23 = (bf16[2,256,128]{2,1,0:T(8,128)(2,1)S(1)}, bf16[2,256,128]{2,1,0:T(8,128)(2,1)S(1)}, u32[]{:S(2)}, u32[]{:S(2)}) collective-permute-start(bf16[2,256,128]{2,1,0:T(8,128)(2,1)S(1)} %get-tuple-element.85), channel_id=1, source_target_pairs={{0,7},{1,0},{2,1},{3,2},{4,3},{5,4},{6,5},{7,6},{8,15},{9,8},{10,9... | collective-permute-start | bytes 393224 | tf_op jit(solution)/shard_map/ppermute | solution.py:40
  91.1 10.5 %collective-permute-start.24 = (bf16[4,256,128]{2,1,0:T(8,128)(2,1)S(1)}, bf16[4,256,128]{2,1,0:T(8,128)(2,1)S(1)}, u32[]{:S(2)}, u32[]{:S(2)}) collective-permute-start(bf16[4,256,128]{2,1,0:T(8,128)(2,1)S(1)} %pad_maximum_fusion), channel_id=1, source_target_pairs={{0,1},{1,2},{2,3},{3,4},{4,5},{5,6},{6,7},{7,0},{8,9},{9,10},{10,1... | collective-permute-start | bytes 786440 | tf_op jit(solution)/shard_map/ppermute | solution.py:40
  91.3 10.3 %collective-permute-start.25 = (bf16[4,256,128]{2,1,0:T(8,128)(2,1)S(1)}, bf16[4,256,128]{2,1,0:T(8,128)(2,1)S(1)}, u32[]{:S(2)}, u32[]{:S(2)}) collective-permute-start(bf16[4,256,128]{2,1,0:T(8,128)(2,1)S(1)} %pad_maximum_fusion.1), channel_id=1, source_target_pairs={{0,7},{1,0},{2,1},{3,2},{4,3},{5,4},{6,5},{7,6},{8,15},{9,8},{10,9... | collective-permute-start | bytes 786440 | tf_op jit(solution)/shard_map/ppermute | solution.py:40
  96.4 9.2 %collective-permute-start.27 = (bf16[28,32,128]{2,1,0:T(8,128)(2,1)S(1)}, bf16[28,32,128]{2,1,0:T(8,128)(2,1)S(1)}, u32[]{:S(2)}, u32[]{:S(2)}) collective-permute-start(bf16[28,32,128]{2,1,0:T(8,128)(2,1)S(1)} %get-tuple-element.100), channel_id=1, source_target_pairs={{0,64},{1,65},{2,66},{3,67},{4,68},{5,69},{6,70},{7,71},{8,72},{9,... | collective-permute-start | bytes 688136 | tf_op jit(solution)/shard_map/ppermute | solution.py:40
  98.8 10.9 %collective-permute-start.28 = (bf16[28,32,128]{2,1,0:T(8,128)(2,1)S(1)}, bf16[28,32,128]{2,1,0:T(8,128)(2,1)S(1)}, u32[]{:S(2)}, u32[]{:S(2)}) collective-permute-start(bf16[28,32,128]{2,1,0:T(8,128)(2,1)S(1)} %get-tuple-element.101), channel_id=1, source_target_pairs={{0,128},{1,129},{2,130},{3,131},{4,132},{5,133},{6,134},{7,135},{8... | collective-permute-start | bytes 688136 | tf_op jit(solution)/shard_map/ppermute | solution.py:40
  100.3 9.4 %collective-permute-start.29 = (bf16[28,32,128]{2,1,0:T(8,128)(2,1)S(1)}, bf16[28,32,128]{2,1,0:T(8,128)(2,1)S(1)}, u32[]{:S(2)}, u32[]{:S(2)}) collective-permute-start(bf16[28,32,128]{2,1,0:T(8,128)(2,1)S(1)} %get-tuple-element.102), channel_id=1, source_target_pairs={{0,192},{1,193},{2,194},{3,195},{4,196},{5,197},{6,198},{7,199},{8... | collective-permute-start | bytes 688136 | tf_op jit(solution)/shard_map/ppermute | solution.py:40
  101.8 8.0 %collective-permute-start.26 = (bf16[256,128]{1,0:T(8,128)(2,1)S(1)}, bf16[256,128]{1,0:T(8,128)(2,1)S(1)}, u32[]{:S(2)}, u32[]{:S(2)}) collective-permute-start(bf16[256,128]{1,0:T(8,128)(2,1)S(1)} %get-tuple-element.121), channel_id=1, source_target_pairs={{0,8},{1,9},{2,10},{3,11},{4,12},{5,13},{6,14},{7,15},{8,16},{9,17... | collective-permute-start | bytes 196616 | tf_op jit(solution)/shard_map/ppermute | solution.py:40
  101.9 14.8 %collective-permute-start.30 = (bf16[2,256,128]{2,1,0:T(8,128)(2,1)S(1)}, bf16[2,256,128]{2,1,0:T(8,128)(2,1)S(1)}, u32[]{:S(2)}, u32[]{:S(2)}) collective-permute-start(bf16[2,256,128]{2,1,0:T(8,128)(2,1)S(1)} %get-tuple-element.104), channel_id=1, source_target_pairs={{0,0},{1,8},{2,16},{3,24},{4,32},{5,40},{6,48},{7,56},{8,36},{9,44... | collective-permute-start | bytes 393224 | tf_op jit(solution)/shard_map/ppermute | solution.py:40
  105.6 20.7 %collective-permute-start.31 = (bf16[2,256,128]{2,1,0:T(8,128)(2,1)S(1)}, bf16[2,256,128]{2,1,0:T(8,128)(2,1)S(1)}, u32[]{:S(2)}, u32[]{:S(2)}) collective-permute-start(bf16[2,256,128]{2,1,0:T(8,128)(2,1)S(1)} %get-tuple-element.105), channel_id=1, source_target_pairs={{0,32},{1,40},{2,48},{3,56},{4,0},{5,8},{6,16},{7,24},{8,4},{9,12}... | collective-permute-start | bytes 393224 | tf_op jit(solution)/shard_map/ppermute | solution.py:40
  109.9 17.3 %collective-permute-start.33 = (bf16[27,32,128]{2,1,0:T(8,128)(2,1)S(1)}, bf16[27,32,128]{2,1,0:T(8,128)(2,1)S(1)}, u32[]{:S(2)}, u32[]{:S(2)}) collective-permute-start(bf16[27,32,128]{2,1,0:T(8,128)(2,1)S(1)} %slice.143), channel_id=1, source_target_pairs={{0,0},{1,1},{2,2},{3,3},{4,4},{5,5},{6,6},{7,7},{8,128},{9,129},{1... | collective-permute-start | bytes 663560 | tf_op jit(solution)/shard_map/ppermute | solution.py:40
  126.4 3.8 %collective-permute-start.32 = (bf16[256,128]{1,0:T(8,128)(2,1)S(1)}, bf16[256,128]{1,0:T(8,128)(2,1)S(1)}, u32[]{:S(2)}, u32[]{:S(2)}) collective-permute-start(bf16[256,128]{1,0:T(8,128)(2,1)S(1)} %get-tuple-element.119), channel_id=1, source_target_pairs={{0,8},{1,9},{2,10},{3,11},{4,12},{5,13},{6,14},{7,15},{8,16},{9,17... | collective-permute-start | bytes 196616 | tf_op jit(solution)/shard_map/ppermute | solution.py:40

commit v7 on v6

--- a/solution.py
+++ b/solution.py
@@ -321,53 +321,46 @@
         flops,
     )
     where, terms = lax.optimization_barrier((where, terms))
-    def parts(steps, where, kinds):
+    def parts(steps, where, outs):
         return call(
             lambda *refs: product_kernel(lambda where: ring_pairs(where, steps), *refs),
             where,
             [slope_columns, back_weights],
-            [shaped((2, FACE, size), kind) for kind in kinds],
+            outs,
             [],
             flops * len(steps) // NZ,
         )
 
-    up, down = parts((2, -2), where, [bf16, bf16])
+    received = [permuted(terms[2], lambda x, q, z: at(x + 2, q, z))]
+    up, down = parts((2, -3, -2, 3), where, [shaped((4, FACE, size), bf16)] * 2)
     up, down, where = lax.optimization_barrier((up, down, where))
-    up, down = along_z(up, 1).astype(f32), along_z(down, -1).astype(f32)
-    above, far_above, below, far_below = parts((1, -3, -1, 3), where, [f32, bf16, f32, bf16])
-    above, below, where = lax.optimization_barrier((above, below, where))
-    above = jnp.concatenate([(above + up).astype(bf16), far_above])
-    below = jnp.concatenate([(below + down).astype(bf16), far_below])
-    above, below, where = lax.optimization_barrier((above, below, where))
-    near, beyond = parts((0, 4), where, [f32, f32])
-    near, beyond, terms = lax.optimization_barrier((near, beyond, terms))
-    received = [
-        permuted(terms[r], lambda x, q, z: at(x + r, q, z)) for r in range(1, NX)
-    ]
-    above, below = along_z(above, 1).astype(f32), along_z(below, -1).astype(f32)
-    near = (near + above[:2] + below[:2]).astype(bf16)
-    beyond = (beyond + above[2:] + below[2:]).astype(bf16)
-
-    near, beyond, activated = lax.optimization_barrier((near, beyond, activated))
-
-    def next_slab(plane):
-        return permuted(plane, lambda x, q, z: device(NQ * x + q + 1, z))
-
-    def home(step):
-        return lambda x, q, z: device(NQ * x + (z - group(q) - step) % NZ, group(q))
-
-    near, beyond = permuted(near, home(0)).astype(f32), permuted(beyond, home(4)).astype(f32)
-    summed = (near + beyond).astype(bf16)
-    shifted, received = lax.optimization_barrier((next_slab(activated[1]), received))
+    up, down = along_z(up, 1), along_z(down, -1)
+    above, below, beyond, summed = parts((1, -1, 4, 0), where, [shaped((2, FACE, size), f32)] * 4)
+    above, below, beyond, summed, *later = lax.optimization_barrier(
+        (above, below, beyond, summed, terms[1], terms[3])
+    )
+    received.append(permuted(later[0], lambda x, q, z: at(x + 1, q, z)))
+    received.append(permuted(later[1], lambda x, q, z: at(x + 3, q, z)))
+    above = (above + up[:2].astype(f32)).astype(bf16)
+    below = (below + down[:2].astype(f32)).astype(bf16)
+    beyond = (beyond + up[2:].astype(f32) + down[2:].astype(f32)).astype(bf16)
+    beyond, above, below = along_z(beyond, 4), along_z(above, 1), along_z(below, -1)
     held = sum((piece.astype(f32) for piece in received), terms[0].astype(f32))
     grad_bias = held[27, 0] + held[27, 1]
     grad_filters = permuted(
         held[:27].astype(bf16), lambda x, q, z: device(NX * group(q) + swapped(x), z)
     ).astype(f32)
-
+    summed = summed + beyond.astype(f32) + above.astype(f32) + below.astype(f32)
+    summed, activated = lax.optimization_barrier((summed.astype(bf16), activated))
+
+    def home(half):
+        return lambda x, q, z: device(NQ * x + (z - group(q)) % NZ + half, group(q))
+
+    first, second = permuted(summed[0], home(0)), permuted(summed[1], home(1))
+    shifted = permuted(activated[1], lambda x, q, z: device(NQ * x + q + 1, z))
     activated = jnp.stack([shifted, activated[0]])
-    second, grad_filters = lax.optimization_barrier((next_slab(summed[1]), grad_filters))
-    grad_input = jnp.stack([second, summed[0]])
+    second, grad_filters = lax.optimization_barrier((second, grad_filters))
+    grad_input = jnp.stack([second, first])
     shape = (2, GRID, GRID)
     return (
         activated.reshape(*shape, out_size),

time: 132 us -> 130 us (0.985)
  waiting for transfers between devices: 40.8 us -> 33.9 us
  starting transfers between devices: 61 us -> 67.5 us
    ppermute x34, waiting for transfers between devices: 40.8 us -> 33.9 us  [permuted(): return lax.ppermute(array, ('space', 'chan'), pairs)]
    ppermute x34, starting transfers between devices: 61 us -> 67.5 us  [permuted(): return lax.ppermute(array, ('space', 'chan'), pairs)]
    pallas_call x10 -> x9, Pallas kernels: 23.2 us -> 22.5 us  [call(): pl.pallas_call(kernel, out_shape=outs, in_specs=[pl.BlockSpec(memory_spac...]
  transfers between devices with their start and end apart: 34 -> 34, of which waited for: 17 -> 15; matrix products, arithmetic and copies ran while one was open for 2% -> 2% of each run, Pallas kernels for 8% -> 7%
where the time goes in v7:
time: 130 us; the launch traced here: 129 us
  starting transfers between devices  67.5 us (52%)
  waiting for transfers between devices  33.9 us (26%)
  Pallas kernels  22.5 us (17%)
  other arithmetic  3.55 us (3%)
    ppermute x34, starting transfers between devices, permuted(): return lax.ppermute(array, ('space', 'chan'), pairs)  67.5 us
    ppermute x34, waiting for transfers between devices, permuted(): return lax.ppermute(array, ('space', 'chan'), pairs)  33.9 us
    pallas_call x9, Pallas kernels, call(): pl.pallas_call(kernel, out_shape=outs, in_specs=[pl.BlockSpec(memory_spac...  22.5 us
  transfers between devices with their start and end apart: 34, of which 15 were waited for; matrix products, arithmetic and copies ran while one was open for 2% of the time, Pallas kernels for 7%

profile of v7, /device:TPU:16, one launch (start us, length us, event | category | flops | bytes accessed | tf_op | source)
XLA Modules:
  0.0 129.4 jit_solution(1277487708521233767)
XLA Ops:
  0.6 1.0 fusion.14
  1.7 2.5 %collective-permute-done = bf16[2,16,16,128]{3,2,1,0:T(8,128)(2,1)S(1)} collective-permute-done((bf16[2,16,16,128]{3,2,1,0:T(8,128)(2,1)S(1)}, bf16[2,16,16,128]{3,2,1,0:T(8,128)(2,1)S(1)}, u32[]{:S(2)}, u32[]{:S(2)}) %collective-permute-start) | collective-permute-done | bytes 131104 | tf_op jit(solution)/shard_map/ppermute | solution.py:40
  4.3 13.5 %collective-permute-start.1 = (bf16[2,256,128]{2,1,0:T(8,128)(2,1)S(1)}, bf16[2,256,128]{2,1,0:T(8,128)(2,1)S(1)}, u32[]{:S(2)}, u32[]{:S(2)}) collective-permute-start(bf16[2,256,128]{2,1,0:T(8,128)(2,1)S(1)} %bitcast.22), channel_id=1, source_target_pairs={{0,0},{1,17},{2,34},{3,51},{4,12},{5,29},{6,46},{7,63},{8,1},{9,18... | collective-permute-start | bytes 393224 | tf_op jit(solution)/shard_map/ppermute | solution.py:40
  17.8 1.9 %collective-permute-start.2 = (bf16[2,256,128]{2,1,0:T(8,128)(2,1)S(1)}, bf16[2,256,128]{2,1,0:T(8,128)(2,1)S(1)}, u32[]{:S(2)}, u32[]{:S(2)}) collective-permute-start(bf16[2,256,128]{2,1,0:T(8,128)(2,1)S(1)} %bitcast.23), channel_id=1, source_target_pairs={{0,4},{1,21},{2,38},{3,55},{4,8},{5,25},{6,42},{7,59},{8,5},{9,22}... | collective-permute-start | bytes 393224 | tf_op jit(solution)/shard_map/ppermute | solution.py:40
  19.7 1.9 %collective-permute-start.5 = (bf16[27,32,128]{2,1,0:T(8,128)(2,1)}, bf16[27,32,128]{2,1,0:T(8,128)(2,1)S(1)}, u32[]{:S(2)}, u32[]{:S(2)}) collective-permute-start(bf16[27,32,128]{2,1,0:T(8,128)(2,1)} %bitcast.27), channel_id=1, source_target_pairs={{0,0},{1,1},{2,2},{3,3},{4,4},{5,5},{6,6},{7,7},{8,128},{9,129},{1... | collective-permute-start | bytes 663560 | tf_op jit(solution)/shard_map/ppermute | solution.py:40
  21.7 4.8 %collective-permute-done.2 = bf16[2,256,128]{2,1,0:T(8,128)(2,1)S(1)} collective-permute-done((bf16[2,256,128]{2,1,0:T(8,128)(2,1)S(1)}, bf16[2,256,128]{2,1,0:T(8,128)(2,1)S(1)}, u32[]{:S(2)}, u32[]{:S(2)}) %collective-permute-start.2) | collective-permute-done | bytes 131104 | tf_op jit(solution)/shard_map/ppermute | solution.py:40
  26.5 6.7 %collective-permute-start.3 = (bf16[4,256,128]{2,1,0:T(8,128)(2,1)S(1)}, bf16[4,256,128]{2,1,0:T(8,128)(2,1)S(1)}, u32[]{:S(2)}, u32[]{:S(2)}) collective-permute-start(bf16[4,256,128]{2,1,0:T(8,128)(2,1)S(1)} %constant_dynamic-update-slice_fusion.refs_0_), channel_id=1, source_target_pairs={{0,7},{1,0},{2,1},{3,2},{4,3},{5,4},{6,5},{7,6},{8,15},{9,8},{10,9... | collective-permute-start | bytes 786440 | tf_op jit(solution)/shard_map/ppermute | solution.py:40
  33.3 0.9 collective-permute-start.9
  34.2 2.3 %collective-permute-start.8 = (bf16[27,32,128]{2,1,0:T(8,128)(2,1)S(1)}, bf16[27,32,128]{2,1,0:T(8,128)(2,1)S(1)}, u32[]{:S(2)}, u32[]{:S(2)}) collective-permute-start(bf16[27,32,128]{2,1,0:T(8,128)(2,1)S(1)} %collective-permute-done.5.refs_1_), channel_id=1, source_target_pairs={{0,192},{1,193},{2,194},{3,195},{4,196},{5,197},{6,198},{7,199},{8... | collective-permute-start | bytes 663560 | tf_op jit(solution)/shard_map/ppermute | solution.py:40
  36.5 1.9 %collective-permute-start.10 = (bf16[27,32,128]{2,1,0:T(8,128)(2,1)S(1)}, bf16[27,32,128]{2,1,0:T(8,128)(2,1)S(1)}, u32[]{:S(2)}, u32[]{:S(2)}) collective-permute-start(bf16[27,32,128]{2,1,0:T(8,128)(2,1)S(1)} %collective-permute-done.5.refs_1_), channel_id=1, source_target_pairs={{0,128},{1,129},{2,130},{3,131},{4,132},{5,133},{6,134},{7,135},{8... | collective-permute-start | bytes 663560 | tf_op jit(solution)/shard_map/ppermute | solution.py:40
  38.5 3.2 %collective-permute-start.6 = (bf16[2,256,128]{2,1,0:T(8,128)(2,1)S(1)}, bf16[2,256,128]{2,1,0:T(8,128)(2,1)S(1)}, u32[]{:S(2)}, u32[]{:S(2)}) collective-permute-start(bf16[2,256,128]{2,1,0:T(8,128)(2,1)S(1)} %slice.74), channel_id=1, source_target_pairs={{0,7},{1,0},{2,1},{3,2},{4,3},{5,4},{6,5},{7,6},{8,15},{9,8},{10,9... | collective-permute-start | bytes 393224 | tf_op jit(solution)/shard_map/ppermute | solution.py:40
  41.8 2.9 %collective-permute-done.7.refs_4_ = bf16[2,256,128]{2,1,0:T(8,128)(2,1)S(1)} collective-permute-done((bf16[2,256,128]{2,1,0:T(8,128)(2,1)S(1)}, bf16[2,256,128]{2,1,0:T(8,128)(2,1)S(1)}, u32[]{:S(2)}, u32[]{:S(2)}) %collective-permute-start.7) | collective-permute-done | bytes 131104 | tf_op jit(solution)/shard_map/ppermute | solution.py:40
  44.7 1.4 %shard_map.75.refs_1_ = bf16[18,288,384]{2,1,0:T(8,128)(2,1)S(1)} custom-call(s32[2]{0:T(128)S(1)} %pad_add_fusion.where.refs_0_, bf16[4,256,128]{2,1,0:T(8,128)(2,1)S(1)} %constant_dynamic-update-slice_fusion.refs_0_, bf16[4,256,128]{2,1,0:T(8,128)(2,1)S(1)} %collective-permute-done.3.refs_1_, bf16[4,256,128]{2,1,0:T(8,128)(2,1)S(1)} %collective-permute-done.4.refs_2_, ...), custom_call_target="tpu_custom_call" | custom-call | bytes 5029888 | tf_op jit(solution)/shard_map/pallas_call | solution.py:209
  46.2 0.9 shard_map.76.refs_2_
  47.1 3.1 %shard_map.77 = bf16[8,256,128]{2,1,0:T(8,128)(2,1)S(1)} custom-call(s32[2]{0:T(128)S(1)} %pad_add_fusion.where.refs_0_, bf16[18,288,384]{2,1,0:T(8,128)(2,1)S(1)} %shard_map.75.refs_1_, bf16[4608,256]{1,0:T(8,128)(2,1)S(1)} %shard_map.76.refs_2_), custom_call_target="tpu_custom_call" | custom-call | flops 1811939328 | bytes 6864896 | tf_op jit(solution)/shard_map/pallas_call | solution.py:209
  50.3 3.1 %shard_map.78 = (f32[2,256,128]{2,1,0:T(8,128)S(1)}, f32[2,256,128]{2,1,0:T(8,128)S(1)}, f32[2,256,128]{2,1,0:T(8,128)S(1)}, f32[2,256,128]{2,1,0:T(8,128)S(1)}) custom-call(s32[2]{0:T(128)S(1)} %pad_add_fusion.where.refs_0_, bf16[18,288,384]{2,1,0:T(8,128)(2,1)S(1)} %shard_map.75.refs_1_, bf16[4608,256]{1,0:T(8,128)(2,1)S(1)} %shard_map.76.refs_2_), custom_call_target="tpu_custom_call" | custom-call | flops 1811939328 | bytes 7389184 | tf_op jit(solution)/shard_map/pallas_call | solution.py:209
  53.8 1.1 collective-permute-start.14
  54.8 1.3 %collective-permute-start.13 = (bf16[2,256,128]{2,1,0:T(8,128)(2,1)S(1)}, bf16[2,256,128]{2,1,0:T(8,128)(2,1)S(1)}, u32[]{:S(2)}, u32[]{:S(2)}) collective-permute-start(bf16[2,256,128]{2,1,0:T(8,128)(2,1)S(1)} %get-tuple-element.88), channel_id=1, source_target_pairs={{0,16},{1,17},{2,18},{3,19},{4,20},{5,21},{6,22},{7,23},{8,24},{9,... | collective-permute-start | bytes 393224 | tf_op jit(solution)/shard_map/ppermute | solution.py:40
  56.2 1.0 shard_map.79.refs_2_
  57.2 4.4 %collective-permute-done.12 = bf16[2,256,128]{2,1,0:T(8,128)(2,1)S(1)} collective-permute-done((bf16[2,256,128]{2,1,0:T(8,128)(2,1)S(1)}, bf16[2,256,128]{2,1,0:T(8,128)(2,1)S(1)}, u32[]{:S(2)}, u32[]{:S(2)}) %collective-permute-start.12) | collective-permute-done | bytes 131104 | tf_op jit(solution)/shard_map/ppermute | solution.py:40
  61.6 1.3 collective-permute-done.14
  62.8 1.1 collective-permute-done.13
  64.3 0.7 collective-permute-start.17
  65.0 1.1 collective-permute-start.16
  66.1 1.7 %collective-permute-start.15 = (bf16[2,256,128]{2,1,0:T(8,128)(2,1)S(1)}, bf16[2,256,128]{2,1,0:T(8,128)(2,1)S(1)}, u32[]{:S(2)}, u32[]{:S(2)}) collective-permute-start(bf16[2,256,128]{2,1,0:T(8,128)(2,1)S(1)} %get-tuple-element.90.refs_2_.refs_0_), channel_id=1, source_target_pairs={{0,16},{1,17},{2,18},{3,19},{4,20},{5,21},{6,22},{7,23},{8,24},{9,... | collective-permute-start | bytes 393224 | tf_op jit(solution)/shard_map/ppermute | solution.py:40
  67.8 2.9 %collective-permute-done.17.refs_5_.refs_3_ = bf16[2,256,128]{2,1,0:T(8,128)(2,1)S(1)} collective-permute-done((bf16[2,256,128]{2,1,0:T(8,128)(2,1)S(1)}, bf16[2,256,128]{2,1,0:T(8,128)(2,1)S(1)}, u32[]{:S(2)}, u32[]{:S(2)}) %collective-permute-start.17) | collective-permute-done | bytes 131104 | tf_op jit(solution)/shard_map/ppermute | solution.py:40
  70.7 2.1 %collective-permute-done.16.refs_4_.refs_2_ = bf16[2,256,128]{2,1,0:T(8,128)(2,1)S(1)} collective-permute-done((bf16[2,256,128]{2,1,0:T(8,128)(2,1)S(1)}, bf16[2,256,128]{2,1,0:T(8,128)(2,1)S(1)}, u32[]{:S(2)}, u32[]{:S(2)}) %collective-permute-start.16) | collective-permute-done | bytes 131104 | tf_op jit(solution)/shard_map/ppermute | solution.py:40
  72.9 0.9 collective-permute-done.15.refs_3_.refs_1_
  74.2 0.9 collective-permute-done.19.refs_7_.refs_5_
  75.1 5.2 %shard_map.80 = (bf16[28,32,128]{2,1,0:T(8,128)(2,1)S(1)}, bf16[28,32,128]{2,1,0:T(8,128)(2,1)S(1)}, bf16[28,32,128]{2,1,0:T(8,128)(2,1)S(1)}, bf16[28,32,128]{2,1,0:T(8,128)(2,1)S(1)}) custom-call(s32[2]{0:T(128)S(1)} %pad_add_fusion.where.refs_0_, bf16[18,288,384]{2,1,0:T(8,128)(2,1)S(1)} %shard_map.75.refs_1_, ...), custom_call_target="tpu_custom_call" | custom-call | flops 3623878656 | bytes 5947392 | tf_op jit(solution)/shard_map/pallas_call | solution.py:209
  80.4 1.4 %shard_map.81.refs_1_ = bf16[18,288,384]{2,1,0:T(8,128)(2,1)S(1)} custom-call(s32[2]{0:T(128)S(1)} %pad_add_fusion.where.refs_0_, bf16[2,256,128]{2,1,0:T(8,128)(2,1)S(1)} %get-tuple-element.90.refs_2_.refs_0_, bf16[2,256,128]{2,1,0:T(8,128)(2,1)S(1)} %collective-permute-done.15.refs_3_.refs_1_, ...), custom_call_target="tpu_custom_call" | custom-call | bytes 5029888 | tf_op jit(solution)/shard_map/pallas_call | solution.py:209
  81.8 3.1 %shard_map.82 = (bf16[4,256,128]{2,1,0:T(8,128)(2,1)S(1)}, bf16[4,256,128]{2,1,0:T(8,128)(2,1)S(1)}) custom-call(s32[2]{0:T(128)S(1)} %pad_add_fusion.where.refs_0_, bf16[18,288,384]{2,1,0:T(8,128)(2,1)S(1)} %shard_map.81.refs_1_, bf16[4608,256]{1,0:T(8,128)(2,1)S(1)} %shard_map.79.refs_2_), custom_call_target="tpu_custom_call" | custom-call | flops 1811939328 | bytes 6864896 | tf_op jit(solution)/shard_map/pallas_call | solution.py:209
  84.9 0.7 collective-permute-start.22
  85.6 3.0 %collective-permute-start.23 = (bf16[4,256,128]{2,1,0:T(8,128)(2,1)S(1)}, bf16[4,256,128]{2,1,0:T(8,128)(2,1)S(1)}, u32[]{:S(2)}, u32[]{:S(2)}) collective-permute-start(bf16[4,256,128]{2,1,0:T(8,128)(2,1)S(1)} %get-tuple-element.75), channel_id=1, source_target_pairs={{0,7},{1,0},{2,1},{3,2},{4,3},{5,4},{6,5},{7,6},{8,15},{9,8},{10,9... | collective-permute-start | bytes 786440 | tf_op jit(solution)/shard_map/ppermute | solution.py:40
  88.6 2.3 %collective-permute-start.29 = (bf16[28,32,128]{2,1,0:T(8,128)(2,1)S(1)}, bf16[28,32,128]{2,1,0:T(8,128)(2,1)S(1)}, u32[]{:S(2)}, u32[]{:S(2)}) collective-permute-start(bf16[28,32,128]{2,1,0:T(8,128)(2,1)S(1)} %get-tuple-element.81), channel_id=1, source_target_pairs={{0,128},{1,129},{2,130},{3,131},{4,132},{5,133},{6,134},{7,135},{8... | collective-permute-start | bytes 688136 | tf_op jit(solution)/shard_map/ppermute | solution.py:40
  91.0 3.1 %shard_map.83 = (f32[2,256,128]{2,1,0:T(8,128)S(1)}, f32[2,256,128]{2,1,0:T(8,128)S(1)}, f32[2,256,128]{2,1,0:T(8,128)S(1)}, f32[2,256,128]{2,1,0:T(8,128)S(1)}) custom-call(s32[2]{0:T(128)S(1)} %pad_add_fusion.where.refs_0_, bf16[18,288,384]{2,1,0:T(8,128)(2,1)S(1)} %shard_map.81.refs_1_, bf16[4608,256]{1,0:T(8,128)(2,1)S(1)} %shard_map.79.refs_2_), custom_call_target="tpu_custom_call" | custom-call | flops 1811939328 | bytes 7389184 | tf_op jit(solution)/shard_map/pallas_call | solution.py:209
  94.1 0.9 collective-permute-start.30
  95.1 2.4 %collective-permute-start.31 = (bf16[28,32,128]{2,1,0:T(8,128)(2,1)S(1)}, bf16[28,32,128]{2,1,0:T(8,128)(2,1)S(1)}, u32[]{:S(2)}, u32[]{:S(2)}) collective-permute-start(bf16[28,32,128]{2,1,0:T(8,128)(2,1)S(1)} %get-tuple-element.83), channel_id=1, source_target_pairs={{0,192},{1,193},{2,194},{3,195},{4,196},{5,197},{6,198},{7,199},{8... | collective-permute-start | bytes 688136 | tf_op jit(solution)/shard_map/ppermute | solution.py:40
  97.6 3.1 %collective-permute-start.24 = (bf16[2,256,128]{2,1,0:T(8,128)(2,1)S(1)}, bf16[2,256,128]{2,1,0:T(8,128)(2,1)S(1)}, u32[]{:S(2)}, u32[]{:S(2)}) collective-permute-start(bf16[2,256,128]{2,1,0:T(8,128)(2,1)S(1)} %get-tuple-element.91), channel_id=1, source_target_pairs={{0,4},{1,5},{2,6},{3,7},{4,0},{5,1},{6,2},{7,3},{8,12},{9,13},{10,... | collective-permute-start | bytes 393224 | tf_op jit(solution)/shard_map/ppermute | solution.py:40
  100.6 0.8 collective-permute-start.25
  101.5 2.4 %collective-permute-start.26 = (bf16[2,256,128]{2,1,0:T(8,128)(2,1)S(1)}, bf16[2,256,128]{2,1,0:T(8,128)(2,1)S(1)}, u32[]{:S(2)}, u32[]{:S(2)}) collective-permute-start(bf16[2,256,128]{2,1,0:T(8,128)(2,1)S(1)} %get-tuple-element.93), channel_id=1, source_target_pairs={{0,7},{1,0},{2,1},{3,2},{4,3},{5,4},{6,5},{7,6},{8,15},{9,8},{10,9... | collective-permute-start | bytes 393224 | tf_op jit(solution)/shard_map/ppermute | solution.py:40
  104.0 5.0 %collective-permute-start.32 = (bf16[27,32,128]{2,1,0:T(8,128)(2,1)S(1)}, bf16[27,32,128]{2,1,0:T(8,128)(2,1)S(1)}, u32[]{:S(2)}, u32[]{:S(2)}) collective-permute-start(bf16[27,32,128]{2,1,0:T(8,128)(2,1)S(1)} %slice.134), channel_id=1, source_target_pairs={{0,0},{1,1},{2,2},{3,3},{4,4},{5,5},{6,6},{7,7},{8,128},{9,129},{1... | collective-permute-start | bytes 663560 | tf_op jit(solution)/shard_map/ppermute | solution.py:40
  109.8 6.0 %collective-permute-start.28 = (bf16[256,128]{1,0:T(8,128)(2,1)S(1)}, bf16[256,128]{1,0:T(8,128)(2,1)S(1)}, u32[]{:S(2)}, u32[]{:S(2)}) collective-permute-start(bf16[256,128]{1,0:T(8,128)(2,1)S(1)} %get-tuple-element.94), channel_id=1, source_target_pairs={{0,8},{1,16},{2,24},{3,32},{4,40},{5,48},{6,56},{7,64},{8,44},{9,5... | collective-permute-start | bytes 196616 | tf_op jit(solution)/shard_map/ppermute | solution.py:40
  116.3 1.9 %collective-permute-start.33 = (bf16[256,128]{1,0:T(8,128)(2,1)S(1)}, bf16[256,128]{1,0:T(8,128)(2,1)S(1)}, u32[]{:S(2)}, u32[]{:S(2)}) collective-permute-start(bf16[256,128]{1,0:T(8,128)(2,1)S(1)} %get-tuple-element.95), channel_id=1, source_target_pairs={{0,0},{1,8},{2,16},{3,24},{4,32},{5,40},{6,48},{7,56},{8,36},{9,44... | collective-permute-start | bytes 196616 | tf_op jit(solution)/shard_map/ppermute | solution.py:40
  118.2 0.8 convert_element_type.108
  119.1 1.1 collective-permute-done.28
  120.2 0.7 pad_maximum_fusion.3
  120.8 7.9 %collective-permute-done.33 = bf16[256,128]{1,0:T(8,128)(2,1)S(1)} collective-permute-done((bf16[256,128]{1,0:T(8,128)(2,1)S(1)}, bf16[256,128]{1,0:T(8,128)(2,1)S(1)}, u32[]{:S(2)}, u32[]{:S(2)}) %collective-permute-start.33) | collective-permute-done | bytes 65568 | tf_op jit(solution)/shard_map/ppermute | solution.py:40
  (55 shorter events, 3.7 us)
Async XLA Ops:
  1.6 2.6 %collective-permute-start = (bf16[2,16,16,128]{3,2,1,0:T(8,128)(2,1)S(1)}, bf16[2,16,16,128]{3,2,1,0:T(8,128)(2,1)S(1)}, u32[]{:S(2)}, u32[]{:S(2)}) collective-permute-start(bf16[2,16,16,128]{3,2,1,0:T(8,128)(2,1)S(1)} %pad_maximum_fusion), channel_id=1, source_target_pairs={{0,248},{1,249},{2,250},{3,251},{4,252},{5,253},{6,254},{7,255},{8... | collective-permute-start | bytes 393224 | tf_op jit(solution)/shard_map/ppermute | solution.py:40
  4.3 17.4 %collective-permute-start.1 = (bf16[2,256,128]{2,1,0:T(8,128)(2,1)S(1)}, bf16[2,256,128]{2,1,0:T(8,128)(2,1)S(1)}, u32[]{:S(2)}, u32[]{:S(2)}) collective-permute-start(bf16[2,256,128]{2,1,0:T(8,128)(2,1)S(1)} %bitcast.22), channel_id=1, source_target_pairs={{0,0},{1,17},{2,34},{3,51},{4,12},{5,29},{6,46},{7,63},{8,1},{9,18... | collective-permute-start | bytes 393224 | tf_op jit(solution)/shard_map/ppermute | solution.py:40
  17.8 8.7 %collective-permute-start.2 = (bf16[2,256,128]{2,1,0:T(8,128)(2,1)S(1)}, bf16[2,256,128]{2,1,0:T(8,128)(2,1)S(1)}, u32[]{:S(2)}, u32[]{:S(2)}) collective-permute-start(bf16[2,256,128]{2,1,0:T(8,128)(2,1)S(1)} %bitcast.23), channel_id=1, source_target_pairs={{0,4},{1,21},{2,38},{3,55},{4,8},{5,25},{6,42},{7,59},{8,5},{9,22}... | collective-permute-start | bytes 393224 | tf_op jit(solution)/shard_map/ppermute | solution.py:40
  19.7 13.6 %collective-permute-start.5 = (bf16[27,32,128]{2,1,0:T(8,128)(2,1)}, bf16[27,32,128]{2,1,0:T(8,128)(2,1)S(1)}, u32[]{:S(2)}, u32[]{:S(2)}) collective-permute-start(bf16[27,32,128]{2,1,0:T(8,128)(2,1)} %bitcast.27), channel_id=1, source_target_pairs={{0,0},{1,1},{2,2},{3,3},{4,4},{5,5},{6,6},{7,7},{8,128},{9,129},{1... | collective-permute-start | bytes 663560 | tf_op jit(solution)/shard_map/ppermute | solution.py:40
  26.5 12.0 %collective-permute-start.4 = (bf16[4,256,128]{2,1,0:T(8,128)(2,1)S(1)}, bf16[4,256,128]{2,1,0:T(8,128)(2,1)S(1)}, u32[]{:S(2)}, u32[]{:S(2)}) collective-permute-start(bf16[4,256,128]{2,1,0:T(8,128)(2,1)S(1)} %constant_dynamic-update-slice_fusion.refs_0_), channel_id=1, source_target_pairs={{0,1},{1,2},{2,3},{3,4},{4,5},{5,6},{6,7},{7,0},{8,9},{9,10},{10,1... | collective-permute-start | bytes 786440 | tf_op jit(solution)/shard_map/ppermute | solution.py:40
  26.5 11.9 %collective-permute-start.3 = (bf16[4,256,128]{2,1,0:T(8,128)(2,1)S(1)}, bf16[4,256,128]{2,1,0:T(8,128)(2,1)S(1)}, u32[]{:S(2)}, u32[]{:S(2)}) collective-permute-start(bf16[4,256,128]{2,1,0:T(8,128)(2,1)S(1)} %constant_dynamic-update-slice_fusion.refs_0_), channel_id=1, source_target_pairs={{0,7},{1,0},{2,1},{3,2},{4,3},{5,4},{6,5},{7,6},{8,15},{9,8},{10,9... | collective-permute-start | bytes 786440 | tf_op jit(solution)/shard_map/ppermute | solution.py:40
  33.3 12.9 %collective-permute-start.9 = (bf16[27,32,128]{2,1,0:T(8,128)(2,1)S(1)}, bf16[27,32,128]{2,1,0:T(8,128)(2,1)S(1)}, u32[]{:S(2)}, u32[]{:S(2)}) collective-permute-start(bf16[27,32,128]{2,1,0:T(8,128)(2,1)S(1)} %collective-permute-done.5.refs_1_), channel_id=1, source_target_pairs={{0,64},{1,65},{2,66},{3,67},{4,68},{5,69},{6,70},{7,71},{8,72},{9,... | collective-permute-start | bytes 663560 | tf_op jit(solution)/shard_map/ppermute | solution.py:40
  34.2 11.9 %collective-permute-start.8 = (bf16[27,32,128]{2,1,0:T(8,128)(2,1)S(1)}, bf16[27,32,128]{2,1,0:T(8,128)(2,1)S(1)}, u32[]{:S(2)}, u32[]{:S(2)}) collective-permute-start(bf16[27,32,128]{2,1,0:T(8,128)(2,1)S(1)} %collective-permute-done.5.refs_1_), channel_id=1, source_target_pairs={{0,192},{1,193},{2,194},{3,195},{4,196},{5,197},{6,198},{7,199},{8... | collective-permute-start | bytes 663560 | tf_op jit(solution)/shard_map/ppermute | solution.py:40
  36.5 9.6 %collective-permute-start.10 = (bf16[27,32,128]{2,1,0:T(8,128)(2,1)S(1)}, bf16[27,32,128]{2,1,0:T(8,128)(2,1)S(1)}, u32[]{:S(2)}, u32[]{:S(2)}) collective-permute-start(bf16[27,32,128]{2,1,0:T(8,128)(2,1)S(1)} %collective-permute-done.5.refs_1_), channel_id=1, source_target_pairs={{0,128},{1,129},{2,130},{3,131},{4,132},{5,133},{6,134},{7,135},{8... | collective-permute-start | bytes 663560 | tf_op jit(solution)/shard_map/ppermute | solution.py:40
  38.5 6.3 %collective-permute-start.7 = (bf16[2,256,128]{2,1,0:T(8,128)(2,1)S(1)}, bf16[2,256,128]{2,1,0:T(8,128)(2,1)S(1)}, u32[]{:S(2)}, u32[]{:S(2)}) collective-permute-start(bf16[2,256,128]{2,1,0:T(8,128)(2,1)S(1)} %slice.75), channel_id=1, source_target_pairs={{0,1},{1,2},{2,3},{3,4},{4,5},{5,6},{6,7},{7,0},{8,9},{9,10},{10,1... | collective-permute-start | bytes 393224 | tf_op jit(solution)/shard_map/ppermute | solution.py:40
  38.5 6.2 %collective-permute-start.6 = (bf16[2,256,128]{2,1,0:T(8,128)(2,1)S(1)}, bf16[2,256,128]{2,1,0:T(8,128)(2,1)S(1)}, u32[]{:S(2)}, u32[]{:S(2)}) collective-permute-start(bf16[2,256,128]{2,1,0:T(8,128)(2,1)S(1)} %slice.74), channel_id=1, source_target_pairs={{0,7},{1,0},{2,1},{3,2},{4,3},{5,4},{6,5},{7,6},{8,15},{9,8},{10,9... | collective-permute-start | bytes 393224 | tf_op jit(solution)/shard_map/ppermute | solution.py:40
  50.2 3.3 %collective-permute-start.11 = (bf16[8,256,128]{2,1,0:T(8,128)(2,1)S(1)}, bf16[8,256,128]{2,1,0:T(8,128)(2,1)S(1)}, u32[]{:S(2)}, u32[]{:S(2)}) collective-permute-start(bf16[8,256,128]{2,1,0:T(8,128)(2,1)S(1)} %shard_map.77), channel_id=1, source_target_pairs={{0,8},{1,9},{2,10},{3,11},{4,12},{5,13},{6,14},{7,15},{8,0},{9,1},... | collective-permute-start | bytes 1572872 | tf_op jit(solution)/shard_map/ppermute | solution.py:40
  53.5 10.6 %copy-start = (f32[128]{0:T(128)S(1)}, f32[128]{0:T(128)}, u32[]{:S(2)}) copy-start(f32[128]{0:T(128)} %param.6) | copy-start | bytes 1540
  53.7 7.9 %collective-permute-start.12 = (bf16[2,256,128]{2,1,0:T(8,128)(2,1)S(1)}, bf16[2,256,128]{2,1,0:T(8,128)(2,1)S(1)}, u32[]{:S(2)}, u32[]{:S(2)}) collective-permute-start(bf16[2,256,128]{2,1,0:T(8,128)(2,1)S(1)} %get-tuple-element.86), channel_id=1, source_target_pairs={{0,32},{1,33},{2,34},{3,35},{4,36},{5,37},{6,38},{7,39},{8,40},{9,... | collective-permute-start | bytes 393224 | tf_op jit(solution)/shard_map/ppermute | solution.py:40
  53.8 9.1 %collective-permute-start.14 = (bf16[2,256,128]{2,1,0:T(8,128)(2,1)S(1)}, bf16[2,256,128]{2,1,0:T(8,128)(2,1)S(1)}, u32[]{:S(2)}, u32[]{:S(2)}) collective-permute-start(bf16[2,256,128]{2,1,0:T(8,128)(2,1)S(1)} %get-tuple-element.87), channel_id=1, source_target_pairs={{0,48},{1,49},{2,50},{3,51},{4,52},{5,53},{6,54},{7,55},{8,56},{9,... | collective-permute-start | bytes 393224 | tf_op jit(solution)/shard_map/ppermute | solution.py:40
  54.8 9.1 %collective-permute-start.13 = (bf16[2,256,128]{2,1,0:T(8,128)(2,1)S(1)}, bf16[2,256,128]{2,1,0:T(8,128)(2,1)S(1)}, u32[]{:S(2)}, u32[]{:S(2)}) collective-permute-start(bf16[2,256,128]{2,1,0:T(8,128)(2,1)S(1)} %get-tuple-element.88), channel_id=1, source_target_pairs={{0,16},{1,17},{2,18},{3,19},{4,20},{5,21},{6,22},{7,23},{8,24},{9,... | collective-permute-start | bytes 393224 | tf_op jit(solution)/shard_map/ppermute | solution.py:40
  64.3 6.4 %collective-permute-start.17 = (bf16[2,256,128]{2,1,0:T(8,128)(2,1)S(1)}, bf16[2,256,128]{2,1,0:T(8,128)(2,1)S(1)}, u32[]{:S(2)}, u32[]{:S(2)}) collective-permute-start(bf16[2,256,128]{2,1,0:T(8,128)(2,1)S(1)} %get-tuple-element.90.refs_2_.refs_0_), channel_id=1, source_target_pairs={{0,48},{1,49},{2,50},{3,51},{4,52},{5,53},{6,54},{7,55},{8,56},{9,... | collective-permute-start | bytes 393224 | tf_op jit(solution)/shard_map/ppermute | solution.py:40
  65.0 7.9 %collective-permute-start.16 = (bf16[2,256,128]{2,1,0:T(8,128)(2,1)S(1)}, bf16[2,256,128]{2,1,0:T(8,128)(2,1)S(1)}, u32[]{:S(2)}, u32[]{:S(2)}) collective-permute-start(bf16[2,256,128]{2,1,0:T(8,128)(2,1)S(1)} %get-tuple-element.90.refs_2_.refs_0_), channel_id=1, source_target_pairs={{0,32},{1,33},{2,34},{3,35},{4,36},{5,37},{6,38},{7,39},{8,40},{9,... | collective-permute-start | bytes 393224 | tf_op jit(solution)/shard_map/ppermute | solution.py:40
  66.1 7.7 %collective-permute-start.15 = (bf16[2,256,128]{2,1,0:T(8,128)(2,1)S(1)}, bf16[2,256,128]{2,1,0:T(8,128)(2,1)S(1)}, u32[]{:S(2)}, u32[]{:S(2)}) collective-permute-start(bf16[2,256,128]{2,1,0:T(8,128)(2,1)S(1)} %get-tuple-element.90.refs_2_.refs_0_), channel_id=1, source_target_pairs={{0,16},{1,17},{2,18},{3,19},{4,20},{5,21},{6,22},{7,23},{8,24},{9,... | collective-permute-start | bytes 393224 | tf_op jit(solution)/shard_map/ppermute | solution.py:40
  67.8 6.0 %collective-permute-start.18 = (bf16[2,256,128]{2,1,0:T(8,128)(2,1)S(1)}, bf16[2,256,128]{2,1,0:T(8,128)(2,1)S(1)}, u32[]{:S(2)}, u32[]{:S(2)}) collective-permute-start(bf16[2,256,128]{2,1,0:T(8,128)(2,1)S(1)} %get-tuple-element.90.refs_2_.refs_0_), channel_id=1, source_target_pairs={{0,8},{1,9},{2,10},{3,11},{4,12},{5,13},{6,14},{7,15},{8,0},{9,1},... | collective-permute-start | bytes 393224 | tf_op jit(solution)/shard_map/ppermute | solution.py:40
  70.7 3.1 %collective-permute-start.21 = (bf16[2,256,128]{2,1,0:T(8,128)(2,1)S(1)}, bf16[2,256,128]{2,1,0:T(8,128)(2,1)S(1)}, u32[]{:S(2)}, u32[]{:S(2)}) collective-permute-start(bf16[2,256,128]{2,1,0:T(8,128)(2,1)S(1)} %collective-permute-done.17.refs_5_.refs_3_), channel_id=1, source_target_pairs={{0,8},{1,9},{2,10},{3,11},{4,12},{5,13},{6,14},{7,15},{8,0},{9,1},... | collective-permute-start | bytes 393224 | tf_op jit(solution)/shard_map/ppermute | solution.py:40
  72.9 1.3 %collective-permute-start.20 = (bf16[2,256,128]{2,1,0:T(8,128)(2,1)S(1)}, bf16[2,256,128]{2,1,0:T(8,128)(2,1)S(1)}, u32[]{:S(2)}, u32[]{:S(2)}) collective-permute-start(bf16[2,256,128]{2,1,0:T(8,128)(2,1)S(1)} %collective-permute-done.16.refs_4_.refs_2_), channel_id=1, source_target_pairs={{0,8},{1,9},{2,10},{3,11},{4,12},{5,13},{6,14},{7,15},{8,0},{9,1},... | collective-permute-start | bytes 393224 | tf_op jit(solution)/shard_map/ppermute | solution.py:40
  73.8 1.3 %collective-permute-start.19 = (bf16[2,256,128]{2,1,0:T(8,128)(2,1)S(1)}, bf16[2,256,128]{2,1,0:T(8,128)(2,1)S(1)}, u32[]{:S(2)}, u32[]{:S(2)}) collective-permute-start(bf16[2,256,128]{2,1,0:T(8,128)(2,1)S(1)} %collective-permute-done.15.refs_3_.refs_1_), channel_id=1, source_target_pairs={{0,8},{1,9},{2,10},{3,11},{4,12},{5,13},{6,14},{7,15},{8,0},{9,1},... | collective-permute-start | bytes 393224 | tf_op jit(solution)/shard_map/ppermute | solution.py:40
  84.9 12.5 %collective-permute-start.22 = (bf16[4,256,128]{2,1,0:T(8,128)(2,1)S(1)}, bf16[4,256,128]{2,1,0:T(8,128)(2,1)S(1)}, u32[]{:S(2)}, u32[]{:S(2)}) collective-permute-start(bf16[4,256,128]{2,1,0:T(8,128)(2,1)S(1)} %get-tuple-element.74), channel_id=1, source_target_pairs={{0,1},{1,2},{2,3},{3,4},{4,5},{5,6},{6,7},{7,0},{8,9},{9,10},{10,1... | collective-permute-start | bytes 786440 | tf_op jit(solution)/shard_map/ppermute | solution.py:40
  85.6 11.8 %collective-permute-start.23 = (bf16[4,256,128]{2,1,0:T(8,128)(2,1)S(1)}, bf16[4,256,128]{2,1,0:T(8,128)(2,1)S(1)}, u32[]{:S(2)}, u32[]{:S(2)}) collective-permute-start(bf16[4,256,128]{2,1,0:T(8,128)(2,1)S(1)} %get-tuple-element.75), channel_id=1, source_target_pairs={{0,7},{1,0},{2,1},{3,2},{4,3},{5,4},{6,5},{7,6},{8,15},{9,8},{10,9... | collective-permute-start | bytes 786440 | tf_op jit(solution)/shard_map/ppermute | solution.py:40
  88.6 12.8 %collective-permute-start.29 = (bf16[28,32,128]{2,1,0:T(8,128)(2,1)S(1)}, bf16[28,32,128]{2,1,0:T(8,128)(2,1)S(1)}, u32[]{:S(2)}, u32[]{:S(2)}) collective-permute-start(bf16[28,32,128]{2,1,0:T(8,128)(2,1)S(1)} %get-tuple-element.81), channel_id=1, source_target_pairs={{0,128},{1,129},{2,130},{3,131},{4,132},{5,133},{6,134},{7,135},{8... | collective-permute-start | bytes 688136 | tf_op jit(solution)/shard_map/ppermute | solution.py:40
  94.1 9.7 %collective-permute-start.30 = (bf16[28,32,128]{2,1,0:T(8,128)(2,1)S(1)}, bf16[28,32,128]{2,1,0:T(8,128)(2,1)S(1)}, u32[]{:S(2)}, u32[]{:S(2)}) collective-permute-start(bf16[28,32,128]{2,1,0:T(8,128)(2,1)S(1)} %get-tuple-element.82), channel_id=1, source_target_pairs={{0,64},{1,65},{2,66},{3,67},{4,68},{5,69},{6,70},{7,71},{8,72},{9,... | collective-permute-start | bytes 688136 | tf_op jit(solution)/shard_map/ppermute | solution.py:40
  95.1 8.8 %collective-permute-start.31 = (bf16[28,32,128]{2,1,0:T(8,128)(2,1)S(1)}, bf16[28,32,128]{2,1,0:T(8,128)(2,1)S(1)}, u32[]{:S(2)}, u32[]{:S(2)}) collective-permute-start(bf16[28,32,128]{2,1,0:T(8,128)(2,1)S(1)} %get-tuple-element.83), channel_id=1, source_target_pairs={{0,192},{1,193},{2,194},{3,195},{4,196},{5,197},{6,198},{7,199},{8... | collective-permute-start | bytes 688136 | tf_op jit(solution)/shard_map/ppermute | solution.py:40
  97.6 11.5 %collective-permute-start.24 = (bf16[2,256,128]{2,1,0:T(8,128)(2,1)S(1)}, bf16[2,256,128]{2,1,0:T(8,128)(2,1)S(1)}, u32[]{:S(2)}, u32[]{:S(2)}) collective-permute-start(bf16[2,256,128]{2,1,0:T(8,128)(2,1)S(1)} %get-tuple-element.91), channel_id=1, source_target_pairs={{0,4},{1,5},{2,6},{3,7},{4,0},{5,1},{6,2},{7,3},{8,12},{9,13},{10,... | collective-permute-start | bytes 393224 | tf_op jit(solution)/shard_map/ppermute | solution.py:40
  100.6 9.0 %collective-permute-start.25 = (bf16[2,256,128]{2,1,0:T(8,128)(2,1)S(1)}, bf16[2,256,128]{2,1,0:T(8,128)(2,1)S(1)}, u32[]{:S(2)}, u32[]{:S(2)}) collective-permute-start(bf16[2,256,128]{2,1,0:T(8,128)(2,1)S(1)} %get-tuple-element.92), channel_id=1, source_target_pairs={{0,1},{1,2},{2,3},{3,4},{4,5},{5,6},{6,7},{7,0},{8,9},{9,10},{10,1... | collective-permute-start | bytes 393224 | tf_op jit(solution)/shard_map/ppermute | solution.py:40
  101.5 8.1 %collective-permute-start.26 = (bf16[2,256,128]{2,1,0:T(8,128)(2,1)S(1)}, bf16[2,256,128]{2,1,0:T(8,128)(2,1)S(1)}, u32[]{:S(2)}, u32[]{:S(2)}) collective-permute-start(bf16[2,256,128]{2,1,0:T(8,128)(2,1)S(1)} %get-tuple-element.93), channel_id=1, source_target_pairs={{0,7},{1,0},{2,1},{3,2},{4,3},{5,4},{6,5},{7,6},{8,15},{9,8},{10,9... | collective-permute-start | bytes 393224 | tf_op jit(solution)/shard_map/ppermute | solution.py:40
  104.0 14.2 %collective-permute-start.32 = (bf16[27,32,128]{2,1,0:T(8,128)(2,1)S(1)}, bf16[27,32,128]{2,1,0:T(8,128)(2,1)S(1)}, u32[]{:S(2)}, u32[]{:S(2)}) collective-permute-start(bf16[27,32,128]{2,1,0:T(8,128)(2,1)S(1)} %slice.134), channel_id=1, source_target_pairs={{0,0},{1,1},{2,2},{3,3},{4,4},{5,5},{6,6},{7,7},{8,128},{9,129},{1... | collective-permute-start | bytes 663560 | tf_op jit(solution)/shard_map/ppermute | solution.py:40
  109.7 10.5 %collective-permute-start.27 = (bf16[256,128]{1,0:T(8,128)(2,1)S(1)}, bf16[256,128]{1,0:T(8,128)(2,1)S(1)}, u32[]{:S(2)}, u32[]{:S(2)}) collective-permute-start(bf16[256,128]{1,0:T(8,128)(2,1)S(1)} %get-tuple-element.96), channel_id=1, source_target_pairs={{0,8},{1,9},{2,10},{3,11},{4,12},{5,13},{6,14},{7,15},{8,16},{9,17... | collective-permute-start | bytes 196616 | tf_op jit(solution)/shard_map/ppermute | solution.py:40
  109.8 10.4 %collective-permute-start.28 = (bf16[256,128]{1,0:T(8,128)(2,1)S(1)}, bf16[256,128]{1,0:T(8,128)(2,1)S(1)}, u32[]{:S(2)}, u32[]{:S(2)}) collective-permute-start(bf16[256,128]{1,0:T(8,128)(2,1)S(1)} %get-tuple-element.94), channel_id=1, source_target_pairs={{0,8},{1,16},{2,24},{3,32},{4,40},{5,48},{6,56},{7,64},{8,44},{9,5... | collective-permute-start | bytes 196616 | tf_op jit(solution)/shard_map/ppermute | solution.py:40
  116.3 12.5 %collective-permute-start.33 = (bf16[256,128]{1,0:T(8,128)(2,1)S(1)}, bf16[256,128]{1,0:T(8,128)(2,1)S(1)}, u32[]{:S(2)}, u32[]{:S(2)}) collective-permute-start(bf16[256,128]{1,0:T(8,128)(2,1)S(1)} %get-tuple-element.95), channel_id=1, source_target_pairs={{0,0},{1,8},{2,16},{3,24},{4,32},{5,40},{6,48},{7,56},{8,36},{9,44... | collective-permute-start | bytes 196616 | tf_op jit(solution)/shard_map/ppermute | solution.py:40

commit v8 on v7

--- a/solution.py
+++ b/solution.py
@@ -239,9 +239,9 @@
     own = jnp.concatenate(
         [permuted(own, lambda x, q, z: at(x, holder(z), z + q + step)) for step in (0, 4)]
     )
-    blocks = [block] + [
-        permuted(block, lambda x, q, z: at(x - shift, q, z)) for shift in range(1, NX)
-    ]
+    blocks = [block] * NX
+    for shift in (2, 1, 3):
+        blocks[shift] = permuted(block, lambda x, q, z: at(x - shift, q, z))
     above, below = along_z(own, -1), along_z(own, 1)
     above, below, block = lax.optimization_barrier((above, below, block))
     planes = [own, above, below, along_z(above[:2], -1), along_z(below[:2], 1)]
@@ -257,7 +257,7 @@
         [],
         0,
     )
-    columns, blocks[1], blocks[3] = lax.optimization_barrier((columns, blocks[1], blocks[3]))
+    columns, blocks[2] = lax.optimization_barrier((columns, blocks[2]))
 
     def weights(turned, where):
         (paired,) = call(
@@ -346,7 +346,7 @@
     beyond = (beyond + up[2:].astype(f32) + down[2:].astype(f32)).astype(bf16)
     beyond, above, below = along_z(beyond, 4), along_z(above, 1), along_z(below, -1)
     held = sum((piece.astype(f32) for piece in received), terms[0].astype(f32))
-    grad_bias = held[27, 0] + held[27, 1]
+    bias_rows = held[27, :2]
     grad_filters = permuted(
         held[:27].astype(bf16), lambda x, q, z: device(NX * group(q) + swapped(x), z)
     ).astype(f32)
@@ -358,7 +358,9 @@
 
     first, second = permuted(summed[0], home(0)), permuted(summed[1], home(1))
     shifted = permuted(activated[1], lambda x, q, z: device(NQ * x + q + 1, z))
+    shifted, bias_rows = lax.optimization_barrier((shifted, bias_rows))
     activated = jnp.stack([shifted, activated[0]])
+    grad_bias = bias_rows[0] + bias_rows[1]
     second, grad_filters = lax.optimization_barrier((second, grad_filters))
     grad_input = jnp.stack([second, first])
     shape = (2, GRID, GRID)

time: 130 us -> 137 us (1.054)
  waiting for transfers between devices: 33.9 us -> 41.9 us
  starting transfers between devices: 67.5 us -> 66.1 us
    ppermute x34, waiting for transfers between devices: 33.9 us -> 41.9 us  [permuted(): return lax.ppermute(array, ('space', 'chan'), pairs)]
  transfers between devices with their start and end apart: 34 -> 34, of which waited for: 15 -> 16; matrix products, arithmetic and copies ran while one was open for 2% -> 2% of each run, Pallas kernels for 7% -> 10%
where the time goes in v8:
time: 137 us; the launch traced here: 136 us
  starting transfers between devices  66.1 us (48%)
  waiting for transfers between devices  41.9 us (31%)
  Pallas kernels  22.5 us (16%)
  other arithmetic  3.55 us (3%)
    ppermute x34, starting transfers between devices, permuted(): return lax.ppermute(array, ('space', 'chan'), pairs)  66.1 us
    ppermute x34, waiting for transfers between devices, permuted(): return lax.ppermute(array, ('space', 'chan'), pairs)  41.9 us
    pallas_call x9, Pallas kernels, call(): pl.pallas_call(kernel, out_shape=outs, in_specs=[pl.BlockSpec(memory_spac...  22.5 us
  transfers between devices with their start and end apart: 34, of which 16 were waited for; matrix products, arithmetic and copies ran while one was open for 2% of the time, Pallas kernels for 10%

profile of v8, /device:TPU:16, one launch (start us, length us, event | category | flops | bytes accessed | tf_op | source)
XLA Modules:
  0.0 136.1 jit_solution(13016014675856252838)
XLA Ops:
  0.6 1.0 fusion.13
  1.7 2.5 %collective-permute-done = bf16[2,16,16,128]{3,2,1,0:T(8,128)(2,1)S(1)} collective-permute-done((bf16[2,16,16,128]{3,2,1,0:T(8,128)(2,1)S(1)}, bf16[2,16,16,128]{3,2,1,0:T(8,128)(2,1)S(1)}, u32[]{:S(2)}, u32[]{:S(2)}) %collective-permute-start) | collective-permute-done | bytes 131104 | tf_op jit(solution)/shard_map/ppermute | solution.py:40
  4.3 13.5 %collective-permute-start.1 = (bf16[2,256,128]{2,1,0:T(8,128)(2,1)S(1)}, bf16[2,256,128]{2,1,0:T(8,128)(2,1)S(1)}, u32[]{:S(2)}, u32[]{:S(2)}) collective-permute-start(bf16[2,256,128]{2,1,0:T(8,128)(2,1)S(1)} %bitcast.24), channel_id=1, source_target_pairs={{0,0},{1,17},{2,34},{3,51},{4,12},{5,29},{6,46},{7,63},{8,1},{9,18... | collective-permute-start | bytes 393224 | tf_op jit(solution)/shard_map/ppermute | solution.py:40
  17.8 1.9 %collective-permute-start.2 = (bf16[2,256,128]{2,1,0:T(8,128)(2,1)S(1)}, bf16[2,256,128]{2,1,0:T(8,128)(2,1)S(1)}, u32[]{:S(2)}, u32[]{:S(2)}) collective-permute-start(bf16[2,256,128]{2,1,0:T(8,128)(2,1)S(1)} %bitcast.25), channel_id=1, source_target_pairs={{0,4},{1,21},{2,38},{3,55},{4,8},{5,25},{6,42},{7,59},{8,5},{9,22}... | collective-permute-start | bytes 393224 | tf_op jit(solution)/shard_map/ppermute | solution.py:40
  19.7 1.9 %collective-permute-start.5 = (bf16[27,32,128]{2,1,0:T(8,128)(2,1)}, bf16[27,32,128]{2,1,0:T(8,128)(2,1)S(1)}, u32[]{:S(2)}, u32[]{:S(2)}) collective-permute-start(bf16[27,32,128]{2,1,0:T(8,128)(2,1)} %bitcast.29), channel_id=1, source_target_pairs={{0,0},{1,1},{2,2},{3,3},{4,4},{5,5},{6,6},{7,7},{8,128},{9,129},{1... | collective-permute-start | bytes 663560 | tf_op jit(solution)/shard_map/ppermute | solution.py:40
  21.7 4.8 %collective-permute-done.2 = bf16[2,256,128]{2,1,0:T(8,128)(2,1)S(1)} collective-permute-done((bf16[2,256,128]{2,1,0:T(8,128)(2,1)S(1)}, bf16[2,256,128]{2,1,0:T(8,128)(2,1)S(1)}, u32[]{:S(2)}, u32[]{:S(2)}) %collective-permute-start.2) | collective-permute-done | bytes 131104 | tf_op jit(solution)/shard_map/ppermute | solution.py:40
  26.5 6.7 %collective-permute-start.3 = (bf16[4,256,128]{2,1,0:T(8,128)(2,1)S(1)}, bf16[4,256,128]{2,1,0:T(8,128)(2,1)S(1)}, u32[]{:S(2)}, u32[]{:S(2)}) collective-permute-start(bf16[4,256,128]{2,1,0:T(8,128)(2,1)S(1)} %constant_dynamic-update-slice_fusion.refs_0_), channel_id=1, source_target_pairs={{0,7},{1,0},{2,1},{3,2},{4,3},{5,4},{6,5},{7,6},{8,15},{9,8},{10,9... | collective-permute-start | bytes 786440 | tf_op jit(solution)/shard_map/ppermute | solution.py:40
  33.3 3.1 %collective-permute-start.8 = (bf16[27,32,128]{2,1,0:T(8,128)(2,1)S(1)}, bf16[27,32,128]{2,1,0:T(8,128)(2,1)S(1)}, u32[]{:S(2)}, u32[]{:S(2)}) collective-permute-start(bf16[27,32,128]{2,1,0:T(8,128)(2,1)S(1)} %collective-permute-done.5.refs_1_), channel_id=1, source_target_pairs={{0,128},{1,129},{2,130},{3,131},{4,132},{5,133},{6,134},{7,135},{8... | collective-permute-start | bytes 663560 | tf_op jit(solution)/shard_map/ppermute | solution.py:40
  36.9 2.7 %collective-permute-start.9 = (bf16[27,32,128]{2,1,0:T(8,128)(2,1)S(1)}, bf16[27,32,128]{2,1,0:T(8,128)(2,1)S(1)}, u32[]{:S(2)}, u32[]{:S(2)}) collective-permute-start(bf16[27,32,128]{2,1,0:T(8,128)(2,1)S(1)} %collective-permute-done.5.refs_1_), channel_id=1, source_target_pairs={{0,192},{1,193},{2,194},{3,195},{4,196},{5,197},{6,198},{7,199},{8... | collective-permute-start | bytes 663560 | tf_op jit(solution)/shard_map/ppermute | solution.py:40
  39.8 3.2 %collective-permute-start.6 = (bf16[2,256,128]{2,1,0:T(8,128)(2,1)S(1)}, bf16[2,256,128]{2,1,0:T(8,128)(2,1)S(1)}, u32[]{:S(2)}, u32[]{:S(2)}) collective-permute-start(bf16[2,256,128]{2,1,0:T(8,128)(2,1)S(1)} %slice.77), channel_id=1, source_target_pairs={{0,7},{1,0},{2,1},{3,2},{4,3},{5,4},{6,5},{7,6},{8,15},{9,8},{10,9... | collective-permute-start | bytes 393224 | tf_op jit(solution)/shard_map/ppermute | solution.py:40
  43.1 2.9 %collective-permute-done.7.refs_4_ = bf16[2,256,128]{2,1,0:T(8,128)(2,1)S(1)} collective-permute-done((bf16[2,256,128]{2,1,0:T(8,128)(2,1)S(1)}, bf16[2,256,128]{2,1,0:T(8,128)(2,1)S(1)}, u32[]{:S(2)}, u32[]{:S(2)}) %collective-permute-start.7) | collective-permute-done | bytes 131104 | tf_op jit(solution)/shard_map/ppermute | solution.py:40
  45.9 1.4 %shard_map.75.refs_1_ = bf16[18,288,384]{2,1,0:T(8,128)(2,1)S(1)} custom-call(s32[2]{0:T(128)S(1)} %pad_add_fusion.where.refs_0_, bf16[4,256,128]{2,1,0:T(8,128)(2,1)S(1)} %constant_dynamic-update-slice_fusion.refs_0_, bf16[4,256,128]{2,1,0:T(8,128)(2,1)S(1)} %collective-permute-done.3.refs_1_, bf16[4,256,128]{2,1,0:T(8,128)(2,1)S(1)} %collective-permute-done.4.refs_2_, ...), custom_call_target="tpu_custom_call" | custom-call | bytes 5029888 | tf_op jit(solution)/shard_map/pallas_call | solution.py:209
  47.4 0.9 shard_map.76.refs_2_
  48.3 3.1 %shard_map.77 = bf16[8,256,128]{2,1,0:T(8,128)(2,1)S(1)} custom-call(s32[2]{0:T(128)S(1)} %pad_add_fusion.where.refs_0_, bf16[18,288,384]{2,1,0:T(8,128)(2,1)S(1)} %shard_map.75.refs_1_, bf16[4608,256]{1,0:T(8,128)(2,1)S(1)} %shard_map.76.refs_2_), custom_call_target="tpu_custom_call" | custom-call | flops 1811939328 | bytes 6864896 | tf_op jit(solution)/shard_map/pallas_call | solution.py:209
  51.5 3.1 %shard_map.78 = (f32[2,256,128]{2,1,0:T(8,128)S(1)}, f32[2,256,128]{2,1,0:T(8,128)S(1)}, f32[2,256,128]{2,1,0:T(8,128)S(1)}, f32[2,256,128]{2,1,0:T(8,128)S(1)}) custom-call(s32[2]{0:T(128)S(1)} %pad_add_fusion.where.refs_0_, bf16[18,288,384]{2,1,0:T(8,128)(2,1)S(1)} %shard_map.75.refs_1_, bf16[4608,256]{1,0:T(8,128)(2,1)S(1)} %shard_map.76.refs_2_), custom_call_target="tpu_custom_call" | custom-call | flops 1811939328 | bytes 7389184 | tf_op jit(solution)/shard_map/pallas_call | solution.py:209
  55.0 1.1 collective-permute-start.14
  56.0 1.2 collective-permute-start.13
  57.3 1.0 shard_map.79.refs_2_
  58.2 4.5 %collective-permute-done.12 = bf16[2,256,128]{2,1,0:T(8,128)(2,1)S(1)} collective-permute-done((bf16[2,256,128]{2,1,0:T(8,128)(2,1)S(1)}, bf16[2,256,128]{2,1,0:T(8,128)(2,1)S(1)}, u32[]{:S(2)}, u32[]{:S(2)}) %collective-permute-start.12) | collective-permute-done | bytes 131104 | tf_op jit(solution)/shard_map/ppermute | solution.py:40
  62.8 2.4 %collective-permute-done.13 = bf16[2,256,128]{2,1,0:T(8,128)(2,1)S(1)} collective-permute-done((bf16[2,256,128]{2,1,0:T(8,128)(2,1)S(1)}, bf16[2,256,128]{2,1,0:T(8,128)(2,1)S(1)}, u32[]{:S(2)}, u32[]{:S(2)}) %collective-permute-start.13) | collective-permute-done | bytes 131104 | tf_op jit(solution)/shard_map/ppermute | solution.py:40
  65.5 0.7 collective-permute-start.17
  66.2 1.1 collective-permute-start.16
  67.2 1.3 collective-permute-start.15
  68.5 3.4 %collective-permute-done.17.refs_5_.refs_3_ = bf16[2,256,128]{2,1,0:T(8,128)(2,1)S(1)} collective-permute-done((bf16[2,256,128]{2,1,0:T(8,128)(2,1)S(1)}, bf16[2,256,128]{2,1,0:T(8,128)(2,1)S(1)}, u32[]{:S(2)}, u32[]{:S(2)}) %collective-permute-start.17) | collective-permute-done | bytes 131104 | tf_op jit(solution)/shard_map/ppermute | solution.py:40
  71.9 2.1 %collective-permute-done.16.refs_4_.refs_2_ = bf16[2,256,128]{2,1,0:T(8,128)(2,1)S(1)} collective-permute-done((bf16[2,256,128]{2,1,0:T(8,128)(2,1)S(1)}, bf16[2,256,128]{2,1,0:T(8,128)(2,1)S(1)}, u32[]{:S(2)}, u32[]{:S(2)}) %collective-permute-start.16) | collective-permute-done | bytes 131104 | tf_op jit(solution)/shard_map/ppermute | solution.py:40
  74.1 0.9 collective-permute-done.15.refs_3_.refs_1_
  75.4 0.9 collective-permute-done.19.refs_7_.refs_5_
  76.3 5.2 %shard_map.80 = (bf16[28,32,128]{2,1,0:T(8,128)(2,1)S(1)}, bf16[28,32,128]{2,1,0:T(8,128)(2,1)S(1)}, bf16[28,32,128]{2,1,0:T(8,128)(2,1)S(1)}, bf16[28,32,128]{2,1,0:T(8,128)(2,1)S(1)}) custom-call(s32[2]{0:T(128)S(1)} %pad_add_fusion.where.refs_0_, bf16[18,288,384]{2,1,0:T(8,128)(2,1)S(1)} %shard_map.75.refs_1_, ...), custom_call_target="tpu_custom_call" | custom-call | flops 3623878656 | bytes 5947392 | tf_op jit(solution)/shard_map/pallas_call | solution.py:209
  81.6 1.4 %collective-permute-start.28 = (bf16[28,32,128]{2,1,0:T(8,128)(2,1)S(1)}, bf16[28,32,128]{2,1,0:T(8,128)(2,1)S(1)}, u32[]{:S(2)}, u32[]{:S(2)}) collective-permute-start(bf16[28,32,128]{2,1,0:T(8,128)(2,1)S(1)} %get-tuple-element.80), channel_id=1, source_target_pairs={{0,128},{1,129},{2,130},{3,131},{4,132},{5,133},{6,134},{7,135},{8... | collective-permute-start | bytes 688136 | tf_op jit(solution)/shard_map/ppermute | solution.py:40
  83.0 1.4 %shard_map.81.refs_1_ = bf16[18,288,384]{2,1,0:T(8,128)(2,1)S(1)} custom-call(s32[2]{0:T(128)S(1)} %pad_add_fusion.where.refs_0_, bf16[2,256,128]{2,1,0:T(8,128)(2,1)S(1)} %get-tuple-element.92.refs_2_.refs_0_, bf16[2,256,128]{2,1,0:T(8,128)(2,1)S(1)} %collective-permute-done.15.refs_3_.refs_1_, ...), custom_call_target="tpu_custom_call" | custom-call | bytes 5029888 | tf_op jit(solution)/shard_map/pallas_call | solution.py:209
  84.4 3.1 %shard_map.82 = (bf16[4,256,128]{2,1,0:T(8,128)(2,1)S(1)}, bf16[4,256,128]{2,1,0:T(8,128)(2,1)S(1)}) custom-call(s32[2]{0:T(128)S(1)} %pad_add_fusion.where.refs_0_, bf16[18,288,384]{2,1,0:T(8,128)(2,1)S(1)} %shard_map.81.refs_1_, bf16[4608,256]{1,0:T(8,128)(2,1)S(1)} %shard_map.79.refs_2_), custom_call_target="tpu_custom_call" | custom-call | flops 1811939328 | bytes 6864896 | tf_op jit(solution)/shard_map/pallas_call | solution.py:209
  87.6 3.1 %shard_map.83 = (f32[2,256,128]{2,1,0:T(8,128)S(1)}, f32[2,256,128]{2,1,0:T(8,128)S(1)}, f32[2,256,128]{2,1,0:T(8,128)S(1)}, f32[2,256,128]{2,1,0:T(8,128)S(1)}) custom-call(s32[2]{0:T(128)S(1)} %pad_add_fusion.where.refs_0_, bf16[18,288,384]{2,1,0:T(8,128)(2,1)S(1)} %shard_map.81.refs_1_, bf16[4608,256]{1,0:T(8,128)(2,1)S(1)} %shard_map.79.refs_2_), custom_call_target="tpu_custom_call" | custom-call | flops 1811939328 | bytes 7389184 | tf_op jit(solution)/shard_map/pallas_call | solution.py:209
  90.7 1.0 collective-permute-start.29
  91.7 2.3 %collective-permute-start.30 = (bf16[28,32,128]{2,1,0:T(8,128)(2,1)S(1)}, bf16[28,32,128]{2,1,0:T(8,128)(2,1)S(1)}, u32[]{:S(2)}, u32[]{:S(2)}) collective-permute-start(bf16[28,32,128]{2,1,0:T(8,128)(2,1)S(1)} %get-tuple-element.82), channel_id=1, source_target_pairs={{0,192},{1,193},{2,194},{3,195},{4,196},{5,197},{6,198},{7,199},{8... | collective-permute-start | bytes 688136 | tf_op jit(solution)/shard_map/ppermute | solution.py:40
  94.0 3.3 %collective-permute-start.23 = (bf16[4,256,128]{2,1,0:T(8,128)(2,1)S(1)}, bf16[4,256,128]{2,1,0:T(8,128)(2,1)S(1)}, u32[]{:S(2)}, u32[]{:S(2)}) collective-permute-start(bf16[4,256,128]{2,1,0:T(8,128)(2,1)S(1)} %get-tuple-element.75), channel_id=1, source_target_pairs={{0,7},{1,0},{2,1},{3,2},{4,3},{5,4},{6,5},{7,6},{8,15},{9,8},{10,9... | collective-permute-start | bytes 786440 | tf_op jit(solution)/shard_map/ppermute | solution.py:40
  97.3 2.1 %collective-permute-done.29 = bf16[28,32,128]{2,1,0:T(8,128)(2,1)S(1)} collective-permute-done((bf16[28,32,128]{2,1,0:T(8,128)(2,1)S(1)}, bf16[28,32,128]{2,1,0:T(8,128)(2,1)S(1)}, u32[]{:S(2)}, u32[]{:S(2)}) %collective-permute-start.29) | collective-permute-done | bytes 229408 | tf_op jit(solution)/shard_map/ppermute | solution.py:40
  99.5 4.0 %collective-permute-start.32 = (bf16[27,32,128]{2,1,0:T(8,128)(2,1)S(1)}, bf16[27,32,128]{2,1,0:T(8,128)(2,1)S(1)}, u32[]{:S(2)}, u32[]{:S(2)}) collective-permute-start(bf16[27,32,128]{2,1,0:T(8,128)(2,1)S(1)} %slice.136), channel_id=1, source_target_pairs={{0,0},{1,1},{2,2},{3,3},{4,4},{5,5},{6,6},{7,7},{8,128},{9,129},{1... | collective-permute-start | bytes 663560 | tf_op jit(solution)/shard_map/ppermute | solution.py:40
  103.7 4.4 %collective-permute-start.24 = (bf16[2,256,128]{2,1,0:T(8,128)(2,1)S(1)}, bf16[2,256,128]{2,1,0:T(8,128)(2,1)S(1)}, u32[]{:S(2)}, u32[]{:S(2)}) collective-permute-start(bf16[2,256,128]{2,1,0:T(8,128)(2,1)S(1)} %get-tuple-element.93), channel_id=1, source_target_pairs={{0,4},{1,5},{2,6},{3,7},{4,0},{5,1},{6,2},{7,3},{8,12},{9,13},{10,... | collective-permute-start | bytes 393224 | tf_op jit(solution)/shard_map/ppermute | solution.py:40
  108.5 2.8 %collective-permute-start.26 = (bf16[2,256,128]{2,1,0:T(8,128)(2,1)S(1)}, bf16[2,256,128]{2,1,0:T(8,128)(2,1)S(1)}, u32[]{:S(2)}, u32[]{:S(2)}) collective-permute-start(bf16[2,256,128]{2,1,0:T(8,128)(2,1)S(1)} %get-tuple-element.95), channel_id=1, source_target_pairs={{0,7},{1,0},{2,1},{3,2},{4,3},{5,4},{6,5},{7,6},{8,15},{9,8},{10,9... | collective-permute-start | bytes 393224 | tf_op jit(solution)/shard_map/ppermute | solution.py:40
  111.3 2.3 %collective-permute-done.24 = bf16[2,256,128]{2,1,0:T(8,128)(2,1)S(1)} collective-permute-done((bf16[2,256,128]{2,1,0:T(8,128)(2,1)S(1)}, bf16[2,256,128]{2,1,0:T(8,128)(2,1)S(1)}, u32[]{:S(2)}, u32[]{:S(2)}) %collective-permute-start.24) | collective-permute-done | bytes 131104 | tf_op jit(solution)/shard_map/ppermute | solution.py:40
  113.6 4.5 %collective-permute-done.25 = bf16[2,256,128]{2,1,0:T(8,128)(2,1)S(1)} collective-permute-done((bf16[2,256,128]{2,1,0:T(8,128)(2,1)S(1)}, bf16[2,256,128]{2,1,0:T(8,128)(2,1)S(1)}, u32[]{:S(2)}, u32[]{:S(2)}) %collective-permute-start.25) | collective-permute-done | bytes 131104 | tf_op jit(solution)/shard_map/ppermute | solution.py:40
  118.9 4.0 %collective-permute-start.31 = (bf16[256,128]{1,0:T(8,128)(2,1)S(1)}, bf16[256,128]{1,0:T(8,128)(2,1)S(1)}, u32[]{:S(2)}, u32[]{:S(2)}) collective-permute-start(bf16[256,128]{1,0:T(8,128)(2,1)S(1)} %get-tuple-element.96), channel_id=1, source_target_pairs={{0,8},{1,16},{2,24},{3,32},{4,40},{5,48},{6,56},{7,64},{8,44},{9,5... | collective-permute-start | bytes 196616 | tf_op jit(solution)/shard_map/ppermute | solution.py:40
  122.9 2.7 %collective-permute-start.33 = (bf16[256,128]{1,0:T(8,128)(2,1)S(1)}, bf16[256,128]{1,0:T(8,128)(2,1)S(1)}, u32[]{:S(2)}, u32[]{:S(2)}) collective-permute-start(bf16[256,128]{1,0:T(8,128)(2,1)S(1)} %get-tuple-element.97), channel_id=1, source_target_pairs={{0,0},{1,8},{2,16},{3,24},{4,32},{5,40},{6,48},{7,56},{8,36},{9,44... | collective-permute-start | bytes 196616 | tf_op jit(solution)/shard_map/ppermute | solution.py:40
  125.7 0.8 convert_element_type.108
  127.0 2.3 %collective-permute-done.31 = bf16[256,128]{1,0:T(8,128)(2,1)S(1)} collective-permute-done((bf16[256,128]{1,0:T(8,128)(2,1)S(1)}, bf16[256,128]{1,0:T(8,128)(2,1)S(1)}, u32[]{:S(2)}, u32[]{:S(2)}) %collective-permute-start.31) | collective-permute-done | bytes 65568 | tf_op jit(solution)/shard_map/ppermute | solution.py:40
  129.3 0.7 pad_maximum_fusion.3
  130.0 5.4 %collective-permute-done.33 = bf16[256,128]{1,0:T(8,128)(2,1)S(1)} collective-permute-done((bf16[256,128]{1,0:T(8,128)(2,1)S(1)}, bf16[256,128]{1,0:T(8,128)(2,1)S(1)}, u32[]{:S(2)}, u32[]{:S(2)}) %collective-permute-start.33) | collective-permute-done | bytes 65568 | tf_op jit(solution)/shard_map/ppermute | solution.py:40
  135.4 0.7 pad_maximum_fusion.4
  (56 shorter events, 4.2 us)
Async XLA Ops:
  1.6 2.6 %collective-permute-start = (bf16[2,16,16,128]{3,2,1,0:T(8,128)(2,1)S(1)}, bf16[2,16,16,128]{3,2,1,0:T(8,128)(2,1)S(1)}, u32[]{:S(2)}, u32[]{:S(2)}) collective-permute-start(bf16[2,16,16,128]{3,2,1,0:T(8,128)(2,1)S(1)} %pad_maximum_fusion), channel_id=1, source_target_pairs={{0,248},{1,249},{2,250},{3,251},{4,252},{5,253},{6,254},{7,255},{8... | collective-permute-start | bytes 393224 | tf_op jit(solution)/shard_map/ppermute | solution.py:40
  4.3 17.4 %collective-permute-start.1 = (bf16[2,256,128]{2,1,0:T(8,128)(2,1)S(1)}, bf16[2,256,128]{2,1,0:T(8,128)(2,1)S(1)}, u32[]{:S(2)}, u32[]{:S(2)}) collective-permute-start(bf16[2,256,128]{2,1,0:T(8,128)(2,1)S(1)} %bitcast.24), channel_id=1, source_target_pairs={{0,0},{1,17},{2,34},{3,51},{4,12},{5,29},{6,46},{7,63},{8,1},{9,18... | collective-permute-start | bytes 393224 | tf_op jit(solution)/shard_map/ppermute | solution.py:40
  17.8 8.7 %collective-permute-start.2 = (bf16[2,256,128]{2,1,0:T(8,128)(2,1)S(1)}, bf16[2,256,128]{2,1,0:T(8,128)(2,1)S(1)}, u32[]{:S(2)}, u32[]{:S(2)}) collective-permute-start(bf16[2,256,128]{2,1,0:T(8,128)(2,1)S(1)} %bitcast.25), channel_id=1, source_target_pairs={{0,4},{1,21},{2,38},{3,55},{4,8},{5,25},{6,42},{7,59},{8,5},{9,22}... | collective-permute-start | bytes 393224 | tf_op jit(solution)/shard_map/ppermute | solution.py:40
  19.7 13.6 %collective-permute-start.5 = (bf16[27,32,128]{2,1,0:T(8,128)(2,1)}, bf16[27,32,128]{2,1,0:T(8,128)(2,1)S(1)}, u32[]{:S(2)}, u32[]{:S(2)}) collective-permute-start(bf16[27,32,128]{2,1,0:T(8,128)(2,1)} %bitcast.29), channel_id=1, source_target_pairs={{0,0},{1,1},{2,2},{3,3},{4,4},{5,5},{6,6},{7,7},{8,128},{9,129},{1... | collective-permute-start | bytes 663560 | tf_op jit(solution)/shard_map/ppermute | solution.py:40
  26.5 13.2 %collective-permute-start.4 = (bf16[4,256,128]{2,1,0:T(8,128)(2,1)S(1)}, bf16[4,256,128]{2,1,0:T(8,128)(2,1)S(1)}, u32[]{:S(2)}, u32[]{:S(2)}) collective-permute-start(bf16[4,256,128]{2,1,0:T(8,128)(2,1)S(1)} %constant_dynamic-update-slice_fusion.refs_0_), channel_id=1, source_target_pairs={{0,1},{1,2},{2,3},{3,4},{4,5},{5,6},{6,7},{7,0},{8,9},{9,10},{10,1... | collective-permute-start | bytes 786440 | tf_op jit(solution)/shard_map/ppermute | solution.py:40
  26.5 13.1 %collective-permute-start.3 = (bf16[4,256,128]{2,1,0:T(8,128)(2,1)S(1)}, bf16[4,256,128]{2,1,0:T(8,128)(2,1)S(1)}, u32[]{:S(2)}, u32[]{:S(2)}) collective-permute-start(bf16[4,256,128]{2,1,0:T(8,128)(2,1)S(1)} %constant_dynamic-update-slice_fusion.refs_0_), channel_id=1, source_target_pairs={{0,7},{1,0},{2,1},{3,2},{4,3},{5,4},{6,5},{7,6},{8,15},{9,8},{10,9... | collective-permute-start | bytes 786440 | tf_op jit(solution)/shard_map/ppermute | solution.py:40
  33.3 14.1 %collective-permute-start.8 = (bf16[27,32,128]{2,1,0:T(8,128)(2,1)S(1)}, bf16[27,32,128]{2,1,0:T(8,128)(2,1)S(1)}, u32[]{:S(2)}, u32[]{:S(2)}) collective-permute-start(bf16[27,32,128]{2,1,0:T(8,128)(2,1)S(1)} %collective-permute-done.5.refs_1_), channel_id=1, source_target_pairs={{0,128},{1,129},{2,130},{3,131},{4,132},{5,133},{6,134},{7,135},{8... | collective-permute-start | bytes 663560 | tf_op jit(solution)/shard_map/ppermute | solution.py:40
  36.4 11.0 %collective-permute-start.10 = (bf16[27,32,128]{2,1,0:T(8,128)(2,1)S(1)}, bf16[27,32,128]{2,1,0:T(8,128)(2,1)S(1)}, u32[]{:S(2)}, u32[]{:S(2)}) collective-permute-start(bf16[27,32,128]{2,1,0:T(8,128)(2,1)S(1)} %collective-permute-done.5.refs_1_), channel_id=1, source_target_pairs={{0,64},{1,65},{2,66},{3,67},{4,68},{5,69},{6,70},{7,71},{8,72},{9,... | collective-permute-start | bytes 663560 | tf_op jit(solution)/shard_map/ppermute | solution.py:40
  36.9 10.5 %collective-permute-start.9 = (bf16[27,32,128]{2,1,0:T(8,128)(2,1)S(1)}, bf16[27,32,128]{2,1,0:T(8,128)(2,1)S(1)}, u32[]{:S(2)}, u32[]{:S(2)}) collective-permute-start(bf16[27,32,128]{2,1,0:T(8,128)(2,1)S(1)} %collective-permute-done.5.refs_1_), channel_id=1, source_target_pairs={{0,192},{1,193},{2,194},{3,195},{4,196},{5,197},{6,198},{7,199},{8... | collective-permute-start | bytes 663560 | tf_op jit(solution)/shard_map/ppermute | solution.py:40
  39.7 6.3 %collective-permute-start.7 = (bf16[2,256,128]{2,1,0:T(8,128)(2,1)S(1)}, bf16[2,256,128]{2,1,0:T(8,128)(2,1)S(1)}, u32[]{:S(2)}, u32[]{:S(2)}) collective-permute-start(bf16[2,256,128]{2,1,0:T(8,128)(2,1)S(1)} %slice.78), channel_id=1, source_target_pairs={{0,1},{1,2},{2,3},{3,4},{4,5},{5,6},{6,7},{7,0},{8,9},{9,10},{10,1... | collective-permute-start | bytes 393224 | tf_op jit(solution)/shard_map/ppermute | solution.py:40
  39.8 6.2 %collective-permute-start.6 = (bf16[2,256,128]{2,1,0:T(8,128)(2,1)S(1)}, bf16[2,256,128]{2,1,0:T(8,128)(2,1)S(1)}, u32[]{:S(2)}, u32[]{:S(2)}) collective-permute-start(bf16[2,256,128]{2,1,0:T(8,128)(2,1)S(1)} %slice.77), channel_id=1, source_target_pairs={{0,7},{1,0},{2,1},{3,2},{4,3},{5,4},{6,5},{7,6},{8,15},{9,8},{10,9... | collective-permute-start | bytes 393224 | tf_op jit(solution)/shard_map/ppermute | solution.py:40
  51.4 3.3 %collective-permute-start.11 = (bf16[8,256,128]{2,1,0:T(8,128)(2,1)S(1)}, bf16[8,256,128]{2,1,0:T(8,128)(2,1)S(1)}, u32[]{:S(2)}, u32[]{:S(2)}) collective-permute-start(bf16[8,256,128]{2,1,0:T(8,128)(2,1)S(1)} %shard_map.77), channel_id=1, source_target_pairs={{0,8},{1,9},{2,10},{3,11},{4,12},{5,13},{6,14},{7,15},{8,0},{9,1},... | collective-permute-start | bytes 1572872 | tf_op jit(solution)/shard_map/ppermute | solution.py:40
  54.7 10.6 %copy-start = (f32[128]{0:T(128)S(1)}, f32[128]{0:T(128)}, u32[]{:S(2)}) copy-start(f32[128]{0:T(128)} %param.6) | copy-start | bytes 1540
  54.9 7.9 %collective-permute-start.12 = (bf16[2,256,128]{2,1,0:T(8,128)(2,1)S(1)}, bf16[2,256,128]{2,1,0:T(8,128)(2,1)S(1)}, u32[]{:S(2)}, u32[]{:S(2)}) collective-permute-start(bf16[2,256,128]{2,1,0:T(8,128)(2,1)S(1)} %get-tuple-element.88), channel_id=1, source_target_pairs={{0,32},{1,33},{2,34},{3,35},{4,36},{5,37},{6,38},{7,39},{8,40},{9,... | collective-permute-start | bytes 393224 | tf_op jit(solution)/shard_map/ppermute | solution.py:40
  55.0 7.8 %collective-permute-start.14 = (bf16[2,256,128]{2,1,0:T(8,128)(2,1)S(1)}, bf16[2,256,128]{2,1,0:T(8,128)(2,1)S(1)}, u32[]{:S(2)}, u32[]{:S(2)}) collective-permute-start(bf16[2,256,128]{2,1,0:T(8,128)(2,1)S(1)} %get-tuple-element.89), channel_id=1, source_target_pairs={{0,48},{1,49},{2,50},{3,51},{4,52},{5,53},{6,54},{7,55},{8,56},{9,... | collective-permute-start | bytes 393224 | tf_op jit(solution)/shard_map/ppermute | solution.py:40
  56.0 9.1 %collective-permute-start.13 = (bf16[2,256,128]{2,1,0:T(8,128)(2,1)S(1)}, bf16[2,256,128]{2,1,0:T(8,128)(2,1)S(1)}, u32[]{:S(2)}, u32[]{:S(2)}) collective-permute-start(bf16[2,256,128]{2,1,0:T(8,128)(2,1)S(1)} %get-tuple-element.90), channel_id=1, source_target_pairs={{0,16},{1,17},{2,18},{3,19},{4,20},{5,21},{6,22},{7,23},{8,24},{9,... | collective-permute-start | bytes 393224 | tf_op jit(solution)/shard_map/ppermute | solution.py:40
  65.5 6.4 %collective-permute-start.17 = (bf16[2,256,128]{2,1,0:T(8,128)(2,1)S(1)}, bf16[2,256,128]{2,1,0:T(8,128)(2,1)S(1)}, u32[]{:S(2)}, u32[]{:S(2)}) collective-permute-start(bf16[2,256,128]{2,1,0:T(8,128)(2,1)S(1)} %get-tuple-element.92.refs_2_.refs_0_), channel_id=1, source_target_pairs={{0,48},{1,49},{2,50},{3,51},{4,52},{5,53},{6,54},{7,55},{8,56},{9,... | collective-permute-start | bytes 393224 | tf_op jit(solution)/shard_map/ppermute | solution.py:40
  66.2 7.9 %collective-permute-start.16 = (bf16[2,256,128]{2,1,0:T(8,128)(2,1)S(1)}, bf16[2,256,128]{2,1,0:T(8,128)(2,1)S(1)}, u32[]{:S(2)}, u32[]{:S(2)}) collective-permute-start(bf16[2,256,128]{2,1,0:T(8,128)(2,1)S(1)} %get-tuple-element.92.refs_2_.refs_0_), channel_id=1, source_target_pairs={{0,32},{1,33},{2,34},{3,35},{4,36},{5,37},{6,38},{7,39},{8,40},{9,... | collective-permute-start | bytes 393224 | tf_op jit(solution)/shard_map/ppermute | solution.py:40
  67.2 7.8 %collective-permute-start.15 = (bf16[2,256,128]{2,1,0:T(8,128)(2,1)S(1)}, bf16[2,256,128]{2,1,0:T(8,128)(2,1)S(1)}, u32[]{:S(2)}, u32[]{:S(2)}) collective-permute-start(bf16[2,256,128]{2,1,0:T(8,128)(2,1)S(1)} %get-tuple-element.92.refs_2_.refs_0_), channel_id=1, source_target_pairs={{0,16},{1,17},{2,18},{3,19},{4,20},{5,21},{6,22},{7,23},{8,24},{9,... | collective-permute-start | bytes 393224 | tf_op jit(solution)/shard_map/ppermute | solution.py:40
  68.5 6.5 %collective-permute-start.18 = (bf16[2,256,128]{2,1,0:T(8,128)(2,1)S(1)}, bf16[2,256,128]{2,1,0:T(8,128)(2,1)S(1)}, u32[]{:S(2)}, u32[]{:S(2)}) collective-permute-start(bf16[2,256,128]{2,1,0:T(8,128)(2,1)S(1)} %get-tuple-element.92.refs_2_.refs_0_), channel_id=1, source_target_pairs={{0,8},{1,9},{2,10},{3,11},{4,12},{5,13},{6,14},{7,15},{8,0},{9,1},... | collective-permute-start | bytes 393224 | tf_op jit(solution)/shard_map/ppermute | solution.py:40
  71.9 3.1 %collective-permute-start.21 = (bf16[2,256,128]{2,1,0:T(8,128)(2,1)S(1)}, bf16[2,256,128]{2,1,0:T(8,128)(2,1)S(1)}, u32[]{:S(2)}, u32[]{:S(2)}) collective-permute-start(bf16[2,256,128]{2,1,0:T(8,128)(2,1)S(1)} %collective-permute-done.17.refs_5_.refs_3_), channel_id=1, source_target_pairs={{0,8},{1,9},{2,10},{3,11},{4,12},{5,13},{6,14},{7,15},{8,0},{9,1},... | collective-permute-start | bytes 393224 | tf_op jit(solution)/shard_map/ppermute | solution.py:40
  74.1 1.3 collective-permute-start.20
  75.0 1.3 collective-permute-start.19
  81.6 15.8 %collective-permute-start.28 = (bf16[28,32,128]{2,1,0:T(8,128)(2,1)S(1)}, bf16[28,32,128]{2,1,0:T(8,128)(2,1)S(1)}, u32[]{:S(2)}, u32[]{:S(2)}) collective-permute-start(bf16[28,32,128]{2,1,0:T(8,128)(2,1)S(1)} %get-tuple-element.80), channel_id=1, source_target_pairs={{0,128},{1,129},{2,130},{3,131},{4,132},{5,133},{6,134},{7,135},{8... | collective-permute-start | bytes 688136 | tf_op jit(solution)/shard_map/ppermute | solution.py:40
  90.7 8.7 %collective-permute-start.29 = (bf16[28,32,128]{2,1,0:T(8,128)(2,1)S(1)}, bf16[28,32,128]{2,1,0:T(8,128)(2,1)S(1)}, u32[]{:S(2)}, u32[]{:S(2)}) collective-permute-start(bf16[28,32,128]{2,1,0:T(8,128)(2,1)S(1)} %get-tuple-element.81), channel_id=1, source_target_pairs={{0,64},{1,65},{2,66},{3,67},{4,68},{5,69},{6,70},{7,71},{8,72},{9,... | collective-permute-start | bytes 688136 | tf_op jit(solution)/shard_map/ppermute | solution.py:40
  91.7 7.7 %collective-permute-start.30 = (bf16[28,32,128]{2,1,0:T(8,128)(2,1)S(1)}, bf16[28,32,128]{2,1,0:T(8,128)(2,1)S(1)}, u32[]{:S(2)}, u32[]{:S(2)}) collective-permute-start(bf16[28,32,128]{2,1,0:T(8,128)(2,1)S(1)} %get-tuple-element.82), channel_id=1, source_target_pairs={{0,192},{1,193},{2,194},{3,195},{4,196},{5,197},{6,198},{7,199},{8... | collective-permute-start | bytes 688136 | tf_op jit(solution)/shard_map/ppermute | solution.py:40
  94.0 9.5 %collective-permute-start.22 = (bf16[4,256,128]{2,1,0:T(8,128)(2,1)S(1)}, bf16[4,256,128]{2,1,0:T(8,128)(2,1)S(1)}, u32[]{:S(2)}, u32[]{:S(2)}) collective-permute-start(bf16[4,256,128]{2,1,0:T(8,128)(2,1)S(1)} %get-tuple-element.74), channel_id=1, source_target_pairs={{0,1},{1,2},{2,3},{3,4},{4,5},{5,6},{6,7},{7,0},{8,9},{9,10},{10,1... | collective-permute-start | bytes 786440 | tf_op jit(solution)/shard_map/ppermute | solution.py:40
  94.0 9.5 %collective-permute-start.23 = (bf16[4,256,128]{2,1,0:T(8,128)(2,1)S(1)}, bf16[4,256,128]{2,1,0:T(8,128)(2,1)S(1)}, u32[]{:S(2)}, u32[]{:S(2)}) collective-permute-start(bf16[4,256,128]{2,1,0:T(8,128)(2,1)S(1)} %get-tuple-element.75), channel_id=1, source_target_pairs={{0,7},{1,0},{2,1},{3,2},{4,3},{5,4},{6,5},{7,6},{8,15},{9,8},{10,9... | collective-permute-start | bytes 786440 | tf_op jit(solution)/shard_map/ppermute | solution.py:40
  99.5 26.1 %collective-permute-start.32 = (bf16[27,32,128]{2,1,0:T(8,128)(2,1)S(1)}, bf16[27,32,128]{2,1,0:T(8,128)(2,1)S(1)}, u32[]{:S(2)}, u32[]{:S(2)}) collective-permute-start(bf16[27,32,128]{2,1,0:T(8,128)(2,1)S(1)} %slice.136), channel_id=1, source_target_pairs={{0,0},{1,1},{2,2},{3,3},{4,4},{5,5},{6,6},{7,7},{8,128},{9,129},{1... | collective-permute-start | bytes 663560 | tf_op jit(solution)/shard_map/ppermute | solution.py:40
  103.7 9.9 %collective-permute-start.24 = (bf16[2,256,128]{2,1,0:T(8,128)(2,1)S(1)}, bf16[2,256,128]{2,1,0:T(8,128)(2,1)S(1)}, u32[]{:S(2)}, u32[]{:S(2)}) collective-permute-start(bf16[2,256,128]{2,1,0:T(8,128)(2,1)S(1)} %get-tuple-element.93), channel_id=1, source_target_pairs={{0,4},{1,5},{2,6},{3,7},{4,0},{5,1},{6,2},{7,3},{8,12},{9,13},{10,... | collective-permute-start | bytes 393224 | tf_op jit(solution)/shard_map/ppermute | solution.py:40
  108.0 10.0 %collective-permute-start.25 = (bf16[2,256,128]{2,1,0:T(8,128)(2,1)S(1)}, bf16[2,256,128]{2,1,0:T(8,128)(2,1)S(1)}, u32[]{:S(2)}, u32[]{:S(2)}) collective-permute-start(bf16[2,256,128]{2,1,0:T(8,128)(2,1)S(1)} %get-tuple-element.94), channel_id=1, source_target_pairs={{0,1},{1,2},{2,3},{3,4},{4,5},{5,6},{6,7},{7,0},{8,9},{9,10},{10,1... | collective-permute-start | bytes 393224 | tf_op jit(solution)/shard_map/ppermute | solution.py:40
  108.5 9.9 %collective-permute-start.26 = (bf16[2,256,128]{2,1,0:T(8,128)(2,1)S(1)}, bf16[2,256,128]{2,1,0:T(8,128)(2,1)S(1)}, u32[]{:S(2)}, u32[]{:S(2)}) collective-permute-start(bf16[2,256,128]{2,1,0:T(8,128)(2,1)S(1)} %get-tuple-element.95), channel_id=1, source_target_pairs={{0,7},{1,0},{2,1},{3,2},{4,3},{5,4},{6,5},{7,6},{8,15},{9,8},{10,9... | collective-permute-start | bytes 393224 | tf_op jit(solution)/shard_map/ppermute | solution.py:40
  118.5 8.0 %collective-permute-start.27 = (bf16[256,128]{1,0:T(8,128)(2,1)S(1)}, bf16[256,128]{1,0:T(8,128)(2,1)S(1)}, u32[]{:S(2)}, u32[]{:S(2)}) collective-permute-start(bf16[256,128]{1,0:T(8,128)(2,1)S(1)} %get-tuple-element.98), channel_id=1, source_target_pairs={{0,8},{1,9},{2,10},{3,11},{4,12},{5,13},{6,14},{7,15},{8,16},{9,17... | collective-permute-start | bytes 196616 | tf_op jit(solution)/shard_map/ppermute | solution.py:40
  118.9 10.4 %collective-permute-start.31 = (bf16[256,128]{1,0:T(8,128)(2,1)S(1)}, bf16[256,128]{1,0:T(8,128)(2,1)S(1)}, u32[]{:S(2)}, u32[]{:S(2)}) collective-permute-start(bf16[256,128]{1,0:T(8,128)(2,1)S(1)} %get-tuple-element.96), channel_id=1, source_target_pairs={{0,8},{1,16},{2,24},{3,32},{4,40},{5,48},{6,56},{7,64},{8,44},{9,5... | collective-permute-start | bytes 196616 | tf_op jit(solution)/shard_map/ppermute | solution.py:40
  122.9 12.5 %collective-permute-start.33 = (bf16[256,128]{1,0:T(8,128)(2,1)S(1)}, bf16[256,128]{1,0:T(8,128)(2,1)S(1)}, u32[]{:S(2)}, u32[]{:S(2)}) collective-permute-start(bf16[256,128]{1,0:T(8,128)(2,1)S(1)} %get-tuple-element.97), channel_id=1, source_target_pairs={{0,0},{1,8},{2,16},{3,24},{4,32},{5,40},{6,48},{7,56},{8,36},{9,44... | collective-permute-start | bytes 196616 | tf_op jit(solution)/shard_map/ppermute | solution.py:40

commit v9 on v8

--- a/solution.py
+++ b/solution.py
@@ -257,7 +257,6 @@
         [],
         0,
     )
-    columns, blocks[2] = lax.optimization_barrier((columns, blocks[2]))
 
     def weights(turned, where):
         (paired,) = call(
@@ -346,7 +345,7 @@
     beyond = (beyond + up[2:].astype(f32) + down[2:].astype(f32)).astype(bf16)
     beyond, above, below = along_z(beyond, 4), along_z(above, 1), along_z(below, -1)
     held = sum((piece.astype(f32) for piece in received), terms[0].astype(f32))
-    bias_rows = held[27, :2]
+    grad_bias = held[27, 0] + held[27, 1]
     grad_filters = permuted(
         held[:27].astype(bf16), lambda x, q, z: device(NX * group(q) + swapped(x), z)
     ).astype(f32)
@@ -358,9 +357,7 @@
 
     first, second = permuted(summed[0], home(0)), permuted(summed[1], home(1))
     shifted = permuted(activated[1], lambda x, q, z: device(NQ * x + q + 1, z))
-    shifted, bias_rows = lax.optimization_barrier((shifted, bias_rows))
     activated = jnp.stack([shifted, activated[0]])
-    grad_bias = bias_rows[0] + bias_rows[1]
     second, grad_filters = lax.optimization_barrier((second, grad_filters))
     grad_input = jnp.stack([second, first])
     shape = (2, GRID, GRID)

time: 137 us -> 129 us (0.942)
  waiting for transfers between devices: 41.9 us -> 35.8 us
    ppermute x34, waiting for transfers between devices: 41.9 us -> 35.8 us  [permuted(): return lax.ppermute(array, ('space', 'chan'), pairs)]
  transfers between devices with their start and end apart: 34 -> 34, of which waited for: 16 -> 16; matrix products, arithmetic and copies ran while one was open for 2% -> 2% of each run, Pallas kernels for 10% -> 6%
where the time goes in v9:
time: 129 us
  starting transfers between devices  65.3 us (51%)
  waiting for transfers between devices  35.8 us (28%)
  Pallas kernels  22.5 us (17%)
  other arithmetic  3.55 us (3%)
    ppermute x34, starting transfers between devices, permuted(): return lax.ppermute(array, ('space', 'chan'), pairs)  65.3 us
    ppermute x34, waiting for transfers between devices, permuted(): return lax.ppermute(array, ('space', 'chan'), pairs)  35.8 us
    pallas_call x9, Pallas kernels, call(): pl.pallas_call(kernel, out_shape=outs, in_specs=[pl.BlockSpec(memory_spac...  22.5 us
  transfers between devices with their start and end apart: 34, of which 16 were waited for; matrix products, arithmetic and copies ran while one was open for 2% of the time, Pallas kernels for 6%

profile of v9, /device:TPU:16, one launch (start us, length us, event | category | flops | bytes accessed | tf_op | source)
XLA Modules:
  0.0 129.2 jit_solution(1685262958639309252)
XLA Ops:
  0.6 1.0 fusion.14
  1.7 2.5 %collective-permute-done = bf16[2,16,16,128]{3,2,1,0:T(8,128)(2,1)S(1)} collective-permute-done((bf16[2,16,16,128]{3,2,1,0:T(8,128)(2,1)S(1)}, bf16[2,16,16,128]{3,2,1,0:T(8,128)(2,1)S(1)}, u32[]{:S(2)}, u32[]{:S(2)}) %collective-permute-start) | collective-permute-done | bytes 131104 | tf_op jit(solution)/shard_map/ppermute | solution.py:40
  4.3 13.5 %collective-permute-start.1 = (bf16[2,256,128]{2,1,0:T(8,128)(2,1)S(1)}, bf16[2,256,128]{2,1,0:T(8,128)(2,1)S(1)}, u32[]{:S(2)}, u32[]{:S(2)}) collective-permute-start(bf16[2,256,128]{2,1,0:T(8,128)(2,1)S(1)} %bitcast.22), channel_id=1, source_target_pairs={{0,0},{1,17},{2,34},{3,51},{4,12},{5,29},{6,46},{7,63},{8,1},{9,18... | collective-permute-start | bytes 393224 | tf_op jit(solution)/shard_map/ppermute | solution.py:40
  17.8 1.9 %collective-permute-start.2 = (bf16[2,256,128]{2,1,0:T(8,128)(2,1)S(1)}, bf16[2,256,128]{2,1,0:T(8,128)(2,1)S(1)}, u32[]{:S(2)}, u32[]{:S(2)}) collective-permute-start(bf16[2,256,128]{2,1,0:T(8,128)(2,1)S(1)} %bitcast.23), channel_id=1, source_target_pairs={{0,4},{1,21},{2,38},{3,55},{4,8},{5,25},{6,42},{7,59},{8,5},{9,22}... | collective-permute-start | bytes 393224 | tf_op jit(solution)/shard_map/ppermute | solution.py:40
  19.7 1.9 %collective-permute-start.5 = (bf16[27,32,128]{2,1,0:T(8,128)(2,1)}, bf16[27,32,128]{2,1,0:T(8,128)(2,1)S(1)}, u32[]{:S(2)}, u32[]{:S(2)}) collective-permute-start(bf16[27,32,128]{2,1,0:T(8,128)(2,1)} %bitcast.27), channel_id=1, source_target_pairs={{0,0},{1,1},{2,2},{3,3},{4,4},{5,5},{6,6},{7,7},{8,128},{9,129},{1... | collective-permute-start | bytes 663560 | tf_op jit(solution)/shard_map/ppermute | solution.py:40
  21.7 4.8 %collective-permute-done.2 = bf16[2,256,128]{2,1,0:T(8,128)(2,1)S(1)} collective-permute-done((bf16[2,256,128]{2,1,0:T(8,128)(2,1)S(1)}, bf16[2,256,128]{2,1,0:T(8,128)(2,1)S(1)}, u32[]{:S(2)}, u32[]{:S(2)}) %collective-permute-start.2) | collective-permute-done | bytes 131104 | tf_op jit(solution)/shard_map/ppermute | solution.py:40
  26.5 6.7 %collective-permute-start.3 = (bf16[4,256,128]{2,1,0:T(8,128)(2,1)S(1)}, bf16[4,256,128]{2,1,0:T(8,128)(2,1)S(1)}, u32[]{:S(2)}, u32[]{:S(2)}) collective-permute-start(bf16[4,256,128]{2,1,0:T(8,128)(2,1)S(1)} %constant_dynamic-update-slice_fusion.refs_0_), channel_id=1, source_target_pairs={{0,7},{1,0},{2,1},{3,2},{4,3},{5,4},{6,5},{7,6},{8,15},{9,8},{10,9... | collective-permute-start | bytes 786440 | tf_op jit(solution)/shard_map/ppermute | solution.py:40
  33.3 0.9 collective-permute-start.10
  34.2 3.3 %collective-permute-start.9 = (bf16[27,32,128]{2,1,0:T(8,128)(2,1)S(1)}, bf16[27,32,128]{2,1,0:T(8,128)(2,1)S(1)}, u32[]{:S(2)}, u32[]{:S(2)}) collective-permute-start(bf16[27,32,128]{2,1,0:T(8,128)(2,1)S(1)} %collective-permute-done.5.refs_1_), channel_id=1, source_target_pairs={{0,128},{1,129},{2,130},{3,131},{4,132},{5,133},{6,134},{7,135},{8... | collective-permute-start | bytes 663560 | tf_op jit(solution)/shard_map/ppermute | solution.py:40
  37.5 1.5 %collective-permute-start.8 = (bf16[27,32,128]{2,1,0:T(8,128)(2,1)S(1)}, bf16[27,32,128]{2,1,0:T(8,128)(2,1)S(1)}, u32[]{:S(2)}, u32[]{:S(2)}) collective-permute-start(bf16[27,32,128]{2,1,0:T(8,128)(2,1)S(1)} %collective-permute-done.5.refs_1_), channel_id=1, source_target_pairs={{0,192},{1,193},{2,194},{3,195},{4,196},{5,197},{6,198},{7,199},{8... | collective-permute-start | bytes 663560 | tf_op jit(solution)/shard_map/ppermute | solution.py:40
  39.2 3.2 %collective-permute-start.6 = (bf16[2,256,128]{2,1,0:T(8,128)(2,1)S(1)}, bf16[2,256,128]{2,1,0:T(8,128)(2,1)S(1)}, u32[]{:S(2)}, u32[]{:S(2)}) collective-permute-start(bf16[2,256,128]{2,1,0:T(8,128)(2,1)S(1)} %slice.74), channel_id=1, source_target_pairs={{0,7},{1,0},{2,1},{3,2},{4,3},{5,4},{6,5},{7,6},{8,15},{9,8},{10,9... | collective-permute-start | bytes 393224 | tf_op jit(solution)/shard_map/ppermute | solution.py:40
  42.5 3.2 %collective-permute-done.10.refs_4_ = bf16[27,32,128]{2,1,0:T(8,128)(2,1)S(1)} collective-permute-done((bf16[27,32,128]{2,1,0:T(8,128)(2,1)S(1)}, bf16[27,32,128]{2,1,0:T(8,128)(2,1)S(1)}, u32[]{:S(2)}, u32[]{:S(2)}) %collective-permute-start.10) | collective-permute-done | bytes 221216 | tf_op jit(solution)/shard_map/ppermute | solution.py:40
  46.2 0.9 shard_map.76.refs_2_
  47.1 1.4 %shard_map.75.refs_1_ = bf16[18,288,384]{2,1,0:T(8,128)(2,1)S(1)} custom-call(s32[2]{0:T(128)S(1)} %pad_add_fusion.where.refs_0_, bf16[4,256,128]{2,1,0:T(8,128)(2,1)S(1)} %constant_dynamic-update-slice_fusion.refs_0_, bf16[4,256,128]{2,1,0:T(8,128)(2,1)S(1)} %collective-permute-done.3.refs_1_, bf16[4,256,128]{2,1,0:T(8,128)(2,1)S(1)} %collective-permute-done.4.refs_2_, ...), custom_call_target="tpu_custom_call" | custom-call | bytes 5029888 | tf_op jit(solution)/shard_map/pallas_call | solution.py:209
  48.6 3.1 %shard_map.77 = bf16[8,256,128]{2,1,0:T(8,128)(2,1)S(1)} custom-call(s32[2]{0:T(128)S(1)} %pad_add_fusion.where.refs_0_, bf16[18,288,384]{2,1,0:T(8,128)(2,1)S(1)} %shard_map.75.refs_1_, bf16[4608,256]{1,0:T(8,128)(2,1)S(1)} %shard_map.76.refs_2_), custom_call_target="tpu_custom_call" | custom-call | flops 1811939328 | bytes 6864896 | tf_op jit(solution)/shard_map/pallas_call | solution.py:209
  51.8 3.1 %shard_map.78 = (f32[2,256,128]{2,1,0:T(8,128)S(1)}, f32[2,256,128]{2,1,0:T(8,128)S(1)}, f32[2,256,128]{2,1,0:T(8,128)S(1)}, f32[2,256,128]{2,1,0:T(8,128)S(1)}) custom-call(s32[2]{0:T(128)S(1)} %pad_add_fusion.where.refs_0_, bf16[18,288,384]{2,1,0:T(8,128)(2,1)S(1)} %shard_map.75.refs_1_, bf16[4608,256]{1,0:T(8,128)(2,1)S(1)} %shard_map.76.refs_2_), custom_call_target="tpu_custom_call" | custom-call | flops 1811939328 | bytes 7389184 | tf_op jit(solution)/shard_map/pallas_call | solution.py:209
  55.2 0.7 collective-permute-start.14
  55.9 1.7 %collective-permute-start.13 = (bf16[2,256,128]{2,1,0:T(8,128)(2,1)S(1)}, bf16[2,256,128]{2,1,0:T(8,128)(2,1)S(1)}, u32[]{:S(2)}, u32[]{:S(2)}) collective-permute-start(bf16[2,256,128]{2,1,0:T(8,128)(2,1)S(1)} %get-tuple-element.82), channel_id=1, source_target_pairs={{0,16},{1,17},{2,18},{3,19},{4,20},{5,21},{6,22},{7,23},{8,24},{9,... | collective-permute-start | bytes 393224 | tf_op jit(solution)/shard_map/ppermute | solution.py:40
  57.7 1.0 shard_map.79.refs_2_
  58.7 4.4 %collective-permute-done.12 = bf16[2,256,128]{2,1,0:T(8,128)(2,1)S(1)} collective-permute-done((bf16[2,256,128]{2,1,0:T(8,128)(2,1)S(1)}, bf16[2,256,128]{2,1,0:T(8,128)(2,1)S(1)}, u32[]{:S(2)}, u32[]{:S(2)}) %collective-permute-start.12) | collective-permute-done | bytes 131104 | tf_op jit(solution)/shard_map/ppermute | solution.py:40
  63.1 1.2 collective-permute-done.14
  64.3 1.2 collective-permute-done.13
  65.8 0.7 collective-permute-start.17
  66.4 0.7 collective-permute-start.16
  67.2 2.0 %collective-permute-start.15 = (bf16[2,256,128]{2,1,0:T(8,128)(2,1)S(1)}, bf16[2,256,128]{2,1,0:T(8,128)(2,1)S(1)}, u32[]{:S(2)}, u32[]{:S(2)}) collective-permute-start(bf16[2,256,128]{2,1,0:T(8,128)(2,1)S(1)} %get-tuple-element.84.refs_2_.refs_0_), channel_id=1, source_target_pairs={{0,16},{1,17},{2,18},{3,19},{4,20},{5,21},{6,22},{7,23},{8,24},{9,... | collective-permute-start | bytes 393224 | tf_op jit(solution)/shard_map/ppermute | solution.py:40
  69.2 3.0 %collective-permute-done.17.refs_5_.refs_3_ = bf16[2,256,128]{2,1,0:T(8,128)(2,1)S(1)} collective-permute-done((bf16[2,256,128]{2,1,0:T(8,128)(2,1)S(1)}, bf16[2,256,128]{2,1,0:T(8,128)(2,1)S(1)}, u32[]{:S(2)}, u32[]{:S(2)}) %collective-permute-start.17) | collective-permute-done | bytes 131104 | tf_op jit(solution)/shard_map/ppermute | solution.py:40
  72.2 2.1 %collective-permute-done.16.refs_4_.refs_2_ = bf16[2,256,128]{2,1,0:T(8,128)(2,1)S(1)} collective-permute-done((bf16[2,256,128]{2,1,0:T(8,128)(2,1)S(1)}, bf16[2,256,128]{2,1,0:T(8,128)(2,1)S(1)}, u32[]{:S(2)}, u32[]{:S(2)}) %collective-permute-start.16) | collective-permute-done | bytes 131104 | tf_op jit(solution)/shard_map/ppermute | solution.py:40
  74.3 0.9 collective-permute-done.15.refs_3_.refs_1_
  75.7 0.9 collective-permute-done.19.refs_7_.refs_5_
  76.6 5.2 %shard_map.80 = (bf16[28,32,128]{2,1,0:T(8,128)(2,1)S(1)}, bf16[28,32,128]{2,1,0:T(8,128)(2,1)S(1)}, bf16[28,32,128]{2,1,0:T(8,128)(2,1)S(1)}, bf16[28,32,128]{2,1,0:T(8,128)(2,1)S(1)}) custom-call(s32[2]{0:T(128)S(1)} %pad_add_fusion.where.refs_0_, bf16[18,288,384]{2,1,0:T(8,128)(2,1)S(1)} %shard_map.75.refs_1_, ...), custom_call_target="tpu_custom_call" | custom-call | flops 3623878656 | bytes 5947392 | tf_op jit(solution)/shard_map/pallas_call | solution.py:209
  81.8 1.4 %shard_map.81.refs_1_ = bf16[18,288,384]{2,1,0:T(8,128)(2,1)S(1)} custom-call(s32[2]{0:T(128)S(1)} %pad_add_fusion.where.refs_0_, bf16[2,256,128]{2,1,0:T(8,128)(2,1)S(1)} %get-tuple-element.84.refs_2_.refs_0_, bf16[2,256,128]{2,1,0:T(8,128)(2,1)S(1)} %collective-permute-done.15.refs_3_.refs_1_, ...), custom_call_target="tpu_custom_call" | custom-call | bytes 5029888 | tf_op jit(solution)/shard_map/pallas_call | solution.py:209
  83.3 3.1 %shard_map.82 = (bf16[4,256,128]{2,1,0:T(8,128)(2,1)S(1)}, bf16[4,256,128]{2,1,0:T(8,128)(2,1)S(1)}) custom-call(s32[2]{0:T(128)S(1)} %pad_add_fusion.where.refs_0_, bf16[18,288,384]{2,1,0:T(8,128)(2,1)S(1)} %shard_map.81.refs_1_, bf16[4608,256]{1,0:T(8,128)(2,1)S(1)} %shard_map.79.refs_2_), custom_call_target="tpu_custom_call" | custom-call | flops 1811939328 | bytes 6864896 | tf_op jit(solution)/shard_map/pallas_call | solution.py:209
  86.7 3.2 %collective-permute-start.23 = (bf16[4,256,128]{2,1,0:T(8,128)(2,1)S(1)}, bf16[4,256,128]{2,1,0:T(8,128)(2,1)S(1)}, u32[]{:S(2)}, u32[]{:S(2)}) collective-permute-start(bf16[4,256,128]{2,1,0:T(8,128)(2,1)S(1)} %get-tuple-element.69), channel_id=1, source_target_pairs={{0,7},{1,0},{2,1},{3,2},{4,3},{5,4},{6,5},{7,6},{8,15},{9,8},{10,9... | collective-permute-start | bytes 786440 | tf_op jit(solution)/shard_map/ppermute | solution.py:40
  90.0 2.1 %collective-permute-start.29 = (bf16[28,32,128]{2,1,0:T(8,128)(2,1)S(1)}, bf16[28,32,128]{2,1,0:T(8,128)(2,1)S(1)}, u32[]{:S(2)}, u32[]{:S(2)}) collective-permute-start(bf16[28,32,128]{2,1,0:T(8,128)(2,1)S(1)} %get-tuple-element.75), channel_id=1, source_target_pairs={{0,128},{1,129},{2,130},{3,131},{4,132},{5,133},{6,134},{7,135},{8... | collective-permute-start | bytes 688136 | tf_op jit(solution)/shard_map/ppermute | solution.py:40
  92.1 3.1 %shard_map.83 = (f32[2,256,128]{2,1,0:T(8,128)S(1)}, f32[2,256,128]{2,1,0:T(8,128)S(1)}, f32[2,256,128]{2,1,0:T(8,128)S(1)}, f32[2,256,128]{2,1,0:T(8,128)S(1)}) custom-call(s32[2]{0:T(128)S(1)} %pad_add_fusion.where.refs_0_, bf16[18,288,384]{2,1,0:T(8,128)(2,1)S(1)} %shard_map.81.refs_1_, bf16[4608,256]{1,0:T(8,128)(2,1)S(1)} %shard_map.79.refs_2_), custom_call_target="tpu_custom_call" | custom-call | flops 1811939328 | bytes 7389184 | tf_op jit(solution)/shard_map/pallas_call | solution.py:209
  95.2 1.5 %collective-permute-start.30 = (bf16[28,32,128]{2,1,0:T(8,128)(2,1)S(1)}, bf16[28,32,128]{2,1,0:T(8,128)(2,1)S(1)}, u32[]{:S(2)}, u32[]{:S(2)}) collective-permute-start(bf16[28,32,128]{2,1,0:T(8,128)(2,1)S(1)} %get-tuple-element.76), channel_id=1, source_target_pairs={{0,64},{1,65},{2,66},{3,67},{4,68},{5,69},{6,70},{7,71},{8,72},{9,... | collective-permute-start | bytes 688136 | tf_op jit(solution)/shard_map/ppermute | solution.py:40
  96.7 1.8 %collective-permute-start.31 = (bf16[28,32,128]{2,1,0:T(8,128)(2,1)S(1)}, bf16[28,32,128]{2,1,0:T(8,128)(2,1)S(1)}, u32[]{:S(2)}, u32[]{:S(2)}) collective-permute-start(bf16[28,32,128]{2,1,0:T(8,128)(2,1)S(1)} %get-tuple-element.77), channel_id=1, source_target_pairs={{0,192},{1,193},{2,194},{3,195},{4,196},{5,197},{6,198},{7,199},{8... | collective-permute-start | bytes 688136 | tf_op jit(solution)/shard_map/ppermute | solution.py:40
  98.7 1.3 %collective-permute-start.24 = (bf16[2,256,128]{2,1,0:T(8,128)(2,1)S(1)}, bf16[2,256,128]{2,1,0:T(8,128)(2,1)S(1)}, u32[]{:S(2)}, u32[]{:S(2)}) collective-permute-start(bf16[2,256,128]{2,1,0:T(8,128)(2,1)S(1)} %get-tuple-element.85), channel_id=1, source_target_pairs={{0,4},{1,5},{2,6},{3,7},{4,0},{5,1},{6,2},{7,3},{8,12},{9,13},{10,... | collective-permute-start | bytes 393224 | tf_op jit(solution)/shard_map/ppermute | solution.py:40
  100.0 0.8 collective-permute-start.25
  100.8 2.4 %collective-permute-start.26 = (bf16[2,256,128]{2,1,0:T(8,128)(2,1)S(1)}, bf16[2,256,128]{2,1,0:T(8,128)(2,1)S(1)}, u32[]{:S(2)}, u32[]{:S(2)}) collective-permute-start(bf16[2,256,128]{2,1,0:T(8,128)(2,1)S(1)} %get-tuple-element.87), channel_id=1, source_target_pairs={{0,7},{1,0},{2,1},{3,2},{4,3},{5,4},{6,5},{7,6},{8,15},{9,8},{10,9... | collective-permute-start | bytes 393224 | tf_op jit(solution)/shard_map/ppermute | solution.py:40
  103.6 4.5 %collective-permute-start.32 = (bf16[27,32,128]{2,1,0:T(8,128)(2,1)S(1)}, bf16[27,32,128]{2,1,0:T(8,128)(2,1)S(1)}, u32[]{:S(2)}, u32[]{:S(2)}) collective-permute-start(bf16[27,32,128]{2,1,0:T(8,128)(2,1)S(1)} %slice.134), channel_id=1, source_target_pairs={{0,0},{1,1},{2,2},{3,3},{4,4},{5,5},{6,6},{7,7},{8,128},{9,129},{1... | collective-permute-start | bytes 663560 | tf_op jit(solution)/shard_map/ppermute | solution.py:40
  108.2 2.6 %collective-permute-done.24 = bf16[2,256,128]{2,1,0:T(8,128)(2,1)S(1)} collective-permute-done((bf16[2,256,128]{2,1,0:T(8,128)(2,1)S(1)}, bf16[2,256,128]{2,1,0:T(8,128)(2,1)S(1)}, u32[]{:S(2)}, u32[]{:S(2)}) %collective-permute-start.24) | collective-permute-done | bytes 131104 | tf_op jit(solution)/shard_map/ppermute | solution.py:40
  111.0 4.6 %collective-permute-start.28 = (bf16[256,128]{1,0:T(8,128)(2,1)S(1)}, bf16[256,128]{1,0:T(8,128)(2,1)S(1)}, u32[]{:S(2)}, u32[]{:S(2)}) collective-permute-start(bf16[256,128]{1,0:T(8,128)(2,1)S(1)} %get-tuple-element.88), channel_id=1, source_target_pairs={{0,8},{1,16},{2,24},{3,32},{4,40},{5,48},{6,56},{7,64},{8,44},{9,5... | collective-permute-start | bytes 196616 | tf_op jit(solution)/shard_map/ppermute | solution.py:40
  116.1 3.2 %collective-permute-start.33 = (bf16[256,128]{1,0:T(8,128)(2,1)S(1)}, bf16[256,128]{1,0:T(8,128)(2,1)S(1)}, u32[]{:S(2)}, u32[]{:S(2)}) collective-permute-start(bf16[256,128]{1,0:T(8,128)(2,1)S(1)} %get-tuple-element.89), channel_id=1, source_target_pairs={{0,0},{1,8},{2,16},{3,24},{4,32},{5,40},{6,48},{7,56},{8,36},{9,44... | collective-permute-start | bytes 196616 | tf_op jit(solution)/shard_map/ppermute | solution.py:40
  119.3 0.8 convert_element_type.108
  120.1 1.2 collective-permute-done.28
  121.3 0.7 pad_maximum_fusion.3
  122.0 6.5 %collective-permute-done.33 = bf16[256,128]{1,0:T(8,128)(2,1)S(1)} collective-permute-done((bf16[256,128]{1,0:T(8,128)(2,1)S(1)}, bf16[256,128]{1,0:T(8,128)(2,1)S(1)}, u32[]{:S(2)}, u32[]{:S(2)}) %collective-permute-start.33) | collective-permute-done | bytes 65568 | tf_op jit(solution)/shard_map/ppermute | solution.py:40
  (55 shorter events, 4.3 us)
Async XLA Ops:
  1.6 2.6 %collective-permute-start = (bf16[2,16,16,128]{3,2,1,0:T(8,128)(2,1)S(1)}, bf16[2,16,16,128]{3,2,1,0:T(8,128)(2,1)S(1)}, u32[]{:S(2)}, u32[]{:S(2)}) collective-permute-start(bf16[2,16,16,128]{3,2,1,0:T(8,128)(2,1)S(1)} %pad_maximum_fusion), channel_id=1, source_target_pairs={{0,248},{1,249},{2,250},{3,251},{4,252},{5,253},{6,254},{7,255},{8... | collective-permute-start | bytes 393224 | tf_op jit(solution)/shard_map/ppermute | solution.py:40
  4.3 17.4 %collective-permute-start.1 = (bf16[2,256,128]{2,1,0:T(8,128)(2,1)S(1)}, bf16[2,256,128]{2,1,0:T(8,128)(2,1)S(1)}, u32[]{:S(2)}, u32[]{:S(2)}) collective-permute-start(bf16[2,256,128]{2,1,0:T(8,128)(2,1)S(1)} %bitcast.22), channel_id=1, source_target_pairs={{0,0},{1,17},{2,34},{3,51},{4,12},{5,29},{6,46},{7,63},{8,1},{9,18... | collective-permute-start | bytes 393224 | tf_op jit(solution)/shard_map/ppermute | solution.py:40
  17.8 8.7 %collective-permute-start.2 = (bf16[2,256,128]{2,1,0:T(8,128)(2,1)S(1)}, bf16[2,256,128]{2,1,0:T(8,128)(2,1)S(1)}, u32[]{:S(2)}, u32[]{:S(2)}) collective-permute-start(bf16[2,256,128]{2,1,0:T(8,128)(2,1)S(1)} %bitcast.23), channel_id=1, source_target_pairs={{0,4},{1,21},{2,38},{3,55},{4,8},{5,25},{6,42},{7,59},{8,5},{9,22}... | collective-permute-start | bytes 393224 | tf_op jit(solution)/shard_map/ppermute | solution.py:40
  19.7 13.6 %collective-permute-start.5 = (bf16[27,32,128]{2,1,0:T(8,128)(2,1)}, bf16[27,32,128]{2,1,0:T(8,128)(2,1)S(1)}, u32[]{:S(2)}, u32[]{:S(2)}) collective-permute-start(bf16[27,32,128]{2,1,0:T(8,128)(2,1)} %bitcast.27), channel_id=1, source_target_pairs={{0,0},{1,1},{2,2},{3,3},{4,4},{5,5},{6,6},{7,7},{8,128},{9,129},{1... | collective-permute-start | bytes 663560 | tf_op jit(solution)/shard_map/ppermute | solution.py:40
  26.5 12.6 %collective-permute-start.4 = (bf16[4,256,128]{2,1,0:T(8,128)(2,1)S(1)}, bf16[4,256,128]{2,1,0:T(8,128)(2,1)S(1)}, u32[]{:S(2)}, u32[]{:S(2)}) collective-permute-start(bf16[4,256,128]{2,1,0:T(8,128)(2,1)S(1)} %constant_dynamic-update-slice_fusion.refs_0_), channel_id=1, source_target_pairs={{0,1},{1,2},{2,3},{3,4},{4,5},{5,6},{6,7},{7,0},{8,9},{9,10},{10,1... | collective-permute-start | bytes 786440 | tf_op jit(solution)/shard_map/ppermute | solution.py:40
  26.5 12.5 %collective-permute-start.3 = (bf16[4,256,128]{2,1,0:T(8,128)(2,1)S(1)}, bf16[4,256,128]{2,1,0:T(8,128)(2,1)S(1)}, u32[]{:S(2)}, u32[]{:S(2)}) collective-permute-start(bf16[4,256,128]{2,1,0:T(8,128)(2,1)S(1)} %constant_dynamic-update-slice_fusion.refs_0_), channel_id=1, source_target_pairs={{0,7},{1,0},{2,1},{3,2},{4,3},{5,4},{6,5},{7,6},{8,15},{9,8},{10,9... | collective-permute-start | bytes 786440 | tf_op jit(solution)/shard_map/ppermute | solution.py:40
  33.3 12.4 %collective-permute-start.10 = (bf16[27,32,128]{2,1,0:T(8,128)(2,1)S(1)}, bf16[27,32,128]{2,1,0:T(8,128)(2,1)S(1)}, u32[]{:S(2)}, u32[]{:S(2)}) collective-permute-start(bf16[27,32,128]{2,1,0:T(8,128)(2,1)S(1)} %collective-permute-done.5.refs_1_), channel_id=1, source_target_pairs={{0,64},{1,65},{2,66},{3,67},{4,68},{5,69},{6,70},{7,71},{8,72},{9,... | collective-permute-start | bytes 663560 | tf_op jit(solution)/shard_map/ppermute | solution.py:40
  34.2 11.4 %collective-permute-start.9 = (bf16[27,32,128]{2,1,0:T(8,128)(2,1)S(1)}, bf16[27,32,128]{2,1,0:T(8,128)(2,1)S(1)}, u32[]{:S(2)}, u32[]{:S(2)}) collective-permute-start(bf16[27,32,128]{2,1,0:T(8,128)(2,1)S(1)} %collective-permute-done.5.refs_1_), channel_id=1, source_target_pairs={{0,128},{1,129},{2,130},{3,131},{4,132},{5,133},{6,134},{7,135},{8... | collective-permute-start | bytes 663560 | tf_op jit(solution)/shard_map/ppermute | solution.py:40
  37.5 8.7 %collective-permute-start.8 = (bf16[27,32,128]{2,1,0:T(8,128)(2,1)S(1)}, bf16[27,32,128]{2,1,0:T(8,128)(2,1)S(1)}, u32[]{:S(2)}, u32[]{:S(2)}) collective-permute-start(bf16[27,32,128]{2,1,0:T(8,128)(2,1)S(1)} %collective-permute-done.5.refs_1_), channel_id=1, source_target_pairs={{0,192},{1,193},{2,194},{3,195},{4,196},{5,197},{6,198},{7,199},{8... | collective-permute-start | bytes 663560 | tf_op jit(solution)/shard_map/ppermute | solution.py:40
  39.1 8.1 %collective-permute-start.7 = (bf16[2,256,128]{2,1,0:T(8,128)(2,1)S(1)}, bf16[2,256,128]{2,1,0:T(8,128)(2,1)S(1)}, u32[]{:S(2)}, u32[]{:S(2)}) collective-permute-start(bf16[2,256,128]{2,1,0:T(8,128)(2,1)S(1)} %slice.75), channel_id=1, source_target_pairs={{0,1},{1,2},{2,3},{3,4},{4,5},{5,6},{6,7},{7,0},{8,9},{9,10},{10,1... | collective-permute-start | bytes 393224 | tf_op jit(solution)/shard_map/ppermute | solution.py:40
  39.2 8.0 %collective-permute-start.6 = (bf16[2,256,128]{2,1,0:T(8,128)(2,1)S(1)}, bf16[2,256,128]{2,1,0:T(8,128)(2,1)S(1)}, u32[]{:S(2)}, u32[]{:S(2)}) collective-permute-start(bf16[2,256,128]{2,1,0:T(8,128)(2,1)S(1)} %slice.74), channel_id=1, source_target_pairs={{0,7},{1,0},{2,1},{3,2},{4,3},{5,4},{6,5},{7,6},{8,15},{9,8},{10,9... | collective-permute-start | bytes 393224 | tf_op jit(solution)/shard_map/ppermute | solution.py:40
  51.7 3.3 %collective-permute-start.11 = (bf16[8,256,128]{2,1,0:T(8,128)(2,1)S(1)}, bf16[8,256,128]{2,1,0:T(8,128)(2,1)S(1)}, u32[]{:S(2)}, u32[]{:S(2)}) collective-permute-start(bf16[8,256,128]{2,1,0:T(8,128)(2,1)S(1)} %shard_map.77), channel_id=1, source_target_pairs={{0,8},{1,9},{2,10},{3,11},{4,12},{5,13},{6,14},{7,15},{8,0},{9,1},... | collective-permute-start | bytes 1572872 | tf_op jit(solution)/shard_map/ppermute | solution.py:40
  54.9 10.6 %copy-start = (f32[128]{0:T(128)S(1)}, f32[128]{0:T(128)}, u32[]{:S(2)}) copy-start(f32[128]{0:T(128)} %param.6) | copy-start | bytes 1540
  55.1 7.9 %collective-permute-start.12 = (bf16[2,256,128]{2,1,0:T(8,128)(2,1)S(1)}, bf16[2,256,128]{2,1,0:T(8,128)(2,1)S(1)}, u32[]{:S(2)}, u32[]{:S(2)}) collective-permute-start(bf16[2,256,128]{2,1,0:T(8,128)(2,1)S(1)} %get-tuple-element.80), channel_id=1, source_target_pairs={{0,32},{1,33},{2,34},{3,35},{4,36},{5,37},{6,38},{7,39},{8,40},{9,... | collective-permute-start | bytes 393224 | tf_op jit(solution)/shard_map/ppermute | solution.py:40
  55.2 9.0 %collective-permute-start.14 = (bf16[2,256,128]{2,1,0:T(8,128)(2,1)S(1)}, bf16[2,256,128]{2,1,0:T(8,128)(2,1)S(1)}, u32[]{:S(2)}, u32[]{:S(2)}) collective-permute-start(bf16[2,256,128]{2,1,0:T(8,128)(2,1)S(1)} %get-tuple-element.81), channel_id=1, source_target_pairs={{0,48},{1,49},{2,50},{3,51},{4,52},{5,53},{6,54},{7,55},{8,56},{9,... | collective-permute-start | bytes 393224 | tf_op jit(solution)/shard_map/ppermute | solution.py:40
  55.9 9.5 %collective-permute-start.13 = (bf16[2,256,128]{2,1,0:T(8,128)(2,1)S(1)}, bf16[2,256,128]{2,1,0:T(8,128)(2,1)S(1)}, u32[]{:S(2)}, u32[]{:S(2)}) collective-permute-start(bf16[2,256,128]{2,1,0:T(8,128)(2,1)S(1)} %get-tuple-element.82), channel_id=1, source_target_pairs={{0,16},{1,17},{2,18},{3,19},{4,20},{5,21},{6,22},{7,23},{8,24},{9,... | collective-permute-start | bytes 393224 | tf_op jit(solution)/shard_map/ppermute | solution.py:40
  65.8 6.4 %collective-permute-start.17 = (bf16[2,256,128]{2,1,0:T(8,128)(2,1)S(1)}, bf16[2,256,128]{2,1,0:T(8,128)(2,1)S(1)}, u32[]{:S(2)}, u32[]{:S(2)}) collective-permute-start(bf16[2,256,128]{2,1,0:T(8,128)(2,1)S(1)} %get-tuple-element.84.refs_2_.refs_0_), channel_id=1, source_target_pairs={{0,48},{1,49},{2,50},{3,51},{4,52},{5,53},{6,54},{7,55},{8,56},{9,... | collective-permute-start | bytes 393224 | tf_op jit(solution)/shard_map/ppermute | solution.py:40
  66.4 7.9 %collective-permute-start.16 = (bf16[2,256,128]{2,1,0:T(8,128)(2,1)S(1)}, bf16[2,256,128]{2,1,0:T(8,128)(2,1)S(1)}, u32[]{:S(2)}, u32[]{:S(2)}) collective-permute-start(bf16[2,256,128]{2,1,0:T(8,128)(2,1)S(1)} %get-tuple-element.84.refs_2_.refs_0_), channel_id=1, source_target_pairs={{0,32},{1,33},{2,34},{3,35},{4,36},{5,37},{6,38},{7,39},{8,40},{9,... | collective-permute-start | bytes 393224 | tf_op jit(solution)/shard_map/ppermute | solution.py:40
  67.2 8.1 %collective-permute-start.15 = (bf16[2,256,128]{2,1,0:T(8,128)(2,1)S(1)}, bf16[2,256,128]{2,1,0:T(8,128)(2,1)S(1)}, u32[]{:S(2)}, u32[]{:S(2)}) collective-permute-start(bf16[2,256,128]{2,1,0:T(8,128)(2,1)S(1)} %get-tuple-element.84.refs_2_.refs_0_), channel_id=1, source_target_pairs={{0,16},{1,17},{2,18},{3,19},{4,20},{5,21},{6,22},{7,23},{8,24},{9,... | collective-permute-start | bytes 393224 | tf_op jit(solution)/shard_map/ppermute | solution.py:40
  69.2 6.1 %collective-permute-start.18 = (bf16[2,256,128]{2,1,0:T(8,128)(2,1)S(1)}, bf16[2,256,128]{2,1,0:T(8,128)(2,1)S(1)}, u32[]{:S(2)}, u32[]{:S(2)}) collective-permute-start(bf16[2,256,128]{2,1,0:T(8,128)(2,1)S(1)} %get-tuple-element.84.refs_2_.refs_0_), channel_id=1, source_target_pairs={{0,8},{1,9},{2,10},{3,11},{4,12},{5,13},{6,14},{7,15},{8,0},{9,1},... | collective-permute-start | bytes 393224 | tf_op jit(solution)/shard_map/ppermute | solution.py:40
  72.2 3.1 %collective-permute-start.21 = (bf16[2,256,128]{2,1,0:T(8,128)(2,1)S(1)}, bf16[2,256,128]{2,1,0:T(8,128)(2,1)S(1)}, u32[]{:S(2)}, u32[]{:S(2)}) collective-permute-start(bf16[2,256,128]{2,1,0:T(8,128)(2,1)S(1)} %collective-permute-done.17.refs_5_.refs_3_), channel_id=1, source_target_pairs={{0,8},{1,9},{2,10},{3,11},{4,12},{5,13},{6,14},{7,15},{8,0},{9,1},... | collective-permute-start | bytes 393224 | tf_op jit(solution)/shard_map/ppermute | solution.py:40
  74.3 1.3 %collective-permute-start.20 = (bf16[2,256,128]{2,1,0:T(8,128)(2,1)S(1)}, bf16[2,256,128]{2,1,0:T(8,128)(2,1)S(1)}, u32[]{:S(2)}, u32[]{:S(2)}) collective-permute-start(bf16[2,256,128]{2,1,0:T(8,128)(2,1)S(1)} %collective-permute-done.16.refs_4_.refs_2_), channel_id=1, source_target_pairs={{0,8},{1,9},{2,10},{3,11},{4,12},{5,13},{6,14},{7,15},{8,0},{9,1},... | collective-permute-start | bytes 393224 | tf_op jit(solution)/shard_map/ppermute | solution.py:40
  75.3 1.3 %collective-permute-start.19 = (bf16[2,256,128]{2,1,0:T(8,128)(2,1)S(1)}, bf16[2,256,128]{2,1,0:T(8,128)(2,1)S(1)}, u32[]{:S(2)}, u32[]{:S(2)}) collective-permute-start(bf16[2,256,128]{2,1,0:T(8,128)(2,1)S(1)} %collective-permute-done.15.refs_3_.refs_1_), channel_id=1, source_target_pairs={{0,8},{1,9},{2,10},{3,11},{4,12},{5,13},{6,14},{7,15},{8,0},{9,1},... | collective-permute-start | bytes 393224 | tf_op jit(solution)/shard_map/ppermute | solution.py:40
  86.4 12.1 %collective-permute-start.22 = (bf16[4,256,128]{2,1,0:T(8,128)(2,1)S(1)}, bf16[4,256,128]{2,1,0:T(8,128)(2,1)S(1)}, u32[]{:S(2)}, u32[]{:S(2)}) collective-permute-start(bf16[4,256,128]{2,1,0:T(8,128)(2,1)S(1)} %get-tuple-element.68), channel_id=1, source_target_pairs={{0,1},{1,2},{2,3},{3,4},{4,5},{5,6},{6,7},{7,0},{8,9},{9,10},{10,1... | collective-permute-start | bytes 786440 | tf_op jit(solution)/shard_map/ppermute | solution.py:40
  86.7 11.8 %collective-permute-start.23 = (bf16[4,256,128]{2,1,0:T(8,128)(2,1)S(1)}, bf16[4,256,128]{2,1,0:T(8,128)(2,1)S(1)}, u32[]{:S(2)}, u32[]{:S(2)}) collective-permute-start(bf16[4,256,128]{2,1,0:T(8,128)(2,1)S(1)} %get-tuple-element.69), channel_id=1, source_target_pairs={{0,7},{1,0},{2,1},{3,2},{4,3},{5,4},{6,5},{7,6},{8,15},{9,8},{10,9... | collective-permute-start | bytes 786440 | tf_op jit(solution)/shard_map/ppermute | solution.py:40
  90.0 10.8 %collective-permute-start.29 = (bf16[28,32,128]{2,1,0:T(8,128)(2,1)S(1)}, bf16[28,32,128]{2,1,0:T(8,128)(2,1)S(1)}, u32[]{:S(2)}, u32[]{:S(2)}) collective-permute-start(bf16[28,32,128]{2,1,0:T(8,128)(2,1)S(1)} %get-tuple-element.75), channel_id=1, source_target_pairs={{0,128},{1,129},{2,130},{3,131},{4,132},{5,133},{6,134},{7,135},{8... | collective-permute-start | bytes 688136 | tf_op jit(solution)/shard_map/ppermute | solution.py:40
  95.2 8.3 %collective-permute-start.30 = (bf16[28,32,128]{2,1,0:T(8,128)(2,1)S(1)}, bf16[28,32,128]{2,1,0:T(8,128)(2,1)S(1)}, u32[]{:S(2)}, u32[]{:S(2)}) collective-permute-start(bf16[28,32,128]{2,1,0:T(8,128)(2,1)S(1)} %get-tuple-element.76), channel_id=1, source_target_pairs={{0,64},{1,65},{2,66},{3,67},{4,68},{5,69},{6,70},{7,71},{8,72},{9,... | collective-permute-start | bytes 688136 | tf_op jit(solution)/shard_map/ppermute | solution.py:40
  96.7 6.8 %collective-permute-start.31 = (bf16[28,32,128]{2,1,0:T(8,128)(2,1)S(1)}, bf16[28,32,128]{2,1,0:T(8,128)(2,1)S(1)}, u32[]{:S(2)}, u32[]{:S(2)}) collective-permute-start(bf16[28,32,128]{2,1,0:T(8,128)(2,1)S(1)} %get-tuple-element.77), channel_id=1, source_target_pairs={{0,192},{1,193},{2,194},{3,195},{4,196},{5,197},{6,198},{7,199},{8... | collective-permute-start | bytes 688136 | tf_op jit(solution)/shard_map/ppermute | solution.py:40
  98.7 12.1 %collective-permute-start.24 = (bf16[2,256,128]{2,1,0:T(8,128)(2,1)S(1)}, bf16[2,256,128]{2,1,0:T(8,128)(2,1)S(1)}, u32[]{:S(2)}, u32[]{:S(2)}) collective-permute-start(bf16[2,256,128]{2,1,0:T(8,128)(2,1)S(1)} %get-tuple-element.85), channel_id=1, source_target_pairs={{0,4},{1,5},{2,6},{3,7},{4,0},{5,1},{6,2},{7,3},{8,12},{9,13},{10,... | collective-permute-start | bytes 393224 | tf_op jit(solution)/shard_map/ppermute | solution.py:40
  100.0 10.8 %collective-permute-start.25 = (bf16[2,256,128]{2,1,0:T(8,128)(2,1)S(1)}, bf16[2,256,128]{2,1,0:T(8,128)(2,1)S(1)}, u32[]{:S(2)}, u32[]{:S(2)}) collective-permute-start(bf16[2,256,128]{2,1,0:T(8,128)(2,1)S(1)} %get-tuple-element.86), channel_id=1, source_target_pairs={{0,1},{1,2},{2,3},{3,4},{4,5},{5,6},{6,7},{7,0},{8,9},{9,10},{10,1... | collective-permute-start | bytes 393224 | tf_op jit(solution)/shard_map/ppermute | solution.py:40
  100.8 10.0 %collective-permute-start.26 = (bf16[2,256,128]{2,1,0:T(8,128)(2,1)S(1)}, bf16[2,256,128]{2,1,0:T(8,128)(2,1)S(1)}, u32[]{:S(2)}, u32[]{:S(2)}) collective-permute-start(bf16[2,256,128]{2,1,0:T(8,128)(2,1)S(1)} %get-tuple-element.87), channel_id=1, source_target_pairs={{0,7},{1,0},{2,1},{3,2},{4,3},{5,4},{6,5},{7,6},{8,15},{9,8},{10,9... | collective-permute-start | bytes 393224 | tf_op jit(solution)/shard_map/ppermute | solution.py:40
  103.6 15.7 %collective-permute-start.32 = (bf16[27,32,128]{2,1,0:T(8,128)(2,1)S(1)}, bf16[27,32,128]{2,1,0:T(8,128)(2,1)S(1)}, u32[]{:S(2)}, u32[]{:S(2)}) collective-permute-start(bf16[27,32,128]{2,1,0:T(8,128)(2,1)S(1)} %slice.134), channel_id=1, source_target_pairs={{0,0},{1,1},{2,2},{3,3},{4,4},{5,5},{6,6},{7,7},{8,128},{9,129},{1... | collective-permute-start | bytes 663560 | tf_op jit(solution)/shard_map/ppermute | solution.py:40
  110.9 10.5 %collective-permute-start.27 = (bf16[256,128]{1,0:T(8,128)(2,1)S(1)}, bf16[256,128]{1,0:T(8,128)(2,1)S(1)}, u32[]{:S(2)}, u32[]{:S(2)}) collective-permute-start(bf16[256,128]{1,0:T(8,128)(2,1)S(1)} %get-tuple-element.90), channel_id=1, source_target_pairs={{0,8},{1,9},{2,10},{3,11},{4,12},{5,13},{6,14},{7,15},{8,16},{9,17... | collective-permute-start | bytes 196616 | tf_op jit(solution)/shard_map/ppermute | solution.py:40
  111.0 10.4 %collective-permute-start.28 = (bf16[256,128]{1,0:T(8,128)(2,1)S(1)}, bf16[256,128]{1,0:T(8,128)(2,1)S(1)}, u32[]{:S(2)}, u32[]{:S(2)}) collective-permute-start(bf16[256,128]{1,0:T(8,128)(2,1)S(1)} %get-tuple-element.88), channel_id=1, source_target_pairs={{0,8},{1,16},{2,24},{3,32},{4,40},{5,48},{6,56},{7,64},{8,44},{9,5... | collective-permute-start | bytes 196616 | tf_op jit(solution)/shard_map/ppermute | solution.py:40
  116.1 12.5 %collective-permute-start.33 = (bf16[256,128]{1,0:T(8,128)(2,1)S(1)}, bf16[256,128]{1,0:T(8,128)(2,1)S(1)}, u32[]{:S(2)}, u32[]{:S(2)}) collective-permute-start(bf16[256,128]{1,0:T(8,128)(2,1)S(1)} %get-tuple-element.89), channel_id=1, source_target_pairs={{0,0},{1,8},{2,16},{3,24},{4,32},{5,40},{6,48},{7,56},{8,36},{9,44... | collective-permute-start | bytes 196616 | tf_op jit(solution)/shard_map/ppermute | solution.py:40

commit v10 on v7

--- a/solution.py
+++ b/solution.py
@@ -320,7 +320,8 @@
         ],
         flops,
     )
-    where, terms = lax.optimization_barrier((where, terms))
+    shifted = permuted(activated[1], lambda x, q, z: device(NQ * x + q + 1, z))
+    where, terms, shifted = lax.optimization_barrier((where, terms, shifted))
     def parts(steps, where, outs):
         return call(
             lambda *refs: product_kernel(lambda where: ring_pairs(where, steps), *refs),
@@ -351,13 +352,12 @@
         held[:27].astype(bf16), lambda x, q, z: device(NX * group(q) + swapped(x), z)
     ).astype(f32)
     summed = summed + beyond.astype(f32) + above.astype(f32) + below.astype(f32)
-    summed, activated = lax.optimization_barrier((summed.astype(bf16), activated))
+    summed = summed.astype(bf16)
 
     def home(half):
         return lambda x, q, z: device(NQ * x + (z - group(q)) % NZ + half, group(q))
 
     first, second = permuted(summed[0], home(0)), permuted(summed[1], home(1))
-    shifted = permuted(activated[1], lambda x, q, z: device(NQ * x + q + 1, z))
     activated = jnp.stack([shifted, activated[0]])
     second, grad_filters = lax.optimization_barrier((second, grad_filters))
     grad_input = jnp.stack([second, first])

time: 130 us -> 129 us (level)
  waiting for transfers between devices: 33.9 us -> 30.9 us
  starting transfers between devices: 67.5 us -> 69.9 us
    ppermute x34, waiting for transfers between devices: 33.9 us -> 30.9 us  [permuted(): return lax.ppermute(array, ('space', 'chan'), pairs)]
    ppermute x34, starting transfers between devices: 67.5 us -> 69.9 us  [permuted(): return lax.ppermute(array, ('space', 'chan'), pairs)]
  transfers between devices with their start and end apart: 34 -> 34, of which waited for: 15 -> 12; matrix products, arithmetic and copies ran while one was open for 2% -> 2% of each run, Pallas kernels for 7% -> 14%
where the time goes in v10:
time: 129 us
  starting transfers between devices  69.9 us (54%)
  waiting for transfers between devices  30.9 us (24%)
  Pallas kernels  22.5 us (17%)
  other arithmetic  3.54 us (3%)
    ppermute x34, starting transfers between devices, permuted(): return lax.ppermute(array, ('space', 'chan'), pairs)  69.9 us
    ppermute x34, waiting for transfers between devices, permuted(): return lax.ppermute(array, ('space', 'chan'), pairs)  30.9 us
    pallas_call x9, Pallas kernels, call(): pl.pallas_call(kernel, out_shape=outs, in_specs=[pl.BlockSpec(memory_spac...  22.5 us
  transfers between devices with their start and end apart: 34, of which 12 were waited for; matrix products, arithmetic and copies ran while one was open for 2% of the time, Pallas kernels for 14%

profile of v10, /device:TPU:16, one launch (start us, length us, event | category | flops | bytes accessed | tf_op | source)
XLA Modules:
  0.0 128.9 jit_solution(14327792063924158610)
XLA Ops:
  0.6 1.0 fusion.14
  1.7 2.5 %collective-permute-done = bf16[2,16,16,128]{3,2,1,0:T(8,128)(2,1)S(1)} collective-permute-done((bf16[2,16,16,128]{3,2,1,0:T(8,128)(2,1)S(1)}, bf16[2,16,16,128]{3,2,1,0:T(8,128)(2,1)S(1)}, u32[]{:S(2)}, u32[]{:S(2)}) %collective-permute-start) | collective-permute-done | bytes 131104 | tf_op jit(solution)/shard_map/ppermute | solution.py:40
  4.3 13.5 %collective-permute-start.1 = (bf16[2,256,128]{2,1,0:T(8,128)(2,1)S(1)}, bf16[2,256,128]{2,1,0:T(8,128)(2,1)S(1)}, u32[]{:S(2)}, u32[]{:S(2)}) collective-permute-start(bf16[2,256,128]{2,1,0:T(8,128)(2,1)S(1)} %bitcast.22), channel_id=1, source_target_pairs={{0,0},{1,17},{2,34},{3,51},{4,12},{5,29},{6,46},{7,63},{8,1},{9,18... | collective-permute-start | bytes 393224 | tf_op jit(solution)/shard_map/ppermute | solution.py:40
  17.8 1.9 %collective-permute-start.2 = (bf16[2,256,128]{2,1,0:T(8,128)(2,1)S(1)}, bf16[2,256,128]{2,1,0:T(8,128)(2,1)S(1)}, u32[]{:S(2)}, u32[]{:S(2)}) collective-permute-start(bf16[2,256,128]{2,1,0:T(8,128)(2,1)S(1)} %bitcast.23), channel_id=1, source_target_pairs={{0,4},{1,21},{2,38},{3,55},{4,8},{5,25},{6,42},{7,59},{8,5},{9,22}... | collective-permute-start | bytes 393224 | tf_op jit(solution)/shard_map/ppermute | solution.py:40
  19.7 1.9 %collective-permute-start.5 = (bf16[27,32,128]{2,1,0:T(8,128)(2,1)}, bf16[27,32,128]{2,1,0:T(8,128)(2,1)S(1)}, u32[]{:S(2)}, u32[]{:S(2)}) collective-permute-start(bf16[27,32,128]{2,1,0:T(8,128)(2,1)} %bitcast.27), channel_id=1, source_target_pairs={{0,0},{1,1},{2,2},{3,3},{4,4},{5,5},{6,6},{7,7},{8,128},{9,129},{1... | collective-permute-start | bytes 663560 | tf_op jit(solution)/shard_map/ppermute | solution.py:40
  21.7 4.8 %collective-permute-done.2 = bf16[2,256,128]{2,1,0:T(8,128)(2,1)S(1)} collective-permute-done((bf16[2,256,128]{2,1,0:T(8,128)(2,1)S(1)}, bf16[2,256,128]{2,1,0:T(8,128)(2,1)S(1)}, u32[]{:S(2)}, u32[]{:S(2)}) %collective-permute-start.2) | collective-permute-done | bytes 131104 | tf_op jit(solution)/shard_map/ppermute | solution.py:40
  26.5 6.7 %collective-permute-start.3 = (bf16[4,256,128]{2,1,0:T(8,128)(2,1)S(1)}, bf16[4,256,128]{2,1,0:T(8,128)(2,1)S(1)}, u32[]{:S(2)}, u32[]{:S(2)}) collective-permute-start(bf16[4,256,128]{2,1,0:T(8,128)(2,1)S(1)} %constant_dynamic-update-slice_fusion.refs_0_), channel_id=1, source_target_pairs={{0,7},{1,0},{2,1},{3,2},{4,3},{5,4},{6,5},{7,6},{8,15},{9,8},{10,9... | collective-permute-start | bytes 786440 | tf_op jit(solution)/shard_map/ppermute | solution.py:40
  33.3 0.9 collective-permute-start.9
  34.2 2.3 %collective-permute-start.8 = (bf16[27,32,128]{2,1,0:T(8,128)(2,1)S(1)}, bf16[27,32,128]{2,1,0:T(8,128)(2,1)S(1)}, u32[]{:S(2)}, u32[]{:S(2)}) collective-permute-start(bf16[27,32,128]{2,1,0:T(8,128)(2,1)S(1)} %collective-permute-done.5.refs_1_), channel_id=1, source_target_pairs={{0,192},{1,193},{2,194},{3,195},{4,196},{5,197},{6,198},{7,199},{8... | collective-permute-start | bytes 663560 | tf_op jit(solution)/shard_map/ppermute | solution.py:40
  36.5 1.9 %collective-permute-start.10 = (bf16[27,32,128]{2,1,0:T(8,128)(2,1)S(1)}, bf16[27,32,128]{2,1,0:T(8,128)(2,1)S(1)}, u32[]{:S(2)}, u32[]{:S(2)}) collective-permute-start(bf16[27,32,128]{2,1,0:T(8,128)(2,1)S(1)} %collective-permute-done.5.refs_1_), channel_id=1, source_target_pairs={{0,128},{1,129},{2,130},{3,131},{4,132},{5,133},{6,134},{7,135},{8... | collective-permute-start | bytes 663560 | tf_op jit(solution)/shard_map/ppermute | solution.py:40
  38.5 3.2 %collective-permute-start.6 = (bf16[2,256,128]{2,1,0:T(8,128)(2,1)S(1)}, bf16[2,256,128]{2,1,0:T(8,128)(2,1)S(1)}, u32[]{:S(2)}, u32[]{:S(2)}) collective-permute-start(bf16[2,256,128]{2,1,0:T(8,128)(2,1)S(1)} %slice.74), channel_id=1, source_target_pairs={{0,7},{1,0},{2,1},{3,2},{4,3},{5,4},{6,5},{7,6},{8,15},{9,8},{10,9... | collective-permute-start | bytes 393224 | tf_op jit(solution)/shard_map/ppermute | solution.py:40
  41.8 2.9 %collective-permute-done.7.refs_4_ = bf16[2,256,128]{2,1,0:T(8,128)(2,1)S(1)} collective-permute-done((bf16[2,256,128]{2,1,0:T(8,128)(2,1)S(1)}, bf16[2,256,128]{2,1,0:T(8,128)(2,1)S(1)}, u32[]{:S(2)}, u32[]{:S(2)}) %collective-permute-start.7) | collective-permute-done | bytes 131104 | tf_op jit(solution)/shard_map/ppermute | solution.py:40
  44.7 1.4 %shard_map.75.refs_1_ = bf16[18,288,384]{2,1,0:T(8,128)(2,1)S(1)} custom-call(s32[2]{0:T(128)S(1)} %pad_add_fusion.where.refs_0_, bf16[4,256,128]{2,1,0:T(8,128)(2,1)S(1)} %constant_dynamic-update-slice_fusion.refs_0_, bf16[4,256,128]{2,1,0:T(8,128)(2,1)S(1)} %collective-permute-done.3.refs_1_, bf16[4,256,128]{2,1,0:T(8,128)(2,1)S(1)} %collective-permute-done.4.refs_2_, ...), custom_call_target="tpu_custom_call" | custom-call | bytes 5029888 | tf_op jit(solution)/shard_map/pallas_call | solution.py:209
  46.2 0.9 shard_map.76.refs_2_
  47.1 3.1 %shard_map.77 = bf16[8,256,128]{2,1,0:T(8,128)(2,1)S(1)} custom-call(s32[2]{0:T(128)S(1)} %pad_add_fusion.where.refs_0_, bf16[18,288,384]{2,1,0:T(8,128)(2,1)S(1)} %shard_map.75.refs_1_, bf16[4608,256]{1,0:T(8,128)(2,1)S(1)} %shard_map.76.refs_2_), custom_call_target="tpu_custom_call" | custom-call | flops 1811939328 | bytes 6864896 | tf_op jit(solution)/shard_map/pallas_call | solution.py:209
  50.3 3.1 %shard_map.78 = (f32[2,256,128]{2,1,0:T(8,128)S(1)}, f32[2,256,128]{2,1,0:T(8,128)S(1)}, f32[2,256,128]{2,1,0:T(8,128)S(1)}, f32[2,256,128]{2,1,0:T(8,128)S(1)}) custom-call(s32[2]{0:T(128)S(1)} %pad_add_fusion.where.refs_0_, bf16[18,288,384]{2,1,0:T(8,128)(2,1)S(1)} %shard_map.75.refs_1_, bf16[4608,256]{1,0:T(8,128)(2,1)S(1)} %shard_map.76.refs_2_), custom_call_target="tpu_custom_call" | custom-call | flops 1811939328 | bytes 7389184 | tf_op jit(solution)/shard_map/pallas_call | solution.py:209
  53.8 1.1 collective-permute-start.14
  54.8 1.3 %collective-permute-start.13 = (bf16[2,256,128]{2,1,0:T(8,128)(2,1)S(1)}, bf16[2,256,128]{2,1,0:T(8,128)(2,1)S(1)}, u32[]{:S(2)}, u32[]{:S(2)}) collective-permute-start(bf16[2,256,128]{2,1,0:T(8,128)(2,1)S(1)} %get-tuple-element.86), channel_id=1, source_target_pairs={{0,16},{1,17},{2,18},{3,19},{4,20},{5,21},{6,22},{7,23},{8,24},{9,... | collective-permute-start | bytes 393224 | tf_op jit(solution)/shard_map/ppermute | solution.py:40
  56.2 1.0 shard_map.79.refs_2_
  57.2 4.4 %collective-permute-done.12 = bf16[2,256,128]{2,1,0:T(8,128)(2,1)S(1)} collective-permute-done((bf16[2,256,128]{2,1,0:T(8,128)(2,1)S(1)}, bf16[2,256,128]{2,1,0:T(8,128)(2,1)S(1)}, u32[]{:S(2)}, u32[]{:S(2)}) %collective-permute-start.12) | collective-permute-done | bytes 131104 | tf_op jit(solution)/shard_map/ppermute | solution.py:40
  61.6 1.3 collective-permute-done.14
  62.8 1.1 collective-permute-done.13
  64.3 0.7 collective-permute-start.17
  65.0 1.1 collective-permute-start.16
  66.1 1.7 %collective-permute-start.15 = (bf16[2,256,128]{2,1,0:T(8,128)(2,1)S(1)}, bf16[2,256,128]{2,1,0:T(8,128)(2,1)S(1)}, u32[]{:S(2)}, u32[]{:S(2)}) collective-permute-start(bf16[2,256,128]{2,1,0:T(8,128)(2,1)S(1)} %get-tuple-element.87.refs_2_.refs_0_), channel_id=1, source_target_pairs={{0,16},{1,17},{2,18},{3,19},{4,20},{5,21},{6,22},{7,23},{8,24},{9,... | collective-permute-start | bytes 393224 | tf_op jit(solution)/shard_map/ppermute | solution.py:40
  67.8 2.9 %collective-permute-done.17.refs_5_.refs_3_ = bf16[2,256,128]{2,1,0:T(8,128)(2,1)S(1)} collective-permute-done((bf16[2,256,128]{2,1,0:T(8,128)(2,1)S(1)}, bf16[2,256,128]{2,1,0:T(8,128)(2,1)S(1)}, u32[]{:S(2)}, u32[]{:S(2)}) %collective-permute-start.17) | collective-permute-done | bytes 131104 | tf_op jit(solution)/shard_map/ppermute | solution.py:40
  70.7 2.1 %collective-permute-done.16.refs_4_.refs_2_ = bf16[2,256,128]{2,1,0:T(8,128)(2,1)S(1)} collective-permute-done((bf16[2,256,128]{2,1,0:T(8,128)(2,1)S(1)}, bf16[2,256,128]{2,1,0:T(8,128)(2,1)S(1)}, u32[]{:S(2)}, u32[]{:S(2)}) %collective-permute-start.16) | collective-permute-done | bytes 131104 | tf_op jit(solution)/shard_map/ppermute | solution.py:40
  72.9 0.9 collective-permute-done.15.refs_3_.refs_1_
  74.4 0.7 collective-permute-done.19.refs_7_.refs_5_
  75.1 5.2 %shard_map.80 = (bf16[28,32,128]{2,1,0:T(8,128)(2,1)S(1)}, bf16[28,32,128]{2,1,0:T(8,128)(2,1)S(1)}, bf16[28,32,128]{2,1,0:T(8,128)(2,1)S(1)}, bf16[28,32,128]{2,1,0:T(8,128)(2,1)S(1)}) custom-call(s32[2]{0:T(128)S(1)} %pad_add_fusion.where.refs_0_, bf16[18,288,384]{2,1,0:T(8,128)(2,1)S(1)} %shard_map.75.refs_1_, ...), custom_call_target="tpu_custom_call" | custom-call | flops 3623878656 | bytes 5947392 | tf_op jit(solution)/shard_map/pallas_call | solution.py:209
  80.4 2.7 %collective-permute-start.29 = (bf16[28,32,128]{2,1,0:T(8,128)(2,1)S(1)}, bf16[28,32,128]{2,1,0:T(8,128)(2,1)S(1)}, u32[]{:S(2)}, u32[]{:S(2)}) collective-permute-start(bf16[28,32,128]{2,1,0:T(8,128)(2,1)S(1)} %get-tuple-element.79), channel_id=1, source_target_pairs={{0,128},{1,129},{2,130},{3,131},{4,132},{5,133},{6,134},{7,135},{8... | collective-permute-start | bytes 688136 | tf_op jit(solution)/shard_map/ppermute | solution.py:40
  83.1 1.4 %shard_map.81.refs_1_ = bf16[18,288,384]{2,1,0:T(8,128)(2,1)S(1)} custom-call(s32[2]{0:T(128)S(1)} %pad_add_fusion.where.refs_0_, bf16[2,256,128]{2,1,0:T(8,128)(2,1)S(1)} %get-tuple-element.87.refs_2_.refs_0_, bf16[2,256,128]{2,1,0:T(8,128)(2,1)S(1)} %collective-permute-done.15.refs_3_.refs_1_, ...), custom_call_target="tpu_custom_call" | custom-call | bytes 5029888 | tf_op jit(solution)/shard_map/pallas_call | solution.py:209
  84.5 3.1 %shard_map.82 = (bf16[4,256,128]{2,1,0:T(8,128)(2,1)S(1)}, bf16[4,256,128]{2,1,0:T(8,128)(2,1)S(1)}) custom-call(s32[2]{0:T(128)S(1)} %pad_add_fusion.where.refs_0_, bf16[18,288,384]{2,1,0:T(8,128)(2,1)S(1)} %shard_map.81.refs_1_, bf16[4608,256]{1,0:T(8,128)(2,1)S(1)} %shard_map.79.refs_2_), custom_call_target="tpu_custom_call" | custom-call | flops 1811939328 | bytes 6864896 | tf_op jit(solution)/shard_map/pallas_call | solution.py:209
  87.8 3.3 %collective-permute-start.24 = (bf16[4,256,128]{2,1,0:T(8,128)(2,1)S(1)}, bf16[4,256,128]{2,1,0:T(8,128)(2,1)S(1)}, u32[]{:S(2)}, u32[]{:S(2)}) collective-permute-start(bf16[4,256,128]{2,1,0:T(8,128)(2,1)S(1)} %get-tuple-element.75), channel_id=1, source_target_pairs={{0,7},{1,0},{2,1},{3,2},{4,3},{5,4},{6,5},{7,6},{8,15},{9,8},{10,9... | collective-permute-start | bytes 786440 | tf_op jit(solution)/shard_map/ppermute | solution.py:40
  91.1 3.1 %shard_map.83 = (f32[2,256,128]{2,1,0:T(8,128)S(1)}, f32[2,256,128]{2,1,0:T(8,128)S(1)}, f32[2,256,128]{2,1,0:T(8,128)S(1)}, f32[2,256,128]{2,1,0:T(8,128)S(1)}) custom-call(s32[2]{0:T(128)S(1)} %pad_add_fusion.where.refs_0_, bf16[18,288,384]{2,1,0:T(8,128)(2,1)S(1)} %shard_map.81.refs_1_, bf16[4608,256]{1,0:T(8,128)(2,1)S(1)} %shard_map.79.refs_2_), custom_call_target="tpu_custom_call" | custom-call | flops 1811939328 | bytes 7389184 | tf_op jit(solution)/shard_map/pallas_call | solution.py:209
  94.2 1.0 collective-permute-start.30
  95.2 2.4 %collective-permute-start.31 = (bf16[28,32,128]{2,1,0:T(8,128)(2,1)S(1)}, bf16[28,32,128]{2,1,0:T(8,128)(2,1)S(1)}, u32[]{:S(2)}, u32[]{:S(2)}) collective-permute-start(bf16[28,32,128]{2,1,0:T(8,128)(2,1)S(1)} %get-tuple-element.81), channel_id=1, source_target_pairs={{0,192},{1,193},{2,194},{3,195},{4,196},{5,197},{6,198},{7,199},{8... | collective-permute-start | bytes 688136 | tf_op jit(solution)/shard_map/ppermute | solution.py:40
  97.5 0.7 pad_maximum_fusion.3
  98.3 3.1 %collective-permute-start.25 = (bf16[2,256,128]{2,1,0:T(8,128)(2,1)S(1)}, bf16[2,256,128]{2,1,0:T(8,128)(2,1)S(1)}, u32[]{:S(2)}, u32[]{:S(2)}) collective-permute-start(bf16[2,256,128]{2,1,0:T(8,128)(2,1)S(1)} %get-tuple-element.89), channel_id=1, source_target_pairs={{0,4},{1,5},{2,6},{3,7},{4,0},{5,1},{6,2},{7,3},{8,12},{9,13},{10,... | collective-permute-start | bytes 393224 | tf_op jit(solution)/shard_map/ppermute | solution.py:40
  101.4 0.8 collective-permute-start.26
  102.2 2.4 %collective-permute-start.27 = (bf16[2,256,128]{2,1,0:T(8,128)(2,1)S(1)}, bf16[2,256,128]{2,1,0:T(8,128)(2,1)S(1)}, u32[]{:S(2)}, u32[]{:S(2)}) collective-permute-start(bf16[2,256,128]{2,1,0:T(8,128)(2,1)S(1)} %get-tuple-element.91), channel_id=1, source_target_pairs={{0,7},{1,0},{2,1},{3,2},{4,3},{5,4},{6,5},{7,6},{8,15},{9,8},{10,9... | collective-permute-start | bytes 393224 | tf_op jit(solution)/shard_map/ppermute | solution.py:40
  104.8 5.1 %collective-permute-start.32 = (bf16[27,32,128]{2,1,0:T(8,128)(2,1)S(1)}, bf16[27,32,128]{2,1,0:T(8,128)(2,1)S(1)}, u32[]{:S(2)}, u32[]{:S(2)}) collective-permute-start(bf16[27,32,128]{2,1,0:T(8,128)(2,1)S(1)} %slice.138), channel_id=1, source_target_pairs={{0,0},{1,1},{2,2},{3,3},{4,4},{5,5},{6,6},{7,7},{8,128},{9,129},{1... | collective-permute-start | bytes 663560 | tf_op jit(solution)/shard_map/ppermute | solution.py:40
  109.9 0.7 collective-permute-done.26
  110.8 4.9 %collective-permute-start.28 = (bf16[256,128]{1,0:T(8,128)(2,1)S(1)}, bf16[256,128]{1,0:T(8,128)(2,1)S(1)}, u32[]{:S(2)}, u32[]{:S(2)}) collective-permute-start(bf16[256,128]{1,0:T(8,128)(2,1)S(1)} %get-tuple-element.92), channel_id=1, source_target_pairs={{0,8},{1,16},{2,24},{3,32},{4,40},{5,48},{6,56},{7,64},{8,44},{9,5... | collective-permute-start | bytes 196616 | tf_op jit(solution)/shard_map/ppermute | solution.py:40
  115.7 4.7 %collective-permute-start.33 = (bf16[256,128]{1,0:T(8,128)(2,1)S(1)}, bf16[256,128]{1,0:T(8,128)(2,1)S(1)}, u32[]{:S(2)}, u32[]{:S(2)}) collective-permute-start(bf16[256,128]{1,0:T(8,128)(2,1)S(1)} %get-tuple-element.93), channel_id=1, source_target_pairs={{0,0},{1,8},{2,16},{3,24},{4,32},{5,40},{6,48},{7,56},{8,36},{9,44... | collective-permute-start | bytes 196616 | tf_op jit(solution)/shard_map/ppermute | solution.py:40
  121.0 0.8 convert_element_type.108
  121.8 6.4 %collective-permute-done.33 = bf16[256,128]{1,0:T(8,128)(2,1)S(1)} collective-permute-done((bf16[256,128]{1,0:T(8,128)(2,1)S(1)}, bf16[256,128]{1,0:T(8,128)(2,1)S(1)}, u32[]{:S(2)}, u32[]{:S(2)}) %collective-permute-start.33) | collective-permute-done | bytes 65568 | tf_op jit(solution)/shard_map/ppermute | solution.py:40
  128.2 0.7 pad_maximum_fusion.4
  (55 shorter events, 2.7 us)
Async XLA Ops:
  1.6 2.6 %collective-permute-start = (bf16[2,16,16,128]{3,2,1,0:T(8,128)(2,1)S(1)}, bf16[2,16,16,128]{3,2,1,0:T(8,128)(2,1)S(1)}, u32[]{:S(2)}, u32[]{:S(2)}) collective-permute-start(bf16[2,16,16,128]{3,2,1,0:T(8,128)(2,1)S(1)} %pad_maximum_fusion), channel_id=1, source_target_pairs={{0,248},{1,249},{2,250},{3,251},{4,252},{5,253},{6,254},{7,255},{8... | collective-permute-start | bytes 393224 | tf_op jit(solution)/shard_map/ppermute | solution.py:40
  4.3 17.4 %collective-permute-start.1 = (bf16[2,256,128]{2,1,0:T(8,128)(2,1)S(1)}, bf16[2,256,128]{2,1,0:T(8,128)(2,1)S(1)}, u32[]{:S(2)}, u32[]{:S(2)}) collective-permute-start(bf16[2,256,128]{2,1,0:T(8,128)(2,1)S(1)} %bitcast.22), channel_id=1, source_target_pairs={{0,0},{1,17},{2,34},{3,51},{4,12},{5,29},{6,46},{7,63},{8,1},{9,18... | collective-permute-start | bytes 393224 | tf_op jit(solution)/shard_map/ppermute | solution.py:40
  17.8 8.7 %collective-permute-start.2 = (bf16[2,256,128]{2,1,0:T(8,128)(2,1)S(1)}, bf16[2,256,128]{2,1,0:T(8,128)(2,1)S(1)}, u32[]{:S(2)}, u32[]{:S(2)}) collective-permute-start(bf16[2,256,128]{2,1,0:T(8,128)(2,1)S(1)} %bitcast.23), channel_id=1, source_target_pairs={{0,4},{1,21},{2,38},{3,55},{4,8},{5,25},{6,42},{7,59},{8,5},{9,22}... | collective-permute-start | bytes 393224 | tf_op jit(solution)/shard_map/ppermute | solution.py:40
  19.7 13.6 %collective-permute-start.5 = (bf16[27,32,128]{2,1,0:T(8,128)(2,1)}, bf16[27,32,128]{2,1,0:T(8,128)(2,1)S(1)}, u32[]{:S(2)}, u32[]{:S(2)}) collective-permute-start(bf16[27,32,128]{2,1,0:T(8,128)(2,1)} %bitcast.27), channel_id=1, source_target_pairs={{0,0},{1,1},{2,2},{3,3},{4,4},{5,5},{6,6},{7,7},{8,128},{9,129},{1... | collective-permute-start | bytes 663560 | tf_op jit(solution)/shard_map/ppermute | solution.py:40
  26.5 12.0 %collective-permute-start.4 = (bf16[4,256,128]{2,1,0:T(8,128)(2,1)S(1)}, bf16[4,256,128]{2,1,0:T(8,128)(2,1)S(1)}, u32[]{:S(2)}, u32[]{:S(2)}) collective-permute-start(bf16[4,256,128]{2,1,0:T(8,128)(2,1)S(1)} %constant_dynamic-update-slice_fusion.refs_0_), channel_id=1, source_target_pairs={{0,1},{1,2},{2,3},{3,4},{4,5},{5,6},{6,7},{7,0},{8,9},{9,10},{10,1... | collective-permute-start | bytes 786440 | tf_op jit(solution)/shard_map/ppermute | solution.py:40
  26.5 11.9 %collective-permute-start.3 = (bf16[4,256,128]{2,1,0:T(8,128)(2,1)S(1)}, bf16[4,256,128]{2,1,0:T(8,128)(2,1)S(1)}, u32[]{:S(2)}, u32[]{:S(2)}) collective-permute-start(bf16[4,256,128]{2,1,0:T(8,128)(2,1)S(1)} %constant_dynamic-update-slice_fusion.refs_0_), channel_id=1, source_target_pairs={{0,7},{1,0},{2,1},{3,2},{4,3},{5,4},{6,5},{7,6},{8,15},{9,8},{10,9... | collective-permute-start | bytes 786440 | tf_op jit(solution)/shard_map/ppermute | solution.py:40
  33.3 12.9 %collective-permute-start.9 = (bf16[27,32,128]{2,1,0:T(8,128)(2,1)S(1)}, bf16[27,32,128]{2,1,0:T(8,128)(2,1)S(1)}, u32[]{:S(2)}, u32[]{:S(2)}) collective-permute-start(bf16[27,32,128]{2,1,0:T(8,128)(2,1)S(1)} %collective-permute-done.5.refs_1_), channel_id=1, source_target_pairs={{0,64},{1,65},{2,66},{3,67},{4,68},{5,69},{6,70},{7,71},{8,72},{9,... | collective-permute-start | bytes 663560 | tf_op jit(solution)/shard_map/ppermute | solution.py:40
  34.2 11.9 %collective-permute-start.8 = (bf16[27,32,128]{2,1,0:T(8,128)(2,1)S(1)}, bf16[27,32,128]{2,1,0:T(8,128)(2,1)S(1)}, u32[]{:S(2)}, u32[]{:S(2)}) collective-permute-start(bf16[27,32,128]{2,1,0:T(8,128)(2,1)S(1)} %collective-permute-done.5.refs_1_), channel_id=1, source_target_pairs={{0,192},{1,193},{2,194},{3,195},{4,196},{5,197},{6,198},{7,199},{8... | collective-permute-start | bytes 663560 | tf_op jit(solution)/shard_map/ppermute | solution.py:40
  36.5 9.6 %collective-permute-start.10 = (bf16[27,32,128]{2,1,0:T(8,128)(2,1)S(1)}, bf16[27,32,128]{2,1,0:T(8,128)(2,1)S(1)}, u32[]{:S(2)}, u32[]{:S(2)}) collective-permute-start(bf16[27,32,128]{2,1,0:T(8,128)(2,1)S(1)} %collective-permute-done.5.refs_1_), channel_id=1, source_target_pairs={{0,128},{1,129},{2,130},{3,131},{4,132},{5,133},{6,134},{7,135},{8... | collective-permute-start | bytes 663560 | tf_op jit(solution)/shard_map/ppermute | solution.py:40
  38.5 6.3 %collective-permute-start.7 = (bf16[2,256,128]{2,1,0:T(8,128)(2,1)S(1)}, bf16[2,256,128]{2,1,0:T(8,128)(2,1)S(1)}, u32[]{:S(2)}, u32[]{:S(2)}) collective-permute-start(bf16[2,256,128]{2,1,0:T(8,128)(2,1)S(1)} %slice.75), channel_id=1, source_target_pairs={{0,1},{1,2},{2,3},{3,4},{4,5},{5,6},{6,7},{7,0},{8,9},{9,10},{10,1... | collective-permute-start | bytes 393224 | tf_op jit(solution)/shard_map/ppermute | solution.py:40
  38.5 6.2 %collective-permute-start.6 = (bf16[2,256,128]{2,1,0:T(8,128)(2,1)S(1)}, bf16[2,256,128]{2,1,0:T(8,128)(2,1)S(1)}, u32[]{:S(2)}, u32[]{:S(2)}) collective-permute-start(bf16[2,256,128]{2,1,0:T(8,128)(2,1)S(1)} %slice.74), channel_id=1, source_target_pairs={{0,7},{1,0},{2,1},{3,2},{4,3},{5,4},{6,5},{7,6},{8,15},{9,8},{10,9... | collective-permute-start | bytes 393224 | tf_op jit(solution)/shard_map/ppermute | solution.py:40
  50.2 3.3 %collective-permute-start.11 = (bf16[8,256,128]{2,1,0:T(8,128)(2,1)S(1)}, bf16[8,256,128]{2,1,0:T(8,128)(2,1)S(1)}, u32[]{:S(2)}, u32[]{:S(2)}) collective-permute-start(bf16[8,256,128]{2,1,0:T(8,128)(2,1)S(1)} %shard_map.77), channel_id=1, source_target_pairs={{0,8},{1,9},{2,10},{3,11},{4,12},{5,13},{6,14},{7,15},{8,0},{9,1},... | collective-permute-start | bytes 1572872 | tf_op jit(solution)/shard_map/ppermute | solution.py:40
  53.5 10.6 %copy-start = (f32[128]{0:T(128)S(1)}, f32[128]{0:T(128)}, u32[]{:S(2)}) copy-start(f32[128]{0:T(128)} %param.6) | copy-start | bytes 1540
  53.7 7.9 %collective-permute-start.12 = (bf16[2,256,128]{2,1,0:T(8,128)(2,1)S(1)}, bf16[2,256,128]{2,1,0:T(8,128)(2,1)S(1)}, u32[]{:S(2)}, u32[]{:S(2)}) collective-permute-start(bf16[2,256,128]{2,1,0:T(8,128)(2,1)S(1)} %get-tuple-element.84), channel_id=1, source_target_pairs={{0,32},{1,33},{2,34},{3,35},{4,36},{5,37},{6,38},{7,39},{8,40},{9,... | collective-permute-start | bytes 393224 | tf_op jit(solution)/shard_map/ppermute | solution.py:40
  53.8 9.1 %collective-permute-start.14 = (bf16[2,256,128]{2,1,0:T(8,128)(2,1)S(1)}, bf16[2,256,128]{2,1,0:T(8,128)(2,1)S(1)}, u32[]{:S(2)}, u32[]{:S(2)}) collective-permute-start(bf16[2,256,128]{2,1,0:T(8,128)(2,1)S(1)} %get-tuple-element.85), channel_id=1, source_target_pairs={{0,48},{1,49},{2,50},{3,51},{4,52},{5,53},{6,54},{7,55},{8,56},{9,... | collective-permute-start | bytes 393224 | tf_op jit(solution)/shard_map/ppermute | solution.py:40
  54.8 9.1 %collective-permute-start.13 = (bf16[2,256,128]{2,1,0:T(8,128)(2,1)S(1)}, bf16[2,256,128]{2,1,0:T(8,128)(2,1)S(1)}, u32[]{:S(2)}, u32[]{:S(2)}) collective-permute-start(bf16[2,256,128]{2,1,0:T(8,128)(2,1)S(1)} %get-tuple-element.86), channel_id=1, source_target_pairs={{0,16},{1,17},{2,18},{3,19},{4,20},{5,21},{6,22},{7,23},{8,24},{9,... | collective-permute-start | bytes 393224 | tf_op jit(solution)/shard_map/ppermute | solution.py:40
  64.3 6.4 %collective-permute-start.17 = (bf16[2,256,128]{2,1,0:T(8,128)(2,1)S(1)}, bf16[2,256,128]{2,1,0:T(8,128)(2,1)S(1)}, u32[]{:S(2)}, u32[]{:S(2)}) collective-permute-start(bf16[2,256,128]{2,1,0:T(8,128)(2,1)S(1)} %get-tuple-element.87.refs_2_.refs_0_), channel_id=1, source_target_pairs={{0,48},{1,49},{2,50},{3,51},{4,52},{5,53},{6,54},{7,55},{8,56},{9,... | collective-permute-start | bytes 393224 | tf_op jit(solution)/shard_map/ppermute | solution.py:40
  65.0 7.9 %collective-permute-start.16 = (bf16[2,256,128]{2,1,0:T(8,128)(2,1)S(1)}, bf16[2,256,128]{2,1,0:T(8,128)(2,1)S(1)}, u32[]{:S(2)}, u32[]{:S(2)}) collective-permute-start(bf16[2,256,128]{2,1,0:T(8,128)(2,1)S(1)} %get-tuple-element.87.refs_2_.refs_0_), channel_id=1, source_target_pairs={{0,32},{1,33},{2,34},{3,35},{4,36},{5,37},{6,38},{7,39},{8,40},{9,... | collective-permute-start | bytes 393224 | tf_op jit(solution)/shard_map/ppermute | solution.py:40
  66.1 7.7 %collective-permute-start.15 = (bf16[2,256,128]{2,1,0:T(8,128)(2,1)S(1)}, bf16[2,256,128]{2,1,0:T(8,128)(2,1)S(1)}, u32[]{:S(2)}, u32[]{:S(2)}) collective-permute-start(bf16[2,256,128]{2,1,0:T(8,128)(2,1)S(1)} %get-tuple-element.87.refs_2_.refs_0_), channel_id=1, source_target_pairs={{0,16},{1,17},{2,18},{3,19},{4,20},{5,21},{6,22},{7,23},{8,24},{9,... | collective-permute-start | bytes 393224 | tf_op jit(solution)/shard_map/ppermute | solution.py:40
  67.8 6.6 %collective-permute-start.18 = (bf16[2,256,128]{2,1,0:T(8,128)(2,1)S(1)}, bf16[2,256,128]{2,1,0:T(8,128)(2,1)S(1)}, u32[]{:S(2)}, u32[]{:S(2)}) collective-permute-start(bf16[2,256,128]{2,1,0:T(8,128)(2,1)S(1)} %get-tuple-element.87.refs_2_.refs_0_), channel_id=1, source_target_pairs={{0,8},{1,9},{2,10},{3,11},{4,12},{5,13},{6,14},{7,15},{8,0},{9,1},... | collective-permute-start | bytes 393224 | tf_op jit(solution)/shard_map/ppermute | solution.py:40
  70.7 3.7 %collective-permute-start.21 = (bf16[2,256,128]{2,1,0:T(8,128)(2,1)S(1)}, bf16[2,256,128]{2,1,0:T(8,128)(2,1)S(1)}, u32[]{:S(2)}, u32[]{:S(2)}) collective-permute-start(bf16[2,256,128]{2,1,0:T(8,128)(2,1)S(1)} %collective-permute-done.17.refs_5_.refs_3_), channel_id=1, source_target_pairs={{0,8},{1,9},{2,10},{3,11},{4,12},{5,13},{6,14},{7,15},{8,0},{9,1},... | collective-permute-start | bytes 393224 | tf_op jit(solution)/shard_map/ppermute | solution.py:40
  72.9 1.5 %collective-permute-start.20 = (bf16[2,256,128]{2,1,0:T(8,128)(2,1)S(1)}, bf16[2,256,128]{2,1,0:T(8,128)(2,1)S(1)}, u32[]{:S(2)}, u32[]{:S(2)}) collective-permute-start(bf16[2,256,128]{2,1,0:T(8,128)(2,1)S(1)} %collective-permute-done.16.refs_4_.refs_2_), channel_id=1, source_target_pairs={{0,8},{1,9},{2,10},{3,11},{4,12},{5,13},{6,14},{7,15},{8,0},{9,1},... | collective-permute-start | bytes 393224 | tf_op jit(solution)/shard_map/ppermute | solution.py:40
  73.8 1.3 %collective-permute-start.19 = (bf16[2,256,128]{2,1,0:T(8,128)(2,1)S(1)}, bf16[2,256,128]{2,1,0:T(8,128)(2,1)S(1)}, u32[]{:S(2)}, u32[]{:S(2)}) collective-permute-start(bf16[2,256,128]{2,1,0:T(8,128)(2,1)S(1)} %collective-permute-done.15.refs_3_.refs_1_), channel_id=1, source_target_pairs={{0,8},{1,9},{2,10},{3,11},{4,12},{5,13},{6,14},{7,15},{8,0},{9,1},... | collective-permute-start | bytes 393224 | tf_op jit(solution)/shard_map/ppermute | solution.py:40
  73.8 6.6 %collective-permute-start.22 = (bf16[256,128]{1,0:T(8,128)(2,1)S(1)}, bf16[256,128]{1,0:T(8,128)(2,1)S(1)}, u32[]{:S(2)}, u32[]{:S(2)}) collective-permute-start(bf16[256,128]{1,0:T(8,128)(2,1)S(1)} %get-tuple-element.94), channel_id=1, source_target_pairs={{0,8},{1,9},{2,10},{3,11},{4,12},{5,13},{6,14},{7,15},{8,16},{9,17... | collective-permute-start | bytes 196616 | tf_op jit(solution)/shard_map/ppermute | solution.py:40
  80.4 21.8 %collective-permute-start.29 = (bf16[28,32,128]{2,1,0:T(8,128)(2,1)S(1)}, bf16[28,32,128]{2,1,0:T(8,128)(2,1)S(1)}, u32[]{:S(2)}, u32[]{:S(2)}) collective-permute-start(bf16[28,32,128]{2,1,0:T(8,128)(2,1)S(1)} %get-tuple-element.79), channel_id=1, source_target_pairs={{0,128},{1,129},{2,130},{3,131},{4,132},{5,133},{6,134},{7,135},{8... | collective-permute-start | bytes 688136 | tf_op jit(solution)/shard_map/ppermute | solution.py:40
  87.7 10.5 %collective-permute-start.23 = (bf16[4,256,128]{2,1,0:T(8,128)(2,1)S(1)}, bf16[4,256,128]{2,1,0:T(8,128)(2,1)S(1)}, u32[]{:S(2)}, u32[]{:S(2)}) collective-permute-start(bf16[4,256,128]{2,1,0:T(8,128)(2,1)S(1)} %get-tuple-element.74), channel_id=1, source_target_pairs={{0,1},{1,2},{2,3},{3,4},{4,5},{5,6},{6,7},{7,0},{8,9},{9,10},{10,1... | collective-permute-start | bytes 786440 | tf_op jit(solution)/shard_map/ppermute | solution.py:40
  87.8 10.5 %collective-permute-start.24 = (bf16[4,256,128]{2,1,0:T(8,128)(2,1)S(1)}, bf16[4,256,128]{2,1,0:T(8,128)(2,1)S(1)}, u32[]{:S(2)}, u32[]{:S(2)}) collective-permute-start(bf16[4,256,128]{2,1,0:T(8,128)(2,1)S(1)} %get-tuple-element.75), channel_id=1, source_target_pairs={{0,7},{1,0},{2,1},{3,2},{4,3},{5,4},{6,5},{7,6},{8,15},{9,8},{10,9... | collective-permute-start | bytes 786440 | tf_op jit(solution)/shard_map/ppermute | solution.py:40
  94.2 10.4 %collective-permute-start.30 = (bf16[28,32,128]{2,1,0:T(8,128)(2,1)S(1)}, bf16[28,32,128]{2,1,0:T(8,128)(2,1)S(1)}, u32[]{:S(2)}, u32[]{:S(2)}) collective-permute-start(bf16[28,32,128]{2,1,0:T(8,128)(2,1)S(1)} %get-tuple-element.80), channel_id=1, source_target_pairs={{0,64},{1,65},{2,66},{3,67},{4,68},{5,69},{6,70},{7,71},{8,72},{9,... | collective-permute-start | bytes 688136 | tf_op jit(solution)/shard_map/ppermute | solution.py:40
  95.2 9.5 %collective-permute-start.31 = (bf16[28,32,128]{2,1,0:T(8,128)(2,1)S(1)}, bf16[28,32,128]{2,1,0:T(8,128)(2,1)S(1)}, u32[]{:S(2)}, u32[]{:S(2)}) collective-permute-start(bf16[28,32,128]{2,1,0:T(8,128)(2,1)S(1)} %get-tuple-element.81), channel_id=1, source_target_pairs={{0,192},{1,193},{2,194},{3,195},{4,196},{5,197},{6,198},{7,199},{8... | collective-permute-start | bytes 688136 | tf_op jit(solution)/shard_map/ppermute | solution.py:40
  98.3 11.6 %collective-permute-start.25 = (bf16[2,256,128]{2,1,0:T(8,128)(2,1)S(1)}, bf16[2,256,128]{2,1,0:T(8,128)(2,1)S(1)}, u32[]{:S(2)}, u32[]{:S(2)}) collective-permute-start(bf16[2,256,128]{2,1,0:T(8,128)(2,1)S(1)} %get-tuple-element.89), channel_id=1, source_target_pairs={{0,4},{1,5},{2,6},{3,7},{4,0},{5,1},{6,2},{7,3},{8,12},{9,13},{10,... | collective-permute-start | bytes 393224 | tf_op jit(solution)/shard_map/ppermute | solution.py:40
  101.4 9.3 %collective-permute-start.26 = (bf16[2,256,128]{2,1,0:T(8,128)(2,1)S(1)}, bf16[2,256,128]{2,1,0:T(8,128)(2,1)S(1)}, u32[]{:S(2)}, u32[]{:S(2)}) collective-permute-start(bf16[2,256,128]{2,1,0:T(8,128)(2,1)S(1)} %get-tuple-element.90), channel_id=1, source_target_pairs={{0,1},{1,2},{2,3},{3,4},{4,5},{5,6},{6,7},{7,0},{8,9},{9,10},{10,1... | collective-permute-start | bytes 393224 | tf_op jit(solution)/shard_map/ppermute | solution.py:40
  102.2 8.5 %collective-permute-start.27 = (bf16[2,256,128]{2,1,0:T(8,128)(2,1)S(1)}, bf16[2,256,128]{2,1,0:T(8,128)(2,1)S(1)}, u32[]{:S(2)}, u32[]{:S(2)}) collective-permute-start(bf16[2,256,128]{2,1,0:T(8,128)(2,1)S(1)} %get-tuple-element.91), channel_id=1, source_target_pairs={{0,7},{1,0},{2,1},{3,2},{4,3},{5,4},{6,5},{7,6},{8,15},{9,8},{10,9... | collective-permute-start | bytes 393224 | tf_op jit(solution)/shard_map/ppermute | solution.py:40
  104.8 16.2 %collective-permute-start.32 = (bf16[27,32,128]{2,1,0:T(8,128)(2,1)S(1)}, bf16[27,32,128]{2,1,0:T(8,128)(2,1)S(1)}, u32[]{:S(2)}, u32[]{:S(2)}) collective-permute-start(bf16[27,32,128]{2,1,0:T(8,128)(2,1)S(1)} %slice.138), channel_id=1, source_target_pairs={{0,0},{1,1},{2,2},{3,3},{4,4},{5,5},{6,6},{7,7},{8,128},{9,129},{1... | collective-permute-start | bytes 663560 | tf_op jit(solution)/shard_map/ppermute | solution.py:40
  110.8 11.0 %collective-permute-start.28 = (bf16[256,128]{1,0:T(8,128)(2,1)S(1)}, bf16[256,128]{1,0:T(8,128)(2,1)S(1)}, u32[]{:S(2)}, u32[]{:S(2)}) collective-permute-start(bf16[256,128]{1,0:T(8,128)(2,1)S(1)} %get-tuple-element.92), channel_id=1, source_target_pairs={{0,8},{1,16},{2,24},{3,32},{4,40},{5,48},{6,56},{7,64},{8,44},{9,5... | collective-permute-start | bytes 196616 | tf_op jit(solution)/shard_map/ppermute | solution.py:40
  115.7 12.5 %collective-permute-start.33 = (bf16[256,128]{1,0:T(8,128)(2,1)S(1)}, bf16[256,128]{1,0:T(8,128)(2,1)S(1)}, u32[]{:S(2)}, u32[]{:S(2)}) collective-permute-start(bf16[256,128]{1,0:T(8,128)(2,1)S(1)} %get-tuple-element.93), channel_id=1, source_target_pairs={{0,0},{1,8},{2,16},{3,24},{4,32},{5,40},{6,48},{7,56},{8,36},{9,44... | collective-permute-start | bytes 196616 | tf_op jit(solution)/shard_map/ppermute | solution.py:40
